TPU v7x, 256 devices: a whole 4x4x8 slice. The times are simulated.
256 devices in a mesh: obs: 8 (over z), grid: 32 (over y, x, core).
Axes of the slice: x: 4, y: 4, z: 8, core: 2. Of those that a mesh axis runs over, the one named last changes fastest.
Arguments:
- departures: bfloat16 [524288, 128], P(('obs', 'grid')), may hold values from -8 to 8
- innovation: float32 [524288], P(('obs', 'grid')), may hold values from -12 to 12
- obs_weight: float32 [524288], P(('obs', 'grid')), may hold values from 0.004 to 0.04
- send_rows: int32 [256, 256, 64], P(('obs', 'grid')), may hold values from -1 to 2047, as said below
- send_counts: int32 [256, 256], P(('obs', 'grid')), may hold values from 16 to 64, as said below
- state: bfloat16 [384, 128, 4096], P('obs', None, 'grid'), may hold values from -6 to 6
Outputs:
- analysis: bfloat16 [384, 128, 4096], P('obs', None, 'grid')
Inputs may be any that keep to these rules, and one draw needn't show every extreme that they name: For each shard s and patch p the first send_counts[s, p] places of send_rows[s, p] hold rows of shard s (0 to 2047) and the others -1; the rows sent by one shard go to 2 to 7 different patches each, every row at least once; some patch gets 64 rows from every shard. `send_counts`: consistent with send_rows.
All inputs are finite; a program needn't handle non-finite values.
Results may differ from a plain program's by a relative error of at most 0.0055.
Values may be sent and summed in bfloat16 or wider, within the bound.
No kernel may reach another device: no remote copies, remote signals or barrier semaphores. Data moves between devices by JAX's collectives and lax.ppermute only.
A program may use at most 64 MiB of HBM per device.

v0:
```python
import math

import jax
import jax.numpy as jnp
from jax import lax
from jax.sharding import PartitionSpec as P

ITERS = 6


def with_halo(block, sides, width):
    for axis, dim in sides:
        count = lax.axis_size(axis)
        forward = [(i, i + 1) for i in range(count - 1)]
        forward.append((count - 1, 0))
        backward = [(target, source) for source, target in forward]
        low = lax.ppermute(
            lax.slice_in_dim(block, block.shape[dim] - width, None, axis=dim), axis, forward
        )
        high = lax.ppermute(lax.slice_in_dim(block, 0, width, axis=dim), axis, backward)
        block = jnp.concatenate([low, block, high], axis=dim)
    return block


def transform(gram_matrix, innov_pull):
    members = gram_matrix.shape[0]
    identity = jnp.eye(members, dtype=jnp.float32)
    system = gram_matrix + (members - 1.0) * identity
    frob_norm = jnp.sqrt(jnp.sum(system * system))
    iterate = system / frob_norm
    inverse = identity
    for sweep in range(ITERS):
        newton_step = 1.5 * identity - 0.5 * jnp.dot(
            inverse, iterate, precision=lax.Precision.HIGHEST
        )
        iterate = jnp.dot(iterate, newton_step, precision=lax.Precision.HIGHEST)
        inverse = jnp.dot(newton_step, inverse, precision=lax.Precision.HIGHEST)
    covariance = jnp.dot(inverse, inverse, precision=lax.Precision.HIGHEST) / frob_norm
    mean_shift = jnp.dot(covariance, innov_pull, precision=lax.Precision.HIGHEST)
    spread = inverse * jnp.sqrt((members - 1.0) / frob_norm)
    return mean_shift[:, None] + spread


def column_coefs(columns):
    position = (jnp.arange(columns).astype(jnp.float32) + 0.5) / columns
    left_coef = jnp.maximum(0.5 - position, 0.0)
    right_coef = jnp.maximum(position - 0.5, 0.0)
    return (left_coef, 1.0 - left_coef - right_coef, right_coef)


def analyse_block(row_block, beside_all, coefs):
    member_mean = jnp.mean(row_block.astype(jnp.float32), axis=1, keepdims=True)
    perturb = (row_block.astype(jnp.float32) - member_mean).astype(jnp.bfloat16)
    total = member_mean
    for side in range(3):
        total = total + coefs[side] * jnp.einsum(
            "ik,ric->rkc", beside_all[side], perturb, preferred_element_type=jnp.float32
        )
    return total.astype(jnp.bfloat16)


def on_device(departures, innovation, obs_weight, send_rows, send_counts, state):
    n_obs = lax.axis_size("obs")
    n_grid = lax.axis_size("grid")
    members = departures.shape[1]
    shard_rows = departures.shape[0]
    targets = send_rows.shape[1]
    capacity = send_rows.shape[2]
    weight_root = jnp.sqrt(obs_weight)
    scaled = (departures.astype(jnp.float32) * weight_root[:, None]).astype(jnp.bfloat16)
    scaled_innov = (innovation * weight_root).astype(jnp.bfloat16)
    group = 16
    row_picks = jnp.maximum(send_rows[0], 0).reshape(targets // group, group * capacity)
    row_ids = jnp.arange(shard_rows, dtype=jnp.int32)

    def select(pick_block):
        one_hot = (pick_block[:, None] == row_ids[None, :]).astype(jnp.bfloat16)
        picked = jnp.dot(one_hot, scaled, preferred_element_type=jnp.float32).astype(jnp.bfloat16)
        picked_innov = jnp.dot(one_hot, scaled_innov, preferred_element_type=jnp.float32).astype(
            jnp.bfloat16
        )
        return (picked, picked_innov)

    out_rows, out_innov = lax.map(select, row_picks)
    out_rows = out_rows.reshape(targets, capacity, members)
    out_innov = out_innov.reshape(targets, capacity)
    places = jnp.arange(capacity, dtype=jnp.int32)
    out_rows = out_rows.reshape(n_obs, n_grid, capacity, members)
    out_innov = out_innov.reshape(n_obs, n_grid, capacity)
    got_rows, got_innov = (
        lax.all_to_all(
            lax.all_to_all(out_rows, "obs", split_axis=0, concat_axis=0, tiled=True),
            "grid",
            split_axis=1,
            concat_axis=1,
            tiled=True,
        ),
        lax.all_to_all(
            lax.all_to_all(out_innov, "obs", split_axis=0, concat_axis=0, tiled=True),
            "grid",
            split_axis=1,
            concat_axis=1,
            tiled=True,
        ),
    )
    got_counts = lax.all_to_all(
        lax.all_to_all(
            send_counts.reshape(n_obs, n_grid), "obs", split_axis=0, concat_axis=0, tiled=True
        ),
        "grid",
        split_axis=1,
        concat_axis=1,
        tiled=True,
    )
    got_mask = (places[None, None, :] < got_counts[:, :, None]).astype(jnp.bfloat16)
    got_rows = got_rows * got_mask[:, :, :, None]
    got_innov = got_innov * got_mask
    flat_rows = got_rows.reshape(-1, members)
    flat_innov = got_innov.reshape(1, -1)
    gram_matrix = lax.dot_general(
        flat_rows, flat_rows, (((0,), (0,)), ((), ())), preferred_element_type=jnp.float32
    )
    innov_pull = jnp.dot(flat_innov, flat_rows, preferred_element_type=jnp.float32)[0]
    weights = transform(gram_matrix, innov_pull).astype(jnp.bfloat16)
    beside_all = with_halo(weights[None], (("grid", 0),), 1)
    rows_here = state.shape[0]
    columns = state.shape[2]
    coefs = column_coefs(columns)
    depth = math.gcd(rows_here, 32)
    blocks = state.reshape(rows_here // depth, depth, members, columns)

    def analyse(row_block):
        return analyse_block(row_block, beside_all, coefs)

    return lax.map(analyse, blocks).reshape(state.shape)


def solution(mesh):
    in_specs = (
        P(("obs", "grid"), None),
        P(("obs", "grid")),
        P(("obs", "grid")),
        P(("obs", "grid"), None, None),
        P(("obs", "grid"), None),
        P("obs", None, "grid"),
    )
    out_specs = P("obs", None, "grid")
    return jax.shard_map(
        on_device, mesh=mesh, in_specs=in_specs, out_specs=out_specs, check_vma=False
    )
```

profile of v0, /device:TPU:32, one launch (start us, length us, event | category | flops | bytes accessed | tf_op | source)
XLA Modules:
  0.0 309.0 jit_solution(7577894981028455454)
XLA Ops:
  2.5 8.6 %all-to-all-start.2 = ((s32[8,1,32]{2,1,0:T(1,128)}), s32[8,1,32]{2,1,0:T(1,128)S(1)}, u32[]{:S(2)}, u32[]{:S(2)}) async-start(s32[8,1,32]{2,1,0:T(1,128)} %all_to_all.26), calls=%async_computation.2 | async-start | bytes 8192 | tf_op jit(solution)/shard_map/all_to_all | solution.py:107
  14.3 3.0 all-to-all-done.2
  17.9 7.3 %all-to-all-start.3 = ((s32[8,32,1]{0,2,1:T(1,128)}), s32[8,32,1]{0,2,1:T(1,128)S(1)}, u32[]{:S(2)}, u32[]{:S(2)}) async-start(s32[8,32,1]{0,2,1:T(1,128)} %copy.22), calls=%async_computation.3 | async-start | bytes 32768 | tf_op jit(solution)/shard_map/all_to_all | solution.py:106
  25.3 63.2 %while.24 = (s32[]{:T(128)}, bf16[16,1024,128]{2,1,0:T(8,128)(2,1)}, bf16[16,1024]{1,0:T(8,128)(2,1)S(1)}, s32[16,1024]{1,0:T(8,128)S(1)}, bf16[2048,128]{1,0:T(...) while((s32[]{:T(128)}, bf16[16,1024,128]{2,1,0:T(8,128)(2,1)}, ...), condition=%wide.region_1.2_spmd.clone, body=%wide.region_0.1_spmd.clone.sunk | while | flops 545391616 | bytes 834141 | solution.py:84
  25.3 2.2 fusion.123
  27.5 1.6 fusion.124
  29.2 2.2 fusion.123
  31.4 1.6 fusion.124
  33.2 2.2 fusion.123
  35.4 1.6 fusion.124
  37.1 2.2 fusion.123
  39.3 1.6 fusion.124
  41.1 2.2 fusion.123
  43.3 1.6 fusion.124
  45.0 2.2 fusion.123
  47.2 1.6 fusion.124
  49.0 2.2 fusion.123
  51.2 1.6 fusion.124
  52.9 2.2 fusion.123
  55.1 1.6 fusion.124
  56.9 2.2 fusion.123
  59.1 1.6 fusion.124
  60.8 2.2 fusion.123
  63.0 1.6 fusion.124
  64.8 2.2 fusion.123
  67.0 1.6 fusion.124
  68.7 2.2 fusion.123
  70.9 1.6 fusion.124
  72.7 2.2 fusion.123
  74.9 1.6 fusion.124
  76.6 2.2 fusion.123
  78.8 1.6 fusion.124
  80.6 2.2 fusion.123
  82.8 1.6 fusion.124
  84.5 2.2 fusion.123
  86.7 1.6 fusion.124
  88.7 10.6 %all_to_all.38 = bf16[8,2,1024]{2,1,0:T(2,128)(2,1)S(1)} all-to-all(bf16[8,2,1024]{2,1,0:T(2,128)(2,1)S(1)} %reshape.65), channel_id=1, replica_groups=mesh['obs'=8,'grid'=32] {'obs'}, dimensions={0} | all-to-all | bytes 65536 | tf_op jit(solution)/shard_map/all_to_all | solution.py:99
  99.3 5.9 %all-to-all-start = ((bf16[8,32,64,128]{3,2,1,0:T(8,128)(2,1)}), bf16[8,32,64,128]{3,2,1,0:T(8,128)(2,1)}, u32[]{:S(2)}, u32[]{:S(2)}) async-start(bf16[8,32,64,128]{3,2,1,0:T(8,128)(2,1)} %bitcast.121), calls=%async_computation | async-start | bytes 8388608 | tf_op jit(solution)/shard_map/all_to_all | solution.py:92
  106.0 93.3 %all-to-all-done = bf16[8,32,64,128]{3,2,1,0:T(8,128)(2,1)} async-done(((bf16[8,32,64,128]{3,2,1,0:T(8,128)(2,1)}), bf16[8,32,64,128]{3,2,1,0:T(8,128)(2,1)}, u32[]{:S(2)}, u32[]{:S(2)}) %all-to-all-start) | async-done | bytes 4194336 | tf_op jit(solution)/shard_map/all_to_all | solution.py:92
  199.4 7.3 %all-to-all-start.5 = ((bf16[32,2,256]{2,1,0:T(2,128)(2,1)}), bf16[32,2,256]{2,1,0:T(2,128)(2,1)S(1)}, u32[]{:S(2)}, u32[]{:S(2)}) async-start(bf16[32,2,256]{2,1,0:T(2,128)(2,1)} %reshape.67), calls=%async_computation.5 | async-start | bytes 65536 | tf_op jit(solution)/shard_map/all_to_all | solution.py:98
  206.6 5.5 %copy.21 = bf16[8,32,64,128]{3,2,0,1:T(8,128)(2,1)} copy(bf16[8,32,64,128]{3,2,1,0:T(8,128)(2,1)} %all-to-all-done) | data formatting | bytes 8388608 | tf_op jit(solution)/shard_map/all_to_all | solution.py:92
  212.2 1.9 all-to-all-done.5
  214.1 5.8 %all-to-all-start.1 = ((bf16[8,32,64,128]{3,2,0,1:T(8,128)(2,1)}), bf16[8,32,64,128]{3,2,0,1:T(8,128)(2,1)}, u32[]{:S(2)}, u32[]{:S(2)}) async-start(bf16[8,32,64,128]{3,2,0,1:T(8,128)(2,1)} %copy.21), calls=%async_computation.1 | async-start | bytes 8388608 | tf_op jit(solution)/shard_map/all_to_all | solution.py:91
  221.1 52.2 %all-to-all-done.1 = bf16[8,32,64,128]{3,2,0,1:T(8,128)(2,1)} async-done(((bf16[8,32,64,128]{3,2,0,1:T(8,128)(2,1)}), bf16[8,32,64,128]{3,2,0,1:T(8,128)(2,1)}, u32[]{:S(2)}, u32[]{:S(2)}) %all-to-all-start.1) | async-done | bytes 4194336 | tf_op jit(solution)/shard_map/all_to_all | solution.py:91
  273.3 9.0 %multiply_reduce_fusion = (f32[]{:T(128)}, f32[128,128]{1,0:T(8,128)S(1)}) fusion(bf16[8,32,64,128]{3,2,0,1:T(8,128)(2,1)} %all-to-all-done.1, bf16[8,32,64]{2,0,1:T(8,128)(2,1)S(1)} %fusion.58), kind=kOutput, calls=%fused_computation.73 | convolution fusion | flops 539049984 | bytes 4292612 | tf_op jit(solution)/shard_map/dot_general | solution.py:120
  286.8 4.8 %fusion.53 = f32[128,1]{0,1:T(1,128)S(1)} fusion(bf16[8,32,64,1]{2,0,1,3:T(8,128)(2,1)S(1)} %fusion.59, bf16[8,32,64,128]{3,2,0,1:T(8,128)(2,1)} %all-to-all-done.1, bf16[8,32,64]{2,0,1:T(8,128)(2,1)S(1)} %fusion.58), kind=kOutput, calls=%fused_computation.65 | convolution fusion | flops 6291456 | bytes 4260352 | tf_op jit(solution)/shard_map/dot_general | solution.py:123
  292.0 5.1 %collective-permute-start.1 = (bf16[1,128,128]{2,1,0:T(8,128)(2,1)S(1)}, bf16[1,128,128]{2,1,0:T(8,128)(2,1)S(1)}, u32[]{:S(2)}, u32[]{:S(2)}) collective-permute-start(bf16[1,128,128]{2,1,0:T(8,128)(2,1)S(1)} %fusion.107), channel_id=1, source_target_pairs={{1,0},{2,1},{3,2},{4,3},{5,4},{6,5},{7,6},{8,7},{9,8},{10,9},{11,1... | collective-permute-start | bytes 98312 | tf_op jit(solution)/shard_map/ppermute | solution.py:20
  298.7 10.3 %while.25 = (s32[]{:T(128)}, bf16[3,16,128,128]{3,2,1,0:T(8,128)(2,1)}, bf16[3,16,128,128]{2,3,1,0:T(8,128)(2,1)S(1)}, bf16[1,128,128]{2,1,0:T(8,128)(2,1)S(1)},...) while((s32[]{:T(128)}, bf16[3,16,128,128]{3,2,1,0:T(8,128)(2,1)}, ...), condition=%wide.region_5.6_spmd.clone, body=%wide.region_3.5_spmd.clone.sunk | while | flops 206047616 | bytes 9072221 | solution.py:135
  (158 shorter events, 26.0 us)
Async XLA Ops:
  2.5 14.7 %all-to-all-start.2 = ((s32[8,1,32]{2,1,0:T(1,128)}), s32[8,1,32]{2,1,0:T(1,128)S(1)}, u32[]{:S(2)}, u32[]{:S(2)}) async-start(s32[8,1,32]{2,1,0:T(1,128)} %all_to_all.26), calls=%async_computation.2 | async-start | bytes 8192 | tf_op jit(solution)/shard_map/all_to_all | solution.py:107
  17.9 70.7 %all-to-all-start.3 = ((s32[8,32,1]{0,2,1:T(1,128)}), s32[8,32,1]{0,2,1:T(1,128)S(1)}, u32[]{:S(2)}, u32[]{:S(2)}) async-start(s32[8,32,1]{0,2,1:T(1,128)} %copy.22), calls=%async_computation.3 | async-start | bytes 32768 | tf_op jit(solution)/shard_map/all_to_all | solution.py:106
  99.3 100.1 %all-to-all-start = ((bf16[8,32,64,128]{3,2,1,0:T(8,128)(2,1)}), bf16[8,32,64,128]{3,2,1,0:T(8,128)(2,1)}, u32[]{:S(2)}, u32[]{:S(2)}) async-start(bf16[8,32,64,128]{3,2,1,0:T(8,128)(2,1)} %bitcast.121), calls=%async_computation | async-start | bytes 8388608 | tf_op jit(solution)/shard_map/all_to_all | solution.py:92
  199.4 14.7 %all-to-all-start.5 = ((bf16[32,2,256]{2,1,0:T(2,128)(2,1)}), bf16[32,2,256]{2,1,0:T(2,128)(2,1)S(1)}, u32[]{:S(2)}, u32[]{:S(2)}) async-start(bf16[32,2,256]{2,1,0:T(2,128)(2,1)} %reshape.67), calls=%async_computation.5 | async-start | bytes 65536 | tf_op jit(solution)/shard_map/all_to_all | solution.py:98
  212.2 7.7 %copy-start = (bf16[48,128,128]{2,1,0:T(8,128)(2,1)S(1)}, bf16[48,128,128]{2,1,0:T(8,128)(2,1)}, u32[]{:S(2)}) copy-start(bf16[48,128,128]{2,1,0:T(8,128)(2,1)} %param.15) | copy-start | bytes 4718596
  214.1 59.3 %all-to-all-start.1 = ((bf16[8,32,64,128]{3,2,0,1:T(8,128)(2,1)}), bf16[8,32,64,128]{3,2,0,1:T(8,128)(2,1)}, u32[]{:S(2)}, u32[]{:S(2)}) async-start(bf16[8,32,64,128]{3,2,0,1:T(8,128)(2,1)} %copy.21), calls=%async_computation.1 | async-start | bytes 8388608 | tf_op jit(solution)/shard_map/all_to_all | solution.py:91
  292.0 6.7 %collective-permute-start = (bf16[1,128,128]{2,1,0:T(8,128)(2,1)S(1)}, bf16[1,128,128]{2,1,0:T(8,128)(2,1)S(1)}, u32[]{:S(2)}, u32[]{:S(2)}) collective-permute-start(bf16[1,128,128]{2,1,0:T(8,128)(2,1)S(1)} %fusion.107), channel_id=1, source_target_pairs={{0,1},{1,2},{2,3},{3,4},{4,5},{5,6},{6,7},{7,8},{8,9},{9,10},{10,1... | collective-permute-start | bytes 98312 | tf_op jit(solution)/shard_map/ppermute | solution.py:17
  292.0 6.7 %collective-permute-start.1 = (bf16[1,128,128]{2,1,0:T(8,128)(2,1)S(1)}, bf16[1,128,128]{2,1,0:T(8,128)(2,1)S(1)}, u32[]{:S(2)}, u32[]{:S(2)}) collective-permute-start(bf16[1,128,128]{2,1,0:T(8,128)(2,1)S(1)} %fusion.107), channel_id=1, source_target_pairs={{1,0},{2,1},{3,2},{4,3},{5,4},{6,5},{7,6},{8,7},{9,8},{10,9},{11,1... | collective-permute-start | bytes 98312 | tf_op jit(solution)/shard_map/ppermute | solution.py:20
where the time goes:
time: 311 us; the launch traced here: 309 us
  waiting for transfers between devices  152 us (49%)
  matrix products  84.6 us (27%)
  starting transfers between devices  40 us (13%)
  local copies, waits for them, and re-layouts  14.6 us (5%)
  blocking collectives  10.6 us (3%)
  other arithmetic  5.52 us (2%)
    all_to_all x1, waiting for transfers between devices, on_device(): lax.all_to_all(out_rows, 'obs', split_axis=0, concat_axis=0, tiled=True)  93.3 us
    all_to_all x1, waiting for transfers between devices, on_device(): lax.all_to_all(lax.all_to_all(out_rows, 'obs', split_axis=0, concat_axis=...  52.2 us
    dot_general x16, matrix products, select(): jnp.dot(one_hot, scaled, preferred_element_type=jnp.float32)  35 us
    dot_general x16, matrix products, select(): jnp.dot(one_hot, scaled_innov, preferred_element_type=jnp.float32)  26 us
    all_to_all x1, blocking collectives, on_device(): lax.all_to_all(out_innov, 'obs', split_axis=0, concat_axis=0, tiled=True)  10.6 us
    dot_general x1, matrix products, on_device(): lax.dot_general(flat_rows, flat_rows, (((0,), (0,)), ((), ())), preferred...  9 us
    all_to_all x1, starting transfers between devices, on_device(): lax.all_to_all(send_counts.reshape(n_obs, n_grid), 'obs', split_axis=0, c...  8.57 us
    all_to_all x1, starting transfers between devices, on_device(): lax.all_to_all(lax.all_to_all(send_counts.reshape(n_obs, n_grid), 'obs',...  7.32 us
  transfers between devices with their start and end apart: 7, of which 5 were waited for; matrix products, arithmetic and copies ran while one was open for 24% of the time, Pallas kernels for 0%

commit v1 on v0

v1 whole, which is shorter than its diff:
```python
import functools

import jax
import jax.numpy as jnp
from jax import lax
from jax.experimental import pallas as pl
from jax.experimental.pallas import tpu as pltpu
from jax.sharding import PartitionSpec as P

ITERS = 6
Y, X, CORES = 4, 4, 2
F32, BF16 = jnp.float32, jnp.bfloat16
K = 128
LOW = 512
BLOCKS = 4
TABLE = BLOCKS * K + 16
PACK = 112
VMEM = 48 * 1024 * 1024


def hop(value, dy, dx, dc):
    pairs = []
    for place in range(Y * X * CORES):
        y, x, c = place // (X * CORES), place // CORES % X, place % CORES
        pairs.append((place, ((y + dy) % Y * X + (x + dx) % X) * CORES + (c ^ dc)))
    return lax.ppermute(value, "grid", pairs)


def dims(m, n):
    return (((m,), (n,)), ((), ()))


def table_kernel(departures, innovation, obs_weight, table):
    root = jnp.sqrt(obs_weight[...].reshape(1, BLOCKS * LOW))
    innov = innovation[...].reshape(1, BLOCKS * LOW) * root
    row = lax.broadcasted_iota(jnp.int32, (16, LOW), 0)
    tail = jnp.zeros((16, LOW), F32)
    for block in range(BLOCKS):
        span = slice(block * LOW, (block + 1) * LOW)
        rows = departures[span, :].astype(F32).T * root[:, span]
        table[block * K : (block + 1) * K, :] = rows.astype(BF16)
        tail = jnp.where(row == block, innov[:, span], tail)
    table[BLOCKS * K :, :] = tail.astype(BF16)


def make_table(departures, innovation, obs_weight):
    return pl.pallas_call(
        table_kernel,
        out_shape=jax.ShapeDtypeStruct((TABLE, LOW), BF16),
        cost_estimate=pl.CostEstimate(flops=2_000_000, bytes_accessed=1_000_000, transcendentals=0),
    )(departures, innovation, obs_weight)


def picks_kernel(place, send_rows, *parts):
    x, c = place[0], place[1]
    for part in range(X * CORES):
        dx, dc = part // CORES, part % CORES
        cx = lax.rem(x + dx, X) * CORES + jnp.bitwise_xor(c, dc)
        for y in range(Y):
            rows = send_rows[pl.ds(y * X * CORES + cx, 8, stride=Y * X * CORES), :]
            pairs = jnp.concatenate([rows[0:4], rows[4:8]], axis=1)
            parts[part][2 * y : 2 * y + 2, :] = jnp.concatenate([pairs[0:2], pairs[2:4]], axis=1)


def make_picks(place, send_rows):
    vmem = pl.BlockSpec(memory_space=pltpu.VMEM)
    return pl.pallas_call(
        picks_kernel,
        out_shape=[jax.ShapeDtypeStruct((8, 256), jnp.int32)] * (X * CORES),
        in_specs=[pl.BlockSpec(memory_space=pltpu.SMEM), vmem],
        out_specs=[vmem] * (X * CORES),
        cost_estimate=pl.CostEstimate(flops=2_000_000, bytes_accessed=200_000, transcendentals=0),
    )(place, send_rows)


def pick(tables, picks):
    high = lax.shift_right_arithmetic(picks, 9)
    low = jnp.where(picks >= 0, jnp.bitwise_and(picks, LOW - 1), -1)
    one_hot = (lax.broadcasted_iota(jnp.int32, (LOW, 256), 0) == low).astype(BF16)
    found = [jnp.dot(part[...], one_hot, preferred_element_type=F32) for part in tables]
    blocks = []
    for part in found:
        blocks += [part[i * K : (i + 1) * K] for i in range(part.shape[0] // K)]
    tail = found[-1][-16:]
    members, innov = blocks[0], tail[0:1]
    for block in range(1, BLOCKS):
        here = high == block
        members = jnp.where(here, blocks[block], members)
        innov = jnp.where(here, tail[block : block + 1], innov)
    return jnp.concatenate([members, jnp.broadcast_to(innov, (16, 256))], axis=0).astype(BF16)


def grams(first, second, first_picks, second_picks):
    a, b = pick(first, first_picks), pick(second, second_picks)
    even = lax.broadcasted_iota(jnp.int32, (K, 256), 1) % K < K // 2
    totals = []
    for half in range(2):
        span = slice(half * K, (half + 1) * K)
        both = jnp.concatenate([a[:, span], b[:, span]], axis=1)
        rows = both[:K]
        none = jnp.zeros_like(rows)
        split = jnp.concatenate([jnp.where(even, rows, none), jnp.where(even, none, rows)], axis=0)
        totals.append(lax.dot_general(both, split, dims(1, 1), preferred_element_type=F32))
    return totals


def partial_kernel(chained, first, second, first_picks, second_picks, *rest):
    step = pl.program_id(0)
    out = rest[-1]
    picks = [ref[pl.ds(step, 1), :] for ref in (first_picks, second_picks)]
    totals = grams([first], [second], *picks)
    for half in range(2):
        out[0, half] = totals[half] + rest[0][0, half] if chained else totals[half]


def partial_grams(first, second, first_picks, second_picks, before=None):
    whole = lambda shape: pl.BlockSpec(shape, lambda i: (0,) * len(shape))
    spec = pl.BlockSpec((1, 2, 144, 256), lambda i: (i, 0, 0, 0))
    chained = before is not None
    args = (first, second, first_picks, second_picks) + ((before,) if chained else ())
    return pl.pallas_call(
        functools.partial(partial_kernel, chained),
        grid=(8,),
        out_shape=jax.ShapeDtypeStruct((8, 2, 144, 256), F32),
        in_specs=[whole((TABLE, LOW))] * 2 + [whole((8, 256))] * 2 + [spec] * chained,
        out_specs=spec,
        compiler_params=pltpu.CompilerParams(vmem_limit_bytes=VMEM),
        cost_estimate=pl.CostEstimate(
            flops=2 * 2 * TABLE * LOW * 2048, bytes_accessed=4_000_000, transcendentals=0
        ),
    )(*args)


def pack(total, side):
    gram = total[0:K, side * K : (side + 1) * K]
    lane = lax.broadcasted_iota(jnp.int32, (32, K), 1)
    fold = jnp.where(lane < 64, pltpu.roll(gram[64:96], 64, 1), gram[96:128])
    return jnp.concatenate([gram[0:64], fold, total[K : K + 16, side * K : (side + 1) * K]], axis=0)


def unpack(packed):
    lane = lax.broadcasted_iota(jnp.int32, (64, K), 1)
    fold = packed[64:96]
    lower = jnp.where(lane >= 64, jnp.concatenate([pltpu.roll(fold, 64, 1), fold], axis=0), 0.0)
    corner = jnp.concatenate([jnp.where(lane >= 64, packed[0:64], 0.0), jnp.zeros_like(lower)], axis=0)
    return jnp.concatenate([packed[0:64], lower], axis=0) + corner.T, packed[96:97]


def last_kernel(count, shift, place, a_low, a_high, b_low, b_high, a_picks, b_picks, before, *outs):
    step = pl.program_id(0)
    part = step // 2
    row = 2 * lax.rem(place[0] + shift(part), Y) + step % 2
    picks = [ref[pl.ds(row, 1), :] for ref in (a_picks, b_picks)]
    totals = grams([a_low, a_high], [b_low, b_high], *picks)
    totals = [totals[half] + before[0, half] for half in range(2)]
    for which in range(count):

        @pl.when(part == which)
        def _():
            for half in range(2):
                for side in range(2):
                    patch = step % 2 + 2 * half + 4 * side
                    outs[which][patch] = pack(totals[half], side).astype(outs[which].dtype)


def last_grams(shifts, dtype, place, tables, picks, before):
    whole = lambda shape: pl.BlockSpec(shape, lambda i, p: (0,) * len(shape))
    count = len(shifts)

    def shift(part):
        value = jnp.int32(shifts[0])
        for which in range(1, count):
            value = jnp.where(part == which, shifts[which], value)
        return value

    def block(i, p):
        return (2 * lax.rem(p[0] + shift(i // 2), Y) + i % 2, 0, 0, 0)

    return pl.pallas_call(
        functools.partial(last_kernel, count, shift),
        grid_spec=pltpu.PrefetchScalarGridSpec(
            num_scalar_prefetch=1,
            grid=(2 * count,),
            in_specs=[whole((256, LOW)), whole((272, LOW))] * 2
            + [whole((8, 256))] * 2
            + [pl.BlockSpec((1, 2, 144, 256), block)],
            out_specs=[whole((8, PACK, K))] * count,
        ),
        out_shape=[jax.ShapeDtypeStruct((8, PACK, K), dtype)] * count,
        compiler_params=pltpu.CompilerParams(vmem_limit_bytes=VMEM),
        cost_estimate=pl.CostEstimate(
            flops=count * 2 * TABLE * LOW * 1024, bytes_accessed=3_000_000, transcendentals=0
        ),
    )(place, *tables, *picks, before)


def spread_kernel(place, own, a, b, c, *outs):
    for part in range(8):
        row = lax.rem(place[0] + part, 8)
        total = own[row] + a[row].astype(F32) + b[row].astype(F32) + c[row].astype(F32)
        outs[part][...] = total.astype(outs[part].dtype)


def spread(place, own, others):
    vmem = pl.BlockSpec(memory_space=pltpu.VMEM)
    return pl.pallas_call(
        spread_kernel,
        out_shape=[jax.ShapeDtypeStruct((PACK, K), F32)]
        + [jax.ShapeDtypeStruct((PACK, K), BF16)] * 7,
        in_specs=[pl.BlockSpec(memory_space=pltpu.SMEM)] + [vmem] * 4,
        out_specs=[vmem] * 8,
    )(place, own, *others)


def split(value):
    high = value.astype(BF16)
    return high, (value - high.astype(F32)).astype(BF16)


def product(left, right):
    lh, ll = split(left)
    rh, rl = split(right)
    return jnp.dot(
        jnp.concatenate([lh, lh, ll], axis=1),
        jnp.concatenate([rh, rl, rh], axis=0),
        preferred_element_type=F32,
    )


def weights_kernel(own, *rest):
    out = rest[-1]
    total = own[...]
    for ref in rest[:-1]:
        total = total + ref[...].astype(F32)
    gram, pull = unpack(total)
    row = lax.broadcasted_iota(jnp.int32, (K, K), 0)
    col = lax.broadcasted_iota(jnp.int32, (K, K), 1)
    identity = (row == col).astype(F32)
    system = gram + (K - 1.0) * identity
    squares = jnp.sum(jnp.sum(system * system, axis=0, keepdims=True), axis=1, keepdims=True)
    frob = jnp.sqrt(squares)
    iterate = system / frob
    inverse = 1.5 * identity - 0.5 * iterate
    iterate = product(inverse, iterate)
    for sweep in range(1, ITERS):
        newton = 1.5 * identity - 0.5 * product(inverse, iterate)
        if sweep < ITERS - 1:
            both = product(newton, jnp.concatenate([iterate, inverse], axis=1))
            iterate, inverse = both[:, :K], both[:, K:]
        else:
            inverse = product(newton, inverse)
    shift = product(product(jnp.broadcast_to(pull, (16, K)), inverse), inverse)[0:1] / frob
    out[...] = (jnp.sqrt((K - 1.0) / frob) * inverse.T + shift).astype(BF16)


def transposed_weights(parts):
    return pl.pallas_call(
        weights_kernel,
        out_shape=jax.ShapeDtypeStruct((K, K), BF16),
    )(*parts)


def analysis_kernel(own, left, right, state, out):
    rows = state.shape[0]
    weights = jnp.concatenate([own[...], left[...], right[...]], axis=0)
    lane = lax.broadcasted_iota(jnp.int32, (1, 2 * K), 1) % K
    position = (lane.astype(F32) + 0.5) / K
    left_coef = jnp.maximum(0.5 - position, 0.0)
    right_coef = jnp.maximum(position - 0.5, 0.0)
    own_coef = 1.0 - left_coef - right_coef
    side_coef = left_coef + right_coef
    is_left = lane < K // 2
    for pair in range(rows // 2):
        values = [state[2 * pair + i].astype(F32) for i in range(2)]
        means = [jnp.mean(value, axis=0, keepdims=True) for value in values]
        mean = jnp.concatenate(means, axis=1)
        perturb = jnp.concatenate(
            [(values[i] - means[i]).astype(BF16) for i in range(2)], axis=1
        )
        sums = jnp.dot(weights, perturb, preferred_element_type=F32)
        side = jnp.where(is_left, sums[K : 2 * K], sums[2 * K :])
        total = (mean + own_coef * sums[:K] + side_coef * side).astype(BF16)
        for i in range(2):
            out[2 * pair + i] = total[:, i * K : (i + 1) * K]


def analyse(own, left, right, state):
    rows = state.shape[0]
    tile = 8
    small = pl.BlockSpec((K, K), lambda i: (0, 0))
    large = pl.BlockSpec((tile, K, K), lambda i: (i, 0, 0))
    return pl.pallas_call(
        analysis_kernel,
        grid=(rows // tile,),
        out_shape=jax.ShapeDtypeStruct(state.shape, BF16),
        in_specs=[small] * 3 + [large],
        out_specs=large,
        compiler_params=pltpu.CompilerParams(vmem_limit_bytes=VMEM),
        cost_estimate=pl.CostEstimate(
            flops=6 * rows * K * K * K, bytes_accessed=4 * rows * K * K, transcendentals=0
        ),
    )(own, left, right, state)


def on_device(departures, innovation, obs_weight, send_rows, send_counts, state):
    n_obs = lax.axis_size("obs")
    n_grid = lax.axis_size("grid")
    z = lax.axis_index("obs")
    g = lax.axis_index("grid")
    x_and_core = jnp.stack([g // CORES % X, g % CORES]).astype(jnp.int32)
    y_place = (g // (X * CORES)).astype(jnp.int32).reshape(1)
    z_place = z.astype(jnp.int32).reshape(1)

    table = make_table(departures, innovation, obs_weight)
    left = hop(table, 0, 1, 0)
    right = hop(table, 0, -1, 0)
    other = hop(table, 0, 0, 1)

    mine = make_picks(x_and_core, send_rows[0])
    picks = [
        mine[part] if part == 0 else hop(mine[part], 0, part // CORES, part % CORES)
        for part in range(X * CORES)
    ]
    totals = partial_grams(table, other, picks[0], picks[1])

    far_low = hop(left[:256], 0, 1, 0)
    far_high = hop(right[256:], 0, -1, 0)
    left_other = hop(left, 0, 0, 1)
    right_other = hop(right, 0, 0, 1)
    totals = partial_grams(left, right, picks[2], picks[6], totals)
    totals = partial_grams(left_other, right_other, picks[3], picks[7], totals)
    far = (far_low, far_high, hop(far_low, 0, 0, 1), hop(far_high, 0, 0, 1))

    sent = last_grams((2, 1, 3), BF16, y_place, far, (picks[4], picks[5]), totals)
    kept = last_grams((0,), F32, y_place, far, (picks[4], picks[5]), totals)[0]
    arrived = [hop(part, shift, 0, 0) for part, shift in zip(sent, (2, 1, 3))]

    parts = spread(z_place, kept, arrived)
    parts = [parts[0]] + [
        lax.ppermute(parts[i], "obs", [(j, (j + i) % n_obs) for j in range(n_obs)])
        for i in range(1, n_obs)
    ]
    own = transposed_weights(parts)
    low = lax.ppermute(own, "grid", [(j, (j + 1) % n_grid) for j in range(n_grid)])
    high = lax.ppermute(own, "grid", [(j, (j - 1) % n_grid) for j in range(n_grid)])
    return analyse(own, low, high, state)


def solution(mesh):
    in_specs = (
        P(("obs", "grid"), None),
        P(("obs", "grid")),
        P(("obs", "grid")),
        P(("obs", "grid"), None, None),
        P(("obs", "grid"), None),
        P("obs", None, "grid"),
    )
    out_specs = P("obs", None, "grid")
    return jax.shard_map(
        on_device, mesh=mesh, in_specs=in_specs, out_specs=out_specs, check_vma=False
    )
```

time: 311 us -> 123 us (0.40)
  the two profiles are of different devices: /device:TPU:32 before, /device:TPU:31 now
where the time goes in v1:
time: 123 us
  waiting for transfers between devices  39.1 us (32%)
  Pallas kernels  37.1 us (30%)
  starting transfers between devices  37 us (30%)
  local copies, waits for them, and re-layouts  8.75 us (7%)
    ppermute x19, waiting for transfers between devices, hop(): return lax.ppermute(value, 'grid', pairs)  30.1 us
    pallas_call x3, Pallas kernels, partial_grams(): pl.pallas_call(functools.partial(partial_kernel, chained), grid=(8,), out...  16.9 us
    ppermute x7, starting transfers between devices, on_device(): lax.ppermute(parts[i], 'obs', [(j, (j + i) % n_obs) for j in range(n_obs)])  16.5 us
    ppermute x19, starting transfers between devices, hop(): return lax.ppermute(value, 'grid', pairs)  15.7 us
    unnamed x35, local copies, waits for them, and re-layouts  8.71 us
    pallas_call x2, Pallas kernels, last_grams(): pl.pallas_call(functools.partial(last_kernel, count, shift), grid_spec=pl...  6.91 us
    ppermute x1, waiting for transfers between devices, on_device(): lax.ppermute(own, 'grid', [(j, (j - 1) % n_grid) for j in range(n_grid)])  5.53 us
    ppermute x1, starting transfers between devices, on_device(): lax.ppermute(own, 'grid', [(j, (j + 1) % n_grid) for j in range(n_grid)])  4.8 us
  transfers between devices with their start and end apart: 28, of which 12 were waited for; matrix products, arithmetic and copies ran while one was open for 2% of the time, Pallas kernels for 16%

profile of v1, /device:TPU:31, one launch (start us, length us, event | category | flops | bytes accessed | tf_op | source)
XLA Modules:
  0.0 122.8 jit_solution(15997168986932410625)
XLA Ops:
  0.0 2.1 %shard_map.55.first = bf16[528,512]{1,0:T(8,128)(2,1)} custom-call(bf16[2048,128]{1,0:T(8,128)(2,1)} %departures.1, f32[2048]{0:T(1024)} %innovation.1, f32[2048]{0:T(1024)} %obs_weight.1), custom_call_target="tpu_custom_call" | custom-call | flops 2000000 | bytes 1000000 | tf_op jit(solution)/shard_map/pallas_call | solution.py:47
  2.3 1.3 %collective-permute-start.2 = (bf16[528,512]{1,0:T(8,128)(2,1)}, bf16[528,512]{1,0:T(8,128)(2,1)S(1)}, u32[]{:S(2)}, u32[]{:S(2)}) collective-permute-start(bf16[528,512]{1,0:T(8,128)(2,1)} %shard_map.55.first), channel_id=1, source_target_pairs={{0,6},{1,7},{2,0},{3,1},{4,2},{5,3},{6,4},{7,5},{8,14},{9,15},{10,... | collective-permute-start | bytes 1622024 | tf_op jit(solution)/shard_map/ppermute | solution.py:26
  3.5 1.2 %collective-permute-start.14 = (bf16[528,512]{1,0:T(8,128)(2,1)}, bf16[528,512]{1,0:T(8,128)(2,1)S(1)}, u32[]{:S(2)}, u32[]{:S(2)}) collective-permute-start(bf16[528,512]{1,0:T(8,128)(2,1)} %shard_map.55.first), channel_id=1, source_target_pairs={{0,1},{1,0},{2,3},{3,2},{4,5},{5,4},{6,7},{7,6},{8,9},{9,8},{10,11... | collective-permute-start | bytes 1622024 | tf_op jit(solution)/shard_map/ppermute | solution.py:26
  4.8 10.7 %collective-permute-done.first = bf16[528,512]{1,0:T(8,128)(2,1)S(1)} collective-permute-done((bf16[528,512]{1,0:T(8,128)(2,1)}, bf16[528,512]{1,0:T(8,128)(2,1)S(1)}, u32[]{:S(2)}, u32[]{:S(2)}) %collective-permute-start) | collective-permute-done | bytes 540704 | tf_op jit(solution)/shard_map/ppermute | solution.py:26
  15.4 1.5 %collective-permute-start.8 = (bf16[528,512]{1,0:T(8,128)(2,1)S(1)}, bf16[528,512]{1,0:T(8,128)(2,1)S(1)}, u32[]{:S(2)}, u32[]{:S(2)}) collective-permute-start(bf16[528,512]{1,0:T(8,128)(2,1)S(1)} %collective-permute-done.first), channel_id=1, source_target_pairs={{0,1},{1,0},{2,3},{3,2},{4,5},{5,4},{6,7},{7,6},{8,9},{9,8},{10,11... | collective-permute-start | bytes 1622024 | tf_op jit(solution)/shard_map/ppermute | solution.py:26
  17.0 1.4 %collective-permute-start.9 = (bf16[528,512]{1,0:T(8,128)(2,1)S(1)}, bf16[528,512]{1,0:T(8,128)(2,1)}, u32[]{:S(2)}, u32[]{:S(2)}) collective-permute-start(bf16[528,512]{1,0:T(8,128)(2,1)S(1)} %collective-permute-done.2.second), channel_id=1, source_target_pairs={{0,1},{1,0},{2,3},{3,2},{4,5},{5,4},{6,7},{7,6},{8,9},{9,8},{10,11... | collective-permute-start | bytes 1622024 | tf_op jit(solution)/shard_map/ppermute | solution.py:26
  18.4 0.7 pad_add_fusion.place
  19.0 1.6 %copy.6 = s32[1,256,64]{2,1,0:T(8,128)} copy(s32[1,256,64]{1,2,0:T(8,128)} %param.9) | data formatting | bytes 131072 | tf_op args[3]
  20.6 1.7 %shard_map.56 = (s32[8,256]{1,0:T(8,128)}, s32[8,256]{1,0:T(8,128)}, s32[8,256]{1,0:T(8,128)}, s32[8,256]{1,0:T(8,128)}, s32[8,256]{1,0:T(8,128)}, /*index=5*/s3...) custom-call(s32[2]{0:T(128)} %pad_add_fusion.place, s32[256,64]{1,0:T(8,128)} %bitcast.5), custom_call_target="tpu_custom_call" | custom-call | flops 2000000 | bytes 200000 | tf_op jit(solution)/shard_map/pallas_call | solution.py:67
  22.3 0.5 collective-permute-start.12
  22.8 0.8 collective-permute-done.15.second_picks
  23.9 1.1 collective-permute-done.12.first_picks
  25.2 8.0 %collective-permute-done.13.second_picks = s32[8,256]{1,0:T(8,128)S(1)} collective-permute-done((s32[8,256]{1,0:T(8,128)}, s32[8,256]{1,0:T(8,128)S(1)}, u32[]{:S(2)}, u32[]{:S(2)}) %collective-permute-start.13) | collective-permute-done | bytes 8224 | tf_op jit(solution)/shard_map/ppermute | solution.py:26
  33.2 1.1 collective-permute-start.10
  34.3 1.0 copy-done.2
  35.4 0.7 copy-done.6
  36.1 5.3 %shard_map.57.rest_0_ = f32[8,2,144,256]{3,2,1,0:T(8,128)S(1)} custom-call(bf16[528,512]{1,0:T(8,128)(2,1)S(1)} %copy-done.2, bf16[528,512]{1,0:T(8,128)(2,1)S(1)} %collective-permute-done.14.second, s32[8,256]{1,0:T(8,128)S(1)} %copy-done.6, s32[8,256]{1,0:T(8,128)S(1)} %collective-permute-done.15.second_picks), custom_call_target="tpu_custom_call" | custom-call | flops 2214592512 | bytes 4000000 | tf_op jit(solution)/shard_map/pallas_call | solution.py:121
  41.6 1.3 %collective-permute-start.11 = (s32[8,256]{1,0:T(8,128)S(1)}, s32[8,256]{1,0:T(8,128)S(1)}, u32[]{:S(2)}, u32[]{:S(2)}) collective-permute-start(s32[8,256]{1,0:T(8,128)S(1)} %copy-done.16), channel_id=1, source_target_pairs={{0,7},{1,6},{2,1},{3,0},{4,3},{5,2},{6,5},{7,4},{8,15},{9,14},{10,... | collective-permute-start | bytes 24584 | tf_op jit(solution)/shard_map/ppermute | solution.py:26
  43.4 5.3 %shard_map.58.rest_0_ = f32[8,2,144,256]{3,2,1,0:T(8,128)S(1)} custom-call(bf16[528,512]{1,0:T(8,128)(2,1)S(1)} %collective-permute-done.first, bf16[528,512]{1,0:T(8,128)(2,1)S(1)} %collective-permute-done.2.second, s32[8,256]{1,0:T(8,128)S(1)} %collective-permute-done.12.first_picks, s32[8,256]{1,0:T(8,128)S(1)} %collective-permute-done.13.second_picks, ...), custom_call_target="tpu_custom_call" | custom-call | flops 2214592512 | bytes 4000000 | tf_op jit(solution)/shard_map/pallas_call | solution.py:121
  48.7 2.0 %collective-permute-start.6 = (s32[8,256]{1,0:T(8,128)S(1)}, s32[8,256]{1,0:T(8,128)S(1)}, u32[]{:S(2)}, u32[]{:S(2)}) collective-permute-start(s32[8,256]{1,0:T(8,128)S(1)} %copy-done.15), channel_id=1, source_target_pairs={{0,4},{1,5},{2,6},{3,7},{4,0},{5,1},{6,2},{7,3},{8,12},{9,13},{10,... | collective-permute-start | bytes 24584 | tf_op jit(solution)/shard_map/ppermute | solution.py:26
  50.7 0.8 copy-done.4
  51.5 1.4 %collective-permute-start.7 = (s32[8,256]{1,0:T(8,128)S(1)}, s32[8,256]{1,0:T(8,128)S(1)}, u32[]{:S(2)}, u32[]{:S(2)}) collective-permute-start(s32[8,256]{1,0:T(8,128)S(1)} %copy-done.14), channel_id=1, source_target_pairs={{0,5},{1,4},{2,7},{3,6},{4,1},{5,0},{6,3},{7,2},{8,13},{9,12},{10,... | collective-permute-start | bytes 24584 | tf_op jit(solution)/shard_map/ppermute | solution.py:26
  52.9 1.0 copy-done.5
  54.0 6.3 %shard_map.59.before = f32[8,2,144,256]{3,2,1,0:T(8,128)S(1)} custom-call(bf16[528,512]{1,0:T(8,128)(2,1)S(1)} %copy-done.5, bf16[528,512]{1,0:T(8,128)(2,1)} %collective-permute-done.9.second, s32[8,256]{1,0:T(8,128)S(1)} %collective-permute-done.10.first_picks, s32[8,256]{1,0:T(8,128)S(1)} %collective-permute-done.11.second_picks, ...), custom_call_target="tpu_custom_call" | custom-call | flops 2214592512 | bytes 4000000 | tf_op jit(solution)/shard_map/pallas_call | solution.py:121
  60.4 5.4 %shard_map.61 = (bf16[8,112,128]{2,1,0:T(8,128)(2,1)}, bf16[8,112,128]{2,1,0:T(8,128)(2,1)}, bf16[8,112,128]{2,1,0:T(8,128)(2,1)}) custom-call(s32[1]{0:T(128)} %bitcast.1.place, bf16[256,512]{1,0:T(8,128)(2,1)S(1)} %collective-permute-done.1.a_low, bf16[272,512]{1,0:T(8,128)(2,1)S(1)} %collective-permute-done.3.a_high, ...), custom_call_target="tpu_custom_call" | custom-call | flops 1660944384 | bytes 3000000 | tf_op jit(solution)/shard_map/pallas_call | solution.py:179
  65.8 1.0 collective-permute-start.16
  66.7 1.9 %collective-permute-start.17 = (bf16[8,112,128]{2,1,0:T(8,128)(2,1)}, bf16[8,112,128]{2,1,0:T(8,128)(2,1)}, u32[]{:S(2)}, u32[]{:S(2)}) collective-permute-start(bf16[8,112,128]{2,1,0:T(8,128)(2,1)} %get-tuple-element.33), channel_id=1, source_target_pairs={{0,8},{1,9},{2,10},{3,11},{4,12},{5,13},{6,14},{7,15},{8,16},{9,17... | collective-permute-start | bytes 688136 | tf_op jit(solution)/shard_map/ppermute | solution.py:26
  68.6 1.5 %shard_map.60.own = f32[8,112,128]{2,1,0:T(8,128)S(1)} custom-call(s32[1]{0:T(128)} %bitcast.1.place, bf16[256,512]{1,0:T(8,128)(2,1)S(1)} %collective-permute-done.1.a_low, bf16[272,512]{1,0:T(8,128)(2,1)S(1)} %collective-permute-done.3.a_high, bf16[256,512]{1,0:T(8,128)(2,1)S(1)} %collective-permute-done.4.b_low, ...), custom_call_target="tpu_custom_call" | custom-call | flops 553648128 | bytes 3000000 | tf_op jit(solution)/shard_map/pallas_call | solution.py:179
  70.1 0.8 copy-done
  70.9 3.9 %collective-permute-done.16.a = bf16[8,112,128]{2,1,0:T(8,128)(2,1)} collective-permute-done((bf16[8,112,128]{2,1,0:T(8,128)(2,1)}, bf16[8,112,128]{2,1,0:T(8,128)(2,1)}, u32[]{:S(2)}, u32[]{:S(2)}) %collective-permute-start.16) | collective-permute-done | bytes 229408 | tf_op jit(solution)/shard_map/ppermute | solution.py:26
  74.8 2.6 %collective-permute-done.17.b = bf16[8,112,128]{2,1,0:T(8,128)(2,1)} collective-permute-done((bf16[8,112,128]{2,1,0:T(8,128)(2,1)}, bf16[8,112,128]{2,1,0:T(8,128)(2,1)}, u32[]{:S(2)}, u32[]{:S(2)}) %collective-permute-start.17) | collective-permute-done | bytes 229408 | tf_op jit(solution)/shard_map/ppermute | solution.py:26
  77.4 2.7 %collective-permute-done.18.c = bf16[8,112,128]{2,1,0:T(8,128)(2,1)} collective-permute-done((bf16[8,112,128]{2,1,0:T(8,128)(2,1)}, bf16[8,112,128]{2,1,0:T(8,128)(2,1)}, u32[]{:S(2)}, u32[]{:S(2)}) %collective-permute-start.18) | collective-permute-done | bytes 229408 | tf_op jit(solution)/shard_map/ppermute | solution.py:26
  80.0 2.0 %shard_map.62 = (f32[112,128]{1,0:T(8,128)}, bf16[112,128]{1,0:T(8,128)(2,1)}, bf16[112,128]{1,0:T(8,128)(2,1)}, bf16[112,128]{1,0:T(8,128)(2,1)}, bf16[112,128]...) custom-call(s32[1]{0:T(128)} %bitcast.place, ...), custom_call_target="tpu_custom_call" | custom-call | tf_op jit(solution)/shard_map/pallas_call | solution.py:206
  82.1 1.7 %collective-permute-start.19 = (bf16[112,128]{1,0:T(8,128)(2,1)}, bf16[112,128]{1,0:T(8,128)(2,1)S(1)}, u32[]{:S(2)}, u32[]{:S(2)}) collective-permute-start(bf16[112,128]{1,0:T(8,128)(2,1)} %get-tuple-element.36), channel_id=1, source_target_pairs={{0,32},{32,64},{64,96},{96,128},{128,160},{160,192},{192,224},{224... | collective-permute-start | bytes 86024 | tf_op jit(solution)/shard_map/ppermute | solution.py:340
  83.8 3.0 %collective-permute-start.20 = (bf16[112,128]{1,0:T(8,128)(2,1)}, bf16[112,128]{1,0:T(8,128)(2,1)S(1)}, u32[]{:S(2)}, u32[]{:S(2)}) collective-permute-start(bf16[112,128]{1,0:T(8,128)(2,1)} %get-tuple-element.37), channel_id=1, source_target_pairs={{0,64},{32,96},{64,128},{96,160},{128,192},{160,224},{192,0},{224,... | collective-permute-start | bytes 86024 | tf_op jit(solution)/shard_map/ppermute | solution.py:340
  86.7 3.8 %collective-permute-start.21 = (bf16[112,128]{1,0:T(8,128)(2,1)}, bf16[112,128]{1,0:T(8,128)(2,1)S(1)}, u32[]{:S(2)}, u32[]{:S(2)}) collective-permute-start(bf16[112,128]{1,0:T(8,128)(2,1)} %get-tuple-element.38), channel_id=1, source_target_pairs={{0,96},{32,128},{64,160},{96,192},{128,224},{160,0},{192,32},{224,... | collective-permute-start | bytes 86024 | tf_op jit(solution)/shard_map/ppermute | solution.py:340
  90.5 0.5 collective-permute-start.22
  91.0 4.5 %collective-permute-start.23 = (bf16[112,128]{1,0:T(8,128)(2,1)}, bf16[112,128]{1,0:T(8,128)(2,1)S(1)}, u32[]{:S(2)}, u32[]{:S(2)}) collective-permute-start(bf16[112,128]{1,0:T(8,128)(2,1)} %get-tuple-element.40), channel_id=1, source_target_pairs={{0,160},{32,192},{64,224},{96,0},{128,32},{160,64},{192,96},{224,1... | collective-permute-start | bytes 86024 | tf_op jit(solution)/shard_map/ppermute | solution.py:340
  95.4 2.4 %collective-permute-start.24 = (bf16[112,128]{1,0:T(8,128)(2,1)}, bf16[112,128]{1,0:T(8,128)(2,1)S(1)}, u32[]{:S(2)}, u32[]{:S(2)}) collective-permute-start(bf16[112,128]{1,0:T(8,128)(2,1)} %get-tuple-element.41), channel_id=1, source_target_pairs={{0,192},{32,224},{64,0},{96,32},{128,64},{160,96},{192,128},{224,1... | collective-permute-start | bytes 86024 | tf_op jit(solution)/shard_map/ppermute | solution.py:340
  97.8 0.7 collective-permute-start.25
  98.6 1.9 %collective-permute-done.24.rest_5_ = bf16[112,128]{1,0:T(8,128)(2,1)S(1)} collective-permute-done((bf16[112,128]{1,0:T(8,128)(2,1)}, bf16[112,128]{1,0:T(8,128)(2,1)S(1)}, u32[]{:S(2)}, u32[]{:S(2)}) %collective-permute-start.24) | collective-permute-done | bytes 28704 | tf_op jit(solution)/shard_map/ppermute | solution.py:340
  101.4 3.8 %shard_map.63.own = bf16[128,128]{1,0:T(8,128)(2,1)} custom-call(f32[112,128]{1,0:T(8,128)} %get-tuple-element.35.own, bf16[112,128]{1,0:T(8,128)(2,1)} %copy-done.7, bf16[112,128]{1,0:T(8,128)(2,1)} %copy-done.8, bf16[112,128]{1,0:T(8,128)(2,1)} %copy-done.9, bf16[112,128]{1,0:T(8,128)(2,1)} %copy-done.10, bf16[112,128]{1,0:T(8,128)(2,1)} %copy-done.11, ...), custom_call_target="tpu_custom_call" | custom-call | tf_op jit(solution)/shard_map/pallas_call | solution.py:257
  105.2 4.8 %collective-permute-start.26 = (bf16[128,128]{1,0:T(8,128)(2,1)}, bf16[128,128]{1,0:T(8,128)(2,1)S(1)}, u32[]{:S(2)}, u32[]{:S(2)}) collective-permute-start(bf16[128,128]{1,0:T(8,128)(2,1)} %shard_map.63.own), channel_id=1, source_target_pairs={{0,1},{1,2},{2,3},{3,4},{4,5},{5,6},{6,7},{7,8},{8,9},{9,10},{10,1... | collective-permute-start | bytes 98312 | tf_op jit(solution)/shard_map/ppermute | solution.py:344
  110.0 1.3 %collective-permute-done.26.left = bf16[128,128]{1,0:T(8,128)(2,1)S(1)} collective-permute-done((bf16[128,128]{1,0:T(8,128)(2,1)}, bf16[128,128]{1,0:T(8,128)(2,1)S(1)}, u32[]{:S(2)}, u32[]{:S(2)}) %collective-permute-start.26) | collective-permute-done | bytes 32800 | tf_op jit(solution)/shard_map/ppermute | solution.py:344
  111.4 5.5 %collective-permute-done.27.right = bf16[128,128]{1,0:T(8,128)(2,1)S(1)} collective-permute-done((bf16[128,128]{1,0:T(8,128)(2,1)}, bf16[128,128]{1,0:T(8,128)(2,1)S(1)}, u32[]{:S(2)}, u32[]{:S(2)}) %collective-permute-start.27) | collective-permute-done | bytes 32800 | tf_op jit(solution)/shard_map/ppermute | solution.py:345
  116.9 1.4 %copy-done.1 = bf16[48,128,128]{2,1,0:T(8,128)(2,1)S(1)} copy-done((bf16[48,128,128]{2,1,0:T(8,128)(2,1)S(1)}, bf16[48,128,128]{2,1,0:T(8,128)(2,1)}, u32[]{:S(2)}) %copy-start.1) | copy-done | bytes 1572888
  118.3 0.8 copy-done.3
  119.1 3.8 %shard_map.64 = bf16[48,128,128]{2,1,0:T(8,128)(2,1)} custom-call(bf16[128,128]{1,0:T(8,128)(2,1)S(1)} %copy-done.3, bf16[128,128]{1,0:T(8,128)(2,1)S(1)} %collective-permute-done.26.left, bf16[128,128]{1,0:T(8,128)(2,1)S(1)} %collective-permute-done.27.right, bf16[48,128,128]{2,1,0:T(8,128)(2,1)S(1)} %copy-done.1), custom_call_target="tpu_custom_call" | custom-call | flops 603979776 | bytes 3145728 | tf_op jit(solution)/shard_map/pallas_call | solution.py:292
  (56 shorter events, 2.3 us)
Async XLA Ops:
  2.1 13.4 %collective-permute-start = (bf16[528,512]{1,0:T(8,128)(2,1)}, bf16[528,512]{1,0:T(8,128)(2,1)S(1)}, u32[]{:S(2)}, u32[]{:S(2)}) collective-permute-start(bf16[528,512]{1,0:T(8,128)(2,1)} %shard_map.55.first), channel_id=1, source_target_pairs={{0,2},{1,3},{2,4},{3,5},{4,6},{5,7},{6,0},{7,1},{8,10},{9,11},{10,... | collective-permute-start | bytes 1622024 | tf_op jit(solution)/shard_map/ppermute | solution.py:26
  2.3 14.7 %collective-permute-start.2 = (bf16[528,512]{1,0:T(8,128)(2,1)}, bf16[528,512]{1,0:T(8,128)(2,1)S(1)}, u32[]{:S(2)}, u32[]{:S(2)}) collective-permute-start(bf16[528,512]{1,0:T(8,128)(2,1)} %shard_map.55.first), channel_id=1, source_target_pairs={{0,6},{1,7},{2,0},{3,1},{4,2},{5,3},{6,4},{7,5},{8,14},{9,15},{10,... | collective-permute-start | bytes 1622024 | tf_op jit(solution)/shard_map/ppermute | solution.py:26
  3.5 29.6 %collective-permute-start.14 = (bf16[528,512]{1,0:T(8,128)(2,1)}, bf16[528,512]{1,0:T(8,128)(2,1)S(1)}, u32[]{:S(2)}, u32[]{:S(2)}) collective-permute-start(bf16[528,512]{1,0:T(8,128)(2,1)} %shard_map.55.first), channel_id=1, source_target_pairs={{0,1},{1,0},{2,3},{3,2},{4,5},{5,4},{6,7},{7,6},{8,9},{9,8},{10,11... | collective-permute-start | bytes 1622024 | tf_op jit(solution)/shard_map/ppermute | solution.py:26
  15.4 35.3 %collective-permute-start.8 = (bf16[528,512]{1,0:T(8,128)(2,1)S(1)}, bf16[528,512]{1,0:T(8,128)(2,1)S(1)}, u32[]{:S(2)}, u32[]{:S(2)}) collective-permute-start(bf16[528,512]{1,0:T(8,128)(2,1)S(1)} %collective-permute-done.first), channel_id=1, source_target_pairs={{0,1},{1,0},{2,3},{3,2},{4,5},{5,4},{6,7},{7,6},{8,9},{9,8},{10,11... | collective-permute-start | bytes 1622024 | tf_op jit(solution)/shard_map/ppermute | solution.py:26
  17.0 35.9 %collective-permute-start.9 = (bf16[528,512]{1,0:T(8,128)(2,1)S(1)}, bf16[528,512]{1,0:T(8,128)(2,1)}, u32[]{:S(2)}, u32[]{:S(2)}) collective-permute-start(bf16[528,512]{1,0:T(8,128)(2,1)S(1)} %collective-permute-done.2.second), channel_id=1, source_target_pairs={{0,1},{1,0},{2,3},{3,2},{4,5},{5,4},{6,7},{7,6},{8,9},{9,8},{10,11... | collective-permute-start | bytes 1622024 | tf_op jit(solution)/shard_map/ppermute | solution.py:26
  22.3 1.4 %collective-permute-start.15 = (s32[8,256]{1,0:T(8,128)}, s32[8,256]{1,0:T(8,128)S(1)}, u32[]{:S(2)}, u32[]{:S(2)}) collective-permute-start(s32[8,256]{1,0:T(8,128)} %get-tuple-element.31), channel_id=1, source_target_pairs={{0,1},{1,0},{2,3},{3,2},{4,5},{5,4},{6,7},{7,6},{8,9},{9,8},{10,11... | collective-permute-start | bytes 24584 | tf_op jit(solution)/shard_map/ppermute | solution.py:26
  22.3 2.8 %collective-permute-start.12 = (s32[8,256]{1,0:T(8,128)}, s32[8,256]{1,0:T(8,128)S(1)}, u32[]{:S(2)}, u32[]{:S(2)}) collective-permute-start(s32[8,256]{1,0:T(8,128)} %get-tuple-element.28), channel_id=1, source_target_pairs={{0,2},{1,3},{2,4},{3,5},{4,6},{5,7},{6,0},{7,1},{8,10},{9,11},{10,... | collective-permute-start | bytes 24584 | tf_op jit(solution)/shard_map/ppermute | solution.py:26
  23.7 19.4 %collective-permute-start.3 = (bf16[272,512]{1,0:T(8,128)(2,1)S(1)}, bf16[272,512]{1,0:T(8,128)(2,1)S(1)}, u32[]{:S(2)}, u32[]{:S(2)}) collective-permute-start(bf16[272,512]{1,0:T(8,128)(2,1)S(1)} %slice.9), channel_id=1, source_target_pairs={{0,6},{1,7},{2,0},{3,1},{4,2},{5,3},{6,4},{7,5},{8,14},{9,15},{10,... | collective-permute-start | bytes 835592 | tf_op jit(solution)/shard_map/ppermute | solution.py:26
  25.1 8.1 %collective-permute-start.13 = (s32[8,256]{1,0:T(8,128)}, s32[8,256]{1,0:T(8,128)S(1)}, u32[]{:S(2)}, u32[]{:S(2)}) collective-permute-start(s32[8,256]{1,0:T(8,128)} %get-tuple-element.29), channel_id=1, source_target_pairs={{0,6},{1,7},{2,0},{3,1},{4,2},{5,3},{6,4},{7,5},{8,14},{9,15},{10,... | collective-permute-start | bytes 24584 | tf_op jit(solution)/shard_map/ppermute | solution.py:26
  33.2 9.7 %collective-permute-start.1 = (bf16[256,512]{1,0:T(8,128)(2,1)S(1)}, bf16[256,512]{1,0:T(8,128)(2,1)S(1)}, u32[]{:S(2)}, u32[]{:S(2)}) collective-permute-start(bf16[256,512]{1,0:T(8,128)(2,1)S(1)} %slice.8), channel_id=1, source_target_pairs={{0,2},{1,3},{2,4},{3,5},{4,6},{5,7},{6,0},{7,1},{8,10},{9,11},{10,... | collective-permute-start | bytes 786440 | tf_op jit(solution)/shard_map/ppermute | solution.py:26
  33.2 8.4 %collective-permute-start.10 = (s32[8,256]{1,0:T(8,128)}, s32[8,256]{1,0:T(8,128)S(1)}, u32[]{:S(2)}, u32[]{:S(2)}) collective-permute-start(s32[8,256]{1,0:T(8,128)} %get-tuple-element.26), channel_id=1, source_target_pairs={{0,3},{1,2},{2,5},{3,4},{4,7},{5,6},{6,1},{7,0},{8,11},{9,10},{10,... | collective-permute-start | bytes 24584 | tf_op jit(solution)/shard_map/ppermute | solution.py:26
  34.3 1.0 copy-start.2
  35.4 0.7 copy-start.6
  36.1 5.5 %copy-start.16 = (s32[8,256]{1,0:T(8,128)S(1)}, s32[8,256]{1,0:T(8,128)}, u32[]{:S(2)}) copy-start(s32[8,256]{1,0:T(8,128)} %get-tuple-element.27) | copy-start | bytes 24580
  41.6 7.1 %copy-start.15 = (s32[8,256]{1,0:T(8,128)S(1)}, s32[8,256]{1,0:T(8,128)}, u32[]{:S(2)}) copy-start(s32[8,256]{1,0:T(8,128)} %get-tuple-element.24) | copy-start | bytes 24580
  41.6 9.9 %copy-start.14 = (s32[8,256]{1,0:T(8,128)S(1)}, s32[8,256]{1,0:T(8,128)}, u32[]{:S(2)}) copy-start(s32[8,256]{1,0:T(8,128)} %get-tuple-element.25) | copy-start | bytes 24580
  41.6 7.1 %collective-permute-start.11 = (s32[8,256]{1,0:T(8,128)S(1)}, s32[8,256]{1,0:T(8,128)S(1)}, u32[]{:S(2)}, u32[]{:S(2)}) collective-permute-start(s32[8,256]{1,0:T(8,128)S(1)} %copy-done.16), channel_id=1, source_target_pairs={{0,7},{1,6},{2,1},{3,0},{4,3},{5,2},{6,5},{7,4},{8,15},{9,14},{10,... | collective-permute-start | bytes 24584 | tf_op jit(solution)/shard_map/ppermute | solution.py:26
  42.9 17.4 %collective-permute-start.4 = (bf16[256,512]{1,0:T(8,128)(2,1)S(1)}, bf16[256,512]{1,0:T(8,128)(2,1)S(1)}, u32[]{:S(2)}, u32[]{:S(2)}) collective-permute-start(bf16[256,512]{1,0:T(8,128)(2,1)S(1)} %collective-permute-done.1.a_low), channel_id=1, source_target_pairs={{0,1},{1,0},{2,3},{3,2},{4,5},{5,4},{6,7},{7,6},{8,9},{9,8},{10,11... | collective-permute-start | bytes 786440 | tf_op jit(solution)/shard_map/ppermute | solution.py:26
  43.1 17.3 %collective-permute-start.5 = (bf16[272,512]{1,0:T(8,128)(2,1)S(1)}, bf16[272,512]{1,0:T(8,128)(2,1)S(1)}, u32[]{:S(2)}, u32[]{:S(2)}) collective-permute-start(bf16[272,512]{1,0:T(8,128)(2,1)S(1)} %collective-permute-done.3.a_high), channel_id=1, source_target_pairs={{0,1},{1,0},{2,3},{3,2},{4,5},{5,4},{6,7},{7,6},{8,9},{9,8},{10,11... | collective-permute-start | bytes 835592 | tf_op jit(solution)/shard_map/ppermute | solution.py:26
  48.7 11.6 %collective-permute-start.6 = (s32[8,256]{1,0:T(8,128)S(1)}, s32[8,256]{1,0:T(8,128)S(1)}, u32[]{:S(2)}, u32[]{:S(2)}) collective-permute-start(s32[8,256]{1,0:T(8,128)S(1)} %copy-done.15), channel_id=1, source_target_pairs={{0,4},{1,5},{2,6},{3,7},{4,0},{5,1},{6,2},{7,3},{8,12},{9,13},{10,... | collective-permute-start | bytes 24584 | tf_op jit(solution)/shard_map/ppermute | solution.py:26
  50.7 0.8 copy-start.4
  51.5 8.8 %collective-permute-start.7 = (s32[8,256]{1,0:T(8,128)S(1)}, s32[8,256]{1,0:T(8,128)S(1)}, u32[]{:S(2)}, u32[]{:S(2)}) collective-permute-start(s32[8,256]{1,0:T(8,128)S(1)} %copy-done.14), channel_id=1, source_target_pairs={{0,5},{1,4},{2,7},{3,6},{4,1},{5,0},{6,3},{7,2},{8,13},{9,12},{10,... | collective-permute-start | bytes 24584 | tf_op jit(solution)/shard_map/ppermute | solution.py:26
  52.9 1.0 copy-start.5
  65.8 9.0 %collective-permute-start.16 = (bf16[8,112,128]{2,1,0:T(8,128)(2,1)}, bf16[8,112,128]{2,1,0:T(8,128)(2,1)}, u32[]{:S(2)}, u32[]{:S(2)}) collective-permute-start(bf16[8,112,128]{2,1,0:T(8,128)(2,1)} %get-tuple-element.32), channel_id=1, source_target_pairs={{0,16},{1,17},{2,18},{3,19},{4,20},{5,21},{6,22},{7,23},{8,24},{9,... | collective-permute-start | bytes 688136 | tf_op jit(solution)/shard_map/ppermute | solution.py:26
  66.7 10.6 %collective-permute-start.17 = (bf16[8,112,128]{2,1,0:T(8,128)(2,1)}, bf16[8,112,128]{2,1,0:T(8,128)(2,1)}, u32[]{:S(2)}, u32[]{:S(2)}) collective-permute-start(bf16[8,112,128]{2,1,0:T(8,128)(2,1)} %get-tuple-element.33), channel_id=1, source_target_pairs={{0,8},{1,9},{2,10},{3,11},{4,12},{5,13},{6,14},{7,15},{8,16},{9,17... | collective-permute-start | bytes 688136 | tf_op jit(solution)/shard_map/ppermute | solution.py:26
  68.6 11.4 %collective-permute-start.18 = (bf16[8,112,128]{2,1,0:T(8,128)(2,1)}, bf16[8,112,128]{2,1,0:T(8,128)(2,1)}, u32[]{:S(2)}, u32[]{:S(2)}) collective-permute-start(bf16[8,112,128]{2,1,0:T(8,128)(2,1)} %get-tuple-element.34), channel_id=1, source_target_pairs={{0,24},{1,25},{2,26},{3,27},{4,28},{5,29},{6,30},{7,31},{8,0},{9,1... | collective-permute-start | bytes 688136 | tf_op jit(solution)/shard_map/ppermute | solution.py:26
  70.1 0.8 copy-start
  82.1 13.4 %collective-permute-start.19 = (bf16[112,128]{1,0:T(8,128)(2,1)}, bf16[112,128]{1,0:T(8,128)(2,1)S(1)}, u32[]{:S(2)}, u32[]{:S(2)}) collective-permute-start(bf16[112,128]{1,0:T(8,128)(2,1)} %get-tuple-element.36), channel_id=1, source_target_pairs={{0,32},{32,64},{64,96},{96,128},{128,160},{160,192},{192,224},{224... | collective-permute-start | bytes 86024 | tf_op jit(solution)/shard_map/ppermute | solution.py:340
  83.8 14.1 %collective-permute-start.20 = (bf16[112,128]{1,0:T(8,128)(2,1)}, bf16[112,128]{1,0:T(8,128)(2,1)S(1)}, u32[]{:S(2)}, u32[]{:S(2)}) collective-permute-start(bf16[112,128]{1,0:T(8,128)(2,1)} %get-tuple-element.37), channel_id=1, source_target_pairs={{0,64},{32,96},{64,128},{96,160},{128,192},{160,224},{192,0},{224,... | collective-permute-start | bytes 86024 | tf_op jit(solution)/shard_map/ppermute | solution.py:340
  86.7 11.8 %collective-permute-start.21 = (bf16[112,128]{1,0:T(8,128)(2,1)}, bf16[112,128]{1,0:T(8,128)(2,1)S(1)}, u32[]{:S(2)}, u32[]{:S(2)}) collective-permute-start(bf16[112,128]{1,0:T(8,128)(2,1)} %get-tuple-element.38), channel_id=1, source_target_pairs={{0,96},{32,128},{64,160},{96,192},{128,224},{160,0},{192,32},{224,... | collective-permute-start | bytes 86024 | tf_op jit(solution)/shard_map/ppermute | solution.py:340
  90.5 8.1 %collective-permute-start.22 = (bf16[112,128]{1,0:T(8,128)(2,1)}, bf16[112,128]{1,0:T(8,128)(2,1)S(1)}, u32[]{:S(2)}, u32[]{:S(2)}) collective-permute-start(bf16[112,128]{1,0:T(8,128)(2,1)} %get-tuple-element.39), channel_id=1, source_target_pairs={{0,128},{32,160},{64,192},{96,224},{128,0},{160,32},{192,64},{224,... | collective-permute-start | bytes 86024 | tf_op jit(solution)/shard_map/ppermute | solution.py:340
  91.0 7.6 %collective-permute-start.23 = (bf16[112,128]{1,0:T(8,128)(2,1)}, bf16[112,128]{1,0:T(8,128)(2,1)S(1)}, u32[]{:S(2)}, u32[]{:S(2)}) collective-permute-start(bf16[112,128]{1,0:T(8,128)(2,1)} %get-tuple-element.40), channel_id=1, source_target_pairs={{0,160},{32,192},{64,224},{96,0},{128,32},{160,64},{192,96},{224,1... | collective-permute-start | bytes 86024 | tf_op jit(solution)/shard_map/ppermute | solution.py:340
  95.4 5.4 %copy-start.7 = (bf16[112,128]{1,0:T(8,128)(2,1)}, bf16[112,128]{1,0:T(8,128)(2,1)S(1)}, u32[]{:S(2)}) copy-start(bf16[112,128]{1,0:T(8,128)(2,1)S(1)} %collective-permute-done.19.rest_0_) | copy-start | bytes 86020
  95.4 5.1 %collective-permute-start.24 = (bf16[112,128]{1,0:T(8,128)(2,1)}, bf16[112,128]{1,0:T(8,128)(2,1)S(1)}, u32[]{:S(2)}, u32[]{:S(2)}) collective-permute-start(bf16[112,128]{1,0:T(8,128)(2,1)} %get-tuple-element.41), channel_id=1, source_target_pairs={{0,192},{32,224},{64,0},{96,32},{128,64},{160,96},{192,128},{224,1... | collective-permute-start | bytes 86024 | tf_op jit(solution)/shard_map/ppermute | solution.py:340
  97.8 3.0 %copy-start.8 = (bf16[112,128]{1,0:T(8,128)(2,1)}, bf16[112,128]{1,0:T(8,128)(2,1)S(1)}, u32[]{:S(2)}) copy-start(bf16[112,128]{1,0:T(8,128)(2,1)S(1)} %collective-permute-done.20.rest_1_) | copy-start | bytes 86020
  97.8 3.0 %collective-permute-start.25 = (bf16[112,128]{1,0:T(8,128)(2,1)}, bf16[112,128]{1,0:T(8,128)(2,1)S(1)}, u32[]{:S(2)}, u32[]{:S(2)}) collective-permute-start(bf16[112,128]{1,0:T(8,128)(2,1)} %get-tuple-element.42), channel_id=1, source_target_pairs={{0,224},{32,0},{64,32},{96,64},{128,96},{160,128},{192,160},{224,1... | collective-permute-start | bytes 86024 | tf_op jit(solution)/shard_map/ppermute | solution.py:340
  98.6 2.3 %copy-start.9 = (bf16[112,128]{1,0:T(8,128)(2,1)}, bf16[112,128]{1,0:T(8,128)(2,1)S(1)}, u32[]{:S(2)}) copy-start(bf16[112,128]{1,0:T(8,128)(2,1)S(1)} %collective-permute-done.21.rest_2_) | copy-start | bytes 86020
  98.6 2.3 %copy-start.10 = (bf16[112,128]{1,0:T(8,128)(2,1)}, bf16[112,128]{1,0:T(8,128)(2,1)S(1)}, u32[]{:S(2)}) copy-start(bf16[112,128]{1,0:T(8,128)(2,1)S(1)} %collective-permute-done.22.rest_3_) | copy-start | bytes 86020
  98.6 2.2 %copy-start.11 = (bf16[112,128]{1,0:T(8,128)(2,1)}, bf16[112,128]{1,0:T(8,128)(2,1)S(1)}, u32[]{:S(2)}) copy-start(bf16[112,128]{1,0:T(8,128)(2,1)S(1)} %collective-permute-done.23.rest_4_) | copy-start | bytes 86020
  100.5 0.6 copy-start.12
  100.8 0.6 copy-start.13
  105.2 6.1 %collective-permute-start.26 = (bf16[128,128]{1,0:T(8,128)(2,1)}, bf16[128,128]{1,0:T(8,128)(2,1)S(1)}, u32[]{:S(2)}, u32[]{:S(2)}) collective-permute-start(bf16[128,128]{1,0:T(8,128)(2,1)} %shard_map.63.own), channel_id=1, source_target_pairs={{0,1},{1,2},{2,3},{3,4},{4,5},{5,6},{6,7},{7,8},{8,9},{9,10},{10,1... | collective-permute-start | bytes 98312 | tf_op jit(solution)/shard_map/ppermute | solution.py:344
  110.0 6.9 %collective-permute-start.27 = (bf16[128,128]{1,0:T(8,128)(2,1)}, bf16[128,128]{1,0:T(8,128)(2,1)S(1)}, u32[]{:S(2)}, u32[]{:S(2)}) collective-permute-start(bf16[128,128]{1,0:T(8,128)(2,1)} %shard_map.63.own), channel_id=1, source_target_pairs={{0,31},{1,0},{2,1},{3,2},{4,3},{5,4},{6,5},{7,6},{8,7},{9,8},{10,9... | collective-permute-start | bytes 98312 | tf_op jit(solution)/shard_map/ppermute | solution.py:345
  116.9 1.4 %copy-start.1 = (bf16[48,128,128]{2,1,0:T(8,128)(2,1)S(1)}, bf16[48,128,128]{2,1,0:T(8,128)(2,1)}, u32[]{:S(2)}) copy-start(bf16[48,128,128]{2,1,0:T(8,128)(2,1)} %state.1) | copy-start | bytes 4718596
  118.3 0.8 copy-start.3

commit v2 on v1

v2 whole, which is shorter than its diff:
```python
import functools

import jax
import jax.numpy as jnp
from jax import lax
from jax.experimental import pallas as pl
from jax.experimental.pallas import tpu as pltpu
from jax.sharding import PartitionSpec as P

ITERS = 6
Y, X, CORES = 4, 4, 2
F32, BF16 = jnp.float32, jnp.bfloat16
K = 128
LOW = 512
BLOCKS = 4
TABLE = BLOCKS * K + 16
PACK = 112
VMEM = 20 * 1024 * 1024


def params():
    return pltpu.CompilerParams(vmem_limit_bytes=VMEM)


def cost(flops):
    return pl.CostEstimate(flops=int(flops), bytes_accessed=4_000_000, transcendentals=0)


def in_vmem(count):
    return [pl.BlockSpec(memory_space=pltpu.VMEM)] * count


def hop(value, dy, dx, dc):
    pairs = []
    for place in range(Y * X * CORES):
        y, x, c = place // (X * CORES), place // CORES % X, place % CORES
        pairs.append((place, ((y + dy) % Y * X + (x + dx) % X) * CORES + (c ^ dc)))
    return lax.ppermute(value, "grid", pairs)


def dims(m, n):
    return (((m,), (n,)), ((), ()))


def message_kernel(departures, innovation, obs_weight, send_rows, near, to_right, to_left, turned):
    grid = lax.axis_index("grid")
    x, c = lax.rem(lax.div(grid, CORES), X), lax.rem(grid, CORES)
    turned[...] = send_rows[...].T
    groups = []
    for dx in range(X):
        halves = []
        for dc in range(CORES):
            cx = lax.rem(x + dx, X) * CORES + lax.rem(c + dc, CORES)
            lines = []
            for y in range(Y):
                rows = turned[pl.ds(y * X * CORES + cx, 8, stride=Y * X * CORES), :]
                pairs = jnp.concatenate([rows[0:4], rows[4:8]], axis=1)
                fours = jnp.concatenate([pairs[0:2], pairs[2:4]], axis=1)
                lines.append(jnp.concatenate([fours[0:1], fours[1:2]], axis=1))
            picks = jnp.concatenate(lines, axis=0)
            halves.append(lax.shift_right_arithmetic(picks, 8))
            halves.append(jnp.bitwise_and(picks, 255))
        groups.append(jnp.concatenate(halves, axis=0).astype(F32).astype(BF16))
    near[TABLE:, :] = groups[0]
    to_right[:16, :] = groups[2]
    to_right[16 + TABLE :, :] = groups[1]
    to_left[TABLE:, :] = groups[3]
    root = jnp.sqrt(obs_weight[...].reshape(1, BLOCKS * LOW))
    innov = innovation[...].reshape(1, BLOCKS * LOW) * root
    row = lax.broadcasted_iota(jnp.int32, (16, LOW), 0)
    tail = jnp.zeros((16, LOW), F32)
    for block in range(BLOCKS):
        span = slice(block * LOW, (block + 1) * LOW)
        rows = (departures[span, :].astype(F32).T * root[:, span]).astype(BF16)
        near[block * K : (block + 1) * K, :] = rows
        to_right[16 + block * K : 16 + (block + 1) * K, :] = rows
        to_left[block * K : (block + 1) * K, :] = rows
        tail = jnp.where(row == block, innov[:, span], tail)
    tail = tail.astype(BF16)
    near[BLOCKS * K : TABLE, :] = tail
    to_right[16 + BLOCKS * K : 16 + TABLE, :] = tail
    to_left[BLOCKS * K : TABLE, :] = tail


def make_messages(departures, innovation, obs_weight, send_rows):
    return pl.pallas_call(
        message_kernel,
        out_shape=[
            jax.ShapeDtypeStruct((TABLE + extra, LOW), BF16) for extra in (16, 32, 16)
        ],
        in_specs=in_vmem(4),
        out_specs=in_vmem(3),
        scratch_shapes=[pltpu.VMEM((send_rows.shape[1], send_rows.shape[0]), jnp.int32)],
        compiler_params=params(),
        cost_estimate=cost(2e9),
    )(departures, innovation, obs_weight, send_rows)


def read_picks(group, core):
    values = group[8 * core : 8 * core + 8].astype(F32)
    return (values[0:4] * 256.0 + values[4:8]).astype(jnp.int32)


def pick(tables, picks):
    high = lax.shift_right_arithmetic(picks, 9)
    low = jnp.where(picks >= 0, jnp.bitwise_and(picks, LOW - 1), -1)
    one_hot = (lax.broadcasted_iota(jnp.int32, (LOW, 256), 0) == low).astype(BF16)
    found = [jnp.dot(part, one_hot, preferred_element_type=F32) for part in tables]
    blocks = []
    for part in found:
        blocks += [part[i * K : (i + 1) * K] for i in range(part.shape[0] // K)]
    tail = found[-1][-16:]
    members, innov = blocks[0], tail[0:1]
    for block in range(1, BLOCKS):
        here = high == block
        members = jnp.where(here, blocks[block], members)
        innov = jnp.where(here, tail[block : block + 1], innov)
    return jnp.concatenate([members, jnp.broadcast_to(innov, (16, 256))], axis=0).astype(BF16)


def grams(first, second, first_picks, second_picks):
    a, b = pick(first, first_picks), pick(second, second_picks)
    even = lax.broadcasted_iota(jnp.int32, (K, 256), 1) % K < K // 2
    totals = []
    for half in range(2):
        span = slice(half * K, (half + 1) * K)
        both = jnp.concatenate([a[:, span], b[:, span]], axis=1)
        rows = both[:K]
        none = jnp.zeros_like(rows)
        split = jnp.concatenate([jnp.where(even, rows, none), jnp.where(even, none, rows)], axis=0)
        totals.append(lax.dot_general(both, split, dims(1, 1), preferred_element_type=F32))
    return totals


def partial_kernel(starts, cores, first, second, *rest):
    out = rest[-1]
    messages = (first, second)
    picks = [
        read_picks(ref[at : at + 16, :], core)
        for ref, (_, at), core in zip(messages, starts, cores)
    ]
    for step in range(2 * Y):
        y, span = step // 2, slice(step % 2 * 256, step % 2 * 256 + 256)
        tables = [[ref[at : at + TABLE, :]] for ref, (at, _) in zip(messages, starts)]
        totals = grams(*tables, picks[0][y : y + 1, span], picks[1][y : y + 1, span])
        for half in range(2):
            if len(rest) > 1:
                out[step, half] = totals[half] + rest[0][step, half]
            else:
                out[step, half] = totals[half]


def partial_grams(starts, cores, *args):
    return pl.pallas_call(
        functools.partial(partial_kernel, starts, cores),
        out_shape=jax.ShapeDtypeStruct((2 * Y, 2, 144, 256), F32),
        in_specs=in_vmem(len(args)),
        out_specs=in_vmem(1)[0],
        compiler_params=params(),
        cost_estimate=cost(4e9),
    )(*args)


def pack(total, side):
    gram = total[0:K, side * K : (side + 1) * K]
    lane = lax.broadcasted_iota(jnp.int32, (32, K), 1)
    fold = jnp.where(lane < 64, pltpu.roll(gram[64:96], 64, 1), gram[96:128])
    return jnp.concatenate([gram[0:64], fold, total[K : K + 16, side * K : (side + 1) * K]], axis=0)


def unpack(packed):
    lane = lax.broadcasted_iota(jnp.int32, (64, K), 1)
    fold = packed[64:96]
    lower = jnp.where(lane >= 64, jnp.concatenate([pltpu.roll(fold, 64, 1), fold], axis=0), 0.0)
    corner = jnp.concatenate([jnp.where(lane >= 64, packed[0:64], 0.0), jnp.zeros_like(lower)], axis=0)
    return jnp.concatenate([packed[0:64], lower], axis=0) + corner.T, packed[96:97]


def last_kernel(shifts, lowest, a_low, a_high, b_low, b_high, before, *rest):
    outs, a_picks, b_picks = rest[:-2], rest[-2], rest[-1]
    place = lax.div(lax.axis_index("grid"), X * CORES)
    a_picks[...] = read_picks(a_low[0:16, :], 0)
    b_picks[...] = read_picks(b_low[0:16, :], 1)
    tables = [[low[16:, :], high[...]] for low, high in ((a_low, a_high), (b_low, b_high))]
    for shift in sorted(set(shifts)):
        y = lax.rem(place + shift, Y)
        for i in range(2):
            span = slice(i * 256, i * 256 + 256)
            picks = [ref[pl.ds(y, 1), :][:, span] for ref in (a_picks, b_picks)]
            totals = grams(*tables, *picks)
            for half in range(2):
                total = totals[half] + before[2 * y + i, half]
                for side in range(2):
                    patch = i + 2 * half + 4 * side
                    for out, its_shift, low in zip(outs, shifts, lowest):
                        if its_shift == shift and low <= patch < low + out.shape[0]:
                            out[patch - low] = pack(total, side).astype(out.dtype)


def last_grams(shifts, lowest, counts, dtype, tables, before):
    return pl.pallas_call(
        functools.partial(last_kernel, shifts, lowest),
        out_shape=[jax.ShapeDtypeStruct((count, PACK, K), dtype) for count in counts],
        in_specs=in_vmem(5),
        out_specs=in_vmem(len(counts)),
        scratch_shapes=[pltpu.VMEM((Y, LOW), jnp.int32)] * 2,
        compiler_params=params(),
        cost_estimate=cost(1e9 * len(set(shifts))),
    )(*tables, before)


def relay_kernel(up, down, from_up, from_down, out_up, out_down):
    half = from_up.shape[0]
    out_up[:half] = (up[:half] + from_up[...].astype(F32)).astype(BF16)
    out_up[half:] = up[half:].astype(BF16)
    out_down[:half] = down[:half].astype(BF16)
    out_down[half:] = (down[half:] + from_down[...].astype(F32)).astype(BF16)


def relay(*args):
    return pl.pallas_call(
        relay_kernel,
        out_shape=[jax.ShapeDtypeStruct(args[0].shape, BF16)] * 2,
        in_specs=in_vmem(4),
        out_specs=in_vmem(2),
        compiler_params=params(),
        cost_estimate=cost(5e8),
    )(*args)


def sum_kernel(own, a, b, out):
    out[...] = (own[...] + a[...].astype(F32) + b[...].astype(F32)).astype(BF16)


def sum_parts(*args):
    return pl.pallas_call(
        sum_kernel,
        out_shape=jax.ShapeDtypeStruct(args[0].shape, BF16),
        in_specs=in_vmem(3),
        out_specs=in_vmem(1)[0],
        compiler_params=params(),
        cost_estimate=cost(5e8),
    )(*args)


def split(value):
    high = value.astype(BF16)
    return high, (value - high.astype(F32)).astype(BF16)


def product(left, right):
    lh, ll = split(left)
    rh, rl = split(right)
    return jnp.dot(
        jnp.concatenate([lh, lh, ll], axis=1),
        jnp.concatenate([rh, rl, rh], axis=0),
        preferred_element_type=F32,
    )


def weights_kernel(parts, out):
    gram, pull = unpack(jnp.sum(parts[...].astype(F32), axis=0))
    row = lax.broadcasted_iota(jnp.int32, (K, K), 0)
    col = lax.broadcasted_iota(jnp.int32, (K, K), 1)
    identity = (row == col).astype(F32)
    system = gram + (K - 1.0) * identity
    squares = jnp.sum(jnp.sum(system * system, axis=0, keepdims=True), axis=1, keepdims=True)
    frob = jnp.sqrt(squares)
    iterate = system / frob
    inverse = 1.5 * identity - 0.5 * iterate
    iterate = product(inverse, iterate)
    for sweep in range(1, ITERS):
        newton = 1.5 * identity - 0.5 * product(inverse, iterate)
        if sweep < ITERS - 1:
            both = product(newton, jnp.concatenate([iterate, inverse], axis=1))
            iterate, inverse = both[:, :K], both[:, K:]
        else:
            inverse = product(newton, inverse)
    shift = product(product(jnp.broadcast_to(pull, (16, K)), inverse), inverse)[0:1] / frob
    out[...] = (jnp.sqrt((K - 1.0) / frob) * inverse.T + shift).astype(BF16)


def transposed_weights(parts):
    return pl.pallas_call(
        weights_kernel,
        out_shape=jax.ShapeDtypeStruct((K, K), BF16),
        in_specs=in_vmem(1),
        out_specs=in_vmem(1)[0],
        compiler_params=params(),
        cost_estimate=cost(4e9),
    )(parts)


def analysis_kernel(own, left, right, state, out):
    rows = state.shape[0]
    weights = jnp.concatenate([own[...], left[...], right[...]], axis=0)
    lane = lax.broadcasted_iota(jnp.int32, (1, 2 * K), 1) % K
    position = (lane.astype(F32) + 0.5) / K
    left_coef = jnp.maximum(0.5 - position, 0.0)
    right_coef = jnp.maximum(position - 0.5, 0.0)
    own_coef = 1.0 - left_coef - right_coef
    side_coef = left_coef + right_coef
    is_left = lane < K // 2
    for pair in range(rows // 2):
        values = [state[2 * pair + i].astype(F32) for i in range(2)]
        means = [jnp.mean(value, axis=0, keepdims=True) for value in values]
        mean = jnp.concatenate(means, axis=1)
        perturb = jnp.concatenate(
            [(values[i] - means[i]).astype(BF16) for i in range(2)], axis=1
        )
        sums = jnp.dot(weights, perturb, preferred_element_type=F32)
        side = jnp.where(is_left, sums[K : 2 * K], sums[2 * K :])
        total = (mean + own_coef * sums[:K] + side_coef * side).astype(BF16)
        for i in range(2):
            out[2 * pair + i] = total[:, i * K : (i + 1) * K]


def analyse(own, left, right, state):
    rows = state.shape[0]
    tile = 8
    small = pl.BlockSpec((K, K), lambda i: (0, 0))
    large = pl.BlockSpec((tile, K, K), lambda i: (i, 0, 0))
    return pl.pallas_call(
        analysis_kernel,
        grid=(rows // tile,),
        out_shape=jax.ShapeDtypeStruct(state.shape, BF16),
        in_specs=[small] * 3 + [large],
        out_specs=large,
        compiler_params=params(),
        cost_estimate=pl.CostEstimate(
            flops=6 * rows * K * K * K, bytes_accessed=4 * rows * K * K, transcendentals=0
        ),
    )(own, left, right, state)


def on_device(departures, innovation, obs_weight, send_rows, send_counts, state):
    n_grid = lax.axis_size("grid")
    near, to_right, to_left = make_messages(departures, innovation, obs_weight, send_rows[0].T)
    other = hop(near, 0, 0, 1)
    left = hop(to_right, 0, 1, 0)
    right = hop(to_left, 0, -1, 0)

    at_end, at_middle = (0, TABLE), (16, 16 + TABLE)
    totals = partial_grams((at_end, at_end), (0, 1), near, other)
    left, right, totals = lax.optimization_barrier((left, right, totals))

    far_low = hop(left[:272], 0, 1, 0)
    far_high = hop(right[256:TABLE], 0, -1, 0)
    left_other = hop(left, 0, 0, 1)
    right_other = hop(right, 0, 0, 1)
    totals = partial_grams((at_middle, at_end), (0, 0), left, right, totals)
    far_low, far_high, left_other, right_other, totals = lax.optimization_barrier(
        (far_low, far_high, left_other, right_other, totals)
    )
    far = (far_low, far_high, hop(far_low, 0, 0, 1), hop(far_high, 0, 0, 1))
    totals = partial_grams((at_middle, at_end), (1, 1), left_other, right_other, totals)

    up, down = last_grams((2, 2), (0, 4), (4, 4), BF16, far, totals)
    from_up, from_down = hop(up, 1, 0, 0), hop(down, -1, 0, 0)
    up, down = last_grams((1, 3), (0, 0), (8, 8), F32, far, totals)
    up, down = relay(up, down, from_up, from_down)
    from_up, from_down = hop(up, 1, 0, 0), hop(down, -1, 0, 0)
    own = last_grams((0,), (0,), (8,), F32, far, totals)[0]
    parts = sum_parts(own, from_up, from_down)
    parts = lax.all_to_all(parts, "obs", 0, 0, tiled=True)

    own = transposed_weights(parts)
    low = lax.ppermute(own, "grid", [(j, (j + 1) % n_grid) for j in range(n_grid)])
    high = lax.ppermute(own, "grid", [(j, (j - 1) % n_grid) for j in range(n_grid)])
    return analyse(own, low, high, state)


def solution(mesh):
    in_specs = (
        P(("obs", "grid"), None),
        P(("obs", "grid")),
        P(("obs", "grid")),
        P(("obs", "grid"), None, None),
        P(("obs", "grid"), None),
        P("obs", None, "grid"),
    )
    out_specs = P("obs", None, "grid")
    return jax.shard_map(
        on_device, mesh=mesh, in_specs=in_specs, out_specs=out_specs, check_vma=False
    )
```

time: 123 us -> 84.6 us (0.69)
  the two profiles are of different devices: /device:TPU:31 before, /device:TPU:32 now
where the time goes in v2:
time: 84.6 us; the launch traced here: 84.2 us
  waiting for transfers between devices  25.4 us (30%)
  Pallas kernels  24 us (28%)
  blocking collectives  17.1 us (20%)
  starting transfers between devices  14.3 us (17%)
  local copies, waits for them, and re-layouts  3.32 us (4%)
    ppermute x13, waiting for transfers between devices, hop(): return lax.ppermute(value, 'grid', pairs)  19.2 us
    all_to_all x1, blocking collectives, on_device(): parts = lax.all_to_all(parts, 'obs', 0, 0, tiled=True)  17.1 us
    ppermute x13, starting transfers between devices, hop(): return lax.ppermute(value, 'grid', pairs)  13.7 us
    pallas_call x3, Pallas kernels, partial_grams(): pl.pallas_call(functools.partial(partial_kernel, starts, cores), out_shap...  12.6 us
    ppermute x1, waiting for transfers between devices, on_device(): lax.ppermute(own, 'grid', [(j, (j + 1) % n_grid) for j in range(n_grid)])  5.15 us
    pallas_call x3, Pallas kernels, last_grams(): pl.pallas_call(functools.partial(last_kernel, shifts, lowest), out_shape=...  4.76 us
    pallas_call x1, Pallas kernels, analyse(): pl.pallas_call(analysis_kernel, grid=(rows // tile,), out_shape=jax.Shape...  3.76 us
    unnamed x10, local copies, waits for them, and re-layouts  3.28 us
  transfers between devices with their start and end apart: 15, of which 8 were waited for; matrix products, arithmetic and copies ran while one was open for 0% of the time, Pallas kernels for 19%

profile of v2, /device:TPU:32, one launch (start us, length us, event | category | flops | bytes accessed | tf_op | source)
XLA Modules:
  0.0 84.2 jit_solution(11471258424958604908)
XLA Ops:
  0.0 0.0 copy-start.1
  0.0 1.0 %copy-done.1 = bf16[2048,128]{1,0:T(8,128)(2,1)S(1)} copy-done((bf16[2048,128]{1,0:T(8,128)(2,1)S(1)}, bf16[2048,128]{1,0:T(8,128)(2,1)}, u32[]{:S(2)}) %copy-start.1) | copy-done | bytes 524312
  1.0 0.8 copy-done.2
  1.9 0.7 copy-done.3
  2.6 0.7 copy-done.4
  3.3 0.4 shard_map.55
  3.7 0.1 collective-permute-start.2
  3.8 1.6 %collective-permute-start = (bf16[560,512]{1,0:T(8,128)(2,1)S(1)}, bf16[560,512]{1,0:T(8,128)(2,1)S(1)}, u32[]{:S(2)}, u32[]{:S(2)}) collective-permute-start(bf16[560,512]{1,0:T(8,128)(2,1)S(1)} %get-tuple-element.22), channel_id=1, source_target_pairs={{0,2},{1,3},{2,4},{3,5},{4,6},{5,7},{6,0},{7,1},{8,10},{9,11},{10,... | collective-permute-start | bytes 1720328 | tf_op jit(solution)/shard_map/ppermute | solution.py:38
  5.4 1.7 %collective-permute-start.1 = (bf16[544,512]{1,0:T(8,128)(2,1)S(1)}, bf16[544,512]{1,0:T(8,128)(2,1)S(1)}, u32[]{:S(2)}, u32[]{:S(2)}) collective-permute-start(bf16[544,512]{1,0:T(8,128)(2,1)S(1)} %get-tuple-element.23), channel_id=1, source_target_pairs={{0,6},{1,7},{2,0},{3,1},{4,2},{5,3},{6,4},{7,5},{8,14},{9,15},{10,... | collective-permute-start | bytes 1671176 | tf_op jit(solution)/shard_map/ppermute | solution.py:38
  7.1 0.0 collective-permute-done.2.second
  7.1 4.2 %shard_map.56.rest_0_ = f32[8,2,144,256]{3,2,1,0:T(8,128)S(1)} custom-call(bf16[544,512]{1,0:T(8,128)(2,1)S(1)} %get-tuple-element.24.first, bf16[544,512]{1,0:T(8,128)(2,1)S(1)} %collective-permute-done.2.second), custom_call_target="tpu_custom_call" | custom-call | flops 4000000000 | bytes 4000000 | tf_op jit(solution)/shard_map/pallas_call | solution.py:154
  11.3 8.7 %collective-permute-done.1.second = bf16[544,512]{1,0:T(8,128)(2,1)S(1)} collective-permute-done((bf16[544,512]{1,0:T(8,128)(2,1)S(1)}, bf16[544,512]{1,0:T(8,128)(2,1)S(1)}, u32[]{:S(2)}, u32[]{:S(2)}) %collective-permute-start.1) | collective-permute-done | bytes 557088 | tf_op jit(solution)/shard_map/ppermute | solution.py:38
  20.0 0.3 collective-permute-done.first
  20.4 0.0 collective-permute-start.5
  20.4 0.5 collective-permute-start.6
  21.0 2.7 %collective-permute-start.4 = (bf16[272,512]{1,0:T(8,128)(2,1)S(1)}, bf16[272,512]{1,0:T(8,128)(2,1)S(1)}, u32[]{:S(2)}, u32[]{:S(2)}) collective-permute-start(bf16[272,512]{1,0:T(8,128)(2,1)S(1)} %slice.7), channel_id=1, source_target_pairs={{0,6},{1,7},{2,0},{3,1},{4,2},{5,3},{6,4},{7,5},{8,14},{9,15},{10,... | collective-permute-start | bytes 835592 | tf_op jit(solution)/shard_map/ppermute | solution.py:38
  23.6 0.0 collective-permute-start.3
  23.6 4.2 %shard_map.57.rest_0_ = f32[8,2,144,256]{3,2,1,0:T(8,128)S(1)} custom-call(bf16[560,512]{1,0:T(8,128)(2,1)S(1)} %collective-permute-done.first, bf16[544,512]{1,0:T(8,128)(2,1)S(1)} %collective-permute-done.1.second, f32[8,2,144,256]{3,2,1,0:T(8,128)S(1)} %shard_map.56.rest_0_), custom_call_target="tpu_custom_call" | custom-call | flops 4000000000 | bytes 4000000 | tf_op jit(solution)/shard_map/pallas_call | solution.py:154
  27.9 1.9 %collective-permute-done.4.a_high = bf16[272,512]{1,0:T(8,128)(2,1)S(1)} collective-permute-done((bf16[272,512]{1,0:T(8,128)(2,1)S(1)}, bf16[272,512]{1,0:T(8,128)(2,1)S(1)}, u32[]{:S(2)}, u32[]{:S(2)}) %collective-permute-start.4) | collective-permute-done | bytes 278560 | tf_op jit(solution)/shard_map/ppermute | solution.py:38
  29.7 3.4 %collective-permute-done.3.a_low = bf16[272,512]{1,0:T(8,128)(2,1)S(1)} collective-permute-done((bf16[272,512]{1,0:T(8,128)(2,1)S(1)}, bf16[272,512]{1,0:T(8,128)(2,1)S(1)}, u32[]{:S(2)}, u32[]{:S(2)}) %collective-permute-start.3) | collective-permute-done | bytes 278560 | tf_op jit(solution)/shard_map/ppermute | solution.py:38
  33.1 0.0 collective-permute-done.6.second
  33.1 0.0 collective-permute-done.5.first
  33.1 0.0 collective-permute-start.7
  33.2 0.5 collective-permute-start.8
  33.7 4.2 %shard_map.58.before = f32[8,2,144,256]{3,2,1,0:T(8,128)S(1)} custom-call(bf16[560,512]{1,0:T(8,128)(2,1)S(1)} %collective-permute-done.5.first, bf16[544,512]{1,0:T(8,128)(2,1)S(1)} %collective-permute-done.6.second, f32[8,2,144,256]{3,2,1,0:T(8,128)S(1)} %shard_map.57.rest_0_), custom_call_target="tpu_custom_call" | custom-call | flops 4000000000 | bytes 4000000 | tf_op jit(solution)/shard_map/pallas_call | solution.py:154
  37.9 0.0 collective-permute-done.7.b_low
  37.9 0.0 collective-permute-done.8.b_high
  37.9 1.2 %shard_map.61 = (bf16[4,112,128]{2,1,0:T(8,128)(2,1)S(1)}, bf16[4,112,128]{2,1,0:T(8,128)(2,1)S(1)}) custom-call(bf16[272,512]{1,0:T(8,128)(2,1)S(1)} %collective-permute-done.3.a_low, bf16[272,512]{1,0:T(8,128)(2,1)S(1)} %collective-permute-done.4.a_high, bf16[272,512]{1,0:T(8,128)(2,1)S(1)} %collective-permute-done.7.b_low, ...), custom_call_target="tpu_custom_call" | custom-call | flops 1000000000 | bytes 4000000 | tf_op jit(solution)/shard_map/pallas_call | solution.py:201
  39.1 1.6 %collective-permute-start.9 = (bf16[4,112,128]{2,1,0:T(8,128)(2,1)S(1)}, bf16[4,112,128]{2,1,0:T(8,128)(2,1)S(1)}, u32[]{:S(2)}, u32[]{:S(2)}) collective-permute-start(bf16[4,112,128]{2,1,0:T(8,128)(2,1)S(1)} %get-tuple-element.35), channel_id=1, source_target_pairs={{0,8},{1,9},{2,10},{3,11},{4,12},{5,13},{6,14},{7,15},{8,16},{9,17... | collective-permute-start | bytes 344072 | tf_op jit(solution)/shard_map/ppermute | solution.py:38
  40.8 1.7 %collective-permute-start.10 = (bf16[4,112,128]{2,1,0:T(8,128)(2,1)S(1)}, bf16[4,112,128]{2,1,0:T(8,128)(2,1)S(1)}, u32[]{:S(2)}, u32[]{:S(2)}) collective-permute-start(bf16[4,112,128]{2,1,0:T(8,128)(2,1)S(1)} %get-tuple-element.36), channel_id=1, source_target_pairs={{0,24},{1,25},{2,26},{3,27},{4,28},{5,29},{6,30},{7,31},{8,0},{9,1... | collective-permute-start | bytes 344072 | tf_op jit(solution)/shard_map/ppermute | solution.py:38
  42.5 2.3 %shard_map.60 = (f32[8,112,128]{2,1,0:T(8,128)S(1)}, f32[8,112,128]{2,1,0:T(8,128)S(1)}) custom-call(bf16[272,512]{1,0:T(8,128)(2,1)S(1)} %collective-permute-done.3.a_low, bf16[272,512]{1,0:T(8,128)(2,1)S(1)} %collective-permute-done.4.a_high, bf16[272,512]{1,0:T(8,128)(2,1)S(1)} %collective-permute-done.7.b_low, ...), custom_call_target="tpu_custom_call" | custom-call | flops 2000000000 | bytes 4000000 | tf_op jit(solution)/shard_map/pallas_call | solution.py:201
  44.8 1.0 %collective-permute-done.9.from_up = bf16[4,112,128]{2,1,0:T(8,128)(2,1)S(1)} collective-permute-done((bf16[4,112,128]{2,1,0:T(8,128)(2,1)S(1)}, bf16[4,112,128]{2,1,0:T(8,128)(2,1)S(1)}, u32[]{:S(2)}, u32[]{:S(2)}) %collective-permute-start.9) | collective-permute-done | bytes 114720 | tf_op jit(solution)/shard_map/ppermute | solution.py:38
  45.8 0.0 collective-permute-done.10.from_down
  45.8 0.1 shard_map.62
  45.9 1.6 %collective-permute-start.11 = (bf16[8,112,128]{2,1,0:T(8,128)(2,1)S(1)}, bf16[8,112,128]{2,1,0:T(8,128)(2,1)S(1)}, u32[]{:S(2)}, u32[]{:S(2)}) collective-permute-start(bf16[8,112,128]{2,1,0:T(8,128)(2,1)S(1)} %get-tuple-element.37), channel_id=1, source_target_pairs={{0,8},{1,9},{2,10},{3,11},{4,12},{5,13},{6,14},{7,15},{8,16},{9,17... | collective-permute-start | bytes 688136 | tf_op jit(solution)/shard_map/ppermute | solution.py:38
  47.5 1.7 %collective-permute-start.12 = (bf16[8,112,128]{2,1,0:T(8,128)(2,1)S(1)}, bf16[8,112,128]{2,1,0:T(8,128)(2,1)S(1)}, u32[]{:S(2)}, u32[]{:S(2)}) collective-permute-start(bf16[8,112,128]{2,1,0:T(8,128)(2,1)S(1)} %get-tuple-element.38), channel_id=1, source_target_pairs={{0,24},{1,25},{2,26},{3,27},{4,28},{5,29},{6,30},{7,31},{8,0},{9,1... | collective-permute-start | bytes 688136 | tf_op jit(solution)/shard_map/ppermute | solution.py:38
  49.2 1.2 %shard_map.59.own = f32[8,112,128]{2,1,0:T(8,128)S(1)} custom-call(bf16[272,512]{1,0:T(8,128)(2,1)S(1)} %collective-permute-done.3.a_low, bf16[272,512]{1,0:T(8,128)(2,1)S(1)} %collective-permute-done.4.a_high, bf16[272,512]{1,0:T(8,128)(2,1)S(1)} %collective-permute-done.7.b_low, bf16[272,512]{1,0:T(8,128)(2,1)S(1)} %collective-permute-done.8.b_high, ...), custom_call_target="tpu_custom_call" | custom-call | flops 1000000000 | bytes 4000000 | tf_op jit(solution)/shard_map/pallas_call | solution.py:201
  50.4 3.7 %collective-permute-done.11.a = bf16[8,112,128]{2,1,0:T(8,128)(2,1)S(1)} collective-permute-done((bf16[8,112,128]{2,1,0:T(8,128)(2,1)S(1)}, bf16[8,112,128]{2,1,0:T(8,128)(2,1)S(1)}, u32[]{:S(2)}, u32[]{:S(2)}) %collective-permute-start.11) | collective-permute-done | bytes 229408 | tf_op jit(solution)/shard_map/ppermute | solution.py:38
  54.2 0.0 collective-permute-done.12.b
  54.2 0.1 shard_map.63
  54.3 17.1 %all_to_all.5.parts = bf16[8,112,128]{2,1,0:T(8,128)(2,1)S(1)} all-to-all(bf16[8,112,128]{2,1,0:T(8,128)(2,1)S(1)} %shard_map.63), channel_id=1, replica_groups=mesh['obs'=8,'grid'=32] {'obs'}, dimensions={0} | all-to-all | bytes 458752 | tf_op jit(solution)/shard_map/all_to_all | solution.py:365
  71.3 2.3 %shard_map.64.own = bf16[128,128]{1,0:T(8,128)(2,1)S(1)} custom-call(bf16[8,112,128]{2,1,0:T(8,128)(2,1)S(1)} %all_to_all.5.parts), custom_call_target="tpu_custom_call" | custom-call | flops 4000000000 | bytes 4000000 | tf_op jit(solution)/shard_map/pallas_call | solution.py:284
  73.6 0.1 collective-permute-start.14
  73.7 0.5 collective-permute-start.13
  74.2 1.1 %collective-permute-done.14.right = bf16[128,128]{1,0:T(8,128)(2,1)S(1)} collective-permute-done((bf16[128,128]{1,0:T(8,128)(2,1)S(1)}, bf16[128,128]{1,0:T(8,128)(2,1)S(1)}, u32[]{:S(2)}, u32[]{:S(2)}) %collective-permute-start.14) | collective-permute-done | bytes 32800 | tf_op jit(solution)/shard_map/ppermute | solution.py:369
  75.3 5.1 %collective-permute-done.13.left = bf16[128,128]{1,0:T(8,128)(2,1)S(1)} collective-permute-done((bf16[128,128]{1,0:T(8,128)(2,1)S(1)}, bf16[128,128]{1,0:T(8,128)(2,1)S(1)}, u32[]{:S(2)}, u32[]{:S(2)}) %collective-permute-start.13) | collective-permute-done | bytes 32800 | tf_op jit(solution)/shard_map/ppermute | solution.py:368
  80.5 0.0 copy-done
  80.5 3.8 %shard_map.65 = bf16[48,128,128]{2,1,0:T(8,128)(2,1)} custom-call(bf16[128,128]{1,0:T(8,128)(2,1)S(1)} %shard_map.64.own, bf16[128,128]{1,0:T(8,128)(2,1)S(1)} %collective-permute-done.13.left, bf16[128,128]{1,0:T(8,128)(2,1)S(1)} %collective-permute-done.14.right, bf16[48,128,128]{2,1,0:T(8,128)(2,1)S(1)} %copy-done), custom_call_target="tpu_custom_call" | custom-call | flops 603979776 | bytes 3145728 | tf_op jit(solution)/shard_map/pallas_call | solution.py:323
  (6 shorter events, 0.0 us)
Async XLA Ops:
  0.0 1.0 %copy-start.1 = (bf16[2048,128]{1,0:T(8,128)(2,1)S(1)}, bf16[2048,128]{1,0:T(8,128)(2,1)}, u32[]{:S(2)}) copy-start(bf16[2048,128]{1,0:T(8,128)(2,1)} %departures.1) | copy-start | bytes 1572868
  1.0 0.8 copy-start.2
  1.9 0.7 copy-start.3
  2.6 0.7 copy-start.4
  3.7 3.4 %collective-permute-start.2 = (bf16[544,512]{1,0:T(8,128)(2,1)S(1)}, bf16[544,512]{1,0:T(8,128)(2,1)S(1)}, u32[]{:S(2)}, u32[]{:S(2)}) collective-permute-start(bf16[544,512]{1,0:T(8,128)(2,1)S(1)} %get-tuple-element.24.first), channel_id=1, source_target_pairs={{0,1},{1,0},{2,3},{3,2},{4,5},{5,4},{6,7},{7,6},{8,9},{9,8},{10,11... | collective-permute-start | bytes 1671176 | tf_op jit(solution)/shard_map/ppermute | solution.py:38
  3.8 16.6 %collective-permute-start = (bf16[560,512]{1,0:T(8,128)(2,1)S(1)}, bf16[560,512]{1,0:T(8,128)(2,1)S(1)}, u32[]{:S(2)}, u32[]{:S(2)}) collective-permute-start(bf16[560,512]{1,0:T(8,128)(2,1)S(1)} %get-tuple-element.22), channel_id=1, source_target_pairs={{0,2},{1,3},{2,4},{3,5},{4,6},{5,7},{6,0},{7,1},{8,10},{9,11},{10,... | collective-permute-start | bytes 1720328 | tf_op jit(solution)/shard_map/ppermute | solution.py:38
  5.4 14.7 %collective-permute-start.1 = (bf16[544,512]{1,0:T(8,128)(2,1)S(1)}, bf16[544,512]{1,0:T(8,128)(2,1)S(1)}, u32[]{:S(2)}, u32[]{:S(2)}) collective-permute-start(bf16[544,512]{1,0:T(8,128)(2,1)S(1)} %get-tuple-element.23), channel_id=1, source_target_pairs={{0,6},{1,7},{2,0},{3,1},{4,2},{5,3},{6,4},{7,5},{8,14},{9,15},{10,... | collective-permute-start | bytes 1671176 | tf_op jit(solution)/shard_map/ppermute | solution.py:38
  20.4 12.8 %collective-permute-start.5 = (bf16[560,512]{1,0:T(8,128)(2,1)S(1)}, bf16[560,512]{1,0:T(8,128)(2,1)S(1)}, u32[]{:S(2)}, u32[]{:S(2)}) collective-permute-start(bf16[560,512]{1,0:T(8,128)(2,1)S(1)} %collective-permute-done.first), channel_id=1, source_target_pairs={{0,1},{1,0},{2,3},{3,2},{4,5},{5,4},{6,7},{7,6},{8,9},{9,8},{10,11... | collective-permute-start | bytes 1720328 | tf_op jit(solution)/shard_map/ppermute | solution.py:38
  20.4 12.7 %collective-permute-start.6 = (bf16[544,512]{1,0:T(8,128)(2,1)S(1)}, bf16[544,512]{1,0:T(8,128)(2,1)S(1)}, u32[]{:S(2)}, u32[]{:S(2)}) collective-permute-start(bf16[544,512]{1,0:T(8,128)(2,1)S(1)} %collective-permute-done.1.second), channel_id=1, source_target_pairs={{0,1},{1,0},{2,3},{3,2},{4,5},{5,4},{6,7},{7,6},{8,9},{9,8},{10,11... | collective-permute-start | bytes 1671176 | tf_op jit(solution)/shard_map/ppermute | solution.py:38
  21.0 8.8 %collective-permute-start.4 = (bf16[272,512]{1,0:T(8,128)(2,1)S(1)}, bf16[272,512]{1,0:T(8,128)(2,1)S(1)}, u32[]{:S(2)}, u32[]{:S(2)}) collective-permute-start(bf16[272,512]{1,0:T(8,128)(2,1)S(1)} %slice.7), channel_id=1, source_target_pairs={{0,6},{1,7},{2,0},{3,1},{4,2},{5,3},{6,4},{7,5},{8,14},{9,15},{10,... | collective-permute-start | bytes 835592 | tf_op jit(solution)/shard_map/ppermute | solution.py:38
  23.6 9.5 %collective-permute-start.3 = (bf16[272,512]{1,0:T(8,128)(2,1)S(1)}, bf16[272,512]{1,0:T(8,128)(2,1)S(1)}, u32[]{:S(2)}, u32[]{:S(2)}) collective-permute-start(bf16[272,512]{1,0:T(8,128)(2,1)S(1)} %slice.6), channel_id=1, source_target_pairs={{0,2},{1,3},{2,4},{3,5},{4,6},{5,7},{6,0},{7,1},{8,10},{9,11},{10,... | collective-permute-start | bytes 835592 | tf_op jit(solution)/shard_map/ppermute | solution.py:38
  33.1 4.7 %collective-permute-start.7 = (bf16[272,512]{1,0:T(8,128)(2,1)S(1)}, bf16[272,512]{1,0:T(8,128)(2,1)S(1)}, u32[]{:S(2)}, u32[]{:S(2)}) collective-permute-start(bf16[272,512]{1,0:T(8,128)(2,1)S(1)} %collective-permute-done.3.a_low), channel_id=1, source_target_pairs={{0,1},{1,0},{2,3},{3,2},{4,5},{5,4},{6,7},{7,6},{8,9},{9,8},{10,11... | collective-permute-start | bytes 835592 | tf_op jit(solution)/shard_map/ppermute | solution.py:38
  33.2 4.7 %collective-permute-start.8 = (bf16[272,512]{1,0:T(8,128)(2,1)S(1)}, bf16[272,512]{1,0:T(8,128)(2,1)S(1)}, u32[]{:S(2)}, u32[]{:S(2)}) collective-permute-start(bf16[272,512]{1,0:T(8,128)(2,1)S(1)} %collective-permute-done.4.a_high), channel_id=1, source_target_pairs={{0,1},{1,0},{2,3},{3,2},{4,5},{5,4},{6,7},{7,6},{8,9},{9,8},{10,11... | collective-permute-start | bytes 835592 | tf_op jit(solution)/shard_map/ppermute | solution.py:38
  39.1 6.7 %collective-permute-start.9 = (bf16[4,112,128]{2,1,0:T(8,128)(2,1)S(1)}, bf16[4,112,128]{2,1,0:T(8,128)(2,1)S(1)}, u32[]{:S(2)}, u32[]{:S(2)}) collective-permute-start(bf16[4,112,128]{2,1,0:T(8,128)(2,1)S(1)} %get-tuple-element.35), channel_id=1, source_target_pairs={{0,8},{1,9},{2,10},{3,11},{4,12},{5,13},{6,14},{7,15},{8,16},{9,17... | collective-permute-start | bytes 344072 | tf_op jit(solution)/shard_map/ppermute | solution.py:38
  40.8 5.1 %collective-permute-start.10 = (bf16[4,112,128]{2,1,0:T(8,128)(2,1)S(1)}, bf16[4,112,128]{2,1,0:T(8,128)(2,1)S(1)}, u32[]{:S(2)}, u32[]{:S(2)}) collective-permute-start(bf16[4,112,128]{2,1,0:T(8,128)(2,1)S(1)} %get-tuple-element.36), channel_id=1, source_target_pairs={{0,24},{1,25},{2,26},{3,27},{4,28},{5,29},{6,30},{7,31},{8,0},{9,1... | collective-permute-start | bytes 344072 | tf_op jit(solution)/shard_map/ppermute | solution.py:38
  45.9 8.3 %collective-permute-start.11 = (bf16[8,112,128]{2,1,0:T(8,128)(2,1)S(1)}, bf16[8,112,128]{2,1,0:T(8,128)(2,1)S(1)}, u32[]{:S(2)}, u32[]{:S(2)}) collective-permute-start(bf16[8,112,128]{2,1,0:T(8,128)(2,1)S(1)} %get-tuple-element.37), channel_id=1, source_target_pairs={{0,8},{1,9},{2,10},{3,11},{4,12},{5,13},{6,14},{7,15},{8,16},{9,17... | collective-permute-start | bytes 688136 | tf_op jit(solution)/shard_map/ppermute | solution.py:38
  47.5 6.6 %collective-permute-start.12 = (bf16[8,112,128]{2,1,0:T(8,128)(2,1)S(1)}, bf16[8,112,128]{2,1,0:T(8,128)(2,1)S(1)}, u32[]{:S(2)}, u32[]{:S(2)}) collective-permute-start(bf16[8,112,128]{2,1,0:T(8,128)(2,1)S(1)} %get-tuple-element.38), channel_id=1, source_target_pairs={{0,24},{1,25},{2,26},{3,27},{4,28},{5,29},{6,30},{7,31},{8,0},{9,1... | collective-permute-start | bytes 688136 | tf_op jit(solution)/shard_map/ppermute | solution.py:38
  71.3 9.1 %copy-start = (bf16[48,128,128]{2,1,0:T(8,128)(2,1)S(1)}, bf16[48,128,128]{2,1,0:T(8,128)(2,1)}, u32[]{:S(2)}) copy-start(bf16[48,128,128]{2,1,0:T(8,128)(2,1)} %state.1) | copy-start | bytes 4718596
  73.6 1.7 %collective-permute-start.14 = (bf16[128,128]{1,0:T(8,128)(2,1)S(1)}, bf16[128,128]{1,0:T(8,128)(2,1)S(1)}, u32[]{:S(2)}, u32[]{:S(2)}) collective-permute-start(bf16[128,128]{1,0:T(8,128)(2,1)S(1)} %shard_map.64.own), channel_id=1, source_target_pairs={{0,31},{1,0},{2,1},{3,2},{4,3},{5,4},{6,5},{7,6},{8,7},{9,8},{10,9... | collective-permute-start | bytes 98312 | tf_op jit(solution)/shard_map/ppermute | solution.py:369
  73.7 6.7 %collective-permute-start.13 = (bf16[128,128]{1,0:T(8,128)(2,1)S(1)}, bf16[128,128]{1,0:T(8,128)(2,1)S(1)}, u32[]{:S(2)}, u32[]{:S(2)}) collective-permute-start(bf16[128,128]{1,0:T(8,128)(2,1)S(1)} %shard_map.64.own), channel_id=1, source_target_pairs={{0,1},{1,2},{2,3},{3,4},{4,5},{5,6},{6,7},{7,8},{8,9},{9,10},{10,1... | collective-permute-start | bytes 98312 | tf_op jit(solution)/shard_map/ppermute | solution.py:368

commit v3 on v2

--- a/solution.py
+++ b/solution.py
@@ -42,7 +42,17 @@
     return (((m,), (n,)), ((), ()))
 
 
-def message_kernel(departures, innovation, obs_weight, send_rows, near, to_right, to_left, turned):
+def message_kernel(*refs):
+    sources, (near, to_right, to_left), held = refs[:4], refs[4:7], refs[7:11]
+    turned, sems = refs[11:]
+    copies = [
+        pltpu.make_async_copy(source, place, sems.at[i])
+        for i, (source, place) in enumerate(zip(sources, held))
+    ]
+    for copy in copies[::-1]:
+        copy.start()
+    departures, innovation, obs_weight, send_rows = held
+    copies[3].wait()
     grid = lax.axis_index("grid")
     x, c = lax.rem(lax.div(grid, CORES), X), lax.rem(grid, CORES)
     turned[...] = send_rows[...].T
@@ -65,6 +75,8 @@
     to_right[:16, :] = groups[2]
     to_right[16 + TABLE :, :] = groups[1]
     to_left[TABLE:, :] = groups[3]
+    for copy in copies[:3]:
+        copy.wait()
     root = jnp.sqrt(obs_weight[...].reshape(1, BLOCKS * LOW))
     innov = innovation[...].reshape(1, BLOCKS * LOW) * root
     row = lax.broadcasted_iota(jnp.int32, (16, LOW), 0)
@@ -82,18 +94,19 @@
     to_left[BLOCKS * K : TABLE, :] = tail
 
 
-def make_messages(departures, innovation, obs_weight, send_rows):
+def make_messages(*args):
     return pl.pallas_call(
         message_kernel,
         out_shape=[
             jax.ShapeDtypeStruct((TABLE + extra, LOW), BF16) for extra in (16, 32, 16)
         ],
-        in_specs=in_vmem(4),
+        in_specs=[pl.BlockSpec(memory_space=pltpu.HBM)] * 4,
         out_specs=in_vmem(3),
-        scratch_shapes=[pltpu.VMEM((send_rows.shape[1], send_rows.shape[0]), jnp.int32)],
-        compiler_params=params(),
+        scratch_shapes=[pltpu.VMEM(arg.shape, arg.dtype) for arg in args]
+        + [pltpu.VMEM(args[3].shape[::-1], jnp.int32), pltpu.SemaphoreType.DMA((4,))],
+        compiler_params=pltpu.CompilerParams(vmem_limit_bytes=60 * 1024 * 1024),
         cost_estimate=cost(2e9),
-    )(departures, innovation, obs_weight, send_rows)
+    )(*args)
 
 
 def read_picks(group, core):
@@ -118,46 +131,44 @@
     return jnp.concatenate([members, jnp.broadcast_to(innov, (16, 256))], axis=0).astype(BF16)
 
 
-def grams(first, second, first_picks, second_picks):
-    a, b = pick(first, first_picks), pick(second, second_picks)
-    even = lax.broadcasted_iota(jnp.int32, (K, 256), 1) % K < K // 2
+def grams(tables, picks):
+    found = [pick(*pair) for pair in zip(tables, picks)]
+    lane = lax.broadcasted_iota(jnp.int32, (K, len(found) * K), 1)
+    even = lane % K < K // 2
     totals = []
     for half in range(2):
         span = slice(half * K, (half + 1) * K)
-        both = jnp.concatenate([a[:, span], b[:, span]], axis=1)
-        rows = both[:K]
+        parts = [part[:, span] for part in found]
+        joined = jnp.concatenate(parts, axis=1) if len(parts) > 1 else parts[0]
+        rows = joined[:K]
         none = jnp.zeros_like(rows)
         split = jnp.concatenate([jnp.where(even, rows, none), jnp.where(even, none, rows)], axis=0)
-        totals.append(lax.dot_general(both, split, dims(1, 1), preferred_element_type=F32))
+        totals.append(lax.dot_general(joined, split, dims(1, 1), preferred_element_type=F32))
     return totals
 
 
-def partial_kernel(starts, cores, first, second, *rest):
-    out = rest[-1]
-    messages = (first, second)
+def partial_kernel(sources, chained, *refs):
+    out = refs[-1]
     picks = [
-        read_picks(ref[at : at + 16, :], core)
-        for ref, (_, at), core in zip(messages, starts, cores)
+        read_picks(refs[which][at : at + 16, :], core) for _, (which, at, core) in sources
     ]
     for step in range(2 * Y):
         y, span = step // 2, slice(step % 2 * 256, step % 2 * 256 + 256)
-        tables = [[ref[at : at + TABLE, :]] for ref, (at, _) in zip(messages, starts)]
-        totals = grams(*tables, picks[0][y : y + 1, span], picks[1][y : y + 1, span])
+        tables = [[refs[which][at:end, :] for which, at, end in parts] for parts, _ in sources]
+        totals = grams(tables, [values[y : y + 1, span] for values in picks])
         for half in range(2):
-            if len(rest) > 1:
-                out[step, half] = totals[half] + rest[0][step, half]
-            else:
-                out[step, half] = totals[half]
-
-
-def partial_grams(starts, cores, *args):
-    return pl.pallas_call(
-        functools.partial(partial_kernel, starts, cores),
+            out[step, half] = totals[half] + refs[-2][step, half] if chained else totals[half]
+
+
+def partial_grams(sources, messages, before=None):
+    args = tuple(messages) + (() if before is None else (before,))
+    return pl.pallas_call(
+        functools.partial(partial_kernel, sources, before is not None),
         out_shape=jax.ShapeDtypeStruct((2 * Y, 2, 144, 256), F32),
         in_specs=in_vmem(len(args)),
         out_specs=in_vmem(1)[0],
         compiler_params=params(),
-        cost_estimate=cost(4e9),
+        cost_estimate=cost(2e9 * len(sources)),
     )(*args)
 
 
@@ -176,37 +187,35 @@
     return jnp.concatenate([packed[0:64], lower], axis=0) + corner.T, packed[96:97]
 
 
-def last_kernel(shifts, lowest, a_low, a_high, b_low, b_high, before, *rest):
-    outs, a_picks, b_picks = rest[:-2], rest[-2], rest[-1]
+def last_kernel(shifts, lowest, low, high, before, *rest):
+    outs, picks = rest[:-1], rest[-1]
     place = lax.div(lax.axis_index("grid"), X * CORES)
-    a_picks[...] = read_picks(a_low[0:16, :], 0)
-    b_picks[...] = read_picks(b_low[0:16, :], 1)
-    tables = [[low[16:, :], high[...]] for low, high in ((a_low, a_high), (b_low, b_high))]
+    picks[...] = read_picks(low[0:16, :], 1)
+    table = [low[16:, :], high[...]]
     for shift in sorted(set(shifts)):
         y = lax.rem(place + shift, Y)
         for i in range(2):
             span = slice(i * 256, i * 256 + 256)
-            picks = [ref[pl.ds(y, 1), :][:, span] for ref in (a_picks, b_picks)]
-            totals = grams(*tables, *picks)
+            totals = grams([table], [picks[pl.ds(y, 1), :][:, span]])
             for half in range(2):
                 total = totals[half] + before[2 * y + i, half]
                 for side in range(2):
                     patch = i + 2 * half + 4 * side
-                    for out, its_shift, low in zip(outs, shifts, lowest):
-                        if its_shift == shift and low <= patch < low + out.shape[0]:
-                            out[patch - low] = pack(total, side).astype(out.dtype)
-
-
-def last_grams(shifts, lowest, counts, dtype, tables, before):
+                    for out, its_shift, first in zip(outs, shifts, lowest):
+                        if its_shift == shift and first <= patch < first + out.shape[0]:
+                            out[patch - first] = pack(total, side).astype(out.dtype)
+
+
+def last_grams(shifts, lowest, counts, dtype, low, high, before):
     return pl.pallas_call(
         functools.partial(last_kernel, shifts, lowest),
         out_shape=[jax.ShapeDtypeStruct((count, PACK, K), dtype) for count in counts],
-        in_specs=in_vmem(5),
+        in_specs=in_vmem(3),
         out_specs=in_vmem(len(counts)),
-        scratch_shapes=[pltpu.VMEM((Y, LOW), jnp.int32)] * 2,
-        compiler_params=params(),
-        cost_estimate=cost(1e9 * len(set(shifts))),
-    )(*tables, before)
+        scratch_shapes=[pltpu.VMEM((Y, LOW), jnp.int32)],
+        compiler_params=params(),
+        cost_estimate=cost(5e8 * len(set(shifts))),
+    )(low, high, before)
 
 
 def relay_kernel(up, down, from_up, from_down, out_up, out_down):
@@ -291,46 +300,88 @@
     )(parts)
 
 
-def analysis_kernel(own, left, right, state, out):
-    rows = state.shape[0]
-    weights = jnp.concatenate([own[...], left[...], right[...]], axis=0)
+def perturb_kernel(state, mean, perturb):
+    for pair in range(mean.shape[0]):
+        for i in range(2):
+            span = slice(i * K, (i + 1) * K)
+            values = state[2 * pair + i].astype(F32)
+            average = jnp.mean(values, axis=0, keepdims=True)
+            mean[pair : pair + 1, span] = average
+            perturb[pair, :, span] = (values - average).astype(BF16)
+
+
+def perturbations(state):
+    pairs = state.shape[0] // 2
+    return pl.pallas_call(
+        perturb_kernel,
+        out_shape=[
+            jax.ShapeDtypeStruct((pairs, 2 * K), F32),
+            jax.ShapeDtypeStruct((pairs, K, 2 * K), BF16),
+        ],
+        in_specs=in_vmem(1),
+        out_specs=in_vmem(2),
+        compiler_params=params(),
+        cost_estimate=cost(2e9),
+    )(state)
+
+
+def column_coefs():
     lane = lax.broadcasted_iota(jnp.int32, (1, 2 * K), 1) % K
     position = (lane.astype(F32) + 0.5) / K
-    left_coef = jnp.maximum(0.5 - position, 0.0)
-    right_coef = jnp.maximum(position - 0.5, 0.0)
+    return lane, jnp.maximum(0.5 - position, 0.0), jnp.maximum(position - 0.5, 0.0)
+
+
+def own_kernel(own, mean, perturb, out):
+    _, left_coef, right_coef = column_coefs()
     own_coef = 1.0 - left_coef - right_coef
-    side_coef = left_coef + right_coef
-    is_left = lane < K // 2
-    for pair in range(rows // 2):
-        values = [state[2 * pair + i].astype(F32) for i in range(2)]
-        means = [jnp.mean(value, axis=0, keepdims=True) for value in values]
-        mean = jnp.concatenate(means, axis=1)
-        perturb = jnp.concatenate(
-            [(values[i] - means[i]).astype(BF16) for i in range(2)], axis=1
-        )
-        sums = jnp.dot(weights, perturb, preferred_element_type=F32)
-        side = jnp.where(is_left, sums[K : 2 * K], sums[2 * K :])
-        total = (mean + own_coef * sums[:K] + side_coef * side).astype(BF16)
-        for i in range(2):
-            out[2 * pair + i] = total[:, i * K : (i + 1) * K]
-
-
-def analyse(own, left, right, state):
-    rows = state.shape[0]
-    tile = 8
-    small = pl.BlockSpec((K, K), lambda i: (0, 0))
-    large = pl.BlockSpec((tile, K, K), lambda i: (i, 0, 0))
-    return pl.pallas_call(
-        analysis_kernel,
-        grid=(rows // tile,),
-        out_shape=jax.ShapeDtypeStruct(state.shape, BF16),
-        in_specs=[small] * 3 + [large],
-        out_specs=large,
-        compiler_params=params(),
-        cost_estimate=pl.CostEstimate(
-            flops=6 * rows * K * K * K, bytes_accessed=4 * rows * K * K, transcendentals=0
-        ),
-    )(own, left, right, state)
+    for pair in range(mean.shape[0]):
+        sums = jnp.dot(own[...], perturb[pair], preferred_element_type=F32)
+        out[pair] = mean[pair : pair + 1] + own_coef * sums
+
+
+def own_part(own, mean, perturb):
+    return pl.pallas_call(
+        own_kernel,
+        out_shape=jax.ShapeDtypeStruct(perturb.shape, F32),
+        in_specs=in_vmem(3),
+        out_specs=in_vmem(1)[0],
+        compiler_params=params(),
+        cost_estimate=cost(2e9),
+    )(own, mean, perturb)
+
+
+def side_kernel(left, right, part, perturb, out, held, sems):
+    lane, left_coef, right_coef = column_coefs()
+    coef = left_coef + right_coef
+    weights = jnp.concatenate([left[...], right[...]], axis=0)
+    chunks = sems.shape[0]
+    pairs = perturb.shape[0] // chunks
+    copies = []
+    for chunk in range(chunks):
+        for pair in range(chunk * pairs, (chunk + 1) * pairs):
+            sums = jnp.dot(weights, perturb[pair], preferred_element_type=F32)
+            side = jnp.where(lane < K // 2, sums[:K], sums[K:])
+            total = (part[pair] + coef * side).astype(BF16)
+            for i in range(2):
+                held[2 * pair + i] = total[:, i * K : (i + 1) * K]
+        rows = pl.ds(2 * chunk * pairs, 2 * pairs)
+        copies.append(pltpu.make_async_copy(held.at[rows], out.at[rows], sems.at[chunk]))
+        copies[-1].start()
+    for copy in copies:
+        copy.wait()
+
+
+def add_sides(left, right, part, perturb):
+    shape = (2 * perturb.shape[0], K, K)
+    return pl.pallas_call(
+        side_kernel,
+        out_shape=jax.ShapeDtypeStruct(shape, BF16),
+        in_specs=in_vmem(4),
+        out_specs=pl.BlockSpec(memory_space=pltpu.HBM),
+        scratch_shapes=[pltpu.VMEM(shape, BF16), pltpu.SemaphoreType.DMA((6,))],
+        compiler_params=params(),
+        cost_estimate=cost(2e9),
+    )(left, right, part, perturb)
 
 
 def on_device(departures, innovation, obs_weight, send_rows, send_counts, state):
@@ -340,34 +391,47 @@
     left = hop(to_right, 0, 1, 0)
     right = hop(to_left, 0, -1, 0)
 
-    at_end, at_middle = (0, TABLE), (16, 16 + TABLE)
-    totals = partial_grams((at_end, at_end), (0, 1), near, other)
-    left, right, totals = lax.optimization_barrier((left, right, totals))
-
-    far_low = hop(left[:272], 0, 1, 0)
-    far_high = hop(right[256:TABLE], 0, -1, 0)
+    def at_end(which, core):
+        return (((which, 0, TABLE),), (which, TABLE, core))
+
+    def at_middle(which, core):
+        return (((which, 16, 16 + TABLE),), (which, 16 + TABLE, core))
+
+    totals = partial_grams((at_end(0, 0), at_end(1, 1)), (near, other))
+    mean, perturb = perturbations(state)
+    left, right, totals, mean, perturb = lax.optimization_barrier(
+        (left, right, totals, mean, perturb)
+    )
+    far_low, far_high = left[:272], right[256:TABLE]
+    far_low, far_high, left, right = lax.optimization_barrier((far_low, far_high, left, right))
+
+    far_low = hop(far_low, 0, 1, 0)
+    far_high = hop(far_high, 0, -1, 0)
     left_other = hop(left, 0, 0, 1)
     right_other = hop(right, 0, 0, 1)
-    totals = partial_grams((at_middle, at_end), (0, 0), left, right, totals)
-    far_low, far_high, left_other, right_other, totals = lax.optimization_barrier(
-        (far_low, far_high, left_other, right_other, totals)
-    )
-    far = (far_low, far_high, hop(far_low, 0, 0, 1), hop(far_high, 0, 0, 1))
-    totals = partial_grams((at_middle, at_end), (1, 1), left_other, right_other, totals)
-
-    up, down = last_grams((2, 2), (0, 4), (4, 4), BF16, far, totals)
+    totals = partial_grams((at_middle(0, 0), at_end(1, 0)), (left, right), totals)
+    totals = partial_grams((at_middle(0, 1), at_end(1, 1)), (left_other, right_other), totals)
+    far_low, far_high, totals = lax.optimization_barrier((far_low, far_high, totals))
+    far_low_other = hop(far_low, 0, 0, 1)
+    far_high_other = hop(far_high, 0, 0, 1)
+    source = (((0, 16, 272), (1, 0, 272)), (0, 0, 0))
+    totals = partial_grams((source,), (far_low, far_high), totals)
+    last = (far_low_other, far_high_other, totals)
+
+    up, down = last_grams((2, 2), (0, 4), (4, 4), BF16, *last)
     from_up, from_down = hop(up, 1, 0, 0), hop(down, -1, 0, 0)
-    up, down = last_grams((1, 3), (0, 0), (8, 8), F32, far, totals)
+    up, down = last_grams((1, 3), (0, 0), (8, 8), F32, *last)
     up, down = relay(up, down, from_up, from_down)
     from_up, from_down = hop(up, 1, 0, 0), hop(down, -1, 0, 0)
-    own = last_grams((0,), (0,), (8,), F32, far, totals)[0]
+    own = last_grams((0,), (0,), (8,), F32, *last)[0]
     parts = sum_parts(own, from_up, from_down)
     parts = lax.all_to_all(parts, "obs", 0, 0, tiled=True)
 
     own = transposed_weights(parts)
     low = lax.ppermute(own, "grid", [(j, (j + 1) % n_grid) for j in range(n_grid)])
     high = lax.ppermute(own, "grid", [(j, (j - 1) % n_grid) for j in range(n_grid)])
-    return analyse(own, low, high, state)
+    part = own_part(own, mean, perturb)
+    return add_sides(low, high, part, perturb)
 
 
 def solution(mesh):

time: 84.6 us -> 79.6 us (0.941)
  waiting for transfers between devices: 25.4 us -> 20 us
  local copies, waits for them, and re-layouts: 3.32 us -> 0.05 us
  Pallas kernels: 24 us -> 26.7 us
  starting transfers between devices: 14.3 us -> 15.2 us
    ppermute x13, waiting for transfers between devices: 19.2 us -> 14.3 us  [hop(): return lax.ppermute(value, 'grid', pairs)]
    unnamed x10 -> x4, local copies, waits for them, and re-layouts: 3.28 us -> 0.01 us
    pallas_call x1, Pallas kernels: 0.41 us -> 2.66 us  [make_messages(): pl.pallas_call(message_kernel, out_shape=[jax.ShapeDtypeStruct((TABLE + e...]
    pallas_call x4 -> x7, Pallas kernels: 16.4 us -> 18.3 us  [the longest x4 15.4 us: partial_grams(): pl.pallas_call(functools.partial(partial_kernel, sources, before is not N...]
    pallas_call x3, Pallas kernels: 4.76 us -> 3.25 us  [last_grams(): pl.pallas_call(functools.partial(last_kernel, shifts, lowest), out_shape=...]
    ppermute x13, starting transfers between devices: 13.7 us -> 14.7 us  [hop(): return lax.ppermute(value, 'grid', pairs)]
  transfers between devices with their start and end apart: 15 -> 15, of which waited for: 8 -> 6; matrix products, arithmetic and copies ran while one was open for 0% -> 0% of each run, Pallas kernels for 19% -> 24%
where the time goes in v3:
time: 79.6 us; the launch traced here: 79.4 us
  Pallas kernels  26.7 us (34%)
  waiting for transfers between devices  20 us (25%)
  blocking collectives  17 us (21%)
  starting transfers between devices  15.2 us (19%)
    all_to_all x1, blocking collectives, on_device(): parts = lax.all_to_all(parts, 'obs', 0, 0, tiled=True)  17 us
    pallas_call x4, Pallas kernels, partial_grams(): pl.pallas_call(functools.partial(partial_kernel, sources, before is not N...  15.4 us
    ppermute x13, starting transfers between devices, hop(): return lax.ppermute(value, 'grid', pairs)  14.7 us
    ppermute x13, waiting for transfers between devices, hop(): return lax.ppermute(value, 'grid', pairs)  14.3 us
    ppermute x1, waiting for transfers between devices, on_device(): lax.ppermute(own, 'grid', [(j, (j + 1) % n_grid) for j in range(n_grid)])  5.15 us
    pallas_call x3, Pallas kernels, last_grams(): pl.pallas_call(functools.partial(last_kernel, shifts, lowest), out_shape=...  3.25 us
    pallas_call x1, Pallas kernels, make_messages(): pl.pallas_call(message_kernel, out_shape=[jax.ShapeDtypeStruct((TABLE + e...  2.66 us
    pallas_call x1, Pallas kernels, transposed_weights(): pl.pallas_call(weights_kernel, out_shape=jax.ShapeDtypeStruct((K, K), BF1...  2.3 us
  transfers between devices with their start and end apart: 15, of which 6 were waited for; matrix products, arithmetic and copies ran while one was open for 0% of the time, Pallas kernels for 24%

profile of v3, /device:TPU:32, one launch (start us, length us, event | category | flops | bytes accessed | tf_op | source)
XLA Modules:
  0.0 79.4 jit_solution(306930056306720564)
XLA Ops:
  0.0 0.0 copy-start
  0.0 2.7 %shard_map.55 = (bf16[544,512]{1,0:T(8,128)(2,1)}, bf16[560,512]{1,0:T(8,128)(2,1)}, bf16[544,512]{1,0:T(8,128)(2,1)}) custom-call(bf16[2048,128]{1,0:T(8,128)(2,1)} %refs_0_.1, f32[2048]{0:T(1024)} %refs_1_.1, f32[2048]{0:T(1024)} %refs_2_.1, s32[64,256]{1,0:T(8,128)} %bitcast.3), custom_call_target="tpu_custom_call" | custom-call | flops 2000000000 | bytes 4000000 | tf_op jit(solution)/shard_map/pallas_call | solution.py:98
  2.7 0.1 collective-permute-start.2
  2.8 1.6 %collective-permute-start = (bf16[560,512]{1,0:T(8,128)(2,1)}, bf16[560,512]{1,0:T(8,128)(2,1)S(1)}, u32[]{:S(2)}, u32[]{:S(2)}) collective-permute-start(bf16[560,512]{1,0:T(8,128)(2,1)} %get-tuple-element.28), channel_id=1, source_target_pairs={{0,2},{1,3},{2,4},{3,5},{4,6},{5,7},{6,0},{7,1},{8,10},{9,11},{10,... | collective-permute-start | bytes 1720328 | tf_op jit(solution)/shard_map/ppermute | solution.py:38
  4.3 1.7 %collective-permute-start.1 = (bf16[544,512]{1,0:T(8,128)(2,1)}, bf16[544,512]{1,0:T(8,128)(2,1)S(1)}, u32[]{:S(2)}, u32[]{:S(2)}) collective-permute-start(bf16[544,512]{1,0:T(8,128)(2,1)} %get-tuple-element.29), channel_id=1, source_target_pairs={{0,6},{1,7},{2,0},{3,1},{4,2},{5,3},{6,4},{7,5},{8,14},{9,15},{10,... | collective-permute-start | bytes 1671176 | tf_op jit(solution)/shard_map/ppermute | solution.py:38
  6.1 0.0 copy-done
  6.1 0.6 shard_map.57
  6.6 0.0 collective-permute-done.2.refs_1_
  6.7 0.0 copy-done.1
  6.7 4.2 %shard_map.56.refs_2_ = f32[8,2,144,256]{3,2,1,0:T(8,128)S(1)} custom-call(bf16[544,512]{1,0:T(8,128)(2,1)S(1)} %copy-done.1, bf16[544,512]{1,0:T(8,128)(2,1)S(1)} %collective-permute-done.2.refs_1_), custom_call_target="tpu_custom_call" | custom-call | flops 4000000000 | bytes 4000000 | tf_op jit(solution)/shard_map/pallas_call | solution.py:165
  10.9 8.4 %collective-permute-done.1.refs_1_ = bf16[544,512]{1,0:T(8,128)(2,1)S(1)} collective-permute-done((bf16[544,512]{1,0:T(8,128)(2,1)}, bf16[544,512]{1,0:T(8,128)(2,1)S(1)}, u32[]{:S(2)}, u32[]{:S(2)}) %collective-permute-start.1) | collective-permute-done | bytes 557088 | tf_op jit(solution)/shard_map/ppermute | solution.py:38
  19.2 0.3 collective-permute-done.refs_0_
  19.6 0.1 collective-permute-start.5
  19.7 0.5 collective-permute-start.6
  20.2 1.1 %collective-permute-start.3 = (bf16[272,512]{1,0:T(8,128)(2,1)S(1)}, bf16[272,512]{1,0:T(8,128)(2,1)S(1)}, u32[]{:S(2)}, u32[]{:S(2)}) collective-permute-start(bf16[272,512]{1,0:T(8,128)(2,1)S(1)} %slice.6), channel_id=1, source_target_pairs={{0,2},{1,3},{2,4},{3,5},{4,6},{5,7},{6,0},{7,1},{8,10},{9,11},{10,... | collective-permute-start | bytes 835592 | tf_op jit(solution)/shard_map/ppermute | solution.py:38
  21.4 2.1 %collective-permute-start.4 = (bf16[272,512]{1,0:T(8,128)(2,1)S(1)}, bf16[272,512]{1,0:T(8,128)(2,1)S(1)}, u32[]{:S(2)}, u32[]{:S(2)}) collective-permute-start(bf16[272,512]{1,0:T(8,128)(2,1)S(1)} %slice.7), channel_id=1, source_target_pairs={{0,6},{1,7},{2,0},{3,1},{4,2},{5,3},{6,4},{7,5},{8,14},{9,15},{10,... | collective-permute-start | bytes 835592 | tf_op jit(solution)/shard_map/ppermute | solution.py:38
  23.5 4.2 %shard_map.58.refs_2_ = f32[8,2,144,256]{3,2,1,0:T(8,128)S(1)} custom-call(bf16[560,512]{1,0:T(8,128)(2,1)S(1)} %collective-permute-done.refs_0_, bf16[544,512]{1,0:T(8,128)(2,1)S(1)} %collective-permute-done.1.refs_1_, f32[8,2,144,256]{3,2,1,0:T(8,128)S(1)} %shard_map.56.refs_2_), custom_call_target="tpu_custom_call" | custom-call | flops 4000000000 | bytes 4000000 | tf_op jit(solution)/shard_map/pallas_call | solution.py:165
  27.7 0.0 collective-permute-done.6.refs_1_
  27.7 0.0 collective-permute-done.5.refs_0_
  27.7 4.2 %shard_map.59.refs_2_ = f32[8,2,144,256]{3,2,1,0:T(8,128)S(1)} custom-call(bf16[560,512]{1,0:T(8,128)(2,1)S(1)} %collective-permute-done.5.refs_0_, bf16[544,512]{1,0:T(8,128)(2,1)S(1)} %collective-permute-done.6.refs_1_, f32[8,2,144,256]{3,2,1,0:T(8,128)S(1)} %shard_map.58.refs_2_), custom_call_target="tpu_custom_call" | custom-call | flops 4000000000 | bytes 4000000 | tf_op jit(solution)/shard_map/pallas_call | solution.py:165
  31.9 0.0 collective-permute-done.3.refs_0_
  31.9 0.0 collective-permute-done.4.refs_1_
  31.9 0.1 collective-permute-start.7
  32.0 0.5 collective-permute-start.8
  32.5 2.8 %shard_map.60.before = f32[8,2,144,256]{3,2,1,0:T(8,128)S(1)} custom-call(bf16[272,512]{1,0:T(8,128)(2,1)S(1)} %collective-permute-done.3.refs_0_, bf16[272,512]{1,0:T(8,128)(2,1)S(1)} %collective-permute-done.4.refs_1_, f32[8,2,144,256]{3,2,1,0:T(8,128)S(1)} %shard_map.59.refs_2_), custom_call_target="tpu_custom_call" | custom-call | flops 2000000000 | bytes 4000000 | tf_op jit(solution)/shard_map/pallas_call | solution.py:165
  35.3 0.0 collective-permute-done.7.low
  35.4 0.0 collective-permute-done.8.high
  35.4 0.9 %shard_map.63 = (bf16[4,112,128]{2,1,0:T(8,128)(2,1)S(1)}, bf16[4,112,128]{2,1,0:T(8,128)(2,1)S(1)}) custom-call(bf16[272,512]{1,0:T(8,128)(2,1)S(1)} %collective-permute-done.7.low, bf16[272,512]{1,0:T(8,128)(2,1)S(1)} %collective-permute-done.8.high, f32[8,2,144,256]{3,2,1,0:T(8,128)S(1)} %shard_map.60.before), custom_call_target="tpu_custom_call" | custom-call | flops 500000000 | bytes 4000000 | tf_op jit(solution)/shard_map/pallas_call | solution.py:210
  36.3 1.6 %collective-permute-start.9 = (bf16[4,112,128]{2,1,0:T(8,128)(2,1)S(1)}, bf16[4,112,128]{2,1,0:T(8,128)(2,1)S(1)}, u32[]{:S(2)}, u32[]{:S(2)}) collective-permute-start(bf16[4,112,128]{2,1,0:T(8,128)(2,1)S(1)} %get-tuple-element.45), channel_id=1, source_target_pairs={{0,8},{1,9},{2,10},{3,11},{4,12},{5,13},{6,14},{7,15},{8,16},{9,17... | collective-permute-start | bytes 344072 | tf_op jit(solution)/shard_map/ppermute | solution.py:38
  37.9 1.7 %collective-permute-start.10 = (bf16[4,112,128]{2,1,0:T(8,128)(2,1)S(1)}, bf16[4,112,128]{2,1,0:T(8,128)(2,1)S(1)}, u32[]{:S(2)}, u32[]{:S(2)}) collective-permute-start(bf16[4,112,128]{2,1,0:T(8,128)(2,1)S(1)} %get-tuple-element.46), channel_id=1, source_target_pairs={{0,24},{1,25},{2,26},{3,27},{4,28},{5,29},{6,30},{7,31},{8,0},{9,1... | collective-permute-start | bytes 344072 | tf_op jit(solution)/shard_map/ppermute | solution.py:38
  39.6 1.5 %shard_map.62 = (f32[8,112,128]{2,1,0:T(8,128)S(1)}, f32[8,112,128]{2,1,0:T(8,128)S(1)}) custom-call(bf16[272,512]{1,0:T(8,128)(2,1)S(1)} %collective-permute-done.7.low, bf16[272,512]{1,0:T(8,128)(2,1)S(1)} %collective-permute-done.8.high, f32[8,2,144,256]{3,2,1,0:T(8,128)S(1)} %shard_map.60.before), custom_call_target="tpu_custom_call" | custom-call | flops 1000000000 | bytes 4000000 | tf_op jit(solution)/shard_map/pallas_call | solution.py:210
  41.1 1.7 %collective-permute-done.9.from_up = bf16[4,112,128]{2,1,0:T(8,128)(2,1)S(1)} collective-permute-done((bf16[4,112,128]{2,1,0:T(8,128)(2,1)S(1)}, bf16[4,112,128]{2,1,0:T(8,128)(2,1)S(1)}, u32[]{:S(2)}, u32[]{:S(2)}) %collective-permute-start.9) | collective-permute-done | bytes 114720 | tf_op jit(solution)/shard_map/ppermute | solution.py:38
  42.7 0.0 collective-permute-done.10.from_down
  42.8 0.1 shard_map.64
  42.8 1.9 %collective-permute-start.11 = (bf16[8,112,128]{2,1,0:T(8,128)(2,1)S(1)}, bf16[8,112,128]{2,1,0:T(8,128)(2,1)S(1)}, u32[]{:S(2)}, u32[]{:S(2)}) collective-permute-start(bf16[8,112,128]{2,1,0:T(8,128)(2,1)S(1)} %get-tuple-element.47), channel_id=1, source_target_pairs={{0,8},{1,9},{2,10},{3,11},{4,12},{5,13},{6,14},{7,15},{8,16},{9,17... | collective-permute-start | bytes 688136 | tf_op jit(solution)/shard_map/ppermute | solution.py:38
  44.7 1.7 %collective-permute-start.12 = (bf16[8,112,128]{2,1,0:T(8,128)(2,1)S(1)}, bf16[8,112,128]{2,1,0:T(8,128)(2,1)S(1)}, u32[]{:S(2)}, u32[]{:S(2)}) collective-permute-start(bf16[8,112,128]{2,1,0:T(8,128)(2,1)S(1)} %get-tuple-element.48), channel_id=1, source_target_pairs={{0,24},{1,25},{2,26},{3,27},{4,28},{5,29},{6,30},{7,31},{8,0},{9,1... | collective-permute-start | bytes 688136 | tf_op jit(solution)/shard_map/ppermute | solution.py:38
  46.4 0.9 %shard_map.61.own = f32[8,112,128]{2,1,0:T(8,128)S(1)} custom-call(bf16[272,512]{1,0:T(8,128)(2,1)S(1)} %collective-permute-done.7.low, bf16[272,512]{1,0:T(8,128)(2,1)S(1)} %collective-permute-done.8.high, f32[8,2,144,256]{3,2,1,0:T(8,128)S(1)} %shard_map.60.before), custom_call_target="tpu_custom_call" | custom-call | flops 500000000 | bytes 4000000 | tf_op jit(solution)/shard_map/pallas_call | solution.py:210
  47.2 3.9 %collective-permute-done.11.a = bf16[8,112,128]{2,1,0:T(8,128)(2,1)S(1)} collective-permute-done((bf16[8,112,128]{2,1,0:T(8,128)(2,1)S(1)}, bf16[8,112,128]{2,1,0:T(8,128)(2,1)S(1)}, u32[]{:S(2)}, u32[]{:S(2)}) %collective-permute-start.11) | collective-permute-done | bytes 229408 | tf_op jit(solution)/shard_map/ppermute | solution.py:38
  51.2 0.0 collective-permute-done.12.b
  51.2 0.1 shard_map.65
  51.2 17.0 %all_to_all.5.parts = bf16[8,112,128]{2,1,0:T(8,128)(2,1)S(1)} all-to-all(bf16[8,112,128]{2,1,0:T(8,128)(2,1)S(1)} %shard_map.65), channel_id=1, replica_groups=mesh['obs'=8,'grid'=32] {'obs'}, dimensions={0} | all-to-all | bytes 458752 | tf_op jit(solution)/shard_map/all_to_all | solution.py:428
  68.3 2.3 %shard_map.66.own = bf16[128,128]{1,0:T(8,128)(2,1)S(1)} custom-call(bf16[8,112,128]{2,1,0:T(8,128)(2,1)S(1)} %all_to_all.5.parts), custom_call_target="tpu_custom_call" | custom-call | flops 4000000000 | bytes 4000000 | tf_op jit(solution)/shard_map/pallas_call | solution.py:293
  70.6 0.1 collective-permute-start.14
  70.7 0.5 collective-permute-start.13
  71.2 0.6 shard_map.67.part
  71.7 0.5 collective-permute-done.14.right
  72.3 5.1 %collective-permute-done.13.left = bf16[128,128]{1,0:T(8,128)(2,1)S(1)} collective-permute-done((bf16[128,128]{1,0:T(8,128)(2,1)S(1)}, bf16[128,128]{1,0:T(8,128)(2,1)S(1)}, u32[]{:S(2)}, u32[]{:S(2)}) %collective-permute-start.13) | collective-permute-done | bytes 32800 | tf_op jit(solution)/shard_map/ppermute | solution.py:431
  77.4 1.8 %shard_map.68 = bf16[48,128,128]{2,1,0:T(8,128)(2,1)} custom-call(bf16[128,128]{1,0:T(8,128)(2,1)S(1)} %collective-permute-done.13.left, bf16[128,128]{1,0:T(8,128)(2,1)S(1)} %collective-permute-done.14.right, f32[24,128,256]{2,1,0:T(8,128)S(1)} %shard_map.67.part, bf16[24,128,256]{2,1,0:T(8,128)(2,1)S(1)} %get-tuple-element.50.perturb), custom_call_target="tpu_custom_call" | custom-call | flops 2000000000 | bytes 4000000 | tf_op jit(solution)/shard_map/pallas_call | solution.py:376
  (3 shorter events, 0.0 us)
Async XLA Ops:
  0.0 6.1 %copy-start = (bf16[48,128,128]{2,1,0:T(8,128)(2,1)S(1)}, bf16[48,128,128]{2,1,0:T(8,128)(2,1)}, u32[]{:S(2)}) copy-start(bf16[48,128,128]{2,1,0:T(8,128)(2,1)} %state.1) | copy-start | bytes 4718596
  2.7 4.0 %collective-permute-start.2 = (bf16[544,512]{1,0:T(8,128)(2,1)}, bf16[544,512]{1,0:T(8,128)(2,1)S(1)}, u32[]{:S(2)}, u32[]{:S(2)}) collective-permute-start(bf16[544,512]{1,0:T(8,128)(2,1)} %get-tuple-element.30.refs_0_), channel_id=1, source_target_pairs={{0,1},{1,0},{2,3},{3,2},{4,5},{5,4},{6,7},{7,6},{8,9},{9,8},{10,11... | collective-permute-start | bytes 1671176 | tf_op jit(solution)/shard_map/ppermute | solution.py:38
  2.8 16.8 %collective-permute-start = (bf16[560,512]{1,0:T(8,128)(2,1)}, bf16[560,512]{1,0:T(8,128)(2,1)S(1)}, u32[]{:S(2)}, u32[]{:S(2)}) collective-permute-start(bf16[560,512]{1,0:T(8,128)(2,1)} %get-tuple-element.28), channel_id=1, source_target_pairs={{0,2},{1,3},{2,4},{3,5},{4,6},{5,7},{6,0},{7,1},{8,10},{9,11},{10,... | collective-permute-start | bytes 1720328 | tf_op jit(solution)/shard_map/ppermute | solution.py:38
  4.3 2.3 %copy-start.1 = (bf16[544,512]{1,0:T(8,128)(2,1)S(1)}, bf16[544,512]{1,0:T(8,128)(2,1)}, u32[]{:S(2)}) copy-start(bf16[544,512]{1,0:T(8,128)(2,1)} %get-tuple-element.30.refs_0_) | copy-start | bytes 1671172
  4.3 14.9 %collective-permute-start.1 = (bf16[544,512]{1,0:T(8,128)(2,1)}, bf16[544,512]{1,0:T(8,128)(2,1)S(1)}, u32[]{:S(2)}, u32[]{:S(2)}) collective-permute-start(bf16[544,512]{1,0:T(8,128)(2,1)} %get-tuple-element.29), channel_id=1, source_target_pairs={{0,6},{1,7},{2,0},{3,1},{4,2},{5,3},{6,4},{7,5},{8,14},{9,15},{10,... | collective-permute-start | bytes 1671176 | tf_op jit(solution)/shard_map/ppermute | solution.py:38
  19.6 8.1 %collective-permute-start.5 = (bf16[560,512]{1,0:T(8,128)(2,1)S(1)}, bf16[560,512]{1,0:T(8,128)(2,1)S(1)}, u32[]{:S(2)}, u32[]{:S(2)}) collective-permute-start(bf16[560,512]{1,0:T(8,128)(2,1)S(1)} %collective-permute-done.refs_0_), channel_id=1, source_target_pairs={{0,1},{1,0},{2,3},{3,2},{4,5},{5,4},{6,7},{7,6},{8,9},{9,8},{10,11... | collective-permute-start | bytes 1720328 | tf_op jit(solution)/shard_map/ppermute | solution.py:38
  19.7 8.0 %collective-permute-start.6 = (bf16[544,512]{1,0:T(8,128)(2,1)S(1)}, bf16[544,512]{1,0:T(8,128)(2,1)S(1)}, u32[]{:S(2)}, u32[]{:S(2)}) collective-permute-start(bf16[544,512]{1,0:T(8,128)(2,1)S(1)} %collective-permute-done.1.refs_1_), channel_id=1, source_target_pairs={{0,1},{1,0},{2,3},{3,2},{4,5},{5,4},{6,7},{7,6},{8,9},{9,8},{10,11... | collective-permute-start | bytes 1671176 | tf_op jit(solution)/shard_map/ppermute | solution.py:38
  20.2 11.7 %collective-permute-start.3 = (bf16[272,512]{1,0:T(8,128)(2,1)S(1)}, bf16[272,512]{1,0:T(8,128)(2,1)S(1)}, u32[]{:S(2)}, u32[]{:S(2)}) collective-permute-start(bf16[272,512]{1,0:T(8,128)(2,1)S(1)} %slice.6), channel_id=1, source_target_pairs={{0,2},{1,3},{2,4},{3,5},{4,6},{5,7},{6,0},{7,1},{8,10},{9,11},{10,... | collective-permute-start | bytes 835592 | tf_op jit(solution)/shard_map/ppermute | solution.py:38
  21.4 10.5 %collective-permute-start.4 = (bf16[272,512]{1,0:T(8,128)(2,1)S(1)}, bf16[272,512]{1,0:T(8,128)(2,1)S(1)}, u32[]{:S(2)}, u32[]{:S(2)}) collective-permute-start(bf16[272,512]{1,0:T(8,128)(2,1)S(1)} %slice.7), channel_id=1, source_target_pairs={{0,6},{1,7},{2,0},{3,1},{4,2},{5,3},{6,4},{7,5},{8,14},{9,15},{10,... | collective-permute-start | bytes 835592 | tf_op jit(solution)/shard_map/ppermute | solution.py:38
  31.9 3.4 %collective-permute-start.7 = (bf16[272,512]{1,0:T(8,128)(2,1)S(1)}, bf16[272,512]{1,0:T(8,128)(2,1)S(1)}, u32[]{:S(2)}, u32[]{:S(2)}) collective-permute-start(bf16[272,512]{1,0:T(8,128)(2,1)S(1)} %collective-permute-done.3.refs_0_), channel_id=1, source_target_pairs={{0,1},{1,0},{2,3},{3,2},{4,5},{5,4},{6,7},{7,6},{8,9},{9,8},{10,11... | collective-permute-start | bytes 835592 | tf_op jit(solution)/shard_map/ppermute | solution.py:38
  32.0 3.3 %collective-permute-start.8 = (bf16[272,512]{1,0:T(8,128)(2,1)S(1)}, bf16[272,512]{1,0:T(8,128)(2,1)S(1)}, u32[]{:S(2)}, u32[]{:S(2)}) collective-permute-start(bf16[272,512]{1,0:T(8,128)(2,1)S(1)} %collective-permute-done.4.refs_1_), channel_id=1, source_target_pairs={{0,1},{1,0},{2,3},{3,2},{4,5},{5,4},{6,7},{7,6},{8,9},{9,8},{10,11... | collective-permute-start | bytes 835592 | tf_op jit(solution)/shard_map/ppermute | solution.py:38
  36.3 6.5 %collective-permute-start.9 = (bf16[4,112,128]{2,1,0:T(8,128)(2,1)S(1)}, bf16[4,112,128]{2,1,0:T(8,128)(2,1)S(1)}, u32[]{:S(2)}, u32[]{:S(2)}) collective-permute-start(bf16[4,112,128]{2,1,0:T(8,128)(2,1)S(1)} %get-tuple-element.45), channel_id=1, source_target_pairs={{0,8},{1,9},{2,10},{3,11},{4,12},{5,13},{6,14},{7,15},{8,16},{9,17... | collective-permute-start | bytes 344072 | tf_op jit(solution)/shard_map/ppermute | solution.py:38
  37.9 4.9 %collective-permute-start.10 = (bf16[4,112,128]{2,1,0:T(8,128)(2,1)S(1)}, bf16[4,112,128]{2,1,0:T(8,128)(2,1)S(1)}, u32[]{:S(2)}, u32[]{:S(2)}) collective-permute-start(bf16[4,112,128]{2,1,0:T(8,128)(2,1)S(1)} %get-tuple-element.46), channel_id=1, source_target_pairs={{0,24},{1,25},{2,26},{3,27},{4,28},{5,29},{6,30},{7,31},{8,0},{9,1... | collective-permute-start | bytes 344072 | tf_op jit(solution)/shard_map/ppermute | solution.py:38
  42.8 8.3 %collective-permute-start.11 = (bf16[8,112,128]{2,1,0:T(8,128)(2,1)S(1)}, bf16[8,112,128]{2,1,0:T(8,128)(2,1)S(1)}, u32[]{:S(2)}, u32[]{:S(2)}) collective-permute-start(bf16[8,112,128]{2,1,0:T(8,128)(2,1)S(1)} %get-tuple-element.47), channel_id=1, source_target_pairs={{0,8},{1,9},{2,10},{3,11},{4,12},{5,13},{6,14},{7,15},{8,16},{9,17... | collective-permute-start | bytes 688136 | tf_op jit(solution)/shard_map/ppermute | solution.py:38
  44.7 6.5 %collective-permute-start.12 = (bf16[8,112,128]{2,1,0:T(8,128)(2,1)S(1)}, bf16[8,112,128]{2,1,0:T(8,128)(2,1)S(1)}, u32[]{:S(2)}, u32[]{:S(2)}) collective-permute-start(bf16[8,112,128]{2,1,0:T(8,128)(2,1)S(1)} %get-tuple-element.48), channel_id=1, source_target_pairs={{0,24},{1,25},{2,26},{3,27},{4,28},{5,29},{6,30},{7,31},{8,0},{9,1... | collective-permute-start | bytes 688136 | tf_op jit(solution)/shard_map/ppermute | solution.py:38
  70.6 1.7 %collective-permute-start.14 = (bf16[128,128]{1,0:T(8,128)(2,1)S(1)}, bf16[128,128]{1,0:T(8,128)(2,1)S(1)}, u32[]{:S(2)}, u32[]{:S(2)}) collective-permute-start(bf16[128,128]{1,0:T(8,128)(2,1)S(1)} %shard_map.66.own), channel_id=1, source_target_pairs={{0,31},{1,0},{2,1},{3,2},{4,3},{5,4},{6,5},{7,6},{8,7},{9,8},{10,9... | collective-permute-start | bytes 98312 | tf_op jit(solution)/shard_map/ppermute | solution.py:432
  70.7 6.7 %collective-permute-start.13 = (bf16[128,128]{1,0:T(8,128)(2,1)S(1)}, bf16[128,128]{1,0:T(8,128)(2,1)S(1)}, u32[]{:S(2)}, u32[]{:S(2)}) collective-permute-start(bf16[128,128]{1,0:T(8,128)(2,1)S(1)} %shard_map.66.own), channel_id=1, source_target_pairs={{0,1},{1,2},{2,3},{3,4},{4,5},{5,6},{6,7},{7,8},{8,9},{9,10},{10,1... | collective-permute-start | bytes 98312 | tf_op jit(solution)/shard_map/ppermute | solution.py:431

commit v4 on v3

--- a/solution.py
+++ b/solution.py
@@ -13,7 +13,7 @@
 K = 128
 LOW = 512
 BLOCKS = 4
-TABLE = BLOCKS * K + 16
+HALF = 2 * K + 16
 PACK = 112
 VMEM = 20 * 1024 * 1024
 
@@ -22,8 +22,11 @@
     return pltpu.CompilerParams(vmem_limit_bytes=VMEM)
 
 
+LONG, MID, SHORT = 6e10, 6e10, 1e6
+
+
 def cost(flops):
-    return pl.CostEstimate(flops=int(flops), bytes_accessed=4_000_000, transcendentals=0)
+    return pl.CostEstimate(flops=int(flops), bytes_accessed=100_000, transcendentals=0)
 
 
 def in_vmem(count):
@@ -43,8 +46,8 @@
 
 
 def message_kernel(*refs):
-    sources, (near, to_right, to_left), held = refs[:4], refs[4:7], refs[7:11]
-    turned, sems = refs[11:]
+    sources, (near, right_first, right_second, left_first, left_second) = refs[:4], refs[4:9]
+    held, (turned, sems) = refs[9:13], refs[13:]
     copies = [
         pltpu.make_async_copy(source, place, sems.at[i])
         for i, (source, place) in enumerate(zip(sources, held))
@@ -64,44 +67,47 @@
             lines = []
             for y in range(Y):
                 rows = turned[pl.ds(y * X * CORES + cx, 8, stride=Y * X * CORES), :]
-                pairs = jnp.concatenate([rows[0:4], rows[4:8]], axis=1)
+                pair = [rows[0:4], rows[4:8]]
+                pairs = jnp.concatenate(pair[::-1] if dc else pair, axis=1)
                 fours = jnp.concatenate([pairs[0:2], pairs[2:4]], axis=1)
                 lines.append(jnp.concatenate([fours[0:1], fours[1:2]], axis=1))
             picks = jnp.concatenate(lines, axis=0)
             halves.append(lax.shift_right_arithmetic(picks, 8))
             halves.append(jnp.bitwise_and(picks, 255))
         groups.append(jnp.concatenate(halves, axis=0).astype(F32).astype(BF16))
-    near[TABLE:, :] = groups[0]
-    to_right[:16, :] = groups[2]
-    to_right[16 + TABLE :, :] = groups[1]
-    to_left[TABLE:, :] = groups[3]
+    near[2 * HALF :, :] = groups[0]
+    right_first[:16, :] = groups[1]
+    right_first[16:32, :] = groups[2]
+    left_first[:16, :] = groups[3]
     for copy in copies[:3]:
         copy.wait()
     root = jnp.sqrt(obs_weight[...].reshape(1, BLOCKS * LOW))
     innov = innovation[...].reshape(1, BLOCKS * LOW) * root
     row = lax.broadcasted_iota(jnp.int32, (16, LOW), 0)
-    tail = jnp.zeros((16, LOW), F32)
-    for block in range(BLOCKS):
-        span = slice(block * LOW, (block + 1) * LOW)
-        rows = (departures[span, :].astype(F32).T * root[:, span]).astype(BF16)
-        near[block * K : (block + 1) * K, :] = rows
-        to_right[16 + block * K : 16 + (block + 1) * K, :] = rows
-        to_left[block * K : (block + 1) * K, :] = rows
-        tail = jnp.where(row == block, innov[:, span], tail)
-    tail = tail.astype(BF16)
-    near[BLOCKS * K : TABLE, :] = tail
-    to_right[16 + BLOCKS * K : 16 + TABLE, :] = tail
-    to_left[BLOCKS * K : TABLE, :] = tail
+    places = (
+        ((near, 0), (right_first, 32), (left_second, 0)),
+        ((near, HALF), (left_first, 16), (right_second, 0)),
+    )
+    for half in range(2):
+        tail = jnp.zeros((16, LOW), F32)
+        for block in range(2):
+            start = (2 * half + block) * LOW
+            span = slice(start, start + LOW)
+            rows = (departures[span, :].astype(F32).T * root[:, span]).astype(BF16)
+            for ref, at in places[half]:
+                ref[at + block * K : at + (block + 1) * K, :] = rows
+            tail = jnp.where(row == block, innov[:, span], tail)
+        for ref, at in places[half]:
+            ref[at + 2 * K : at + HALF, :] = tail.astype(BF16)
 
 
 def make_messages(*args):
+    rows = (2 * HALF + 16, HALF + 32, HALF, HALF + 16, HALF)
     return pl.pallas_call(
         message_kernel,
-        out_shape=[
-            jax.ShapeDtypeStruct((TABLE + extra, LOW), BF16) for extra in (16, 32, 16)
-        ],
+        out_shape=[jax.ShapeDtypeStruct((count, LOW), BF16) for count in rows],
         in_specs=[pl.BlockSpec(memory_space=pltpu.HBM)] * 4,
-        out_specs=in_vmem(3),
+        out_specs=in_vmem(len(rows)),
         scratch_shapes=[pltpu.VMEM(arg.shape, arg.dtype) for arg in args]
         + [pltpu.VMEM(args[3].shape[::-1], jnp.int32), pltpu.SemaphoreType.DMA((4,))],
         compiler_params=pltpu.CompilerParams(vmem_limit_bytes=60 * 1024 * 1024),
@@ -114,69 +120,57 @@
     return (values[0:4] * 256.0 + values[4:8]).astype(jnp.int32)
 
 
-def pick(tables, picks):
+def pick(parts, picks):
     high = lax.shift_right_arithmetic(picks, 9)
-    low = jnp.where(picks >= 0, jnp.bitwise_and(picks, LOW - 1), -1)
+    first = parts[0][0]
+    live = picks >= 0 if len(parts) == 2 else lax.shift_right_arithmetic(high, 1) == first
+    low = jnp.where(live, jnp.bitwise_and(picks, LOW - 1), -1)
     one_hot = (lax.broadcasted_iota(jnp.int32, (LOW, 256), 0) == low).astype(BF16)
-    found = [jnp.dot(part, one_hot, preferred_element_type=F32) for part in tables]
-    blocks = []
-    for part in found:
-        blocks += [part[i * K : (i + 1) * K] for i in range(part.shape[0] // K)]
-    tail = found[-1][-16:]
-    members, innov = blocks[0], tail[0:1]
-    for block in range(1, BLOCKS):
-        here = high == block
+    blocks, innovs = [], []
+    for _, rows in parts:
+        found = jnp.dot(rows, one_hot, preferred_element_type=F32)
+        blocks += [found[:K], found[K : 2 * K]]
+        innovs += [found[2 * K : 2 * K + 1], found[2 * K + 1 : 2 * K + 2]]
+    members, innov = blocks[0], innovs[0]
+    for block in range(1, len(blocks)):
+        here = high == 2 * first + block
         members = jnp.where(here, blocks[block], members)
-        innov = jnp.where(here, tail[block : block + 1], innov)
+        innov = jnp.where(here, innovs[block], innov)
     return jnp.concatenate([members, jnp.broadcast_to(innov, (16, 256))], axis=0).astype(BF16)
 
 
-def grams(tables, picks):
-    found = [pick(*pair) for pair in zip(tables, picks)]
-    lane = lax.broadcasted_iota(jnp.int32, (K, len(found) * K), 1)
-    even = lane % K < K // 2
-    totals = []
-    for half in range(2):
-        span = slice(half * K, (half + 1) * K)
-        parts = [part[:, span] for part in found]
-        joined = jnp.concatenate(parts, axis=1) if len(parts) > 1 else parts[0]
-        rows = joined[:K]
-        none = jnp.zeros_like(rows)
-        split = jnp.concatenate([jnp.where(even, rows, none), jnp.where(even, none, rows)], axis=0)
-        totals.append(lax.dot_general(joined, split, dims(1, 1), preferred_element_type=F32))
-    return totals
-
-
-def partial_kernel(sources, chained, *refs):
-    out = refs[-1]
-    picks = [
-        read_picks(refs[which][at : at + 16, :], core) for _, (which, at, core) in sources
-    ]
+def pick_kernel(sources, count, *refs):
+    outs = refs[count:]
+    picks = [read_picks(refs[which][at : at + 16, :], core) for _, (which, at, core), _ in sources]
     for step in range(2 * Y):
         y, span = step // 2, slice(step % 2 * 256, step % 2 * 256 + 256)
-        tables = [[refs[which][at:end, :] for which, at, end in parts] for parts, _ in sources]
-        totals = grams(tables, [values[y : y + 1, span] for values in picks])
-        for half in range(2):
-            out[step, half] = totals[half] + refs[-2][step, half] if chained else totals[half]
-
-
-def partial_grams(sources, messages, before=None):
-    args = tuple(messages) + (() if before is None else (before,))
-    return pl.pallas_call(
-        functools.partial(partial_kernel, sources, before is not None),
-        out_shape=jax.ShapeDtypeStruct((2 * Y, 2, 144, 256), F32),
+        for out, (parts, _, before), values in zip(outs, sources, picks):
+            tables = [(half, refs[which][at : at + HALF, :]) for half, which, at in parts]
+            found = pick(tables, values[y : y + 1, span])
+            out[step] = found if before is None else found + refs[before][step]
+
+
+def pick_rows(sources, flops, *args):
+    return pl.pallas_call(
+        functools.partial(pick_kernel, sources, len(args)),
+        out_shape=[jax.ShapeDtypeStruct((2 * Y, 144, 256), BF16)] * len(sources),
         in_specs=in_vmem(len(args)),
-        out_specs=in_vmem(1)[0],
-        compiler_params=params(),
-        cost_estimate=cost(2e9 * len(sources)),
+        out_specs=in_vmem(len(sources)),
+        compiler_params=params(),
+        cost_estimate=cost(flops),
     )(*args)
 
 
-def pack(total, side):
-    gram = total[0:K, side * K : (side + 1) * K]
+def join(first, second):
+    low = lax.broadcasted_iota(jnp.int32, first.shape, 1) < K // 2
+    return jnp.where(low, first, second), jnp.where(low, second, first)
+
+
+def pack(total):
+    gram = total[0:K]
     lane = lax.broadcasted_iota(jnp.int32, (32, K), 1)
     fold = jnp.where(lane < 64, pltpu.roll(gram[64:96], 64, 1), gram[96:128])
-    return jnp.concatenate([gram[0:64], fold, total[K : K + 16, side * K : (side + 1) * K]], axis=0)
+    return jnp.concatenate([gram[0:64], fold, total[K : K + 16]], axis=0)
 
 
 def unpack(packed):
@@ -187,35 +181,42 @@
     return jnp.concatenate([packed[0:64], lower], axis=0) + corner.T, packed[96:97]
 
 
-def last_kernel(shifts, lowest, low, high, before, *rest):
-    outs, picks = rest[:-1], rest[-1]
+def last_kernel(shifts, lowest, low, high, same, *rest):
+    found, outs, picks = rest[:6], rest[6:-1], rest[-1]
     place = lax.div(lax.axis_index("grid"), X * CORES)
-    picks[...] = read_picks(low[0:16, :], 1)
-    table = [low[16:, :], high[...]]
+    picks[...] = read_picks(low[16:32, :], 1)
+    table = ((0, low[32:, :]), (1, high[16:, :]))
     for shift in sorted(set(shifts)):
         y = lax.rem(place + shift, Y)
         for i in range(2):
             span = slice(i * 256, i * 256 + 256)
-            totals = grams([table], [picks[pl.ds(y, 1), :][:, span]])
+            last = pick(table, picks[pl.ds(y, 1), :][:, span])
+            shards = [ref[2 * y + i] for ref in (*found, same)] + [last]
             for half in range(2):
-                total = totals[half] + before[2 * y + i, half]
+                span = slice(half * K, half * K + K)
+                pairs = [
+                    join(shards[n][:, span], shards[n + 1][:, span])
+                    for n in range(0, len(shards), 2)
+                ]
                 for side in range(2):
+                    rows = jnp.concatenate([pair[side] for pair in pairs], axis=1)
+                    total = lax.dot_general(rows, rows[:K], dims(1, 1), preferred_element_type=F32)
                     patch = i + 2 * half + 4 * side
                     for out, its_shift, first in zip(outs, shifts, lowest):
                         if its_shift == shift and first <= patch < first + out.shape[0]:
-                            out[patch - first] = pack(total, side).astype(out.dtype)
-
-
-def last_grams(shifts, lowest, counts, dtype, low, high, before):
+                            out[patch - first] = pack(total).astype(out.dtype)
+
+
+def last_grams(shifts, lowest, counts, dtype, *args):
     return pl.pallas_call(
         functools.partial(last_kernel, shifts, lowest),
         out_shape=[jax.ShapeDtypeStruct((count, PACK, K), dtype) for count in counts],
-        in_specs=in_vmem(3),
+        in_specs=in_vmem(len(args)),
         out_specs=in_vmem(len(counts)),
         scratch_shapes=[pltpu.VMEM((Y, LOW), jnp.int32)],
         compiler_params=params(),
-        cost_estimate=cost(5e8 * len(set(shifts))),
-    )(low, high, before)
+        cost_estimate=cost(1e9 * len(set(shifts))),
+    )(*args)
 
 
 def relay_kernel(up, down, from_up, from_down, out_up, out_down):
@@ -386,37 +387,48 @@
 
 def on_device(departures, innovation, obs_weight, send_rows, send_counts, state):
     n_grid = lax.axis_size("grid")
-    near, to_right, to_left = make_messages(departures, innovation, obs_weight, send_rows[0].T)
+    near, right_first, right_second, left_first, left_second = make_messages(
+        departures, innovation, obs_weight, send_rows[0].T
+    )
+    left = hop(right_first, 0, 1, 0)
+    right = hop(left_first, 0, -1, 0)
     other = hop(near, 0, 0, 1)
-    left = hop(to_right, 0, 1, 0)
-    right = hop(to_left, 0, -1, 0)
-
-    def at_end(which, core):
-        return (((which, 0, TABLE),), (which, TABLE, core))
-
-    def at_middle(which, core):
-        return (((which, 16, 16 + TABLE),), (which, 16 + TABLE, core))
-
-    totals = partial_grams((at_end(0, 0), at_end(1, 1)), (near, other))
+    left_more = hop(right_second, 0, 1, 0)
+    right_more = hop(left_second, 0, -1, 0)
+
+    whole = lambda which: ((0, which, 0), (1, which, HALF))
+    at_end = 2 * HALF
+    found = pick_rows(
+        ((whole(0), (0, at_end, 0), None), (whole(1), (1, at_end, 1), None)), SHORT, near, other
+    )
     mean, perturb = perturbations(state)
-    left, right, totals, mean, perturb = lax.optimization_barrier(
-        (left, right, totals, mean, perturb)
-    )
-    far_low, far_high = left[:272], right[256:TABLE]
-    far_low, far_high, left, right = lax.optimization_barrier((far_low, far_high, left, right))
-
-    far_low = hop(far_low, 0, 1, 0)
-    far_high = hop(far_high, 0, -1, 0)
-    left_other = hop(left, 0, 0, 1)
-    right_other = hop(right, 0, 0, 1)
-    totals = partial_grams((at_middle(0, 0), at_end(1, 0)), (left, right), totals)
-    totals = partial_grams((at_middle(0, 1), at_end(1, 1)), (left_other, right_other), totals)
-    far_low, far_high, totals = lax.optimization_barrier((far_low, far_high, totals))
-    far_low_other = hop(far_low, 0, 0, 1)
-    far_high_other = hop(far_high, 0, 0, 1)
-    source = (((0, 16, 272), (1, 0, 272)), (0, 0, 0))
-    totals = partial_grams((source,), (far_low, far_high), totals)
-    last = (far_low_other, far_high_other, totals)
+    left, right, found, mean, perturb = lax.optimization_barrier(
+        (left, right, found, mean, perturb)
+    )
+    far_low, far_high = hop(left, 0, 1, 0), hop(right, 0, -1, 0)
+
+    def firsts(core):
+        return (((0, 0, 32),), (0, 0, core), None), (((1, 1, 16),), (1, 0, core), None)
+
+    def seconds(core):
+        return (((1, 2, 0),), (0, 0, core), 4), (((0, 3, 0),), (1, 0, core), 5)
+
+    same = pick_rows(firsts(0), LONG, left, right)
+    left, right, same = lax.optimization_barrier((left, right, same))
+    left_other, right_other = hop(left, 0, 0, 1), hop(right, 0, 0, 1)
+    same = pick_rows(seconds(0), MID, left, right, left_more, right_more, *same)
+    left_more, right_more, same = lax.optimization_barrier((left_more, right_more, same))
+    left_more_other, right_more_other = hop(left_more, 0, 0, 1), hop(right_more, 0, 0, 1)
+    cross = pick_rows(firsts(1), SHORT, left_other, right_other)
+    far_low, far_high, cross, left_more_other, right_more_other = lax.optimization_barrier(
+        (far_low, far_high, cross, left_more_other, right_more_other)
+    )
+    far_low_other, far_high_other = hop(far_low, 0, 0, 1), hop(far_high, 0, 0, 1)
+    cross = pick_rows(
+        seconds(1), SHORT, left_other, right_other, left_more_other, right_more_other, *cross
+    )
+    far = pick_rows(((((0, 0, 32), (1, 1, 16)), (0, 16, 0), None),), SHORT, far_low, far_high)[0]
+    last = (far_low_other, far_high_other, far, *found, same[0], cross[0], same[1], cross[1])
 
     up, down = last_grams((2, 2), (0, 4), (4, 4), BF16, *last)
     from_up, from_down = hop(up, 1, 0, 0), hop(down, -1, 0, 0)

time: 79.6 us -> 74.9 us (0.941)
  Pallas kernels: 26.7 us -> 22.6 us
  waiting for transfers between devices: 20 us -> 16.3 us
  starting transfers between devices: 15.2 us -> 18.6 us
    pallas_call x5 -> x7, Pallas kernels: 18.1 us -> 13.4 us  [the longest x6 10.8 us: pick_rows(): pl.pallas_call(functools.partial(pick_kernel, sources, len(args)), out_sh...]
    ppermute x13 -> x17, waiting for transfers between devices: 14.3 us -> 10.2 us  [hop(): return lax.ppermute(value, 'grid', pairs)]
    ppermute x13 -> x17, starting transfers between devices: 14.7 us -> 17.7 us  [hop(): return lax.ppermute(value, 'grid', pairs)]
    ppermute x1, starting transfers between devices: 0.08 us -> 0.92 us  [on_device(): lax.ppermute(own, 'grid', [(j, (j - 1) % n_grid) for j in range(n_grid)])]
  transfers between devices with their start and end apart: 15 -> 19, of which waited for: 6 -> 8; matrix products, arithmetic and copies ran while one was open for 0% -> 0% of each run, Pallas kernels for 24% -> 20%
where the time goes in v4:
time: 74.9 us; the launch traced here: 74.7 us
  Pallas kernels  22.6 us (30%)
  starting transfers between devices  18.6 us (25%)
  blocking collectives  16.8 us (22%)
  waiting for transfers between devices  16.3 us (22%)
    ppermute x17, starting transfers between devices, hop(): return lax.ppermute(value, 'grid', pairs)  17.7 us
    all_to_all x1, blocking collectives, on_device(): parts = lax.all_to_all(parts, 'obs', 0, 0, tiled=True)  16.8 us
    pallas_call x6, Pallas kernels, pick_rows(): pl.pallas_call(functools.partial(pick_kernel, sources, len(args)), out_sh...  10.8 us
    ppermute x17, waiting for transfers between devices, hop(): return lax.ppermute(value, 'grid', pairs)  10.2 us
    ppermute x1, waiting for transfers between devices, on_device(): lax.ppermute(own, 'grid', [(j, (j + 1) % n_grid) for j in range(n_grid)])  5.06 us
    pallas_call x3, Pallas kernels, last_grams(): pl.pallas_call(functools.partial(last_kernel, shifts, lowest), out_shape=...  3.9 us
    pallas_call x1, Pallas kernels, make_messages(): pl.pallas_call(message_kernel, out_shape=[jax.ShapeDtypeStruct((count, LO...  2.63 us
    pallas_call x1, Pallas kernels, transposed_weights(): pl.pallas_call(weights_kernel, out_shape=jax.ShapeDtypeStruct((K, K), BF1...  2.3 us
  transfers between devices with their start and end apart: 19, of which 8 were waited for; matrix products, arithmetic and copies ran while one was open for 0% of the time, Pallas kernels for 20%

profile of v4, /device:TPU:32, one launch (start us, length us, event | category | flops | bytes accessed | tf_op | source)
XLA Modules:
  0.0 74.7 jit_solution(18051299670745836461)
XLA Ops:
  0.0 2.6 %shard_map.55 = (bf16[560,512]{1,0:T(8,128)(2,1)}, bf16[304,512]{1,0:T(8,128)(2,1)}, bf16[272,512]{1,0:T(8,128)(2,1)}, bf16[288,512]{1,0:T(8,128)(2,1)}, bf16[272,512]{1,0:T(8,128)(2,1)}) custom-call(bf16[2048,128]{1,0:T(8,128)(2,1)} %refs_0_.1, f32[2048]{0:T(1024)} %refs_1_.1, f32[2048]{0:T(1024)} %refs_2_.1, s32[64,256]{1,0:T(8,128)} %bitcast.3), custom_call_target="tpu_custom_call" | custom-call | flops 2000000000 | bytes 100000 | tf_op jit(solution)/shard_map/pallas_call | solution.py:106
  2.6 0.1 collective-permute-start.2
  2.7 1.6 %collective-permute-start = (bf16[304,512]{1,0:T(8,128)(2,1)}, bf16[304,512]{1,0:T(8,128)(2,1)S(1)}, u32[]{:S(2)}, u32[]{:S(2)}) collective-permute-start(bf16[304,512]{1,0:T(8,128)(2,1)} %get-tuple-element.48), channel_id=1, source_target_pairs={{0,2},{1,3},{2,4},{3,5},{4,6},{5,7},{6,0},{7,1},{8,10},{9,11},{10,... | collective-permute-start | bytes 933896 | tf_op jit(solution)/shard_map/ppermute | solution.py:41
  4.3 1.7 %collective-permute-start.1 = (bf16[288,512]{1,0:T(8,128)(2,1)}, bf16[288,512]{1,0:T(8,128)(2,1)S(1)}, u32[]{:S(2)}, u32[]{:S(2)}) collective-permute-start(bf16[288,512]{1,0:T(8,128)(2,1)} %get-tuple-element.49), channel_id=1, source_target_pairs={{0,6},{1,7},{2,0},{3,1},{4,2},{5,3},{6,4},{7,5},{8,14},{9,15},{10,... | collective-permute-start | bytes 884744 | tf_op jit(solution)/shard_map/ppermute | solution.py:41
  6.1 0.3 collective-permute-start.7
  6.3 3.0 %collective-permute-start.8 = (bf16[272,512]{1,0:T(8,128)(2,1)}, bf16[272,512]{1,0:T(8,128)(2,1)S(1)}, u32[]{:S(2)}, u32[]{:S(2)}) collective-permute-start(bf16[272,512]{1,0:T(8,128)(2,1)} %get-tuple-element.64), channel_id=1, source_target_pairs={{0,6},{1,7},{2,0},{3,1},{4,2},{5,3},{6,4},{7,5},{8,14},{9,15},{10,... | collective-permute-start | bytes 835592 | tf_op jit(solution)/shard_map/ppermute | solution.py:41
  9.3 0.6 shard_map.57
  9.9 0.0 collective-permute-done.2.refs_1_
  9.9 2.5 %shard_map.56 = (bf16[8,144,256]{2,1,0:T(8,128)(2,1)S(1)}, bf16[8,144,256]{2,1,0:T(8,128)(2,1)S(1)}) custom-call(bf16[560,512]{1,0:T(8,128)(2,1)S(1)} %copy-done, bf16[560,512]{1,0:T(8,128)(2,1)S(1)} %collective-permute-done.2.refs_1_), custom_call_target="tpu_custom_call" | custom-call | flops 1000000 | bytes 100000 | tf_op jit(solution)/shard_map/pallas_call | solution.py:154
  12.4 1.9 %collective-permute-done.1.refs_1_ = bf16[288,512]{1,0:T(8,128)(2,1)S(1)} collective-permute-done((bf16[288,512]{1,0:T(8,128)(2,1)}, bf16[288,512]{1,0:T(8,128)(2,1)S(1)}, u32[]{:S(2)}, u32[]{:S(2)}) %collective-permute-start.1) | collective-permute-done | bytes 294944 | tf_op jit(solution)/shard_map/ppermute | solution.py:41
  14.4 0.0 collective-permute-done.refs_0_
  14.4 2.9 %collective-permute-start.4 = (bf16[288,512]{1,0:T(8,128)(2,1)S(1)}, bf16[288,512]{1,0:T(8,128)(2,1)S(1)}, u32[]{:S(2)}, u32[]{:S(2)}) collective-permute-start(bf16[288,512]{1,0:T(8,128)(2,1)S(1)} %collective-permute-done.1.refs_1_), channel_id=1, source_target_pairs={{0,6},{1,7},{2,0},{3,1},{4,2},{5,3},{6,4},{7,5},{8,14},{9,15},{10,... | collective-permute-start | bytes 884744 | tf_op jit(solution)/shard_map/ppermute | solution.py:41
  17.3 0.0 collective-permute-start.3
  17.3 1.7 %shard_map.58 = (bf16[8,144,256]{2,1,0:T(8,128)(2,1)S(1)}, bf16[8,144,256]{2,1,0:T(8,128)(2,1)S(1)}) custom-call(bf16[304,512]{1,0:T(8,128)(2,1)S(1)} %collective-permute-done.refs_0_, bf16[288,512]{1,0:T(8,128)(2,1)S(1)} %collective-permute-done.1.refs_1_), custom_call_target="tpu_custom_call" | custom-call | flops 60000002048 | bytes 100000 | tf_op jit(solution)/shard_map/pallas_call | solution.py:154
  19.0 0.1 collective-permute-start.6
  19.1 1.3 %collective-permute-done.7.refs_2_ = bf16[272,512]{1,0:T(8,128)(2,1)S(1)} collective-permute-done((bf16[272,512]{1,0:T(8,128)(2,1)}, bf16[272,512]{1,0:T(8,128)(2,1)S(1)}, u32[]{:S(2)}, u32[]{:S(2)}) %collective-permute-start.7) | collective-permute-done | bytes 278560 | tf_op jit(solution)/shard_map/ppermute | solution.py:41
  20.4 0.0 collective-permute-start.5
  20.4 0.0 collective-permute-done.8.refs_3_
  20.4 1.8 %shard_map.60 = (bf16[8,144,256]{2,1,0:T(8,128)(2,1)S(1)}, bf16[8,144,256]{2,1,0:T(8,128)(2,1)S(1)}) custom-call(bf16[304,512]{1,0:T(8,128)(2,1)S(1)} %collective-permute-done.refs_0_, bf16[288,512]{1,0:T(8,128)(2,1)S(1)} %collective-permute-done.1.refs_1_, bf16[272,512]{1,0:T(8,128)(2,1)S(1)} %collective-permute-done.7.refs_2_, ...), custom_call_target="tpu_custom_call" | custom-call | flops 60000002048 | bytes 100000 | tf_op jit(solution)/shard_map/pallas_call | solution.py:154
  22.1 0.6 collective-permute-start.9
  22.7 0.1 collective-permute-start.10
  22.8 0.0 collective-permute-done.5.refs_0_
  22.8 1.7 %shard_map.59 = (bf16[8,144,256]{2,1,0:T(8,128)(2,1)S(1)}, bf16[8,144,256]{2,1,0:T(8,128)(2,1)S(1)}) custom-call(bf16[304,512]{1,0:T(8,128)(2,1)S(1)} %collective-permute-done.5.refs_0_, bf16[288,512]{1,0:T(8,128)(2,1)S(1)} %collective-permute-done.6.refs_1_), custom_call_target="tpu_custom_call" | custom-call | flops 1000000 | bytes 100000 | tf_op jit(solution)/shard_map/pallas_call | solution.py:154
  24.5 0.0 collective-permute-done.10.refs_3_
  24.6 1.3 %collective-permute-done.4.refs_1_ = bf16[288,512]{1,0:T(8,128)(2,1)S(1)} collective-permute-done((bf16[288,512]{1,0:T(8,128)(2,1)S(1)}, bf16[288,512]{1,0:T(8,128)(2,1)S(1)}, u32[]{:S(2)}, u32[]{:S(2)}) %collective-permute-start.4) | collective-permute-done | bytes 294944 | tf_op jit(solution)/shard_map/ppermute | solution.py:41
  25.9 0.7 collective-permute-done.3.refs_0_
  26.6 0.5 collective-permute-start.12
  27.1 1.4 %shard_map.61.same = bf16[8,144,256]{2,1,0:T(8,128)(2,1)S(1)} custom-call(bf16[304,512]{1,0:T(8,128)(2,1)S(1)} %collective-permute-done.3.refs_0_, bf16[288,512]{1,0:T(8,128)(2,1)S(1)} %collective-permute-done.4.refs_1_), custom_call_target="tpu_custom_call" | custom-call | flops 1000000 | bytes 100000 | tf_op jit(solution)/shard_map/pallas_call | solution.py:154
  28.5 1.8 %shard_map.62 = (bf16[8,144,256]{2,1,0:T(8,128)(2,1)S(1)}, bf16[8,144,256]{2,1,0:T(8,128)(2,1)S(1)}) custom-call(bf16[304,512]{1,0:T(8,128)(2,1)S(1)} %collective-permute-done.5.refs_0_, bf16[288,512]{1,0:T(8,128)(2,1)S(1)} %collective-permute-done.6.refs_1_, bf16[272,512]{1,0:T(8,128)(2,1)S(1)} %collective-permute-done.9.refs_2_, ...), custom_call_target="tpu_custom_call" | custom-call | flops 1000000 | bytes 100000 | tf_op jit(solution)/shard_map/pallas_call | solution.py:154
  30.2 1.0 %shard_map.65 = (bf16[4,112,128]{2,1,0:T(8,128)(2,1)S(1)}, bf16[4,112,128]{2,1,0:T(8,128)(2,1)S(1)}) custom-call(bf16[304,512]{1,0:T(8,128)(2,1)S(1)} %collective-permute-done.11.low, bf16[288,512]{1,0:T(8,128)(2,1)S(1)} %collective-permute-done.12.high, bf16[8,144,256]{2,1,0:T(8,128)(2,1)S(1)} %shard_map.61.same, ...), custom_call_target="tpu_custom_call" | custom-call | flops 1000000000 | bytes 100000 | tf_op jit(solution)/shard_map/pallas_call | solution.py:211
  31.3 1.6 %collective-permute-start.13 = (bf16[4,112,128]{2,1,0:T(8,128)(2,1)S(1)}, bf16[4,112,128]{2,1,0:T(8,128)(2,1)S(1)}, u32[]{:S(2)}, u32[]{:S(2)}) collective-permute-start(bf16[4,112,128]{2,1,0:T(8,128)(2,1)S(1)} %get-tuple-element.85), channel_id=1, source_target_pairs={{0,8},{1,9},{2,10},{3,11},{4,12},{5,13},{6,14},{7,15},{8,16},{9,17... | collective-permute-start | bytes 344072 | tf_op jit(solution)/shard_map/ppermute | solution.py:41
  32.9 1.7 %collective-permute-start.14 = (bf16[4,112,128]{2,1,0:T(8,128)(2,1)S(1)}, bf16[4,112,128]{2,1,0:T(8,128)(2,1)S(1)}, u32[]{:S(2)}, u32[]{:S(2)}) collective-permute-start(bf16[4,112,128]{2,1,0:T(8,128)(2,1)S(1)} %get-tuple-element.86), channel_id=1, source_target_pairs={{0,24},{1,25},{2,26},{3,27},{4,28},{5,29},{6,30},{7,31},{8,0},{9,1... | collective-permute-start | bytes 344072 | tf_op jit(solution)/shard_map/ppermute | solution.py:41
  34.6 1.8 %shard_map.64 = (f32[8,112,128]{2,1,0:T(8,128)S(1)}, f32[8,112,128]{2,1,0:T(8,128)S(1)}) custom-call(bf16[304,512]{1,0:T(8,128)(2,1)S(1)} %collective-permute-done.11.low, bf16[288,512]{1,0:T(8,128)(2,1)S(1)} %collective-permute-done.12.high, bf16[8,144,256]{2,1,0:T(8,128)(2,1)S(1)} %shard_map.61.same, bf16[8,144,256]{2,1,0:T(8,128)(2,1)S(1)} %get-tuple-element.73.rest_0_, ...), custom_call_target="tpu_custom_call" | custom-call | flops 2000000000 | bytes 100000 | tf_op jit(solution)/shard_map/pallas_call | solution.py:211
  36.4 1.3 %collective-permute-done.13.from_up = bf16[4,112,128]{2,1,0:T(8,128)(2,1)S(1)} collective-permute-done((bf16[4,112,128]{2,1,0:T(8,128)(2,1)S(1)}, bf16[4,112,128]{2,1,0:T(8,128)(2,1)S(1)}, u32[]{:S(2)}, u32[]{:S(2)}) %collective-permute-start.13) | collective-permute-done | bytes 114720 | tf_op jit(solution)/shard_map/ppermute | solution.py:41
  37.6 0.0 collective-permute-done.14.from_down
  37.7 0.1 shard_map.66
  37.8 1.9 %collective-permute-start.15 = (bf16[8,112,128]{2,1,0:T(8,128)(2,1)S(1)}, bf16[8,112,128]{2,1,0:T(8,128)(2,1)S(1)}, u32[]{:S(2)}, u32[]{:S(2)}) collective-permute-start(bf16[8,112,128]{2,1,0:T(8,128)(2,1)S(1)} %get-tuple-element.87), channel_id=1, source_target_pairs={{0,8},{1,9},{2,10},{3,11},{4,12},{5,13},{6,14},{7,15},{8,16},{9,17... | collective-permute-start | bytes 688136 | tf_op jit(solution)/shard_map/ppermute | solution.py:41
  39.6 1.7 %collective-permute-start.16 = (bf16[8,112,128]{2,1,0:T(8,128)(2,1)S(1)}, bf16[8,112,128]{2,1,0:T(8,128)(2,1)S(1)}, u32[]{:S(2)}, u32[]{:S(2)}) collective-permute-start(bf16[8,112,128]{2,1,0:T(8,128)(2,1)S(1)} %get-tuple-element.88), channel_id=1, source_target_pairs={{0,24},{1,25},{2,26},{3,27},{4,28},{5,29},{6,30},{7,31},{8,0},{9,1... | collective-permute-start | bytes 688136 | tf_op jit(solution)/shard_map/ppermute | solution.py:41
  41.3 1.0 %shard_map.63.own = f32[8,112,128]{2,1,0:T(8,128)S(1)} custom-call(bf16[304,512]{1,0:T(8,128)(2,1)S(1)} %collective-permute-done.11.low, bf16[288,512]{1,0:T(8,128)(2,1)S(1)} %collective-permute-done.12.high, bf16[8,144,256]{2,1,0:T(8,128)(2,1)S(1)} %shard_map.61.same, bf16[8,144,256]{2,1,0:T(8,128)(2,1)S(1)} %get-tuple-element.73.rest_0_, ...), custom_call_target="tpu_custom_call" | custom-call | flops 1000000000 | bytes 100000 | tf_op jit(solution)/shard_map/pallas_call | solution.py:211
  42.3 3.6 %collective-permute-done.15.a = bf16[8,112,128]{2,1,0:T(8,128)(2,1)S(1)} collective-permute-done((bf16[8,112,128]{2,1,0:T(8,128)(2,1)S(1)}, bf16[8,112,128]{2,1,0:T(8,128)(2,1)S(1)}, u32[]{:S(2)}, u32[]{:S(2)}) %collective-permute-start.15) | collective-permute-done | bytes 229408 | tf_op jit(solution)/shard_map/ppermute | solution.py:41
  46.0 0.1 shard_map.67
  46.0 16.8 %all_to_all.5.parts = bf16[8,112,128]{2,1,0:T(8,128)(2,1)S(1)} all-to-all(bf16[8,112,128]{2,1,0:T(8,128)(2,1)S(1)} %shard_map.67), channel_id=1, replica_groups=mesh['obs'=8,'grid'=32] {'obs'}, dimensions={0} | all-to-all | bytes 458752 | tf_op jit(solution)/shard_map/all_to_all | solution.py:440
  62.9 2.3 %shard_map.68.own = bf16[128,128]{1,0:T(8,128)(2,1)S(1)} custom-call(bf16[8,112,128]{2,1,0:T(8,128)(2,1)S(1)} %all_to_all.5.parts), custom_call_target="tpu_custom_call" | custom-call | flops 4000000000 | bytes 100000 | tf_op jit(solution)/shard_map/pallas_call | solution.py:294
  65.2 0.9 %collective-permute-start.18 = (bf16[128,128]{1,0:T(8,128)(2,1)S(1)}, bf16[128,128]{1,0:T(8,128)(2,1)S(1)}, u32[]{:S(2)}, u32[]{:S(2)}) collective-permute-start(bf16[128,128]{1,0:T(8,128)(2,1)S(1)} %shard_map.68.own), channel_id=1, source_target_pairs={{0,31},{1,0},{2,1},{3,2},{4,3},{5,4},{6,5},{7,6},{8,7},{9,8},{10,9... | collective-permute-start | bytes 98312 | tf_op jit(solution)/shard_map/ppermute | solution.py:444
  66.1 0.6 shard_map.69.part
  66.7 1.0 %collective-permute-done.18.right = bf16[128,128]{1,0:T(8,128)(2,1)S(1)} collective-permute-done((bf16[128,128]{1,0:T(8,128)(2,1)S(1)}, bf16[128,128]{1,0:T(8,128)(2,1)S(1)}, u32[]{:S(2)}, u32[]{:S(2)}) %collective-permute-start.18) | collective-permute-done | bytes 32800 | tf_op jit(solution)/shard_map/ppermute | solution.py:444
  67.7 5.1 %collective-permute-done.17.left = bf16[128,128]{1,0:T(8,128)(2,1)S(1)} collective-permute-done((bf16[128,128]{1,0:T(8,128)(2,1)S(1)}, bf16[128,128]{1,0:T(8,128)(2,1)S(1)}, u32[]{:S(2)}, u32[]{:S(2)}) %collective-permute-start.17) | collective-permute-done | bytes 32800 | tf_op jit(solution)/shard_map/ppermute | solution.py:443
  72.8 1.8 %shard_map.70 = bf16[48,128,128]{2,1,0:T(8,128)(2,1)} custom-call(bf16[128,128]{1,0:T(8,128)(2,1)S(1)} %collective-permute-done.17.left, bf16[128,128]{1,0:T(8,128)(2,1)S(1)} %collective-permute-done.18.right, f32[24,128,256]{2,1,0:T(8,128)S(1)} %shard_map.69.part, bf16[24,128,256]{2,1,0:T(8,128)(2,1)S(1)} %get-tuple-element.90.perturb), custom_call_target="tpu_custom_call" | custom-call | flops 2000000000 | bytes 100000 | tf_op jit(solution)/shard_map/pallas_call | solution.py:377
  (11 shorter events, 0.0 us)
Async XLA Ops:
  0.0 9.3 %copy-start.1 = (bf16[48,128,128]{2,1,0:T(8,128)(2,1)S(1)}, bf16[48,128,128]{2,1,0:T(8,128)(2,1)}, u32[]{:S(2)}) copy-start(bf16[48,128,128]{2,1,0:T(8,128)(2,1)} %state.1) | copy-start | bytes 4718596
  2.6 7.2 %collective-permute-start.2 = (bf16[560,512]{1,0:T(8,128)(2,1)}, bf16[560,512]{1,0:T(8,128)(2,1)S(1)}, u32[]{:S(2)}, u32[]{:S(2)}) collective-permute-start(bf16[560,512]{1,0:T(8,128)(2,1)} %get-tuple-element.50.refs_0_), channel_id=1, source_target_pairs={{0,1},{1,0},{2,3},{3,2},{4,5},{5,4},{6,7},{7,6},{8,9},{9,8},{10,11... | collective-permute-start | bytes 1720328 | tf_op jit(solution)/shard_map/ppermute | solution.py:41
  2.7 11.7 %collective-permute-start = (bf16[304,512]{1,0:T(8,128)(2,1)}, bf16[304,512]{1,0:T(8,128)(2,1)S(1)}, u32[]{:S(2)}, u32[]{:S(2)}) collective-permute-start(bf16[304,512]{1,0:T(8,128)(2,1)} %get-tuple-element.48), channel_id=1, source_target_pairs={{0,2},{1,3},{2,4},{3,5},{4,6},{5,7},{6,0},{7,1},{8,10},{9,11},{10,... | collective-permute-start | bytes 933896 | tf_op jit(solution)/shard_map/ppermute | solution.py:41
  4.3 10.1 %collective-permute-start.1 = (bf16[288,512]{1,0:T(8,128)(2,1)}, bf16[288,512]{1,0:T(8,128)(2,1)S(1)}, u32[]{:S(2)}, u32[]{:S(2)}) collective-permute-start(bf16[288,512]{1,0:T(8,128)(2,1)} %get-tuple-element.49), channel_id=1, source_target_pairs={{0,6},{1,7},{2,0},{3,1},{4,2},{5,3},{6,4},{7,5},{8,14},{9,15},{10,... | collective-permute-start | bytes 884744 | tf_op jit(solution)/shard_map/ppermute | solution.py:41
  6.1 14.3 %collective-permute-start.7 = (bf16[272,512]{1,0:T(8,128)(2,1)}, bf16[272,512]{1,0:T(8,128)(2,1)S(1)}, u32[]{:S(2)}, u32[]{:S(2)}) collective-permute-start(bf16[272,512]{1,0:T(8,128)(2,1)} %get-tuple-element.63), channel_id=1, source_target_pairs={{0,2},{1,3},{2,4},{3,5},{4,6},{5,7},{6,0},{7,1},{8,10},{9,11},{10,... | collective-permute-start | bytes 835592 | tf_op jit(solution)/shard_map/ppermute | solution.py:41
  6.3 3.5 %copy-start = (bf16[560,512]{1,0:T(8,128)(2,1)S(1)}, bf16[560,512]{1,0:T(8,128)(2,1)}, u32[]{:S(2)}) copy-start(bf16[560,512]{1,0:T(8,128)(2,1)} %get-tuple-element.50.refs_0_) | copy-start | bytes 1720324
  6.3 14.0 %collective-permute-start.8 = (bf16[272,512]{1,0:T(8,128)(2,1)}, bf16[272,512]{1,0:T(8,128)(2,1)S(1)}, u32[]{:S(2)}, u32[]{:S(2)}) collective-permute-start(bf16[272,512]{1,0:T(8,128)(2,1)} %get-tuple-element.64), channel_id=1, source_target_pairs={{0,6},{1,7},{2,0},{3,1},{4,2},{5,3},{6,4},{7,5},{8,14},{9,15},{10,... | collective-permute-start | bytes 835592 | tf_op jit(solution)/shard_map/ppermute | solution.py:41
  14.4 11.5 %collective-permute-start.4 = (bf16[288,512]{1,0:T(8,128)(2,1)S(1)}, bf16[288,512]{1,0:T(8,128)(2,1)S(1)}, u32[]{:S(2)}, u32[]{:S(2)}) collective-permute-start(bf16[288,512]{1,0:T(8,128)(2,1)S(1)} %collective-permute-done.1.refs_1_), channel_id=1, source_target_pairs={{0,6},{1,7},{2,0},{3,1},{4,2},{5,3},{6,4},{7,5},{8,14},{9,15},{10,... | collective-permute-start | bytes 884744 | tf_op jit(solution)/shard_map/ppermute | solution.py:41
  17.3 9.2 %collective-permute-start.3 = (bf16[304,512]{1,0:T(8,128)(2,1)S(1)}, bf16[304,512]{1,0:T(8,128)(2,1)S(1)}, u32[]{:S(2)}, u32[]{:S(2)}) collective-permute-start(bf16[304,512]{1,0:T(8,128)(2,1)S(1)} %collective-permute-done.refs_0_), channel_id=1, source_target_pairs={{0,2},{1,3},{2,4},{3,5},{4,6},{5,7},{6,0},{7,1},{8,10},{9,11},{10,... | collective-permute-start | bytes 933896 | tf_op jit(solution)/shard_map/ppermute | solution.py:41
  19.0 3.7 %collective-permute-start.6 = (bf16[288,512]{1,0:T(8,128)(2,1)S(1)}, bf16[288,512]{1,0:T(8,128)(2,1)S(1)}, u32[]{:S(2)}, u32[]{:S(2)}) collective-permute-start(bf16[288,512]{1,0:T(8,128)(2,1)S(1)} %collective-permute-done.1.refs_1_), channel_id=1, source_target_pairs={{0,1},{1,0},{2,3},{3,2},{4,5},{5,4},{6,7},{7,6},{8,9},{9,8},{10,11... | collective-permute-start | bytes 884744 | tf_op jit(solution)/shard_map/ppermute | solution.py:41
  20.4 2.5 %collective-permute-start.5 = (bf16[304,512]{1,0:T(8,128)(2,1)S(1)}, bf16[304,512]{1,0:T(8,128)(2,1)S(1)}, u32[]{:S(2)}, u32[]{:S(2)}) collective-permute-start(bf16[304,512]{1,0:T(8,128)(2,1)S(1)} %collective-permute-done.refs_0_), channel_id=1, source_target_pairs={{0,1},{1,0},{2,3},{3,2},{4,5},{5,4},{6,7},{7,6},{8,9},{9,8},{10,11... | collective-permute-start | bytes 933896 | tf_op jit(solution)/shard_map/ppermute | solution.py:41
  22.1 2.4 %collective-permute-start.9 = (bf16[272,512]{1,0:T(8,128)(2,1)S(1)}, bf16[272,512]{1,0:T(8,128)(2,1)S(1)}, u32[]{:S(2)}, u32[]{:S(2)}) collective-permute-start(bf16[272,512]{1,0:T(8,128)(2,1)S(1)} %collective-permute-done.7.refs_2_), channel_id=1, source_target_pairs={{0,1},{1,0},{2,3},{3,2},{4,5},{5,4},{6,7},{7,6},{8,9},{9,8},{10,11... | collective-permute-start | bytes 835592 | tf_op jit(solution)/shard_map/ppermute | solution.py:41
  22.7 1.8 %collective-permute-start.10 = (bf16[272,512]{1,0:T(8,128)(2,1)S(1)}, bf16[272,512]{1,0:T(8,128)(2,1)S(1)}, u32[]{:S(2)}, u32[]{:S(2)}) collective-permute-start(bf16[272,512]{1,0:T(8,128)(2,1)S(1)} %collective-permute-done.8.refs_3_), channel_id=1, source_target_pairs={{0,1},{1,0},{2,3},{3,2},{4,5},{5,4},{6,7},{7,6},{8,9},{9,8},{10,11... | collective-permute-start | bytes 835592 | tf_op jit(solution)/shard_map/ppermute | solution.py:41
  26.6 3.7 %collective-permute-start.11 = (bf16[304,512]{1,0:T(8,128)(2,1)S(1)}, bf16[304,512]{1,0:T(8,128)(2,1)S(1)}, u32[]{:S(2)}, u32[]{:S(2)}) collective-permute-start(bf16[304,512]{1,0:T(8,128)(2,1)S(1)} %collective-permute-done.3.refs_0_), channel_id=1, source_target_pairs={{0,1},{1,0},{2,3},{3,2},{4,5},{5,4},{6,7},{7,6},{8,9},{9,8},{10,11... | collective-permute-start | bytes 933896 | tf_op jit(solution)/shard_map/ppermute | solution.py:41
  26.6 3.6 %collective-permute-start.12 = (bf16[288,512]{1,0:T(8,128)(2,1)S(1)}, bf16[288,512]{1,0:T(8,128)(2,1)S(1)}, u32[]{:S(2)}, u32[]{:S(2)}) collective-permute-start(bf16[288,512]{1,0:T(8,128)(2,1)S(1)} %collective-permute-done.4.refs_1_), channel_id=1, source_target_pairs={{0,1},{1,0},{2,3},{3,2},{4,5},{5,4},{6,7},{7,6},{8,9},{9,8},{10,11... | collective-permute-start | bytes 884744 | tf_op jit(solution)/shard_map/ppermute | solution.py:41
  31.3 6.4 %collective-permute-start.13 = (bf16[4,112,128]{2,1,0:T(8,128)(2,1)S(1)}, bf16[4,112,128]{2,1,0:T(8,128)(2,1)S(1)}, u32[]{:S(2)}, u32[]{:S(2)}) collective-permute-start(bf16[4,112,128]{2,1,0:T(8,128)(2,1)S(1)} %get-tuple-element.85), channel_id=1, source_target_pairs={{0,8},{1,9},{2,10},{3,11},{4,12},{5,13},{6,14},{7,15},{8,16},{9,17... | collective-permute-start | bytes 344072 | tf_op jit(solution)/shard_map/ppermute | solution.py:41
  32.9 4.8 %collective-permute-start.14 = (bf16[4,112,128]{2,1,0:T(8,128)(2,1)S(1)}, bf16[4,112,128]{2,1,0:T(8,128)(2,1)S(1)}, u32[]{:S(2)}, u32[]{:S(2)}) collective-permute-start(bf16[4,112,128]{2,1,0:T(8,128)(2,1)S(1)} %get-tuple-element.86), channel_id=1, source_target_pairs={{0,24},{1,25},{2,26},{3,27},{4,28},{5,29},{6,30},{7,31},{8,0},{9,1... | collective-permute-start | bytes 344072 | tf_op jit(solution)/shard_map/ppermute | solution.py:41
  37.8 8.2 %collective-permute-start.15 = (bf16[8,112,128]{2,1,0:T(8,128)(2,1)S(1)}, bf16[8,112,128]{2,1,0:T(8,128)(2,1)S(1)}, u32[]{:S(2)}, u32[]{:S(2)}) collective-permute-start(bf16[8,112,128]{2,1,0:T(8,128)(2,1)S(1)} %get-tuple-element.87), channel_id=1, source_target_pairs={{0,8},{1,9},{2,10},{3,11},{4,12},{5,13},{6,14},{7,15},{8,16},{9,17... | collective-permute-start | bytes 688136 | tf_op jit(solution)/shard_map/ppermute | solution.py:41
  39.6 6.3 %collective-permute-start.16 = (bf16[8,112,128]{2,1,0:T(8,128)(2,1)S(1)}, bf16[8,112,128]{2,1,0:T(8,128)(2,1)S(1)}, u32[]{:S(2)}, u32[]{:S(2)}) collective-permute-start(bf16[8,112,128]{2,1,0:T(8,128)(2,1)S(1)} %get-tuple-element.88), channel_id=1, source_target_pairs={{0,24},{1,25},{2,26},{3,27},{4,28},{5,29},{6,30},{7,31},{8,0},{9,1... | collective-permute-start | bytes 688136 | tf_op jit(solution)/shard_map/ppermute | solution.py:41
  65.2 2.5 %collective-permute-start.18 = (bf16[128,128]{1,0:T(8,128)(2,1)S(1)}, bf16[128,128]{1,0:T(8,128)(2,1)S(1)}, u32[]{:S(2)}, u32[]{:S(2)}) collective-permute-start(bf16[128,128]{1,0:T(8,128)(2,1)S(1)} %shard_map.68.own), channel_id=1, source_target_pairs={{0,31},{1,0},{2,1},{3,2},{4,3},{5,4},{6,5},{7,6},{8,7},{9,8},{10,9... | collective-permute-start | bytes 98312 | tf_op jit(solution)/shard_map/ppermute | solution.py:444
  66.1 6.7 %collective-permute-start.17 = (bf16[128,128]{1,0:T(8,128)(2,1)S(1)}, bf16[128,128]{1,0:T(8,128)(2,1)S(1)}, u32[]{:S(2)}, u32[]{:S(2)}) collective-permute-start(bf16[128,128]{1,0:T(8,128)(2,1)S(1)} %shard_map.68.own), channel_id=1, source_target_pairs={{0,1},{1,2},{2,3},{3,4},{4,5},{5,6},{6,7},{7,8},{8,9},{9,10},{10,1... | collective-permute-start | bytes 98312 | tf_op jit(solution)/shard_map/ppermute | solution.py:443

commit v5 on v4

--- a/solution.py
+++ b/solution.py
@@ -14,7 +14,7 @@
 LOW = 512
 BLOCKS = 4
 HALF = 2 * K + 16
-PACK = 112
+PACK = 80
 VMEM = 20 * 1024 * 1024
 
 
@@ -167,18 +167,25 @@
 
 
 def pack(total):
-    gram = total[0:K]
-    lane = lax.broadcasted_iota(jnp.int32, (32, K), 1)
-    fold = jnp.where(lane < 64, pltpu.roll(gram[64:96], 64, 1), gram[96:128])
-    return jnp.concatenate([gram[0:64], fold, total[K : K + 16]], axis=0)
+    row = lax.broadcasted_iota(jnp.int32, (64, K), 0)
+    lane = lax.broadcasted_iota(jnp.int32, (64, K), 1)
+    lower = total[64:K]
+    upper = jnp.where(lane < row, pltpu.roll(lower, 64, 1), total[0:64])
+    diagonal = jnp.sum(jnp.where(lane == row + 64, lower, 0.0), axis=0, keepdims=True)
+    tail = jnp.where(lax.broadcasted_iota(jnp.int32, (16, K), 0) == 0, diagonal, total[K:])
+    return jnp.concatenate([upper, tail], axis=0)
 
 
 def unpack(packed):
+    row = lax.broadcasted_iota(jnp.int32, (64, K), 0)
     lane = lax.broadcasted_iota(jnp.int32, (64, K), 1)
-    fold = packed[64:96]
-    lower = jnp.where(lane >= 64, jnp.concatenate([pltpu.roll(fold, 64, 1), fold], axis=0), 0.0)
-    corner = jnp.concatenate([jnp.where(lane >= 64, packed[0:64], 0.0), jnp.zeros_like(lower)], axis=0)
-    return jnp.concatenate([packed[0:64], lower], axis=0) + corner.T, packed[96:97]
+    upper = packed[0:64]
+    above = jnp.where(lane > row, upper, 0.0)
+    below = pltpu.roll(jnp.where(lane < row, upper, 0.0), 64, 1)
+    off = jnp.concatenate([above, below], axis=0)
+    low = jnp.where(lane == row + 64, packed[64:65], 0.0)
+    diagonal = jnp.concatenate([jnp.where(lane == row, upper, 0.0), low], axis=0)
+    return off + off.T + diagonal, packed[65:66]
 
 
 def last_kernel(shifts, lowest, low, high, same, *rest):
@@ -420,13 +427,11 @@
     left_more, right_more, same = lax.optimization_barrier((left_more, right_more, same))
     left_more_other, right_more_other = hop(left_more, 0, 0, 1), hop(right_more, 0, 0, 1)
     cross = pick_rows(firsts(1), SHORT, left_other, right_other)
-    far_low, far_high, cross, left_more_other, right_more_other = lax.optimization_barrier(
-        (far_low, far_high, cross, left_more_other, right_more_other)
-    )
-    far_low_other, far_high_other = hop(far_low, 0, 0, 1), hop(far_high, 0, 0, 1)
     cross = pick_rows(
         seconds(1), SHORT, left_other, right_other, left_more_other, right_more_other, *cross
     )
+    far_low, far_high, cross = lax.optimization_barrier((far_low, far_high, cross))
+    far_low_other, far_high_other = hop(far_low, 0, 0, 1), hop(far_high, 0, 0, 1)
     far = pick_rows(((((0, 0, 32), (1, 1, 16)), (0, 16, 0), None),), SHORT, far_low, far_high)[0]
     last = (far_low_other, far_high_other, far, *found, same[0], cross[0], same[1], cross[1])
 

time: 74.9 us -> 71.5 us (0.955)
  waiting for transfers between devices: 16.3 us -> 13.3 us
    ppermute x17, waiting for transfers between devices: 10.2 us -> 7.2 us  [hop(): return lax.ppermute(value, 'grid', pairs)]
  transfers between devices with their start and end apart: 19 -> 19, of which waited for: 8 -> 10; matrix products, arithmetic and copies ran while one was open for 0% -> 0% of each run, Pallas kernels for 20% -> 21%
where the time goes in v5:
time: 71.5 us; the launch traced here: 71.4 us
  Pallas kernels  22.6 us (32%)
  starting transfers between devices  18.7 us (26%)
  blocking collectives  16.3 us (23%)
  waiting for transfers between devices  13.3 us (19%)
    ppermute x17, starting transfers between devices, hop(): return lax.ppermute(value, 'grid', pairs)  17.7 us
    all_to_all x1, blocking collectives, on_device(): parts = lax.all_to_all(parts, 'obs', 0, 0, tiled=True)  16.3 us
    pallas_call x6, Pallas kernels, pick_rows(): pl.pallas_call(functools.partial(pick_kernel, sources, len(args)), out_sh...  10.8 us
    ppermute x17, waiting for transfers between devices, hop(): return lax.ppermute(value, 'grid', pairs)  7.2 us
    ppermute x1, waiting for transfers between devices, on_device(): lax.ppermute(own, 'grid', [(j, (j + 1) % n_grid) for j in range(n_grid)])  5.06 us
    pallas_call x3, Pallas kernels, last_grams(): pl.pallas_call(functools.partial(last_kernel, shifts, lowest), out_shape=...  3.93 us
    pallas_call x1, Pallas kernels, make_messages(): pl.pallas_call(message_kernel, out_shape=[jax.ShapeDtypeStruct((count, LO...  2.63 us
    pallas_call x1, Pallas kernels, transposed_weights(): pl.pallas_call(weights_kernel, out_shape=jax.ShapeDtypeStruct((K, K), BF1...  2.33 us
  transfers between devices with their start and end apart: 19, of which 10 were waited for; matrix products, arithmetic and copies ran while one was open for 0% of the time, Pallas kernels for 21%

profile of v5, /device:TPU:32, one launch (start us, length us, event | category | flops | bytes accessed | tf_op | source)
XLA Modules:
  0.0 71.4 jit_solution(5065850054299087844)
XLA Ops:
  0.0 2.6 %shard_map.55 = (bf16[560,512]{1,0:T(8,128)(2,1)}, bf16[304,512]{1,0:T(8,128)(2,1)}, bf16[272,512]{1,0:T(8,128)(2,1)}, bf16[288,512]{1,0:T(8,128)(2,1)}, bf16[272,512]{1,0:T(8,128)(2,1)}) custom-call(bf16[2048,128]{1,0:T(8,128)(2,1)} %refs_0_.1, f32[2048]{0:T(1024)} %refs_1_.1, f32[2048]{0:T(1024)} %refs_2_.1, s32[64,256]{1,0:T(8,128)} %bitcast.3), custom_call_target="tpu_custom_call" | custom-call | flops 2000000000 | bytes 100000 | tf_op jit(solution)/shard_map/pallas_call | solution.py:106
  2.6 0.1 collective-permute-start.2
  2.7 1.6 %collective-permute-start = (bf16[304,512]{1,0:T(8,128)(2,1)}, bf16[304,512]{1,0:T(8,128)(2,1)S(1)}, u32[]{:S(2)}, u32[]{:S(2)}) collective-permute-start(bf16[304,512]{1,0:T(8,128)(2,1)} %get-tuple-element.46), channel_id=1, source_target_pairs={{0,2},{1,3},{2,4},{3,5},{4,6},{5,7},{6,0},{7,1},{8,10},{9,11},{10,... | collective-permute-start | bytes 933896 | tf_op jit(solution)/shard_map/ppermute | solution.py:41
  4.3 1.7 %collective-permute-start.1 = (bf16[288,512]{1,0:T(8,128)(2,1)}, bf16[288,512]{1,0:T(8,128)(2,1)S(1)}, u32[]{:S(2)}, u32[]{:S(2)}) collective-permute-start(bf16[288,512]{1,0:T(8,128)(2,1)} %get-tuple-element.47), channel_id=1, source_target_pairs={{0,6},{1,7},{2,0},{3,1},{4,2},{5,3},{6,4},{7,5},{8,14},{9,15},{10,... | collective-permute-start | bytes 884744 | tf_op jit(solution)/shard_map/ppermute | solution.py:41
  6.1 0.3 collective-permute-start.7
  6.3 3.0 %collective-permute-start.8 = (bf16[272,512]{1,0:T(8,128)(2,1)}, bf16[272,512]{1,0:T(8,128)(2,1)S(1)}, u32[]{:S(2)}, u32[]{:S(2)}) collective-permute-start(bf16[272,512]{1,0:T(8,128)(2,1)} %get-tuple-element.60), channel_id=1, source_target_pairs={{0,6},{1,7},{2,0},{3,1},{4,2},{5,3},{6,4},{7,5},{8,14},{9,15},{10,... | collective-permute-start | bytes 835592 | tf_op jit(solution)/shard_map/ppermute | solution.py:41
  9.3 0.6 shard_map.57
  9.9 0.0 collective-permute-done.2.refs_1_
  9.9 2.5 %shard_map.56 = (bf16[8,144,256]{2,1,0:T(8,128)(2,1)S(1)}, bf16[8,144,256]{2,1,0:T(8,128)(2,1)S(1)}) custom-call(bf16[560,512]{1,0:T(8,128)(2,1)S(1)} %copy-done, bf16[560,512]{1,0:T(8,128)(2,1)S(1)} %collective-permute-done.2.refs_1_), custom_call_target="tpu_custom_call" | custom-call | flops 1000000 | bytes 100000 | tf_op jit(solution)/shard_map/pallas_call | solution.py:154
  12.4 1.9 %collective-permute-done.1.refs_1_ = bf16[288,512]{1,0:T(8,128)(2,1)S(1)} collective-permute-done((bf16[288,512]{1,0:T(8,128)(2,1)}, bf16[288,512]{1,0:T(8,128)(2,1)S(1)}, u32[]{:S(2)}, u32[]{:S(2)}) %collective-permute-start.1) | collective-permute-done | bytes 294944 | tf_op jit(solution)/shard_map/ppermute | solution.py:41
  14.4 0.0 collective-permute-done.refs_0_
  14.4 2.9 %collective-permute-start.4 = (bf16[288,512]{1,0:T(8,128)(2,1)S(1)}, bf16[288,512]{1,0:T(8,128)(2,1)S(1)}, u32[]{:S(2)}, u32[]{:S(2)}) collective-permute-start(bf16[288,512]{1,0:T(8,128)(2,1)S(1)} %collective-permute-done.1.refs_1_), channel_id=1, source_target_pairs={{0,6},{1,7},{2,0},{3,1},{4,2},{5,3},{6,4},{7,5},{8,14},{9,15},{10,... | collective-permute-start | bytes 884744 | tf_op jit(solution)/shard_map/ppermute | solution.py:41
  17.3 0.0 collective-permute-start.3
  17.3 1.7 %shard_map.58 = (bf16[8,144,256]{2,1,0:T(8,128)(2,1)S(1)}, bf16[8,144,256]{2,1,0:T(8,128)(2,1)S(1)}) custom-call(bf16[304,512]{1,0:T(8,128)(2,1)S(1)} %collective-permute-done.refs_0_, bf16[288,512]{1,0:T(8,128)(2,1)S(1)} %collective-permute-done.1.refs_1_), custom_call_target="tpu_custom_call" | custom-call | flops 60000002048 | bytes 100000 | tf_op jit(solution)/shard_map/pallas_call | solution.py:154
  19.0 0.1 collective-permute-start.6
  19.1 1.3 %collective-permute-done.7.refs_2_ = bf16[272,512]{1,0:T(8,128)(2,1)S(1)} collective-permute-done((bf16[272,512]{1,0:T(8,128)(2,1)}, bf16[272,512]{1,0:T(8,128)(2,1)S(1)}, u32[]{:S(2)}, u32[]{:S(2)}) %collective-permute-start.7) | collective-permute-done | bytes 278560 | tf_op jit(solution)/shard_map/ppermute | solution.py:41
  20.4 0.0 collective-permute-start.5
  20.4 1.8 %shard_map.59 = (bf16[8,144,256]{2,1,0:T(8,128)(2,1)S(1)}, bf16[8,144,256]{2,1,0:T(8,128)(2,1)S(1)}) custom-call(bf16[304,512]{1,0:T(8,128)(2,1)S(1)} %collective-permute-done.refs_0_, bf16[288,512]{1,0:T(8,128)(2,1)S(1)} %collective-permute-done.1.refs_1_, bf16[272,512]{1,0:T(8,128)(2,1)S(1)} %collective-permute-done.7.refs_2_, ...), custom_call_target="tpu_custom_call" | custom-call | flops 60000002048 | bytes 100000 | tf_op jit(solution)/shard_map/pallas_call | solution.py:154
  22.1 0.6 collective-permute-start.9
  22.7 0.0 collective-permute-done.6.refs_1_
  22.7 0.1 collective-permute-start.10
  22.8 1.7 %shard_map.60 = (bf16[8,144,256]{2,1,0:T(8,128)(2,1)S(1)}, bf16[8,144,256]{2,1,0:T(8,128)(2,1)S(1)}) custom-call(bf16[304,512]{1,0:T(8,128)(2,1)S(1)} %collective-permute-done.5.refs_0_, bf16[288,512]{1,0:T(8,128)(2,1)S(1)} %collective-permute-done.6.refs_1_), custom_call_target="tpu_custom_call" | custom-call | flops 1000000 | bytes 100000 | tf_op jit(solution)/shard_map/pallas_call | solution.py:154
  24.5 0.0 collective-permute-done.9.refs_2_
  24.6 1.8 %shard_map.61 = (bf16[8,144,256]{2,1,0:T(8,128)(2,1)S(1)}, bf16[8,144,256]{2,1,0:T(8,128)(2,1)S(1)}) custom-call(bf16[304,512]{1,0:T(8,128)(2,1)S(1)} %collective-permute-done.5.refs_0_, bf16[288,512]{1,0:T(8,128)(2,1)S(1)} %collective-permute-done.6.refs_1_, bf16[272,512]{1,0:T(8,128)(2,1)S(1)} %collective-permute-done.9.refs_2_, ...), custom_call_target="tpu_custom_call" | custom-call | flops 1000000 | bytes 100000 | tf_op jit(solution)/shard_map/pallas_call | solution.py:154
  26.3 0.3 collective-permute-done.3.refs_0_
  26.6 0.2 collective-permute-start.11
  26.8 0.3 collective-permute-start.12
  27.1 1.4 %shard_map.62.same = bf16[8,144,256]{2,1,0:T(8,128)(2,1)S(1)} custom-call(bf16[304,512]{1,0:T(8,128)(2,1)S(1)} %collective-permute-done.3.refs_0_, bf16[288,512]{1,0:T(8,128)(2,1)S(1)} %collective-permute-done.4.refs_1_), custom_call_target="tpu_custom_call" | custom-call | flops 1000000 | bytes 100000 | tf_op jit(solution)/shard_map/pallas_call | solution.py:154
  28.5 0.1 collective-permute-done.12.high
  28.6 1.0 %shard_map.65 = (bf16[4,80,128]{2,1,0:T(8,128)(2,1)S(1)}, bf16[4,80,128]{2,1,0:T(8,128)(2,1)S(1)}) custom-call(bf16[304,512]{1,0:T(8,128)(2,1)S(1)} %collective-permute-done.11.low, bf16[288,512]{1,0:T(8,128)(2,1)S(1)} %collective-permute-done.12.high, bf16[8,144,256]{2,1,0:T(8,128)(2,1)S(1)} %shard_map.62.same, ...), custom_call_target="tpu_custom_call" | custom-call | flops 1000000000 | bytes 100000 | tf_op jit(solution)/shard_map/pallas_call | solution.py:218
  29.7 1.7 %collective-permute-start.13 = (bf16[4,80,128]{2,1,0:T(8,128)(2,1)S(1)}, bf16[4,80,128]{2,1,0:T(8,128)(2,1)S(1)}, u32[]{:S(2)}, u32[]{:S(2)}) collective-permute-start(bf16[4,80,128]{2,1,0:T(8,128)(2,1)S(1)} %get-tuple-element.81), channel_id=1, source_target_pairs={{0,8},{1,9},{2,10},{3,11},{4,12},{5,13},{6,14},{7,15},{8,16},{9,17... | collective-permute-start | bytes 245768 | tf_op jit(solution)/shard_map/ppermute | solution.py:41
  31.3 1.7 %collective-permute-start.14 = (bf16[4,80,128]{2,1,0:T(8,128)(2,1)S(1)}, bf16[4,80,128]{2,1,0:T(8,128)(2,1)S(1)}, u32[]{:S(2)}, u32[]{:S(2)}) collective-permute-start(bf16[4,80,128]{2,1,0:T(8,128)(2,1)S(1)} %get-tuple-element.82), channel_id=1, source_target_pairs={{0,24},{1,25},{2,26},{3,27},{4,28},{5,29},{6,30},{7,31},{8,0},{9,1... | collective-permute-start | bytes 245768 | tf_op jit(solution)/shard_map/ppermute | solution.py:41
  33.0 1.8 %shard_map.64 = (f32[8,80,128]{2,1,0:T(8,128)S(1)}, f32[8,80,128]{2,1,0:T(8,128)S(1)}) custom-call(bf16[304,512]{1,0:T(8,128)(2,1)S(1)} %collective-permute-done.11.low, bf16[288,512]{1,0:T(8,128)(2,1)S(1)} %collective-permute-done.12.high, bf16[8,144,256]{2,1,0:T(8,128)(2,1)S(1)} %shard_map.62.same, bf16[8,144,256]{2,1,0:T(8,128)(2,1)S(1)} %get-tuple-element.73.rest_0_, ...), custom_call_target="tpu_custom_call" | custom-call | flops 2000000000 | bytes 100000 | tf_op jit(solution)/shard_map/pallas_call | solution.py:218
  34.8 0.8 %collective-permute-done.13.from_up = bf16[4,80,128]{2,1,0:T(8,128)(2,1)S(1)} collective-permute-done((bf16[4,80,128]{2,1,0:T(8,128)(2,1)S(1)}, bf16[4,80,128]{2,1,0:T(8,128)(2,1)S(1)}, u32[]{:S(2)}, u32[]{:S(2)}) %collective-permute-start.13) | collective-permute-done | bytes 81952 | tf_op jit(solution)/shard_map/ppermute | solution.py:41
  35.6 0.1 collective-permute-done.14.from_down
  35.8 1.9 %collective-permute-start.15 = (bf16[8,80,128]{2,1,0:T(8,128)(2,1)S(1)}, bf16[8,80,128]{2,1,0:T(8,128)(2,1)S(1)}, u32[]{:S(2)}, u32[]{:S(2)}) collective-permute-start(bf16[8,80,128]{2,1,0:T(8,128)(2,1)S(1)} %get-tuple-element.83), channel_id=1, source_target_pairs={{0,8},{1,9},{2,10},{3,11},{4,12},{5,13},{6,14},{7,15},{8,16},{9,17... | collective-permute-start | bytes 491528 | tf_op jit(solution)/shard_map/ppermute | solution.py:41
  37.7 1.7 %collective-permute-start.16 = (bf16[8,80,128]{2,1,0:T(8,128)(2,1)S(1)}, bf16[8,80,128]{2,1,0:T(8,128)(2,1)S(1)}, u32[]{:S(2)}, u32[]{:S(2)}) collective-permute-start(bf16[8,80,128]{2,1,0:T(8,128)(2,1)S(1)} %get-tuple-element.84), channel_id=1, source_target_pairs={{0,24},{1,25},{2,26},{3,27},{4,28},{5,29},{6,30},{7,31},{8,0},{9,1... | collective-permute-start | bytes 491528 | tf_op jit(solution)/shard_map/ppermute | solution.py:41
  39.3 1.0 %shard_map.63.own = f32[8,80,128]{2,1,0:T(8,128)S(1)} custom-call(bf16[304,512]{1,0:T(8,128)(2,1)S(1)} %collective-permute-done.11.low, bf16[288,512]{1,0:T(8,128)(2,1)S(1)} %collective-permute-done.12.high, bf16[8,144,256]{2,1,0:T(8,128)(2,1)S(1)} %shard_map.62.same, bf16[8,144,256]{2,1,0:T(8,128)(2,1)S(1)} %get-tuple-element.73.rest_0_, ...), custom_call_target="tpu_custom_call" | custom-call | flops 1000000000 | bytes 100000 | tf_op jit(solution)/shard_map/pallas_call | solution.py:218
  40.4 2.4 %collective-permute-done.15.a = bf16[8,80,128]{2,1,0:T(8,128)(2,1)S(1)} collective-permute-done((bf16[8,80,128]{2,1,0:T(8,128)(2,1)S(1)}, bf16[8,80,128]{2,1,0:T(8,128)(2,1)S(1)}, u32[]{:S(2)}, u32[]{:S(2)}) %collective-permute-start.15) | collective-permute-done | bytes 163872 | tf_op jit(solution)/shard_map/ppermute | solution.py:41
  42.8 0.2 collective-permute-done.16.b
  43.0 0.1 shard_map.67
  43.1 16.3 %all_to_all.5.parts = bf16[8,80,128]{2,1,0:T(8,128)(2,1)S(1)} all-to-all(bf16[8,80,128]{2,1,0:T(8,128)(2,1)S(1)} %shard_map.67), channel_id=1, replica_groups=mesh['obs'=8,'grid'=32] {'obs'}, dimensions={0} | all-to-all | bytes 327680 | tf_op jit(solution)/shard_map/all_to_all | solution.py:445
  59.4 2.3 %shard_map.68.own = bf16[128,128]{1,0:T(8,128)(2,1)S(1)} custom-call(bf16[8,80,128]{2,1,0:T(8,128)(2,1)S(1)} %all_to_all.5.parts), custom_call_target="tpu_custom_call" | custom-call | flops 4000000000 | bytes 100000 | tf_op jit(solution)/shard_map/pallas_call | solution.py:301
  61.7 1.0 %collective-permute-start.18 = (bf16[128,128]{1,0:T(8,128)(2,1)S(1)}, bf16[128,128]{1,0:T(8,128)(2,1)S(1)}, u32[]{:S(2)}, u32[]{:S(2)}) collective-permute-start(bf16[128,128]{1,0:T(8,128)(2,1)S(1)} %shard_map.68.own), channel_id=1, source_target_pairs={{0,31},{1,0},{2,1},{3,2},{4,3},{5,4},{6,5},{7,6},{8,7},{9,8},{10,9... | collective-permute-start | bytes 98312 | tf_op jit(solution)/shard_map/ppermute | solution.py:449
  62.8 0.6 shard_map.69.part
  63.3 1.0 %collective-permute-done.18.right = bf16[128,128]{1,0:T(8,128)(2,1)S(1)} collective-permute-done((bf16[128,128]{1,0:T(8,128)(2,1)S(1)}, bf16[128,128]{1,0:T(8,128)(2,1)S(1)}, u32[]{:S(2)}, u32[]{:S(2)}) %collective-permute-start.18) | collective-permute-done | bytes 32800 | tf_op jit(solution)/shard_map/ppermute | solution.py:449
  64.3 5.1 %collective-permute-done.17.left = bf16[128,128]{1,0:T(8,128)(2,1)S(1)} collective-permute-done((bf16[128,128]{1,0:T(8,128)(2,1)S(1)}, bf16[128,128]{1,0:T(8,128)(2,1)S(1)}, u32[]{:S(2)}, u32[]{:S(2)}) %collective-permute-start.17) | collective-permute-done | bytes 32800 | tf_op jit(solution)/shard_map/ppermute | solution.py:448
  69.4 1.8 %shard_map.70 = bf16[48,128,128]{2,1,0:T(8,128)(2,1)} custom-call(bf16[128,128]{1,0:T(8,128)(2,1)S(1)} %collective-permute-done.17.left, bf16[128,128]{1,0:T(8,128)(2,1)S(1)} %collective-permute-done.18.right, f32[24,128,256]{2,1,0:T(8,128)S(1)} %shard_map.69.part, bf16[24,128,256]{2,1,0:T(8,128)(2,1)S(1)} %get-tuple-element.86.perturb), custom_call_target="tpu_custom_call" | custom-call | flops 2000000000 | bytes 100000 | tf_op jit(solution)/shard_map/pallas_call | solution.py:384
  (11 shorter events, 0.1 us)
Async XLA Ops:
  0.0 9.3 %copy-start.1 = (bf16[48,128,128]{2,1,0:T(8,128)(2,1)S(1)}, bf16[48,128,128]{2,1,0:T(8,128)(2,1)}, u32[]{:S(2)}) copy-start(bf16[48,128,128]{2,1,0:T(8,128)(2,1)} %state.1) | copy-start | bytes 4718596
  2.6 7.2 %collective-permute-start.2 = (bf16[560,512]{1,0:T(8,128)(2,1)}, bf16[560,512]{1,0:T(8,128)(2,1)S(1)}, u32[]{:S(2)}, u32[]{:S(2)}) collective-permute-start(bf16[560,512]{1,0:T(8,128)(2,1)} %get-tuple-element.48.refs_0_), channel_id=1, source_target_pairs={{0,1},{1,0},{2,3},{3,2},{4,5},{5,4},{6,7},{7,6},{8,9},{9,8},{10,11... | collective-permute-start | bytes 1720328 | tf_op jit(solution)/shard_map/ppermute | solution.py:41
  2.7 11.7 %collective-permute-start = (bf16[304,512]{1,0:T(8,128)(2,1)}, bf16[304,512]{1,0:T(8,128)(2,1)S(1)}, u32[]{:S(2)}, u32[]{:S(2)}) collective-permute-start(bf16[304,512]{1,0:T(8,128)(2,1)} %get-tuple-element.46), channel_id=1, source_target_pairs={{0,2},{1,3},{2,4},{3,5},{4,6},{5,7},{6,0},{7,1},{8,10},{9,11},{10,... | collective-permute-start | bytes 933896 | tf_op jit(solution)/shard_map/ppermute | solution.py:41
  4.3 10.1 %collective-permute-start.1 = (bf16[288,512]{1,0:T(8,128)(2,1)}, bf16[288,512]{1,0:T(8,128)(2,1)S(1)}, u32[]{:S(2)}, u32[]{:S(2)}) collective-permute-start(bf16[288,512]{1,0:T(8,128)(2,1)} %get-tuple-element.47), channel_id=1, source_target_pairs={{0,6},{1,7},{2,0},{3,1},{4,2},{5,3},{6,4},{7,5},{8,14},{9,15},{10,... | collective-permute-start | bytes 884744 | tf_op jit(solution)/shard_map/ppermute | solution.py:41
  6.1 14.3 %collective-permute-start.7 = (bf16[272,512]{1,0:T(8,128)(2,1)}, bf16[272,512]{1,0:T(8,128)(2,1)S(1)}, u32[]{:S(2)}, u32[]{:S(2)}) collective-permute-start(bf16[272,512]{1,0:T(8,128)(2,1)} %get-tuple-element.59), channel_id=1, source_target_pairs={{0,2},{1,3},{2,4},{3,5},{4,6},{5,7},{6,0},{7,1},{8,10},{9,11},{10,... | collective-permute-start | bytes 835592 | tf_op jit(solution)/shard_map/ppermute | solution.py:41
  6.3 3.5 %copy-start = (bf16[560,512]{1,0:T(8,128)(2,1)S(1)}, bf16[560,512]{1,0:T(8,128)(2,1)}, u32[]{:S(2)}) copy-start(bf16[560,512]{1,0:T(8,128)(2,1)} %get-tuple-element.48.refs_0_) | copy-start | bytes 1720324
  6.3 14.0 %collective-permute-start.8 = (bf16[272,512]{1,0:T(8,128)(2,1)}, bf16[272,512]{1,0:T(8,128)(2,1)S(1)}, u32[]{:S(2)}, u32[]{:S(2)}) collective-permute-start(bf16[272,512]{1,0:T(8,128)(2,1)} %get-tuple-element.60), channel_id=1, source_target_pairs={{0,6},{1,7},{2,0},{3,1},{4,2},{5,3},{6,4},{7,5},{8,14},{9,15},{10,... | collective-permute-start | bytes 835592 | tf_op jit(solution)/shard_map/ppermute | solution.py:41
  14.4 11.9 %collective-permute-start.4 = (bf16[288,512]{1,0:T(8,128)(2,1)S(1)}, bf16[288,512]{1,0:T(8,128)(2,1)S(1)}, u32[]{:S(2)}, u32[]{:S(2)}) collective-permute-start(bf16[288,512]{1,0:T(8,128)(2,1)S(1)} %collective-permute-done.1.refs_1_), channel_id=1, source_target_pairs={{0,6},{1,7},{2,0},{3,1},{4,2},{5,3},{6,4},{7,5},{8,14},{9,15},{10,... | collective-permute-start | bytes 884744 | tf_op jit(solution)/shard_map/ppermute | solution.py:41
  17.3 9.2 %collective-permute-start.3 = (bf16[304,512]{1,0:T(8,128)(2,1)S(1)}, bf16[304,512]{1,0:T(8,128)(2,1)S(1)}, u32[]{:S(2)}, u32[]{:S(2)}) collective-permute-start(bf16[304,512]{1,0:T(8,128)(2,1)S(1)} %collective-permute-done.refs_0_), channel_id=1, source_target_pairs={{0,2},{1,3},{2,4},{3,5},{4,6},{5,7},{6,0},{7,1},{8,10},{9,11},{10,... | collective-permute-start | bytes 933896 | tf_op jit(solution)/shard_map/ppermute | solution.py:41
  19.0 3.7 %collective-permute-start.6 = (bf16[288,512]{1,0:T(8,128)(2,1)S(1)}, bf16[288,512]{1,0:T(8,128)(2,1)S(1)}, u32[]{:S(2)}, u32[]{:S(2)}) collective-permute-start(bf16[288,512]{1,0:T(8,128)(2,1)S(1)} %collective-permute-done.1.refs_1_), channel_id=1, source_target_pairs={{0,1},{1,0},{2,3},{3,2},{4,5},{5,4},{6,7},{7,6},{8,9},{9,8},{10,11... | collective-permute-start | bytes 884744 | tf_op jit(solution)/shard_map/ppermute | solution.py:41
  20.4 2.5 %collective-permute-start.5 = (bf16[304,512]{1,0:T(8,128)(2,1)S(1)}, bf16[304,512]{1,0:T(8,128)(2,1)S(1)}, u32[]{:S(2)}, u32[]{:S(2)}) collective-permute-start(bf16[304,512]{1,0:T(8,128)(2,1)S(1)} %collective-permute-done.refs_0_), channel_id=1, source_target_pairs={{0,1},{1,0},{2,3},{3,2},{4,5},{5,4},{6,7},{7,6},{8,9},{9,8},{10,11... | collective-permute-start | bytes 933896 | tf_op jit(solution)/shard_map/ppermute | solution.py:41
  22.1 2.4 %collective-permute-start.9 = (bf16[272,512]{1,0:T(8,128)(2,1)S(1)}, bf16[272,512]{1,0:T(8,128)(2,1)S(1)}, u32[]{:S(2)}, u32[]{:S(2)}) collective-permute-start(bf16[272,512]{1,0:T(8,128)(2,1)S(1)} %collective-permute-done.7.refs_2_), channel_id=1, source_target_pairs={{0,1},{1,0},{2,3},{3,2},{4,5},{5,4},{6,7},{7,6},{8,9},{9,8},{10,11... | collective-permute-start | bytes 835592 | tf_op jit(solution)/shard_map/ppermute | solution.py:41
  22.7 1.8 %collective-permute-start.10 = (bf16[272,512]{1,0:T(8,128)(2,1)S(1)}, bf16[272,512]{1,0:T(8,128)(2,1)S(1)}, u32[]{:S(2)}, u32[]{:S(2)}) collective-permute-start(bf16[272,512]{1,0:T(8,128)(2,1)S(1)} %collective-permute-done.8.refs_3_), channel_id=1, source_target_pairs={{0,1},{1,0},{2,3},{3,2},{4,5},{5,4},{6,7},{7,6},{8,9},{9,8},{10,11... | collective-permute-start | bytes 835592 | tf_op jit(solution)/shard_map/ppermute | solution.py:41
  26.6 2.0 %collective-permute-start.11 = (bf16[304,512]{1,0:T(8,128)(2,1)S(1)}, bf16[304,512]{1,0:T(8,128)(2,1)S(1)}, u32[]{:S(2)}, u32[]{:S(2)}) collective-permute-start(bf16[304,512]{1,0:T(8,128)(2,1)S(1)} %collective-permute-done.3.refs_0_), channel_id=1, source_target_pairs={{0,1},{1,0},{2,3},{3,2},{4,5},{5,4},{6,7},{7,6},{8,9},{9,8},{10,11... | collective-permute-start | bytes 933896 | tf_op jit(solution)/shard_map/ppermute | solution.py:41
  26.8 1.8 %collective-permute-start.12 = (bf16[288,512]{1,0:T(8,128)(2,1)S(1)}, bf16[288,512]{1,0:T(8,128)(2,1)S(1)}, u32[]{:S(2)}, u32[]{:S(2)}) collective-permute-start(bf16[288,512]{1,0:T(8,128)(2,1)S(1)} %collective-permute-done.4.refs_1_), channel_id=1, source_target_pairs={{0,1},{1,0},{2,3},{3,2},{4,5},{5,4},{6,7},{7,6},{8,9},{9,8},{10,11... | collective-permute-start | bytes 884744 | tf_op jit(solution)/shard_map/ppermute | solution.py:41
  29.7 6.0 %collective-permute-start.13 = (bf16[4,80,128]{2,1,0:T(8,128)(2,1)S(1)}, bf16[4,80,128]{2,1,0:T(8,128)(2,1)S(1)}, u32[]{:S(2)}, u32[]{:S(2)}) collective-permute-start(bf16[4,80,128]{2,1,0:T(8,128)(2,1)S(1)} %get-tuple-element.81), channel_id=1, source_target_pairs={{0,8},{1,9},{2,10},{3,11},{4,12},{5,13},{6,14},{7,15},{8,16},{9,17... | collective-permute-start | bytes 245768 | tf_op jit(solution)/shard_map/ppermute | solution.py:41
  31.3 4.4 %collective-permute-start.14 = (bf16[4,80,128]{2,1,0:T(8,128)(2,1)S(1)}, bf16[4,80,128]{2,1,0:T(8,128)(2,1)S(1)}, u32[]{:S(2)}, u32[]{:S(2)}) collective-permute-start(bf16[4,80,128]{2,1,0:T(8,128)(2,1)S(1)} %get-tuple-element.82), channel_id=1, source_target_pairs={{0,24},{1,25},{2,26},{3,27},{4,28},{5,29},{6,30},{7,31},{8,0},{9,1... | collective-permute-start | bytes 245768 | tf_op jit(solution)/shard_map/ppermute | solution.py:41
  35.8 7.0 %collective-permute-start.15 = (bf16[8,80,128]{2,1,0:T(8,128)(2,1)S(1)}, bf16[8,80,128]{2,1,0:T(8,128)(2,1)S(1)}, u32[]{:S(2)}, u32[]{:S(2)}) collective-permute-start(bf16[8,80,128]{2,1,0:T(8,128)(2,1)S(1)} %get-tuple-element.83), channel_id=1, source_target_pairs={{0,8},{1,9},{2,10},{3,11},{4,12},{5,13},{6,14},{7,15},{8,16},{9,17... | collective-permute-start | bytes 491528 | tf_op jit(solution)/shard_map/ppermute | solution.py:41
  37.7 5.3 %collective-permute-start.16 = (bf16[8,80,128]{2,1,0:T(8,128)(2,1)S(1)}, bf16[8,80,128]{2,1,0:T(8,128)(2,1)S(1)}, u32[]{:S(2)}, u32[]{:S(2)}) collective-permute-start(bf16[8,80,128]{2,1,0:T(8,128)(2,1)S(1)} %get-tuple-element.84), channel_id=1, source_target_pairs={{0,24},{1,25},{2,26},{3,27},{4,28},{5,29},{6,30},{7,31},{8,0},{9,1... | collective-permute-start | bytes 491528 | tf_op jit(solution)/shard_map/ppermute | solution.py:41
  61.7 2.6 %collective-permute-start.18 = (bf16[128,128]{1,0:T(8,128)(2,1)S(1)}, bf16[128,128]{1,0:T(8,128)(2,1)S(1)}, u32[]{:S(2)}, u32[]{:S(2)}) collective-permute-start(bf16[128,128]{1,0:T(8,128)(2,1)S(1)} %shard_map.68.own), channel_id=1, source_target_pairs={{0,31},{1,0},{2,1},{3,2},{4,3},{5,4},{6,5},{7,6},{8,7},{9,8},{10,9... | collective-permute-start | bytes 98312 | tf_op jit(solution)/shard_map/ppermute | solution.py:449
  62.7 6.7 %collective-permute-start.17 = (bf16[128,128]{1,0:T(8,128)(2,1)S(1)}, bf16[128,128]{1,0:T(8,128)(2,1)S(1)}, u32[]{:S(2)}, u32[]{:S(2)}) collective-permute-start(bf16[128,128]{1,0:T(8,128)(2,1)S(1)} %shard_map.68.own), channel_id=1, source_target_pairs={{0,1},{1,2},{2,3},{3,4},{4,5},{5,6},{6,7},{7,8},{8,9},{9,10},{10,1... | collective-permute-start | bytes 98312 | tf_op jit(solution)/shard_map/ppermute | solution.py:448

commit v6 on v5

--- a/solution.py
+++ b/solution.py
@@ -125,7 +125,9 @@
     first = parts[0][0]
     live = picks >= 0 if len(parts) == 2 else lax.shift_right_arithmetic(high, 1) == first
     low = jnp.where(live, jnp.bitwise_and(picks, LOW - 1), -1)
-    one_hot = (lax.broadcasted_iota(jnp.int32, (LOW, 256), 0) == low).astype(BF16)
+    place = lax.broadcasted_iota(jnp.int32, (LOW, 256), 0).astype(jnp.int16)
+    low = jnp.broadcast_to(low, (LOW, 256)).astype(jnp.int16)
+    one_hot = jnp.where(place == low, jnp.ones((), BF16), jnp.zeros((), BF16))
     blocks, innovs = [], []
     for _, rows in parts:
         found = jnp.dot(rows, one_hot, preferred_element_type=F32)
@@ -188,12 +190,12 @@
     return off + off.T + diagonal, packed[65:66]
 
 
-def last_kernel(shifts, lowest, low, high, same, *rest):
+def last_kernel(shifts, low, high, same, *rest):
     found, outs, picks = rest[:6], rest[6:-1], rest[-1]
     place = lax.div(lax.axis_index("grid"), X * CORES)
     picks[...] = read_picks(low[16:32, :], 1)
     table = ((0, low[32:, :]), (1, high[16:, :]))
-    for shift in sorted(set(shifts)):
+    for out, shift in zip(outs, shifts):
         y = lax.rem(place + shift, Y)
         for i in range(2):
             span = slice(i * 256, i * 256 + 256)
@@ -208,52 +210,31 @@
                 for side in range(2):
                     rows = jnp.concatenate([pair[side] for pair in pairs], axis=1)
                     total = lax.dot_general(rows, rows[:K], dims(1, 1), preferred_element_type=F32)
-                    patch = i + 2 * half + 4 * side
-                    for out, its_shift, first in zip(outs, shifts, lowest):
-                        if its_shift == shift and first <= patch < first + out.shape[0]:
-                            out[patch - first] = pack(total).astype(out.dtype)
-
-
-def last_grams(shifts, lowest, counts, dtype, *args):
-    return pl.pallas_call(
-        functools.partial(last_kernel, shifts, lowest),
-        out_shape=[jax.ShapeDtypeStruct((count, PACK, K), dtype) for count in counts],
+                    out[i + 2 * half + 4 * side] = pack(total).astype(out.dtype)
+
+
+def last_grams(shifts, dtype, *args):
+    return pl.pallas_call(
+        functools.partial(last_kernel, shifts),
+        out_shape=[jax.ShapeDtypeStruct((8, PACK, K), dtype)] * len(shifts),
         in_specs=in_vmem(len(args)),
-        out_specs=in_vmem(len(counts)),
+        out_specs=in_vmem(len(shifts)),
         scratch_shapes=[pltpu.VMEM((Y, LOW), jnp.int32)],
         compiler_params=params(),
-        cost_estimate=cost(1e9 * len(set(shifts))),
+        cost_estimate=cost(1e9 * len(shifts)),
     )(*args)
 
 
-def relay_kernel(up, down, from_up, from_down, out_up, out_down):
-    half = from_up.shape[0]
-    out_up[:half] = (up[:half] + from_up[...].astype(F32)).astype(BF16)
-    out_up[half:] = up[half:].astype(BF16)
-    out_down[:half] = down[:half].astype(BF16)
-    out_down[half:] = (down[half:] + from_down[...].astype(F32)).astype(BF16)
-
-
-def relay(*args):
-    return pl.pallas_call(
-        relay_kernel,
-        out_shape=[jax.ShapeDtypeStruct(args[0].shape, BF16)] * 2,
-        in_specs=in_vmem(4),
-        out_specs=in_vmem(2),
-        compiler_params=params(),
-        cost_estimate=cost(5e8),
-    )(*args)
-
-
-def sum_kernel(own, a, b, out):
-    out[...] = (own[...] + a[...].astype(F32) + b[...].astype(F32)).astype(BF16)
+def sum_kernel(own, a, b, c, out):
+    others = a[...].astype(F32) + b[...].astype(F32) + c[...].astype(F32)
+    out[...] = (own[...] + others).astype(BF16)
 
 
 def sum_parts(*args):
     return pl.pallas_call(
         sum_kernel,
         out_shape=jax.ShapeDtypeStruct(args[0].shape, BF16),
-        in_specs=in_vmem(3),
+        in_specs=in_vmem(4),
         out_specs=in_vmem(1)[0],
         compiler_params=params(),
         cost_estimate=cost(5e8),
@@ -435,13 +416,12 @@
     far = pick_rows(((((0, 0, 32), (1, 1, 16)), (0, 16, 0), None),), SHORT, far_low, far_high)[0]
     last = (far_low_other, far_high_other, far, *found, same[0], cross[0], same[1], cross[1])
 
-    up, down = last_grams((2, 2), (0, 4), (4, 4), BF16, *last)
+    across = last_grams((2,), BF16, *last)[0]
+    from_across = hop(across, 2, 0, 0)
+    up, down = last_grams((1, 3), BF16, *last)
     from_up, from_down = hop(up, 1, 0, 0), hop(down, -1, 0, 0)
-    up, down = last_grams((1, 3), (0, 0), (8, 8), F32, *last)
-    up, down = relay(up, down, from_up, from_down)
-    from_up, from_down = hop(up, 1, 0, 0), hop(down, -1, 0, 0)
-    own = last_grams((0,), (0,), (8,), F32, *last)[0]
-    parts = sum_parts(own, from_up, from_down)
+    own = last_grams((0,), F32, *last)[0]
+    parts = sum_parts(own, from_across, from_up, from_down)
     parts = lax.all_to_all(parts, "obs", 0, 0, tiled=True)
 
     own = transposed_weights(parts)

time: 71.5 us -> 71.1 us (level)
  Pallas kernels: 22.6 us -> 21.1 us
    pallas_call x6, Pallas kernels: 10.8 us -> 9.24 us  [pick_rows(): pl.pallas_call(functools.partial(pick_kernel, sources, len(args)), out_sh...]
    ppermute x17 -> x16, waiting for transfers between devices: 7.2 us -> 7.87 us  [hop(): return lax.ppermute(value, 'grid', pairs)]
    ppermute x17 -> x16, starting transfers between devices: 17.7 us -> 17.7 us  [hop(): return lax.ppermute(value, 'grid', pairs)]
    pallas_call x4 -> x3, Pallas kernels: 3.97 us -> 3.93 us  [last_grams(): pl.pallas_call(functools.partial(last_kernel, shifts), out_shape=[jax.Sha...]
  transfers between devices with their start and end apart: 19 -> 18, of which waited for: 10 -> 8; matrix products, arithmetic and copies ran while one was open for 0% -> 0% of each run, Pallas kernels for 21% -> 19%
where the time goes in v6:
time: 71.1 us; the launch traced here: 71 us
  Pallas kernels  21.1 us (30%)
  starting transfers between devices  19.2 us (27%)
  blocking collectives  16.3 us (23%)
  waiting for transfers between devices  14 us (20%)
    ppermute x16, starting transfers between devices, hop(): return lax.ppermute(value, 'grid', pairs)  17.7 us
    all_to_all x1, blocking collectives, on_device(): parts = lax.all_to_all(parts, 'obs', 0, 0, tiled=True)  16.3 us
    pallas_call x6, Pallas kernels, pick_rows(): pl.pallas_call(functools.partial(pick_kernel, sources, len(args)), out_sh...  9.24 us
    ppermute x16, waiting for transfers between devices, hop(): return lax.ppermute(value, 'grid', pairs)  7.87 us
    ppermute x1, waiting for transfers between devices, on_device(): lax.ppermute(own, 'grid', [(j, (j + 1) % n_grid) for j in range(n_grid)])  5.06 us
    pallas_call x3, Pallas kernels, last_grams(): pl.pallas_call(functools.partial(last_kernel, shifts), out_shape=[jax.Sha...  3.93 us
    pallas_call x1, Pallas kernels, make_messages(): pl.pallas_call(message_kernel, out_shape=[jax.ShapeDtypeStruct((count, LO...  2.63 us
    pallas_call x1, Pallas kernels, transposed_weights(): pl.pallas_call(weights_kernel, out_shape=jax.ShapeDtypeStruct((K, K), BF1...  2.34 us
  transfers between devices with their start and end apart: 18, of which 8 were waited for; matrix products, arithmetic and copies ran while one was open for 0% of the time, Pallas kernels for 19%

profile of v6, /device:TPU:32, one launch (start us, length us, event | category | flops | bytes accessed | tf_op | source)
XLA Modules:
  0.0 71.0 jit_solution(17015244232076660786)
XLA Ops:
  0.0 2.6 %shard_map.55 = (bf16[560,512]{1,0:T(8,128)(2,1)}, bf16[304,512]{1,0:T(8,128)(2,1)}, bf16[272,512]{1,0:T(8,128)(2,1)}, bf16[288,512]{1,0:T(8,128)(2,1)}, bf16[272,512]{1,0:T(8,128)(2,1)}) custom-call(bf16[2048,128]{1,0:T(8,128)(2,1)} %refs_0_.1, f32[2048]{0:T(1024)} %refs_1_.1, f32[2048]{0:T(1024)} %refs_2_.1, s32[64,256]{1,0:T(8,128)} %bitcast.3), custom_call_target="tpu_custom_call" | custom-call | flops 2000000000 | bytes 100000 | tf_op jit(solution)/shard_map/pallas_call | solution.py:106
  2.6 0.1 collective-permute-start.2
  2.7 1.6 %collective-permute-start = (bf16[304,512]{1,0:T(8,128)(2,1)}, bf16[304,512]{1,0:T(8,128)(2,1)S(1)}, u32[]{:S(2)}, u32[]{:S(2)}) collective-permute-start(bf16[304,512]{1,0:T(8,128)(2,1)} %get-tuple-element.42), channel_id=1, source_target_pairs={{0,2},{1,3},{2,4},{3,5},{4,6},{5,7},{6,0},{7,1},{8,10},{9,11},{10,... | collective-permute-start | bytes 933896 | tf_op jit(solution)/shard_map/ppermute | solution.py:41
  4.3 1.7 %collective-permute-start.1 = (bf16[288,512]{1,0:T(8,128)(2,1)}, bf16[288,512]{1,0:T(8,128)(2,1)S(1)}, u32[]{:S(2)}, u32[]{:S(2)}) collective-permute-start(bf16[288,512]{1,0:T(8,128)(2,1)} %get-tuple-element.43), channel_id=1, source_target_pairs={{0,6},{1,7},{2,0},{3,1},{4,2},{5,3},{6,4},{7,5},{8,14},{9,15},{10,... | collective-permute-start | bytes 884744 | tf_op jit(solution)/shard_map/ppermute | solution.py:41
  6.1 0.3 collective-permute-start.7
  6.3 3.0 %collective-permute-start.8 = (bf16[272,512]{1,0:T(8,128)(2,1)}, bf16[272,512]{1,0:T(8,128)(2,1)S(1)}, u32[]{:S(2)}, u32[]{:S(2)}) collective-permute-start(bf16[272,512]{1,0:T(8,128)(2,1)} %get-tuple-element.56), channel_id=1, source_target_pairs={{0,6},{1,7},{2,0},{3,1},{4,2},{5,3},{6,4},{7,5},{8,14},{9,15},{10,... | collective-permute-start | bytes 835592 | tf_op jit(solution)/shard_map/ppermute | solution.py:41
  9.3 0.6 shard_map.57
  9.8 0.0 collective-permute-done.2.refs_1_
  9.9 2.5 %shard_map.56 = (bf16[8,144,256]{2,1,0:T(8,128)(2,1)S(1)}, bf16[8,144,256]{2,1,0:T(8,128)(2,1)S(1)}) custom-call(bf16[560,512]{1,0:T(8,128)(2,1)S(1)} %copy-done, bf16[560,512]{1,0:T(8,128)(2,1)S(1)} %collective-permute-done.2.refs_1_), custom_call_target="tpu_custom_call" | custom-call | flops 1000000 | bytes 100000 | tf_op jit(solution)/shard_map/pallas_call | solution.py:156
  12.4 2.0 %collective-permute-done.1.refs_1_ = bf16[288,512]{1,0:T(8,128)(2,1)S(1)} collective-permute-done((bf16[288,512]{1,0:T(8,128)(2,1)}, bf16[288,512]{1,0:T(8,128)(2,1)S(1)}, u32[]{:S(2)}, u32[]{:S(2)}) %collective-permute-start.1) | collective-permute-done | bytes 294944 | tf_op jit(solution)/shard_map/ppermute | solution.py:41
  14.4 0.0 collective-permute-done.refs_0_
  14.4 2.9 %collective-permute-start.4 = (bf16[288,512]{1,0:T(8,128)(2,1)S(1)}, bf16[288,512]{1,0:T(8,128)(2,1)S(1)}, u32[]{:S(2)}, u32[]{:S(2)}) collective-permute-start(bf16[288,512]{1,0:T(8,128)(2,1)S(1)} %collective-permute-done.1.refs_1_), channel_id=1, source_target_pairs={{0,6},{1,7},{2,0},{3,1},{4,2},{5,3},{6,4},{7,5},{8,14},{9,15},{10,... | collective-permute-start | bytes 884744 | tf_op jit(solution)/shard_map/ppermute | solution.py:41
  17.3 0.0 collective-permute-start.3
  17.3 1.3 %shard_map.58 = (bf16[8,144,256]{2,1,0:T(8,128)(2,1)S(1)}, bf16[8,144,256]{2,1,0:T(8,128)(2,1)S(1)}) custom-call(bf16[304,512]{1,0:T(8,128)(2,1)S(1)} %collective-permute-done.refs_0_, bf16[288,512]{1,0:T(8,128)(2,1)S(1)} %collective-permute-done.1.refs_1_), custom_call_target="tpu_custom_call" | custom-call | flops 60000002048 | bytes 100000 | tf_op jit(solution)/shard_map/pallas_call | solution.py:156
  18.7 0.1 collective-permute-start.6
  18.8 1.6 %collective-permute-done.7.refs_2_ = bf16[272,512]{1,0:T(8,128)(2,1)S(1)} collective-permute-done((bf16[272,512]{1,0:T(8,128)(2,1)}, bf16[272,512]{1,0:T(8,128)(2,1)S(1)}, u32[]{:S(2)}, u32[]{:S(2)}) %collective-permute-start.7) | collective-permute-done | bytes 278560 | tf_op jit(solution)/shard_map/ppermute | solution.py:41
  20.4 0.0 collective-permute-start.5
  20.4 0.0 collective-permute-done.8.refs_3_
  20.4 1.4 %shard_map.59 = (bf16[8,144,256]{2,1,0:T(8,128)(2,1)S(1)}, bf16[8,144,256]{2,1,0:T(8,128)(2,1)S(1)}) custom-call(bf16[304,512]{1,0:T(8,128)(2,1)S(1)} %collective-permute-done.refs_0_, bf16[288,512]{1,0:T(8,128)(2,1)S(1)} %collective-permute-done.1.refs_1_, bf16[272,512]{1,0:T(8,128)(2,1)S(1)} %collective-permute-done.7.refs_2_, ...), custom_call_target="tpu_custom_call" | custom-call | flops 60000002048 | bytes 100000 | tf_op jit(solution)/shard_map/pallas_call | solution.py:156
  21.7 0.6 collective-permute-start.9
  22.3 0.0 collective-permute-done.6.refs_1_
  22.3 0.3 collective-permute-start.10
  22.6 0.0 collective-permute-done.5.refs_0_
  22.6 1.3 %shard_map.60 = (bf16[8,144,256]{2,1,0:T(8,128)(2,1)S(1)}, bf16[8,144,256]{2,1,0:T(8,128)(2,1)S(1)}) custom-call(bf16[304,512]{1,0:T(8,128)(2,1)S(1)} %collective-permute-done.5.refs_0_, bf16[288,512]{1,0:T(8,128)(2,1)S(1)} %collective-permute-done.6.refs_1_), custom_call_target="tpu_custom_call" | custom-call | flops 1000000 | bytes 100000 | tf_op jit(solution)/shard_map/pallas_call | solution.py:156
  24.0 0.0 collective-permute-done.9.refs_2_
  24.0 0.0 collective-permute-done.10.refs_3_
  24.0 1.4 %shard_map.61 = (bf16[8,144,256]{2,1,0:T(8,128)(2,1)S(1)}, bf16[8,144,256]{2,1,0:T(8,128)(2,1)S(1)}) custom-call(bf16[304,512]{1,0:T(8,128)(2,1)S(1)} %collective-permute-done.5.refs_0_, bf16[288,512]{1,0:T(8,128)(2,1)S(1)} %collective-permute-done.6.refs_1_, bf16[272,512]{1,0:T(8,128)(2,1)S(1)} %collective-permute-done.9.refs_2_, ...), custom_call_target="tpu_custom_call" | custom-call | flops 1000000 | bytes 100000 | tf_op jit(solution)/shard_map/pallas_call | solution.py:156
  25.4 0.5 collective-permute-done.4.refs_1_
  25.9 0.7 collective-permute-done.3.refs_0_
  26.6 0.5 collective-permute-start.12
  27.1 1.3 %shard_map.62.same = bf16[8,144,256]{2,1,0:T(8,128)(2,1)S(1)} custom-call(bf16[304,512]{1,0:T(8,128)(2,1)S(1)} %collective-permute-done.3.refs_0_, bf16[288,512]{1,0:T(8,128)(2,1)S(1)} %collective-permute-done.4.refs_1_), custom_call_target="tpu_custom_call" | custom-call | flops 1000000 | bytes 100000 | tf_op jit(solution)/shard_map/pallas_call | solution.py:156
  28.4 0.2 collective-permute-done.12.high
  28.6 1.0 %shard_map.64 = bf16[8,80,128]{2,1,0:T(8,128)(2,1)S(1)} custom-call(bf16[304,512]{1,0:T(8,128)(2,1)S(1)} %collective-permute-done.11.low, bf16[288,512]{1,0:T(8,128)(2,1)S(1)} %collective-permute-done.12.high, bf16[8,144,256]{2,1,0:T(8,128)(2,1)S(1)} %shard_map.62.same, bf16[8,144,256]{2,1,0:T(8,128)(2,1)S(1)} %get-tuple-element.69.rest_0_, ...), custom_call_target="tpu_custom_call" | custom-call | flops 1000000000 | bytes 100000 | tf_op jit(solution)/shard_map/pallas_call | solution.py:217
  29.7 3.3 %collective-permute-start.13 = (bf16[8,80,128]{2,1,0:T(8,128)(2,1)S(1)}, bf16[8,80,128]{2,1,0:T(8,128)(2,1)S(1)}, u32[]{:S(2)}, u32[]{:S(2)}) collective-permute-start(bf16[8,80,128]{2,1,0:T(8,128)(2,1)S(1)} %shard_map.64), channel_id=1, source_target_pairs={{0,16},{1,17},{2,18},{3,19},{4,20},{5,21},{6,22},{7,23},{8,24},{9,... | collective-permute-start | bytes 491528 | tf_op jit(solution)/shard_map/ppermute | solution.py:41
  32.9 1.8 %shard_map.65 = (bf16[8,80,128]{2,1,0:T(8,128)(2,1)S(1)}, bf16[8,80,128]{2,1,0:T(8,128)(2,1)S(1)}) custom-call(bf16[304,512]{1,0:T(8,128)(2,1)S(1)} %collective-permute-done.11.low, bf16[288,512]{1,0:T(8,128)(2,1)S(1)} %collective-permute-done.12.high, bf16[8,144,256]{2,1,0:T(8,128)(2,1)S(1)} %shard_map.62.same, ...), custom_call_target="tpu_custom_call" | custom-call | flops 2000000000 | bytes 100000 | tf_op jit(solution)/shard_map/pallas_call | solution.py:217
  34.8 0.8 %collective-permute-start.14 = (bf16[8,80,128]{2,1,0:T(8,128)(2,1)S(1)}, bf16[8,80,128]{2,1,0:T(8,128)(2,1)S(1)}, u32[]{:S(2)}, u32[]{:S(2)}) collective-permute-start(bf16[8,80,128]{2,1,0:T(8,128)(2,1)S(1)} %get-tuple-element.75), channel_id=1, source_target_pairs={{0,8},{1,9},{2,10},{3,11},{4,12},{5,13},{6,14},{7,15},{8,16},{9,17... | collective-permute-start | bytes 491528 | tf_op jit(solution)/shard_map/ppermute | solution.py:41
  35.6 2.6 %collective-permute-start.15 = (bf16[8,80,128]{2,1,0:T(8,128)(2,1)S(1)}, bf16[8,80,128]{2,1,0:T(8,128)(2,1)S(1)}, u32[]{:S(2)}, u32[]{:S(2)}) collective-permute-start(bf16[8,80,128]{2,1,0:T(8,128)(2,1)S(1)} %get-tuple-element.76), channel_id=1, source_target_pairs={{0,24},{1,25},{2,26},{3,27},{4,28},{5,29},{6,30},{7,31},{8,0},{9,1... | collective-permute-start | bytes 491528 | tf_op jit(solution)/shard_map/ppermute | solution.py:41
  38.1 1.0 %shard_map.63.own = f32[8,80,128]{2,1,0:T(8,128)S(1)} custom-call(bf16[304,512]{1,0:T(8,128)(2,1)S(1)} %collective-permute-done.11.low, bf16[288,512]{1,0:T(8,128)(2,1)S(1)} %collective-permute-done.12.high, bf16[8,144,256]{2,1,0:T(8,128)(2,1)S(1)} %shard_map.62.same, bf16[8,144,256]{2,1,0:T(8,128)(2,1)S(1)} %get-tuple-element.69.rest_0_, ...), custom_call_target="tpu_custom_call" | custom-call | flops 1000000000 | bytes 100000 | tf_op jit(solution)/shard_map/pallas_call | solution.py:217
  39.2 2.9 %collective-permute-done.14.b = bf16[8,80,128]{2,1,0:T(8,128)(2,1)S(1)} collective-permute-done((bf16[8,80,128]{2,1,0:T(8,128)(2,1)S(1)}, bf16[8,80,128]{2,1,0:T(8,128)(2,1)S(1)}, u32[]{:S(2)}, u32[]{:S(2)}) %collective-permute-start.14) | collective-permute-done | bytes 163872 | tf_op jit(solution)/shard_map/ppermute | solution.py:41
  42.0 0.1 shard_map.66
  42.1 16.3 %all_to_all.5.parts = bf16[8,80,128]{2,1,0:T(8,128)(2,1)S(1)} all-to-all(bf16[8,80,128]{2,1,0:T(8,128)(2,1)S(1)} %shard_map.66), channel_id=1, replica_groups=mesh['obs'=8,'grid'=32] {'obs'}, dimensions={0} | all-to-all | bytes 327680 | tf_op jit(solution)/shard_map/all_to_all | solution.py:425
  58.5 2.3 %shard_map.67.own = bf16[128,128]{1,0:T(8,128)(2,1)S(1)} custom-call(bf16[8,80,128]{2,1,0:T(8,128)(2,1)S(1)} %all_to_all.5.parts), custom_call_target="tpu_custom_call" | custom-call | flops 4000000000 | bytes 100000 | tf_op jit(solution)/shard_map/pallas_call | solution.py:282
  60.8 1.6 %collective-permute-start.17 = (bf16[128,128]{1,0:T(8,128)(2,1)S(1)}, bf16[128,128]{1,0:T(8,128)(2,1)S(1)}, u32[]{:S(2)}, u32[]{:S(2)}) collective-permute-start(bf16[128,128]{1,0:T(8,128)(2,1)S(1)} %shard_map.67.own), channel_id=1, source_target_pairs={{0,31},{1,0},{2,1},{3,2},{4,3},{5,4},{6,5},{7,6},{8,7},{9,8},{10,9... | collective-permute-start | bytes 98312 | tf_op jit(solution)/shard_map/ppermute | solution.py:429
  62.4 0.0 collective-permute-start.16
  62.4 0.6 shard_map.68.part
  62.9 1.0 %collective-permute-done.17.right = bf16[128,128]{1,0:T(8,128)(2,1)S(1)} collective-permute-done((bf16[128,128]{1,0:T(8,128)(2,1)S(1)}, bf16[128,128]{1,0:T(8,128)(2,1)S(1)}, u32[]{:S(2)}, u32[]{:S(2)}) %collective-permute-start.17) | collective-permute-done | bytes 32800 | tf_op jit(solution)/shard_map/ppermute | solution.py:429
  64.0 5.1 %collective-permute-done.16.left = bf16[128,128]{1,0:T(8,128)(2,1)S(1)} collective-permute-done((bf16[128,128]{1,0:T(8,128)(2,1)S(1)}, bf16[128,128]{1,0:T(8,128)(2,1)S(1)}, u32[]{:S(2)}, u32[]{:S(2)}) %collective-permute-start.16) | collective-permute-done | bytes 32800 | tf_op jit(solution)/shard_map/ppermute | solution.py:428
  69.0 1.8 %shard_map.69 = bf16[48,128,128]{2,1,0:T(8,128)(2,1)} custom-call(bf16[128,128]{1,0:T(8,128)(2,1)S(1)} %collective-permute-done.16.left, bf16[128,128]{1,0:T(8,128)(2,1)S(1)} %collective-permute-done.17.right, f32[24,128,256]{2,1,0:T(8,128)S(1)} %shard_map.68.part, bf16[24,128,256]{2,1,0:T(8,128)(2,1)S(1)} %get-tuple-element.78.perturb), custom_call_target="tpu_custom_call" | custom-call | flops 2000000000 | bytes 100000 | tf_op jit(solution)/shard_map/pallas_call | solution.py:365
  (8 shorter events, 0.0 us)
Async XLA Ops:
  0.0 9.3 %copy-start.1 = (bf16[48,128,128]{2,1,0:T(8,128)(2,1)S(1)}, bf16[48,128,128]{2,1,0:T(8,128)(2,1)}, u32[]{:S(2)}) copy-start(bf16[48,128,128]{2,1,0:T(8,128)(2,1)} %state.1) | copy-start | bytes 4718596
  2.6 7.2 %collective-permute-start.2 = (bf16[560,512]{1,0:T(8,128)(2,1)}, bf16[560,512]{1,0:T(8,128)(2,1)S(1)}, u32[]{:S(2)}, u32[]{:S(2)}) collective-permute-start(bf16[560,512]{1,0:T(8,128)(2,1)} %get-tuple-element.44.refs_0_), channel_id=1, source_target_pairs={{0,1},{1,0},{2,3},{3,2},{4,5},{5,4},{6,7},{7,6},{8,9},{9,8},{10,11... | collective-permute-start | bytes 1720328 | tf_op jit(solution)/shard_map/ppermute | solution.py:41
  2.7 11.7 %collective-permute-start = (bf16[304,512]{1,0:T(8,128)(2,1)}, bf16[304,512]{1,0:T(8,128)(2,1)S(1)}, u32[]{:S(2)}, u32[]{:S(2)}) collective-permute-start(bf16[304,512]{1,0:T(8,128)(2,1)} %get-tuple-element.42), channel_id=1, source_target_pairs={{0,2},{1,3},{2,4},{3,5},{4,6},{5,7},{6,0},{7,1},{8,10},{9,11},{10,... | collective-permute-start | bytes 933896 | tf_op jit(solution)/shard_map/ppermute | solution.py:41
  4.3 10.1 %collective-permute-start.1 = (bf16[288,512]{1,0:T(8,128)(2,1)}, bf16[288,512]{1,0:T(8,128)(2,1)S(1)}, u32[]{:S(2)}, u32[]{:S(2)}) collective-permute-start(bf16[288,512]{1,0:T(8,128)(2,1)} %get-tuple-element.43), channel_id=1, source_target_pairs={{0,6},{1,7},{2,0},{3,1},{4,2},{5,3},{6,4},{7,5},{8,14},{9,15},{10,... | collective-permute-start | bytes 884744 | tf_op jit(solution)/shard_map/ppermute | solution.py:41
  6.1 14.3 %collective-permute-start.7 = (bf16[272,512]{1,0:T(8,128)(2,1)}, bf16[272,512]{1,0:T(8,128)(2,1)S(1)}, u32[]{:S(2)}, u32[]{:S(2)}) collective-permute-start(bf16[272,512]{1,0:T(8,128)(2,1)} %get-tuple-element.55), channel_id=1, source_target_pairs={{0,2},{1,3},{2,4},{3,5},{4,6},{5,7},{6,0},{7,1},{8,10},{9,11},{10,... | collective-permute-start | bytes 835592 | tf_op jit(solution)/shard_map/ppermute | solution.py:41
  6.3 3.5 %copy-start = (bf16[560,512]{1,0:T(8,128)(2,1)S(1)}, bf16[560,512]{1,0:T(8,128)(2,1)}, u32[]{:S(2)}) copy-start(bf16[560,512]{1,0:T(8,128)(2,1)} %get-tuple-element.44.refs_0_) | copy-start | bytes 1720324
  6.3 14.0 %collective-permute-start.8 = (bf16[272,512]{1,0:T(8,128)(2,1)}, bf16[272,512]{1,0:T(8,128)(2,1)S(1)}, u32[]{:S(2)}, u32[]{:S(2)}) collective-permute-start(bf16[272,512]{1,0:T(8,128)(2,1)} %get-tuple-element.56), channel_id=1, source_target_pairs={{0,6},{1,7},{2,0},{3,1},{4,2},{5,3},{6,4},{7,5},{8,14},{9,15},{10,... | collective-permute-start | bytes 835592 | tf_op jit(solution)/shard_map/ppermute | solution.py:41
  14.4 11.5 %collective-permute-start.4 = (bf16[288,512]{1,0:T(8,128)(2,1)S(1)}, bf16[288,512]{1,0:T(8,128)(2,1)S(1)}, u32[]{:S(2)}, u32[]{:S(2)}) collective-permute-start(bf16[288,512]{1,0:T(8,128)(2,1)S(1)} %collective-permute-done.1.refs_1_), channel_id=1, source_target_pairs={{0,6},{1,7},{2,0},{3,1},{4,2},{5,3},{6,4},{7,5},{8,14},{9,15},{10,... | collective-permute-start | bytes 884744 | tf_op jit(solution)/shard_map/ppermute | solution.py:41
  17.3 9.2 %collective-permute-start.3 = (bf16[304,512]{1,0:T(8,128)(2,1)S(1)}, bf16[304,512]{1,0:T(8,128)(2,1)S(1)}, u32[]{:S(2)}, u32[]{:S(2)}) collective-permute-start(bf16[304,512]{1,0:T(8,128)(2,1)S(1)} %collective-permute-done.refs_0_), channel_id=1, source_target_pairs={{0,2},{1,3},{2,4},{3,5},{4,6},{5,7},{6,0},{7,1},{8,10},{9,11},{10,... | collective-permute-start | bytes 933896 | tf_op jit(solution)/shard_map/ppermute | solution.py:41
  18.7 3.7 %collective-permute-start.6 = (bf16[288,512]{1,0:T(8,128)(2,1)S(1)}, bf16[288,512]{1,0:T(8,128)(2,1)S(1)}, u32[]{:S(2)}, u32[]{:S(2)}) collective-permute-start(bf16[288,512]{1,0:T(8,128)(2,1)S(1)} %collective-permute-done.1.refs_1_), channel_id=1, source_target_pairs={{0,1},{1,0},{2,3},{3,2},{4,5},{5,4},{6,7},{7,6},{8,9},{9,8},{10,11... | collective-permute-start | bytes 884744 | tf_op jit(solution)/shard_map/ppermute | solution.py:41
  20.4 2.3 %collective-permute-start.5 = (bf16[304,512]{1,0:T(8,128)(2,1)S(1)}, bf16[304,512]{1,0:T(8,128)(2,1)S(1)}, u32[]{:S(2)}, u32[]{:S(2)}) collective-permute-start(bf16[304,512]{1,0:T(8,128)(2,1)S(1)} %collective-permute-done.refs_0_), channel_id=1, source_target_pairs={{0,1},{1,0},{2,3},{3,2},{4,5},{5,4},{6,7},{7,6},{8,9},{9,8},{10,11... | collective-permute-start | bytes 933896 | tf_op jit(solution)/shard_map/ppermute | solution.py:41
  21.7 2.2 %collective-permute-start.9 = (bf16[272,512]{1,0:T(8,128)(2,1)S(1)}, bf16[272,512]{1,0:T(8,128)(2,1)S(1)}, u32[]{:S(2)}, u32[]{:S(2)}) collective-permute-start(bf16[272,512]{1,0:T(8,128)(2,1)S(1)} %collective-permute-done.7.refs_2_), channel_id=1, source_target_pairs={{0,1},{1,0},{2,3},{3,2},{4,5},{5,4},{6,7},{7,6},{8,9},{9,8},{10,11... | collective-permute-start | bytes 835592 | tf_op jit(solution)/shard_map/ppermute | solution.py:41
  22.3 1.6 %collective-permute-start.10 = (bf16[272,512]{1,0:T(8,128)(2,1)S(1)}, bf16[272,512]{1,0:T(8,128)(2,1)S(1)}, u32[]{:S(2)}, u32[]{:S(2)}) collective-permute-start(bf16[272,512]{1,0:T(8,128)(2,1)S(1)} %collective-permute-done.8.refs_3_), channel_id=1, source_target_pairs={{0,1},{1,0},{2,3},{3,2},{4,5},{5,4},{6,7},{7,6},{8,9},{9,8},{10,11... | collective-permute-start | bytes 835592 | tf_op jit(solution)/shard_map/ppermute | solution.py:41
  26.6 2.0 %collective-permute-start.11 = (bf16[304,512]{1,0:T(8,128)(2,1)S(1)}, bf16[304,512]{1,0:T(8,128)(2,1)S(1)}, u32[]{:S(2)}, u32[]{:S(2)}) collective-permute-start(bf16[304,512]{1,0:T(8,128)(2,1)S(1)} %collective-permute-done.3.refs_0_), channel_id=1, source_target_pairs={{0,1},{1,0},{2,3},{3,2},{4,5},{5,4},{6,7},{7,6},{8,9},{9,8},{10,11... | collective-permute-start | bytes 933896 | tf_op jit(solution)/shard_map/ppermute | solution.py:41
  26.6 2.0 %collective-permute-start.12 = (bf16[288,512]{1,0:T(8,128)(2,1)S(1)}, bf16[288,512]{1,0:T(8,128)(2,1)S(1)}, u32[]{:S(2)}, u32[]{:S(2)}) collective-permute-start(bf16[288,512]{1,0:T(8,128)(2,1)S(1)} %collective-permute-done.4.refs_1_), channel_id=1, source_target_pairs={{0,1},{1,0},{2,3},{3,2},{4,5},{5,4},{6,7},{7,6},{8,9},{9,8},{10,11... | collective-permute-start | bytes 884744 | tf_op jit(solution)/shard_map/ppermute | solution.py:41
  29.7 9.5 %collective-permute-start.13 = (bf16[8,80,128]{2,1,0:T(8,128)(2,1)S(1)}, bf16[8,80,128]{2,1,0:T(8,128)(2,1)S(1)}, u32[]{:S(2)}, u32[]{:S(2)}) collective-permute-start(bf16[8,80,128]{2,1,0:T(8,128)(2,1)S(1)} %shard_map.64), channel_id=1, source_target_pairs={{0,16},{1,17},{2,18},{3,19},{4,20},{5,21},{6,22},{7,23},{8,24},{9,... | collective-permute-start | bytes 491528 | tf_op jit(solution)/shard_map/ppermute | solution.py:41
  34.8 7.2 %collective-permute-start.14 = (bf16[8,80,128]{2,1,0:T(8,128)(2,1)S(1)}, bf16[8,80,128]{2,1,0:T(8,128)(2,1)S(1)}, u32[]{:S(2)}, u32[]{:S(2)}) collective-permute-start(bf16[8,80,128]{2,1,0:T(8,128)(2,1)S(1)} %get-tuple-element.75), channel_id=1, source_target_pairs={{0,8},{1,9},{2,10},{3,11},{4,12},{5,13},{6,14},{7,15},{8,16},{9,17... | collective-permute-start | bytes 491528 | tf_op jit(solution)/shard_map/ppermute | solution.py:41
  35.6 6.5 %collective-permute-start.15 = (bf16[8,80,128]{2,1,0:T(8,128)(2,1)S(1)}, bf16[8,80,128]{2,1,0:T(8,128)(2,1)S(1)}, u32[]{:S(2)}, u32[]{:S(2)}) collective-permute-start(bf16[8,80,128]{2,1,0:T(8,128)(2,1)S(1)} %get-tuple-element.76), channel_id=1, source_target_pairs={{0,24},{1,25},{2,26},{3,27},{4,28},{5,29},{6,30},{7,31},{8,0},{9,1... | collective-permute-start | bytes 491528 | tf_op jit(solution)/shard_map/ppermute | solution.py:41
  60.8 3.2 %collective-permute-start.17 = (bf16[128,128]{1,0:T(8,128)(2,1)S(1)}, bf16[128,128]{1,0:T(8,128)(2,1)S(1)}, u32[]{:S(2)}, u32[]{:S(2)}) collective-permute-start(bf16[128,128]{1,0:T(8,128)(2,1)S(1)} %shard_map.67.own), channel_id=1, source_target_pairs={{0,31},{1,0},{2,1},{3,2},{4,3},{5,4},{6,5},{7,6},{8,7},{9,8},{10,9... | collective-permute-start | bytes 98312 | tf_op jit(solution)/shard_map/ppermute | solution.py:429
  62.4 6.7 %collective-permute-start.16 = (bf16[128,128]{1,0:T(8,128)(2,1)S(1)}, bf16[128,128]{1,0:T(8,128)(2,1)S(1)}, u32[]{:S(2)}, u32[]{:S(2)}) collective-permute-start(bf16[128,128]{1,0:T(8,128)(2,1)S(1)} %shard_map.67.own), channel_id=1, source_target_pairs={{0,1},{1,2},{2,3},{3,4},{4,5},{5,6},{6,7},{7,8},{8,9},{9,10},{10,1... | collective-permute-start | bytes 98312 | tf_op jit(solution)/shard_map/ppermute | solution.py:428

commit v7 on v6

--- a/solution.py
+++ b/solution.py
@@ -22,7 +22,7 @@
     return pltpu.CompilerParams(vmem_limit_bytes=VMEM)
 
 
-LONG, MID, SHORT = 6e10, 6e10, 1e6
+LONG, SHORT = 6e10, 1e6
 
 
 def cost(flops):
@@ -45,79 +45,101 @@
     return (((m,), (n,)), ((), ()))
 
 
-def message_kernel(*refs):
-    sources, (near, right_first, right_second, left_first, left_second) = refs[:4], refs[4:9]
-    held, (turned, sems) = refs[9:13], refs[13:]
-    copies = [
-        pltpu.make_async_copy(source, place, sems.at[i])
-        for i, (source, place) in enumerate(zip(sources, held))
-    ]
-    for copy in copies[::-1]:
+def send_picks(turned, cx, swapped):
+    lines = []
+    for y in range(Y):
+        rows = turned[pl.ds(y * X * CORES + cx, 8, stride=Y * X * CORES), :]
+        pair = [rows[0:4], rows[4:8]]
+        pairs = jnp.concatenate(pair[::-1] if swapped else pair, axis=1)
+        fours = jnp.concatenate([pairs[0:2], pairs[2:4]], axis=1)
+        lines.append(jnp.concatenate([fours[0:1], fours[1:2]], axis=1))
+    picks = jnp.concatenate(lines, axis=0)
+    power = jnp.maximum(lax.shift_right_arithmetic(picks, 7), 0)
+    code = lax.shift_left(128 + jnp.bitwise_and(picks, 127), power)
+    return jnp.where(picks >= 0, code, 0).astype(F32)
+
+
+def read_picks(rows):
+    left = rows.astype(F32)
+    high = jnp.zeros_like(left)
+    for step in (8, 4, 2, 1):
+        large = left >= 128.0 * 2**step
+        left = jnp.where(large, left * 0.5**step, left)
+        high = jnp.where(large, high + step, high)
+    return jnp.where(left > 0.0, left - 128.0 + 128.0 * high, -1.0).astype(jnp.int32)
+
+
+def message_kernel(departures, innovation, obs_weight, send_rows, *refs):
+    outs, (rows, innov, weight, picks, turned) = refs[:3], refs[3:8]
+    built, (in_sems, out_sems) = refs[8:11], refs[11:]
+    small = ((send_rows, picks), (obs_weight, weight), (innovation, innov))
+    small = [pltpu.make_async_copy(*pair, in_sems.at[i]) for i, pair in enumerate(small)]
+    large = []
+    for block in range(BLOCKS):
+        span = pl.ds(block * LOW, LOW)
+        large.append(
+            pltpu.make_async_copy(departures.at[span], rows.at[span], in_sems.at[3 + block])
+        )
+    for copy in small + large:
         copy.start()
-    departures, innovation, obs_weight, send_rows = held
-    copies[3].wait()
+    small[0].wait()
     grid = lax.axis_index("grid")
     x, c = lax.rem(lax.div(grid, CORES), X), lax.rem(grid, CORES)
-    turned[...] = send_rows[...].T
+    turned[...] = picks[...].T
     groups = []
     for dx in range(X):
-        halves = []
         for dc in range(CORES):
             cx = lax.rem(x + dx, X) * CORES + lax.rem(c + dc, CORES)
-            lines = []
-            for y in range(Y):
-                rows = turned[pl.ds(y * X * CORES + cx, 8, stride=Y * X * CORES), :]
-                pair = [rows[0:4], rows[4:8]]
-                pairs = jnp.concatenate(pair[::-1] if dc else pair, axis=1)
-                fours = jnp.concatenate([pairs[0:2], pairs[2:4]], axis=1)
-                lines.append(jnp.concatenate([fours[0:1], fours[1:2]], axis=1))
-            picks = jnp.concatenate(lines, axis=0)
-            halves.append(lax.shift_right_arithmetic(picks, 8))
-            halves.append(jnp.bitwise_and(picks, 255))
-        groups.append(jnp.concatenate(halves, axis=0).astype(F32).astype(BF16))
-    near[2 * HALF :, :] = groups[0]
-    right_first[:16, :] = groups[1]
-    right_first[16:32, :] = groups[2]
-    left_first[:16, :] = groups[3]
-    for copy in copies[:3]:
-        copy.wait()
-    root = jnp.sqrt(obs_weight[...].reshape(1, BLOCKS * LOW))
-    innov = innovation[...].reshape(1, BLOCKS * LOW) * root
-    row = lax.broadcasted_iota(jnp.int32, (16, LOW), 0)
-    places = (
-        ((near, 0), (right_first, 32), (left_second, 0)),
-        ((near, HALF), (left_first, 16), (right_second, 0)),
-    )
+            groups.append(send_picks(turned, cx, dc == 1))
+    small[1].wait()
+    small[2].wait()
+    root = jnp.sqrt(weight[...].reshape(1, BLOCKS * LOW))
+    scaled = innov[...].reshape(1, BLOCKS * LOW) * root
+    blank = jnp.zeros((2, LOW), F32)
+    both, out_both = built[2], outs[2]
+    copies = []
     for half in range(2):
-        tail = jnp.zeros((16, LOW), F32)
+        one, out_one = built[half], outs[half]
+        at = half * HALF
+        innovs = []
         for block in range(2):
             start = (2 * half + block) * LOW
             span = slice(start, start + LOW)
-            rows = (departures[span, :].astype(F32).T * root[:, span]).astype(BF16)
-            for ref, at in places[half]:
-                ref[at + block * K : at + (block + 1) * K, :] = rows
-            tail = jnp.where(row == block, innov[:, span], tail)
-        for ref, at in places[half]:
-            ref[at + 2 * K : at + HALF, :] = tail.astype(BF16)
+            large[2 * half + block].wait()
+            part = (rows[span, :].astype(F32).T * root[:, span]).astype(BF16)
+            one[block * K : (block + 1) * K, :] = part
+            both[at + block * K : at + (block + 1) * K, :] = part
+            innovs.append(scaled[:, span])
+        top = innovs + [blank, groups[4 + half]]
+        next_one = groups[2:4] if half == 0 else groups[6:8]
+        one[2 * K :, :] = jnp.concatenate(top + next_one, axis=0).astype(BF16)
+        both[at + 2 * K : at + HALF, :] = jnp.concatenate(top + groups[0:2], axis=0).astype(BF16)
+        copies.append(pltpu.make_async_copy(one, out_one, out_sems.at[half]))
+        span = pl.ds(at, HALF)
+        copies.append(
+            pltpu.make_async_copy(both.at[span], out_both.at[span], out_sems.at[2 + half])
+        )
+        for copy in copies[-2:]:
+            copy.start()
+    for copy in copies:
+        copy.wait()
 
 
 def make_messages(*args):
-    rows = (2 * HALF + 16, HALF + 32, HALF, HALF + 16, HALF)
+    shapes = [(HALF, LOW), (HALF, LOW), (2 * HALF, LOW)]
+    hbm = pl.BlockSpec(memory_space=pltpu.HBM)
     return pl.pallas_call(
         message_kernel,
-        out_shape=[jax.ShapeDtypeStruct((count, LOW), BF16) for count in rows],
-        in_specs=[pl.BlockSpec(memory_space=pltpu.HBM)] * 4,
-        out_specs=in_vmem(len(rows)),
+        out_shape=[jax.ShapeDtypeStruct(shape, BF16) for shape in shapes],
+        in_specs=[hbm] * 4,
+        out_specs=[hbm] * 3,
         scratch_shapes=[pltpu.VMEM(arg.shape, arg.dtype) for arg in args]
-        + [pltpu.VMEM(args[3].shape[::-1], jnp.int32), pltpu.SemaphoreType.DMA((4,))],
+        + [pltpu.VMEM(args[3].shape[::-1], jnp.int32)]
+        + [pltpu.VMEM(shape, BF16) for shape in shapes]
+        + [pltpu.SemaphoreType.DMA((3 + BLOCKS,)), pltpu.SemaphoreType.DMA((4,))],
         compiler_params=pltpu.CompilerParams(vmem_limit_bytes=60 * 1024 * 1024),
         cost_estimate=cost(2e9),
     )(*args)
-
-
-def read_picks(group, core):
-    values = group[8 * core : 8 * core + 8].astype(F32)
-    return (values[0:4] * 256.0 + values[4:8]).astype(jnp.int32)
 
 
 def pick(parts, picks):
@@ -141,9 +163,13 @@
     return jnp.concatenate([members, jnp.broadcast_to(innov, (16, 256))], axis=0).astype(BF16)
 
 
+def tail_picks(ref, at, row):
+    return read_picks(ref[at + 2 * K : at + HALF, :].astype(F32)[row : row + 4])
+
+
 def pick_kernel(sources, count, *refs):
     outs = refs[count:]
-    picks = [read_picks(refs[which][at : at + 16, :], core) for _, (which, at, core), _ in sources]
+    picks = [tail_picks(refs[which], at, row) for _, (which, at, row), _ in sources]
     for step in range(2 * Y):
         y, span = step // 2, slice(step % 2 * 256, step % 2 * 256 + 256)
         for out, (parts, _, before), values in zip(outs, sources, picks):
@@ -193,8 +219,8 @@
 def last_kernel(shifts, low, high, same, *rest):
     found, outs, picks = rest[:6], rest[6:-1], rest[-1]
     place = lax.div(lax.axis_index("grid"), X * CORES)
-    picks[...] = read_picks(low[16:32, :], 1)
-    table = ((0, low[32:, :]), (1, high[16:, :]))
+    picks[...] = tail_picks(high, 0, 4)
+    table = ((0, low[...]), (1, high[...]))
     for out, shift in zip(outs, shifts):
         y = lax.rem(place + shift, Y)
         for i in range(2):
@@ -310,7 +336,7 @@
         in_specs=in_vmem(1),
         out_specs=in_vmem(2),
         compiler_params=params(),
-        cost_estimate=cost(2e9),
+        cost_estimate=cost(SHORT),
     )(state)
 
 
@@ -375,19 +401,18 @@
 
 def on_device(departures, innovation, obs_weight, send_rows, send_counts, state):
     n_grid = lax.axis_size("grid")
-    near, right_first, right_second, left_first, left_second = make_messages(
+    low_half, high_half, near = make_messages(
         departures, innovation, obs_weight, send_rows[0].T
     )
-    left = hop(right_first, 0, 1, 0)
-    right = hop(left_first, 0, -1, 0)
+    left = hop(low_half, 0, 1, 0)
+    right = hop(high_half, 0, -1, 0)
     other = hop(near, 0, 0, 1)
-    left_more = hop(right_second, 0, 1, 0)
-    right_more = hop(left_second, 0, -1, 0)
+    left_more = hop(high_half, 0, 1, 0)
+    right_more = hop(low_half, 0, -1, 0)
 
     whole = lambda which: ((0, which, 0), (1, which, HALF))
-    at_end = 2 * HALF
     found = pick_rows(
-        ((whole(0), (0, at_end, 0), None), (whole(1), (1, at_end, 1), None)), SHORT, near, other
+        ((whole(0), (0, 0, 8), None), (whole(1), (1, 0, 12), None)), SHORT, near, other
     )
     mean, perturb = perturbations(state)
     left, right, found, mean, perturb = lax.optimization_barrier(
@@ -396,24 +421,26 @@
     far_low, far_high = hop(left, 0, 1, 0), hop(right, 0, -1, 0)
 
     def firsts(core):
-        return (((0, 0, 32),), (0, 0, core), None), (((1, 1, 16),), (1, 0, core), None)
+        row = 8 + 4 * core
+        return (((0, 0, 0),), (0, 0, row), None), (((1, 1, 0),), (1, 0, row), None)
 
     def seconds(core):
-        return (((1, 2, 0),), (0, 0, core), 4), (((0, 3, 0),), (1, 0, core), 5)
-
-    same = pick_rows(firsts(0), LONG, left, right)
+        row = 8 + 4 * core
+        return (((1, 2, 0),), (0, 0, row), 4), (((0, 3, 0),), (1, 0, row), 5)
+
+    same = pick_rows(firsts(0), SHORT, left, right)
     left, right, same = lax.optimization_barrier((left, right, same))
     left_other, right_other = hop(left, 0, 0, 1), hop(right, 0, 0, 1)
-    same = pick_rows(seconds(0), MID, left, right, left_more, right_more, *same)
+    same = pick_rows(seconds(0), LONG, left, right, left_more, right_more, *same)
     left_more, right_more, same = lax.optimization_barrier((left_more, right_more, same))
     left_more_other, right_more_other = hop(left_more, 0, 0, 1), hop(right_more, 0, 0, 1)
-    cross = pick_rows(firsts(1), SHORT, left_other, right_other)
+    cross = pick_rows(firsts(1), LONG, left_other, right_other)
     cross = pick_rows(
         seconds(1), SHORT, left_other, right_other, left_more_other, right_more_other, *cross
     )
     far_low, far_high, cross = lax.optimization_barrier((far_low, far_high, cross))
     far_low_other, far_high_other = hop(far_low, 0, 0, 1), hop(far_high, 0, 0, 1)
-    far = pick_rows(((((0, 0, 32), (1, 1, 16)), (0, 16, 0), None),), SHORT, far_low, far_high)[0]
+    far = pick_rows(((((0, 0, 0), (1, 1, 0)), (0, 0, 4), None),), SHORT, far_low, far_high)[0]
     last = (far_low_other, far_high_other, far, *found, same[0], cross[0], same[1], cross[1])
 
     across = last_grams((2,), BF16, *last)[0]

time: 71.1 us -> 70.8 us (level)
    ppermute x1, starting transfers between devices: 1.56 us -> 2.52 us  [on_device(): lax.ppermute(own, 'grid', [(j, (j - 1) % n_grid) for j in range(n_grid)])]
    ppermute x16, starting transfers between devices: 17.7 us -> 16.8 us  [hop(): return lax.ppermute(value, 'grid', pairs)]
  transfers between devices with their start and end apart: 18 -> 18, of which waited for: 8 -> 9; matrix products, arithmetic and copies ran while one was open for 0% -> 0% of each run, Pallas kernels for 19% -> 19%
where the time goes in v7:
time: 70.8 us; the launch traced here: 70.7 us
  Pallas kernels  21.1 us (30%)
  starting transfers between devices  19.3 us (27%)
  blocking collectives  16.3 us (23%)
  waiting for transfers between devices  13.5 us (19%)
    ppermute x16, starting transfers between devices, hop(): return lax.ppermute(value, 'grid', pairs)  16.8 us
    all_to_all x1, blocking collectives, on_device(): parts = lax.all_to_all(parts, 'obs', 0, 0, tiled=True)  16.3 us
    pallas_call x6, Pallas kernels, pick_rows(): pl.pallas_call(functools.partial(pick_kernel, sources, len(args)), out_sh...  9.33 us
    ppermute x16, waiting for transfers between devices, hop(): return lax.ppermute(value, 'grid', pairs)  7.45 us
    ppermute x1, waiting for transfers between devices, on_device(): lax.ppermute(own, 'grid', [(j, (j + 1) % n_grid) for j in range(n_grid)])  5.06 us
    pallas_call x3, Pallas kernels, last_grams(): pl.pallas_call(functools.partial(last_kernel, shifts), out_shape=[jax.Sha...  3.96 us
    pallas_call x1, Pallas kernels, make_messages(): pl.pallas_call(message_kernel, out_shape=[jax.ShapeDtypeStruct(shape, BF1...  2.58 us
    ppermute x1, starting transfers between devices, on_device(): lax.ppermute(own, 'grid', [(j, (j - 1) % n_grid) for j in range(n_grid)])  2.52 us
  transfers between devices with their start and end apart: 18, of which 9 were waited for; matrix products, arithmetic and copies ran while one was open for 0% of the time, Pallas kernels for 19%

profile of v7, /device:TPU:32, one launch (start us, length us, event | category | flops | bytes accessed | tf_op | source)
XLA Modules:
  0.0 70.7 jit_solution(16524928949056404627)
XLA Ops:
  0.0 2.6 %shard_map.55 = (bf16[272,512]{1,0:T(8,128)(2,1)}, bf16[272,512]{1,0:T(8,128)(2,1)}, bf16[544,512]{1,0:T(8,128)(2,1)}) custom-call(bf16[2048,128]{1,0:T(8,128)(2,1)} %departures.1, f32[2048]{0:T(1024)} %innovation.1, f32[2048]{0:T(1024)} %obs_weight.1, s32[64,256]{1,0:T(8,128)} %bitcast.3), custom_call_target="tpu_custom_call" | custom-call | flops 2000000000 | bytes 100000 | tf_op jit(solution)/shard_map/pallas_call | solution.py:131
  2.6 0.0 copy-start.1
  2.6 0.1 collective-permute-start.2
  2.7 1.6 %collective-permute-start = (bf16[272,512]{1,0:T(8,128)(2,1)}, bf16[272,512]{1,0:T(8,128)(2,1)S(1)}, u32[]{:S(2)}, u32[]{:S(2)}) collective-permute-start(bf16[272,512]{1,0:T(8,128)(2,1)} %get-tuple-element.40), channel_id=1, source_target_pairs={{0,2},{1,3},{2,4},{3,5},{4,6},{5,7},{6,0},{7,1},{8,10},{9,11},{10,... | collective-permute-start | bytes 835592 | tf_op jit(solution)/shard_map/ppermute | solution.py:41
  4.3 1.7 %collective-permute-start.1 = (bf16[272,512]{1,0:T(8,128)(2,1)}, bf16[272,512]{1,0:T(8,128)(2,1)S(1)}, u32[]{:S(2)}, u32[]{:S(2)}) collective-permute-start(bf16[272,512]{1,0:T(8,128)(2,1)} %get-tuple-element.41), channel_id=1, source_target_pairs={{0,6},{1,7},{2,0},{3,1},{4,2},{5,3},{6,4},{7,5},{8,14},{9,15},{10,... | collective-permute-start | bytes 835592 | tf_op jit(solution)/shard_map/ppermute | solution.py:41
  6.0 1.5 %collective-permute-start.8 = (bf16[272,512]{1,0:T(8,128)(2,1)}, bf16[272,512]{1,0:T(8,128)(2,1)S(1)}, u32[]{:S(2)}, u32[]{:S(2)}) collective-permute-start(bf16[272,512]{1,0:T(8,128)(2,1)} %get-tuple-element.40), channel_id=1, source_target_pairs={{0,6},{1,7},{2,0},{3,1},{4,2},{5,3},{6,4},{7,5},{8,14},{9,15},{10,... | collective-permute-start | bytes 835592 | tf_op jit(solution)/shard_map/ppermute | solution.py:41
  7.6 0.5 collective-permute-start.7
  8.0 0.6 shard_map.57
  8.6 0.0 collective-permute-done.2.refs_1_
  8.6 2.5 %shard_map.56 = (bf16[8,144,256]{2,1,0:T(8,128)(2,1)S(1)}, bf16[8,144,256]{2,1,0:T(8,128)(2,1)S(1)}) custom-call(bf16[544,512]{1,0:T(8,128)(2,1)S(1)} %copy-done.1, bf16[544,512]{1,0:T(8,128)(2,1)S(1)} %collective-permute-done.2.refs_1_), custom_call_target="tpu_custom_call" | custom-call | flops 1000000 | bytes 100000 | tf_op jit(solution)/shard_map/pallas_call | solution.py:182
  11.2 2.5 %collective-permute-done.refs_0_ = bf16[272,512]{1,0:T(8,128)(2,1)S(1)} collective-permute-done((bf16[272,512]{1,0:T(8,128)(2,1)}, bf16[272,512]{1,0:T(8,128)(2,1)S(1)}, u32[]{:S(2)}, u32[]{:S(2)}) %collective-permute-start) | collective-permute-done | bytes 278560 | tf_op jit(solution)/shard_map/ppermute | solution.py:41
  13.7 0.3 collective-permute-done.1.refs_1_
  14.0 1.5 %collective-permute-start.3 = (bf16[272,512]{1,0:T(8,128)(2,1)S(1)}, bf16[272,512]{1,0:T(8,128)(2,1)S(1)}, u32[]{:S(2)}, u32[]{:S(2)}) collective-permute-start(bf16[272,512]{1,0:T(8,128)(2,1)S(1)} %collective-permute-done.refs_0_), channel_id=1, source_target_pairs={{0,2},{1,3},{2,4},{3,5},{4,6},{5,7},{6,0},{7,1},{8,10},{9,11},{10,... | collective-permute-start | bytes 835592 | tf_op jit(solution)/shard_map/ppermute | solution.py:41
  15.5 1.7 %collective-permute-start.4 = (bf16[272,512]{1,0:T(8,128)(2,1)S(1)}, bf16[272,512]{1,0:T(8,128)(2,1)S(1)}, u32[]{:S(2)}, u32[]{:S(2)}) collective-permute-start(bf16[272,512]{1,0:T(8,128)(2,1)S(1)} %collective-permute-done.1.refs_1_), channel_id=1, source_target_pairs={{0,6},{1,7},{2,0},{3,1},{4,2},{5,3},{6,4},{7,5},{8,14},{9,15},{10,... | collective-permute-start | bytes 835592 | tf_op jit(solution)/shard_map/ppermute | solution.py:41
  17.2 1.4 %shard_map.58 = (bf16[8,144,256]{2,1,0:T(8,128)(2,1)S(1)}, bf16[8,144,256]{2,1,0:T(8,128)(2,1)S(1)}) custom-call(bf16[272,512]{1,0:T(8,128)(2,1)S(1)} %collective-permute-done.refs_0_, bf16[272,512]{1,0:T(8,128)(2,1)S(1)} %collective-permute-done.1.refs_1_), custom_call_target="tpu_custom_call" | custom-call | flops 1000000 | bytes 100000 | tf_op jit(solution)/shard_map/pallas_call | solution.py:182
  18.6 0.1 collective-permute-start.5
  18.7 1.3 %collective-permute-done.8.refs_3_ = bf16[272,512]{1,0:T(8,128)(2,1)S(1)} collective-permute-done((bf16[272,512]{1,0:T(8,128)(2,1)}, bf16[272,512]{1,0:T(8,128)(2,1)S(1)}, u32[]{:S(2)}, u32[]{:S(2)}) %collective-permute-start.8) | collective-permute-done | bytes 278560 | tf_op jit(solution)/shard_map/ppermute | solution.py:41
  20.0 0.0 collective-permute-start.6
  20.0 0.0 collective-permute-done.7.refs_2_
  20.0 1.4 %shard_map.59 = (bf16[8,144,256]{2,1,0:T(8,128)(2,1)S(1)}, bf16[8,144,256]{2,1,0:T(8,128)(2,1)S(1)}) custom-call(bf16[272,512]{1,0:T(8,128)(2,1)S(1)} %collective-permute-done.refs_0_, bf16[272,512]{1,0:T(8,128)(2,1)S(1)} %collective-permute-done.1.refs_1_, bf16[272,512]{1,0:T(8,128)(2,1)S(1)} %collective-permute-done.7.refs_2_, ...), custom_call_target="tpu_custom_call" | custom-call | flops 60000002048 | bytes 100000 | tf_op jit(solution)/shard_map/pallas_call | solution.py:182
  21.3 0.8 %collective-permute-start.9 = (bf16[272,512]{1,0:T(8,128)(2,1)S(1)}, bf16[272,512]{1,0:T(8,128)(2,1)S(1)}, u32[]{:S(2)}, u32[]{:S(2)}) collective-permute-start(bf16[272,512]{1,0:T(8,128)(2,1)S(1)} %collective-permute-done.7.refs_2_), channel_id=1, source_target_pairs={{0,1},{1,0},{2,3},{3,2},{4,5},{5,4},{6,7},{7,6},{8,9},{9,8},{10,11... | collective-permute-start | bytes 835592 | tf_op jit(solution)/shard_map/ppermute | solution.py:41
  22.1 0.0 collective-permute-done.5.refs_0_
  22.1 0.1 collective-permute-start.10
  22.2 0.0 collective-permute-done.6.refs_1_
  22.2 1.4 %shard_map.60 = (bf16[8,144,256]{2,1,0:T(8,128)(2,1)S(1)}, bf16[8,144,256]{2,1,0:T(8,128)(2,1)S(1)}) custom-call(bf16[272,512]{1,0:T(8,128)(2,1)S(1)} %collective-permute-done.5.refs_0_, bf16[272,512]{1,0:T(8,128)(2,1)S(1)} %collective-permute-done.6.refs_1_), custom_call_target="tpu_custom_call" | custom-call | flops 60000002048 | bytes 100000 | tf_op jit(solution)/shard_map/pallas_call | solution.py:182
  23.6 0.1 collective-permute-done.10.refs_3_
  23.7 1.4 %shard_map.61 = (bf16[8,144,256]{2,1,0:T(8,128)(2,1)S(1)}, bf16[8,144,256]{2,1,0:T(8,128)(2,1)S(1)}) custom-call(bf16[272,512]{1,0:T(8,128)(2,1)S(1)} %collective-permute-done.5.refs_0_, bf16[272,512]{1,0:T(8,128)(2,1)S(1)} %collective-permute-done.6.refs_1_, bf16[272,512]{1,0:T(8,128)(2,1)S(1)} %collective-permute-done.9.refs_2_, ...), custom_call_target="tpu_custom_call" | custom-call | flops 1000000 | bytes 100000 | tf_op jit(solution)/shard_map/pallas_call | solution.py:182
  25.1 0.1 collective-permute-done.3.refs_0_
  25.1 0.0 collective-permute-done.4.refs_1_
  25.1 0.4 collective-permute-start.11
  25.5 0.1 collective-permute-start.12
  25.7 1.4 %shard_map.62.same = bf16[8,144,256]{2,1,0:T(8,128)(2,1)S(1)} custom-call(bf16[272,512]{1,0:T(8,128)(2,1)S(1)} %collective-permute-done.3.refs_0_, bf16[272,512]{1,0:T(8,128)(2,1)S(1)} %collective-permute-done.4.refs_1_), custom_call_target="tpu_custom_call" | custom-call | flops 1000000 | bytes 100000 | tf_op jit(solution)/shard_map/pallas_call | solution.py:182
  27.1 0.1 collective-permute-done.12.high
  27.1 1.1 %shard_map.64 = bf16[8,80,128]{2,1,0:T(8,128)(2,1)S(1)} custom-call(bf16[272,512]{1,0:T(8,128)(2,1)S(1)} %collective-permute-done.11.low, bf16[272,512]{1,0:T(8,128)(2,1)S(1)} %collective-permute-done.12.high, bf16[8,144,256]{2,1,0:T(8,128)(2,1)S(1)} %shard_map.62.same, bf16[8,144,256]{2,1,0:T(8,128)(2,1)S(1)} %get-tuple-element.65.rest_0_, ...), custom_call_target="tpu_custom_call" | custom-call | flops 1000000000 | bytes 100000 | tf_op jit(solution)/shard_map/pallas_call | solution.py:243
  28.2 3.3 %collective-permute-start.13 = (bf16[8,80,128]{2,1,0:T(8,128)(2,1)S(1)}, bf16[8,80,128]{2,1,0:T(8,128)(2,1)S(1)}, u32[]{:S(2)}, u32[]{:S(2)}) collective-permute-start(bf16[8,80,128]{2,1,0:T(8,128)(2,1)S(1)} %shard_map.64), channel_id=1, source_target_pairs={{0,16},{1,17},{2,18},{3,19},{4,20},{5,21},{6,22},{7,23},{8,24},{9,... | collective-permute-start | bytes 491528 | tf_op jit(solution)/shard_map/ppermute | solution.py:41
  31.5 1.8 %shard_map.65 = (bf16[8,80,128]{2,1,0:T(8,128)(2,1)S(1)}, bf16[8,80,128]{2,1,0:T(8,128)(2,1)S(1)}) custom-call(bf16[272,512]{1,0:T(8,128)(2,1)S(1)} %collective-permute-done.11.low, bf16[272,512]{1,0:T(8,128)(2,1)S(1)} %collective-permute-done.12.high, bf16[8,144,256]{2,1,0:T(8,128)(2,1)S(1)} %shard_map.62.same, ...), custom_call_target="tpu_custom_call" | custom-call | flops 2000000000 | bytes 100000 | tf_op jit(solution)/shard_map/pallas_call | solution.py:243
  33.4 0.8 %collective-permute-start.14 = (bf16[8,80,128]{2,1,0:T(8,128)(2,1)S(1)}, bf16[8,80,128]{2,1,0:T(8,128)(2,1)S(1)}, u32[]{:S(2)}, u32[]{:S(2)}) collective-permute-start(bf16[8,80,128]{2,1,0:T(8,128)(2,1)S(1)} %get-tuple-element.71), channel_id=1, source_target_pairs={{0,8},{1,9},{2,10},{3,11},{4,12},{5,13},{6,14},{7,15},{8,16},{9,17... | collective-permute-start | bytes 491528 | tf_op jit(solution)/shard_map/ppermute | solution.py:41
  34.1 2.6 %collective-permute-start.15 = (bf16[8,80,128]{2,1,0:T(8,128)(2,1)S(1)}, bf16[8,80,128]{2,1,0:T(8,128)(2,1)S(1)}, u32[]{:S(2)}, u32[]{:S(2)}) collective-permute-start(bf16[8,80,128]{2,1,0:T(8,128)(2,1)S(1)} %get-tuple-element.72), channel_id=1, source_target_pairs={{0,24},{1,25},{2,26},{3,27},{4,28},{5,29},{6,30},{7,31},{8,0},{9,1... | collective-permute-start | bytes 491528 | tf_op jit(solution)/shard_map/ppermute | solution.py:41
  36.7 1.1 %shard_map.63.own = f32[8,80,128]{2,1,0:T(8,128)S(1)} custom-call(bf16[272,512]{1,0:T(8,128)(2,1)S(1)} %collective-permute-done.11.low, bf16[272,512]{1,0:T(8,128)(2,1)S(1)} %collective-permute-done.12.high, bf16[8,144,256]{2,1,0:T(8,128)(2,1)S(1)} %shard_map.62.same, bf16[8,144,256]{2,1,0:T(8,128)(2,1)S(1)} %get-tuple-element.65.rest_0_, ...), custom_call_target="tpu_custom_call" | custom-call | flops 1000000000 | bytes 100000 | tf_op jit(solution)/shard_map/pallas_call | solution.py:243
  37.7 3.1 %collective-permute-done.14.b = bf16[8,80,128]{2,1,0:T(8,128)(2,1)S(1)} collective-permute-done((bf16[8,80,128]{2,1,0:T(8,128)(2,1)S(1)}, bf16[8,80,128]{2,1,0:T(8,128)(2,1)S(1)}, u32[]{:S(2)}, u32[]{:S(2)}) %collective-permute-start.14) | collective-permute-done | bytes 163872 | tf_op jit(solution)/shard_map/ppermute | solution.py:41
  40.8 0.1 shard_map.66
  40.9 16.3 %all_to_all.5.parts = bf16[8,80,128]{2,1,0:T(8,128)(2,1)S(1)} all-to-all(bf16[8,80,128]{2,1,0:T(8,128)(2,1)S(1)} %shard_map.66), channel_id=1, replica_groups=mesh['obs'=8,'grid'=32] {'obs'}, dimensions={0} | all-to-all | bytes 327680 | tf_op jit(solution)/shard_map/all_to_all | solution.py:452
  57.2 2.3 %shard_map.67.own = bf16[128,128]{1,0:T(8,128)(2,1)S(1)} custom-call(bf16[8,80,128]{2,1,0:T(8,128)(2,1)S(1)} %all_to_all.5.parts), custom_call_target="tpu_custom_call" | custom-call | flops 4000000000 | bytes 100000 | tf_op jit(solution)/shard_map/pallas_call | solution.py:308
  59.6 2.5 %collective-permute-start.17 = (bf16[128,128]{1,0:T(8,128)(2,1)S(1)}, bf16[128,128]{1,0:T(8,128)(2,1)S(1)}, u32[]{:S(2)}, u32[]{:S(2)}) collective-permute-start(bf16[128,128]{1,0:T(8,128)(2,1)S(1)} %shard_map.67.own), channel_id=1, source_target_pairs={{0,31},{1,0},{2,1},{3,2},{4,3},{5,4},{6,5},{7,6},{8,7},{9,8},{10,9... | collective-permute-start | bytes 98312 | tf_op jit(solution)/shard_map/ppermute | solution.py:456
  62.1 0.6 shard_map.68.part
  62.7 1.0 %collective-permute-done.17.right = bf16[128,128]{1,0:T(8,128)(2,1)S(1)} collective-permute-done((bf16[128,128]{1,0:T(8,128)(2,1)S(1)}, bf16[128,128]{1,0:T(8,128)(2,1)S(1)}, u32[]{:S(2)}, u32[]{:S(2)}) %collective-permute-start.17) | collective-permute-done | bytes 32800 | tf_op jit(solution)/shard_map/ppermute | solution.py:456
  63.7 5.1 %collective-permute-done.16.left = bf16[128,128]{1,0:T(8,128)(2,1)S(1)} collective-permute-done((bf16[128,128]{1,0:T(8,128)(2,1)S(1)}, bf16[128,128]{1,0:T(8,128)(2,1)S(1)}, u32[]{:S(2)}, u32[]{:S(2)}) %collective-permute-start.16) | collective-permute-done | bytes 32800 | tf_op jit(solution)/shard_map/ppermute | solution.py:455
  68.8 1.7 %shard_map.69 = bf16[48,128,128]{2,1,0:T(8,128)(2,1)} custom-call(bf16[128,128]{1,0:T(8,128)(2,1)S(1)} %collective-permute-done.16.left, bf16[128,128]{1,0:T(8,128)(2,1)S(1)} %collective-permute-done.17.right, f32[24,128,256]{2,1,0:T(8,128)S(1)} %shard_map.68.part, bf16[24,128,256]{2,1,0:T(8,128)(2,1)S(1)} %get-tuple-element.74.perturb), custom_call_target="tpu_custom_call" | custom-call | flops 2000000000 | bytes 100000 | tf_op jit(solution)/shard_map/pallas_call | solution.py:391
  (8 shorter events, 0.0 us)
Async XLA Ops:
  0.0 8.0 %copy-start = (bf16[48,128,128]{2,1,0:T(8,128)(2,1)S(1)}, bf16[48,128,128]{2,1,0:T(8,128)(2,1)}, u32[]{:S(2)}) copy-start(bf16[48,128,128]{2,1,0:T(8,128)(2,1)} %state.1) | copy-start | bytes 4718596
  2.6 6.0 %copy-start.1 = (bf16[544,512]{1,0:T(8,128)(2,1)S(1)}, bf16[544,512]{1,0:T(8,128)(2,1)}, u32[]{:S(2)}) copy-start(bf16[544,512]{1,0:T(8,128)(2,1)} %get-tuple-element.42.refs_0_) | copy-start | bytes 1671172
  2.6 6.0 %collective-permute-start.2 = (bf16[544,512]{1,0:T(8,128)(2,1)}, bf16[544,512]{1,0:T(8,128)(2,1)S(1)}, u32[]{:S(2)}, u32[]{:S(2)}) collective-permute-start(bf16[544,512]{1,0:T(8,128)(2,1)} %get-tuple-element.42.refs_0_), channel_id=1, source_target_pairs={{0,1},{1,0},{2,3},{3,2},{4,5},{5,4},{6,7},{7,6},{8,9},{9,8},{10,11... | collective-permute-start | bytes 1671176 | tf_op jit(solution)/shard_map/ppermute | solution.py:41
  2.7 11.0 %collective-permute-start = (bf16[272,512]{1,0:T(8,128)(2,1)}, bf16[272,512]{1,0:T(8,128)(2,1)S(1)}, u32[]{:S(2)}, u32[]{:S(2)}) collective-permute-start(bf16[272,512]{1,0:T(8,128)(2,1)} %get-tuple-element.40), channel_id=1, source_target_pairs={{0,2},{1,3},{2,4},{3,5},{4,6},{5,7},{6,0},{7,1},{8,10},{9,11},{10,... | collective-permute-start | bytes 835592 | tf_op jit(solution)/shard_map/ppermute | solution.py:41
  4.3 9.7 %collective-permute-start.1 = (bf16[272,512]{1,0:T(8,128)(2,1)}, bf16[272,512]{1,0:T(8,128)(2,1)S(1)}, u32[]{:S(2)}, u32[]{:S(2)}) collective-permute-start(bf16[272,512]{1,0:T(8,128)(2,1)} %get-tuple-element.41), channel_id=1, source_target_pairs={{0,6},{1,7},{2,0},{3,1},{4,2},{5,3},{6,4},{7,5},{8,14},{9,15},{10,... | collective-permute-start | bytes 835592 | tf_op jit(solution)/shard_map/ppermute | solution.py:41
  6.0 13.9 %collective-permute-start.8 = (bf16[272,512]{1,0:T(8,128)(2,1)}, bf16[272,512]{1,0:T(8,128)(2,1)S(1)}, u32[]{:S(2)}, u32[]{:S(2)}) collective-permute-start(bf16[272,512]{1,0:T(8,128)(2,1)} %get-tuple-element.40), channel_id=1, source_target_pairs={{0,6},{1,7},{2,0},{3,1},{4,2},{5,3},{6,4},{7,5},{8,14},{9,15},{10,... | collective-permute-start | bytes 835592 | tf_op jit(solution)/shard_map/ppermute | solution.py:41
  7.6 12.4 %collective-permute-start.7 = (bf16[272,512]{1,0:T(8,128)(2,1)}, bf16[272,512]{1,0:T(8,128)(2,1)S(1)}, u32[]{:S(2)}, u32[]{:S(2)}) collective-permute-start(bf16[272,512]{1,0:T(8,128)(2,1)} %get-tuple-element.41), channel_id=1, source_target_pairs={{0,2},{1,3},{2,4},{3,5},{4,6},{5,7},{6,0},{7,1},{8,10},{9,11},{10,... | collective-permute-start | bytes 835592 | tf_op jit(solution)/shard_map/ppermute | solution.py:41
  14.0 11.2 %collective-permute-start.3 = (bf16[272,512]{1,0:T(8,128)(2,1)S(1)}, bf16[272,512]{1,0:T(8,128)(2,1)S(1)}, u32[]{:S(2)}, u32[]{:S(2)}) collective-permute-start(bf16[272,512]{1,0:T(8,128)(2,1)S(1)} %collective-permute-done.refs_0_), channel_id=1, source_target_pairs={{0,2},{1,3},{2,4},{3,5},{4,6},{5,7},{6,0},{7,1},{8,10},{9,11},{10,... | collective-permute-start | bytes 835592 | tf_op jit(solution)/shard_map/ppermute | solution.py:41
  15.5 9.7 %collective-permute-start.4 = (bf16[272,512]{1,0:T(8,128)(2,1)S(1)}, bf16[272,512]{1,0:T(8,128)(2,1)S(1)}, u32[]{:S(2)}, u32[]{:S(2)}) collective-permute-start(bf16[272,512]{1,0:T(8,128)(2,1)S(1)} %collective-permute-done.1.refs_1_), channel_id=1, source_target_pairs={{0,6},{1,7},{2,0},{3,1},{4,2},{5,3},{6,4},{7,5},{8,14},{9,15},{10,... | collective-permute-start | bytes 835592 | tf_op jit(solution)/shard_map/ppermute | solution.py:41
  18.6 3.5 %collective-permute-start.5 = (bf16[272,512]{1,0:T(8,128)(2,1)S(1)}, bf16[272,512]{1,0:T(8,128)(2,1)S(1)}, u32[]{:S(2)}, u32[]{:S(2)}) collective-permute-start(bf16[272,512]{1,0:T(8,128)(2,1)S(1)} %collective-permute-done.refs_0_), channel_id=1, source_target_pairs={{0,1},{1,0},{2,3},{3,2},{4,5},{5,4},{6,7},{7,6},{8,9},{9,8},{10,11... | collective-permute-start | bytes 835592 | tf_op jit(solution)/shard_map/ppermute | solution.py:41
  20.0 2.3 %collective-permute-start.6 = (bf16[272,512]{1,0:T(8,128)(2,1)S(1)}, bf16[272,512]{1,0:T(8,128)(2,1)S(1)}, u32[]{:S(2)}, u32[]{:S(2)}) collective-permute-start(bf16[272,512]{1,0:T(8,128)(2,1)S(1)} %collective-permute-done.1.refs_1_), channel_id=1, source_target_pairs={{0,1},{1,0},{2,3},{3,2},{4,5},{5,4},{6,7},{7,6},{8,9},{9,8},{10,11... | collective-permute-start | bytes 835592 | tf_op jit(solution)/shard_map/ppermute | solution.py:41
  21.3 2.3 %collective-permute-start.9 = (bf16[272,512]{1,0:T(8,128)(2,1)S(1)}, bf16[272,512]{1,0:T(8,128)(2,1)S(1)}, u32[]{:S(2)}, u32[]{:S(2)}) collective-permute-start(bf16[272,512]{1,0:T(8,128)(2,1)S(1)} %collective-permute-done.7.refs_2_), channel_id=1, source_target_pairs={{0,1},{1,0},{2,3},{3,2},{4,5},{5,4},{6,7},{7,6},{8,9},{9,8},{10,11... | collective-permute-start | bytes 835592 | tf_op jit(solution)/shard_map/ppermute | solution.py:41
  22.1 1.6 %collective-permute-start.10 = (bf16[272,512]{1,0:T(8,128)(2,1)S(1)}, bf16[272,512]{1,0:T(8,128)(2,1)S(1)}, u32[]{:S(2)}, u32[]{:S(2)}) collective-permute-start(bf16[272,512]{1,0:T(8,128)(2,1)S(1)} %collective-permute-done.8.refs_3_), channel_id=1, source_target_pairs={{0,1},{1,0},{2,3},{3,2},{4,5},{5,4},{6,7},{7,6},{8,9},{9,8},{10,11... | collective-permute-start | bytes 835592 | tf_op jit(solution)/shard_map/ppermute | solution.py:41
  25.1 1.9 %collective-permute-start.11 = (bf16[272,512]{1,0:T(8,128)(2,1)S(1)}, bf16[272,512]{1,0:T(8,128)(2,1)S(1)}, u32[]{:S(2)}, u32[]{:S(2)}) collective-permute-start(bf16[272,512]{1,0:T(8,128)(2,1)S(1)} %collective-permute-done.3.refs_0_), channel_id=1, source_target_pairs={{0,1},{1,0},{2,3},{3,2},{4,5},{5,4},{6,7},{7,6},{8,9},{9,8},{10,11... | collective-permute-start | bytes 835592 | tf_op jit(solution)/shard_map/ppermute | solution.py:41
  25.5 1.6 %collective-permute-start.12 = (bf16[272,512]{1,0:T(8,128)(2,1)S(1)}, bf16[272,512]{1,0:T(8,128)(2,1)S(1)}, u32[]{:S(2)}, u32[]{:S(2)}) collective-permute-start(bf16[272,512]{1,0:T(8,128)(2,1)S(1)} %collective-permute-done.4.refs_1_), channel_id=1, source_target_pairs={{0,1},{1,0},{2,3},{3,2},{4,5},{5,4},{6,7},{7,6},{8,9},{9,8},{10,11... | collective-permute-start | bytes 835592 | tf_op jit(solution)/shard_map/ppermute | solution.py:41
  28.2 9.5 %collective-permute-start.13 = (bf16[8,80,128]{2,1,0:T(8,128)(2,1)S(1)}, bf16[8,80,128]{2,1,0:T(8,128)(2,1)S(1)}, u32[]{:S(2)}, u32[]{:S(2)}) collective-permute-start(bf16[8,80,128]{2,1,0:T(8,128)(2,1)S(1)} %shard_map.64), channel_id=1, source_target_pairs={{0,16},{1,17},{2,18},{3,19},{4,20},{5,21},{6,22},{7,23},{8,24},{9,... | collective-permute-start | bytes 491528 | tf_op jit(solution)/shard_map/ppermute | solution.py:41
  33.4 7.5 %collective-permute-start.14 = (bf16[8,80,128]{2,1,0:T(8,128)(2,1)S(1)}, bf16[8,80,128]{2,1,0:T(8,128)(2,1)S(1)}, u32[]{:S(2)}, u32[]{:S(2)}) collective-permute-start(bf16[8,80,128]{2,1,0:T(8,128)(2,1)S(1)} %get-tuple-element.71), channel_id=1, source_target_pairs={{0,8},{1,9},{2,10},{3,11},{4,12},{5,13},{6,14},{7,15},{8,16},{9,17... | collective-permute-start | bytes 491528 | tf_op jit(solution)/shard_map/ppermute | solution.py:41
  34.1 6.7 %collective-permute-start.15 = (bf16[8,80,128]{2,1,0:T(8,128)(2,1)S(1)}, bf16[8,80,128]{2,1,0:T(8,128)(2,1)S(1)}, u32[]{:S(2)}, u32[]{:S(2)}) collective-permute-start(bf16[8,80,128]{2,1,0:T(8,128)(2,1)S(1)} %get-tuple-element.72), channel_id=1, source_target_pairs={{0,24},{1,25},{2,26},{3,27},{4,28},{5,29},{6,30},{7,31},{8,0},{9,1... | collective-permute-start | bytes 491528 | tf_op jit(solution)/shard_map/ppermute | solution.py:41
  59.6 4.1 %collective-permute-start.17 = (bf16[128,128]{1,0:T(8,128)(2,1)S(1)}, bf16[128,128]{1,0:T(8,128)(2,1)S(1)}, u32[]{:S(2)}, u32[]{:S(2)}) collective-permute-start(bf16[128,128]{1,0:T(8,128)(2,1)S(1)} %shard_map.67.own), channel_id=1, source_target_pairs={{0,31},{1,0},{2,1},{3,2},{4,3},{5,4},{6,5},{7,6},{8,7},{9,8},{10,9... | collective-permute-start | bytes 98312 | tf_op jit(solution)/shard_map/ppermute | solution.py:456
  62.1 6.7 %collective-permute-start.16 = (bf16[128,128]{1,0:T(8,128)(2,1)S(1)}, bf16[128,128]{1,0:T(8,128)(2,1)S(1)}, u32[]{:S(2)}, u32[]{:S(2)}) collective-permute-start(bf16[128,128]{1,0:T(8,128)(2,1)S(1)} %shard_map.67.own), channel_id=1, source_target_pairs={{0,1},{1,2},{2,3},{3,4},{4,5},{5,6},{6,7},{7,8},{8,9},{9,10},{10,1... | collective-permute-start | bytes 98312 | tf_op jit(solution)/shard_map/ppermute | solution.py:455

commit v8 on v7

--- a/solution.py
+++ b/solution.py
@@ -407,14 +407,17 @@
     left = hop(low_half, 0, 1, 0)
     right = hop(high_half, 0, -1, 0)
     other = hop(near, 0, 0, 1)
-    left_more = hop(high_half, 0, 1, 0)
-    right_more = hop(low_half, 0, -1, 0)
 
     whole = lambda which: ((0, which, 0), (1, which, HALF))
     found = pick_rows(
         ((whole(0), (0, 0, 8), None), (whole(1), (1, 0, 12), None)), SHORT, near, other
     )
     mean, perturb = perturbations(state)
+    low_half, high_half, found, mean, perturb = lax.optimization_barrier(
+        (low_half, high_half, found, mean, perturb)
+    )
+    left_more = hop(high_half, 0, 1, 0)
+    right_more = hop(low_half, 0, -1, 0)
     left, right, found, mean, perturb = lax.optimization_barrier(
         (left, right, found, mean, perturb)
     )

time: 70.8 us -> 70.5 us (level)
  waiting for transfers between devices: 13.5 us -> 12.2 us
  starting transfers between devices: 19.3 us -> 20.3 us
    ppermute x16, waiting for transfers between devices: 7.45 us -> 6.15 us  [hop(): return lax.ppermute(value, 'grid', pairs)]
    ppermute x16, starting transfers between devices: 16.8 us -> 18.1 us  [hop(): return lax.ppermute(value, 'grid', pairs)]
where the time goes in v8:
time: 70.5 us; the launch traced here: 70.4 us
  Pallas kernels  21.1 us (30%)
  starting transfers between devices  20.3 us (29%)
  blocking collectives  16.3 us (23%)
  waiting for transfers between devices  12.2 us (17%)
    ppermute x16, starting transfers between devices, hop(): return lax.ppermute(value, 'grid', pairs)  18.1 us
    all_to_all x1, blocking collectives, on_device(): parts = lax.all_to_all(parts, 'obs', 0, 0, tiled=True)  16.3 us
    pallas_call x6, Pallas kernels, pick_rows(): pl.pallas_call(functools.partial(pick_kernel, sources, len(args)), out_sh...  9.32 us
    ppermute x16, waiting for transfers between devices, hop(): return lax.ppermute(value, 'grid', pairs)  6.15 us
    ppermute x1, waiting for transfers between devices, on_device(): lax.ppermute(own, 'grid', [(j, (j + 1) % n_grid) for j in range(n_grid)])  5.06 us
    pallas_call x3, Pallas kernels, last_grams(): pl.pallas_call(functools.partial(last_kernel, shifts), out_shape=[jax.Sha...  3.95 us
    pallas_call x1, Pallas kernels, make_messages(): pl.pallas_call(message_kernel, out_shape=[jax.ShapeDtypeStruct(shape, BF1...  2.58 us
    pallas_call x1, Pallas kernels, transposed_weights(): pl.pallas_call(weights_kernel, out_shape=jax.ShapeDtypeStruct((K, K), BF1...  2.34 us
  transfers between devices with their start and end apart: 18, of which 9 were waited for; matrix products, arithmetic and copies ran while one was open for 0% of the time, Pallas kernels for 19%

profile of v8, /device:TPU:32, one launch (start us, length us, event | category | flops | bytes accessed | tf_op | source)
XLA Modules:
  0.0 70.4 jit_solution(611016959968590686)
XLA Ops:
  0.0 2.6 %shard_map.55 = (bf16[272,512]{1,0:T(8,128)(2,1)}, bf16[272,512]{1,0:T(8,128)(2,1)}, bf16[544,512]{1,0:T(8,128)(2,1)}) custom-call(bf16[2048,128]{1,0:T(8,128)(2,1)} %departures.1, f32[2048]{0:T(1024)} %innovation.1, f32[2048]{0:T(1024)} %obs_weight.1, s32[64,256]{1,0:T(8,128)} %bitcast.3), custom_call_target="tpu_custom_call" | custom-call | flops 2000000000 | bytes 100000 | tf_op jit(solution)/shard_map/pallas_call | solution.py:131
  2.6 0.0 copy-start.1
  2.6 0.1 collective-permute-start.2
  2.7 1.6 %collective-permute-start = (bf16[272,512]{1,0:T(8,128)(2,1)}, bf16[272,512]{1,0:T(8,128)(2,1)S(1)}, u32[]{:S(2)}, u32[]{:S(2)}) collective-permute-start(bf16[272,512]{1,0:T(8,128)(2,1)} %get-tuple-element.64), channel_id=1, source_target_pairs={{0,2},{1,3},{2,4},{3,5},{4,6},{5,7},{6,0},{7,1},{8,10},{9,11},{10,... | collective-permute-start | bytes 835592 | tf_op jit(solution)/shard_map/ppermute | solution.py:41
  4.3 1.7 %collective-permute-start.1 = (bf16[272,512]{1,0:T(8,128)(2,1)}, bf16[272,512]{1,0:T(8,128)(2,1)S(1)}, u32[]{:S(2)}, u32[]{:S(2)}) collective-permute-start(bf16[272,512]{1,0:T(8,128)(2,1)} %get-tuple-element.63), channel_id=1, source_target_pairs={{0,6},{1,7},{2,0},{3,1},{4,2},{5,3},{6,4},{7,5},{8,14},{9,15},{10,... | collective-permute-start | bytes 835592 | tf_op jit(solution)/shard_map/ppermute | solution.py:41
  6.0 0.6 shard_map.57
  6.6 2.5 %shard_map.56 = (bf16[8,144,256]{2,1,0:T(8,128)(2,1)S(1)}, bf16[8,144,256]{2,1,0:T(8,128)(2,1)S(1)}) custom-call(bf16[544,512]{1,0:T(8,128)(2,1)S(1)} %copy-done.1, bf16[544,512]{1,0:T(8,128)(2,1)S(1)} %collective-permute-done.2.refs_1_), custom_call_target="tpu_custom_call" | custom-call | flops 1000000 | bytes 100000 | tf_op jit(solution)/shard_map/pallas_call | solution.py:182
  9.2 0.4 collective-permute-start.7
  9.5 3.0 %collective-permute-start.8 = (bf16[272,512]{1,0:T(8,128)(2,1)S(1)}, bf16[272,512]{1,0:T(8,128)(2,1)S(1)}, u32[]{:S(2)}, u32[]{:S(2)}) collective-permute-start(bf16[272,512]{1,0:T(8,128)(2,1)S(1)} %copy-done.2), channel_id=1, source_target_pairs={{0,6},{1,7},{2,0},{3,1},{4,2},{5,3},{6,4},{7,5},{8,14},{9,15},{10,... | collective-permute-start | bytes 835592 | tf_op jit(solution)/shard_map/ppermute | solution.py:41
  12.5 1.0 %collective-permute-done.refs_0_ = bf16[272,512]{1,0:T(8,128)(2,1)S(1)} collective-permute-done((bf16[272,512]{1,0:T(8,128)(2,1)}, bf16[272,512]{1,0:T(8,128)(2,1)S(1)}, u32[]{:S(2)}, u32[]{:S(2)}) %collective-permute-start) | collective-permute-done | bytes 278560 | tf_op jit(solution)/shard_map/ppermute | solution.py:41
  13.5 0.5 collective-permute-done.1.refs_1_
  14.0 1.5 %collective-permute-start.3 = (bf16[272,512]{1,0:T(8,128)(2,1)S(1)}, bf16[272,512]{1,0:T(8,128)(2,1)S(1)}, u32[]{:S(2)}, u32[]{:S(2)}) collective-permute-start(bf16[272,512]{1,0:T(8,128)(2,1)S(1)} %collective-permute-done.refs_0_), channel_id=1, source_target_pairs={{0,2},{1,3},{2,4},{3,5},{4,6},{5,7},{6,0},{7,1},{8,10},{9,11},{10,... | collective-permute-start | bytes 835592 | tf_op jit(solution)/shard_map/ppermute | solution.py:41
  15.5 1.7 %collective-permute-start.4 = (bf16[272,512]{1,0:T(8,128)(2,1)S(1)}, bf16[272,512]{1,0:T(8,128)(2,1)S(1)}, u32[]{:S(2)}, u32[]{:S(2)}) collective-permute-start(bf16[272,512]{1,0:T(8,128)(2,1)S(1)} %collective-permute-done.1.refs_1_), channel_id=1, source_target_pairs={{0,6},{1,7},{2,0},{3,1},{4,2},{5,3},{6,4},{7,5},{8,14},{9,15},{10,... | collective-permute-start | bytes 835592 | tf_op jit(solution)/shard_map/ppermute | solution.py:41
  17.2 1.4 %shard_map.58 = (bf16[8,144,256]{2,1,0:T(8,128)(2,1)S(1)}, bf16[8,144,256]{2,1,0:T(8,128)(2,1)S(1)}) custom-call(bf16[272,512]{1,0:T(8,128)(2,1)S(1)} %collective-permute-done.refs_0_, bf16[272,512]{1,0:T(8,128)(2,1)S(1)} %collective-permute-done.1.refs_1_), custom_call_target="tpu_custom_call" | custom-call | flops 1000000 | bytes 100000 | tf_op jit(solution)/shard_map/pallas_call | solution.py:182
  18.6 0.1 collective-permute-start.5
  18.7 1.3 %collective-permute-done.7.refs_2_ = bf16[272,512]{1,0:T(8,128)(2,1)S(1)} collective-permute-done((bf16[272,512]{1,0:T(8,128)(2,1)S(1)}, bf16[272,512]{1,0:T(8,128)(2,1)S(1)}, u32[]{:S(2)}, u32[]{:S(2)}) %collective-permute-start.7) | collective-permute-done | bytes 278560 | tf_op jit(solution)/shard_map/ppermute | solution.py:41
  20.0 0.0 collective-permute-start.6
  20.0 0.0 collective-permute-done.8.refs_3_
  20.0 1.4 %shard_map.59 = (bf16[8,144,256]{2,1,0:T(8,128)(2,1)S(1)}, bf16[8,144,256]{2,1,0:T(8,128)(2,1)S(1)}) custom-call(bf16[272,512]{1,0:T(8,128)(2,1)S(1)} %collective-permute-done.refs_0_, bf16[272,512]{1,0:T(8,128)(2,1)S(1)} %collective-permute-done.1.refs_1_, bf16[272,512]{1,0:T(8,128)(2,1)S(1)} %collective-permute-done.7.refs_2_, ...), custom_call_target="tpu_custom_call" | custom-call | flops 60000002048 | bytes 100000 | tf_op jit(solution)/shard_map/pallas_call | solution.py:182
  21.4 0.8 %collective-permute-start.9 = (bf16[272,512]{1,0:T(8,128)(2,1)S(1)}, bf16[272,512]{1,0:T(8,128)(2,1)S(1)}, u32[]{:S(2)}, u32[]{:S(2)}) collective-permute-start(bf16[272,512]{1,0:T(8,128)(2,1)S(1)} %collective-permute-done.7.refs_2_), channel_id=1, source_target_pairs={{0,1},{1,0},{2,3},{3,2},{4,5},{5,4},{6,7},{7,6},{8,9},{9,8},{10,11... | collective-permute-start | bytes 835592 | tf_op jit(solution)/shard_map/ppermute | solution.py:41
  22.1 0.1 collective-permute-start.10
  22.3 0.0 collective-permute-done.6.refs_1_
  22.3 1.4 %shard_map.60 = (bf16[8,144,256]{2,1,0:T(8,128)(2,1)S(1)}, bf16[8,144,256]{2,1,0:T(8,128)(2,1)S(1)}) custom-call(bf16[272,512]{1,0:T(8,128)(2,1)S(1)} %collective-permute-done.5.refs_0_, bf16[272,512]{1,0:T(8,128)(2,1)S(1)} %collective-permute-done.6.refs_1_), custom_call_target="tpu_custom_call" | custom-call | flops 60000002048 | bytes 100000 | tf_op jit(solution)/shard_map/pallas_call | solution.py:182
  23.6 0.0 collective-permute-done.9.refs_2_
  23.6 0.1 collective-permute-done.10.refs_3_
  23.7 1.4 %shard_map.61 = (bf16[8,144,256]{2,1,0:T(8,128)(2,1)S(1)}, bf16[8,144,256]{2,1,0:T(8,128)(2,1)S(1)}) custom-call(bf16[272,512]{1,0:T(8,128)(2,1)S(1)} %collective-permute-done.5.refs_0_, bf16[272,512]{1,0:T(8,128)(2,1)S(1)} %collective-permute-done.6.refs_1_, bf16[272,512]{1,0:T(8,128)(2,1)S(1)} %collective-permute-done.9.refs_2_, ...), custom_call_target="tpu_custom_call" | custom-call | flops 1000000 | bytes 100000 | tf_op jit(solution)/shard_map/pallas_call | solution.py:182
  25.1 0.1 collective-permute-done.3.refs_0_
  25.2 0.4 collective-permute-start.11
  25.6 0.1 collective-permute-start.12
  25.7 1.4 %shard_map.62.same = bf16[8,144,256]{2,1,0:T(8,128)(2,1)S(1)} custom-call(bf16[272,512]{1,0:T(8,128)(2,1)S(1)} %collective-permute-done.3.refs_0_, bf16[272,512]{1,0:T(8,128)(2,1)S(1)} %collective-permute-done.4.refs_1_), custom_call_target="tpu_custom_call" | custom-call | flops 1000000 | bytes 100000 | tf_op jit(solution)/shard_map/pallas_call | solution.py:182
  27.1 0.0 collective-permute-done.11.low
  27.1 0.1 collective-permute-done.12.high
  27.2 1.1 %shard_map.64 = bf16[8,80,128]{2,1,0:T(8,128)(2,1)S(1)} custom-call(bf16[272,512]{1,0:T(8,128)(2,1)S(1)} %collective-permute-done.11.low, bf16[272,512]{1,0:T(8,128)(2,1)S(1)} %collective-permute-done.12.high, bf16[8,144,256]{2,1,0:T(8,128)(2,1)S(1)} %shard_map.62.same, bf16[8,144,256]{2,1,0:T(8,128)(2,1)S(1)} %get-tuple-element.77.rest_0_, ...), custom_call_target="tpu_custom_call" | custom-call | flops 1000000000 | bytes 100000 | tf_op jit(solution)/shard_map/pallas_call | solution.py:243
  28.2 3.3 %collective-permute-start.13 = (bf16[8,80,128]{2,1,0:T(8,128)(2,1)S(1)}, bf16[8,80,128]{2,1,0:T(8,128)(2,1)S(1)}, u32[]{:S(2)}, u32[]{:S(2)}) collective-permute-start(bf16[8,80,128]{2,1,0:T(8,128)(2,1)S(1)} %shard_map.64), channel_id=1, source_target_pairs={{0,16},{1,17},{2,18},{3,19},{4,20},{5,21},{6,22},{7,23},{8,24},{9,... | collective-permute-start | bytes 491528 | tf_op jit(solution)/shard_map/ppermute | solution.py:41
  31.5 1.8 %shard_map.65 = (bf16[8,80,128]{2,1,0:T(8,128)(2,1)S(1)}, bf16[8,80,128]{2,1,0:T(8,128)(2,1)S(1)}) custom-call(bf16[272,512]{1,0:T(8,128)(2,1)S(1)} %collective-permute-done.11.low, bf16[272,512]{1,0:T(8,128)(2,1)S(1)} %collective-permute-done.12.high, bf16[8,144,256]{2,1,0:T(8,128)(2,1)S(1)} %shard_map.62.same, ...), custom_call_target="tpu_custom_call" | custom-call | flops 2000000000 | bytes 100000 | tf_op jit(solution)/shard_map/pallas_call | solution.py:243
  33.4 0.8 %collective-permute-start.14 = (bf16[8,80,128]{2,1,0:T(8,128)(2,1)S(1)}, bf16[8,80,128]{2,1,0:T(8,128)(2,1)S(1)}, u32[]{:S(2)}, u32[]{:S(2)}) collective-permute-start(bf16[8,80,128]{2,1,0:T(8,128)(2,1)S(1)} %get-tuple-element.83), channel_id=1, source_target_pairs={{0,8},{1,9},{2,10},{3,11},{4,12},{5,13},{6,14},{7,15},{8,16},{9,17... | collective-permute-start | bytes 491528 | tf_op jit(solution)/shard_map/ppermute | solution.py:41
  34.1 2.6 %collective-permute-start.15 = (bf16[8,80,128]{2,1,0:T(8,128)(2,1)S(1)}, bf16[8,80,128]{2,1,0:T(8,128)(2,1)S(1)}, u32[]{:S(2)}, u32[]{:S(2)}) collective-permute-start(bf16[8,80,128]{2,1,0:T(8,128)(2,1)S(1)} %get-tuple-element.84), channel_id=1, source_target_pairs={{0,24},{1,25},{2,26},{3,27},{4,28},{5,29},{6,30},{7,31},{8,0},{9,1... | collective-permute-start | bytes 491528 | tf_op jit(solution)/shard_map/ppermute | solution.py:41
  36.7 1.1 %shard_map.63.own = f32[8,80,128]{2,1,0:T(8,128)S(1)} custom-call(bf16[272,512]{1,0:T(8,128)(2,1)S(1)} %collective-permute-done.11.low, bf16[272,512]{1,0:T(8,128)(2,1)S(1)} %collective-permute-done.12.high, bf16[8,144,256]{2,1,0:T(8,128)(2,1)S(1)} %shard_map.62.same, bf16[8,144,256]{2,1,0:T(8,128)(2,1)S(1)} %get-tuple-element.77.rest_0_, ...), custom_call_target="tpu_custom_call" | custom-call | flops 1000000000 | bytes 100000 | tf_op jit(solution)/shard_map/pallas_call | solution.py:243
  37.7 0.0 collective-permute-done.13.a
  37.8 3.1 %collective-permute-done.14.b = bf16[8,80,128]{2,1,0:T(8,128)(2,1)S(1)} collective-permute-done((bf16[8,80,128]{2,1,0:T(8,128)(2,1)S(1)}, bf16[8,80,128]{2,1,0:T(8,128)(2,1)S(1)}, u32[]{:S(2)}, u32[]{:S(2)}) %collective-permute-start.14) | collective-permute-done | bytes 163872 | tf_op jit(solution)/shard_map/ppermute | solution.py:41
  40.8 0.1 shard_map.66
  40.9 16.3 %all_to_all.5.parts = bf16[8,80,128]{2,1,0:T(8,128)(2,1)S(1)} all-to-all(bf16[8,80,128]{2,1,0:T(8,128)(2,1)S(1)} %shard_map.66), channel_id=1, replica_groups=mesh['obs'=8,'grid'=32] {'obs'}, dimensions={0} | all-to-all | bytes 327680 | tf_op jit(solution)/shard_map/all_to_all | solution.py:455
  57.3 2.3 %shard_map.67.own = bf16[128,128]{1,0:T(8,128)(2,1)S(1)} custom-call(bf16[8,80,128]{2,1,0:T(8,128)(2,1)S(1)} %all_to_all.5.parts), custom_call_target="tpu_custom_call" | custom-call | flops 4000000000 | bytes 100000 | tf_op jit(solution)/shard_map/pallas_call | solution.py:308
  59.6 2.2 %collective-permute-start.17 = (bf16[128,128]{1,0:T(8,128)(2,1)S(1)}, bf16[128,128]{1,0:T(8,128)(2,1)S(1)}, u32[]{:S(2)}, u32[]{:S(2)}) collective-permute-start(bf16[128,128]{1,0:T(8,128)(2,1)S(1)} %shard_map.67.own), channel_id=1, source_target_pairs={{0,31},{1,0},{2,1},{3,2},{4,3},{5,4},{6,5},{7,6},{8,7},{9,8},{10,9... | collective-permute-start | bytes 98312 | tf_op jit(solution)/shard_map/ppermute | solution.py:459
  61.8 0.6 shard_map.68.part
  62.4 1.0 %collective-permute-done.17.right = bf16[128,128]{1,0:T(8,128)(2,1)S(1)} collective-permute-done((bf16[128,128]{1,0:T(8,128)(2,1)S(1)}, bf16[128,128]{1,0:T(8,128)(2,1)S(1)}, u32[]{:S(2)}, u32[]{:S(2)}) %collective-permute-start.17) | collective-permute-done | bytes 32800 | tf_op jit(solution)/shard_map/ppermute | solution.py:459
  63.4 5.1 %collective-permute-done.16.left = bf16[128,128]{1,0:T(8,128)(2,1)S(1)} collective-permute-done((bf16[128,128]{1,0:T(8,128)(2,1)S(1)}, bf16[128,128]{1,0:T(8,128)(2,1)S(1)}, u32[]{:S(2)}, u32[]{:S(2)}) %collective-permute-start.16) | collective-permute-done | bytes 32800 | tf_op jit(solution)/shard_map/ppermute | solution.py:458
  68.5 1.7 %shard_map.69 = bf16[48,128,128]{2,1,0:T(8,128)(2,1)} custom-call(bf16[128,128]{1,0:T(8,128)(2,1)S(1)} %collective-permute-done.16.left, bf16[128,128]{1,0:T(8,128)(2,1)S(1)} %collective-permute-done.17.right, f32[24,128,256]{2,1,0:T(8,128)S(1)} %shard_map.68.part, bf16[24,128,256]{2,1,0:T(8,128)(2,1)S(1)} %get-tuple-element.86.perturb), custom_call_target="tpu_custom_call" | custom-call | flops 2000000000 | bytes 100000 | tf_op jit(solution)/shard_map/pallas_call | solution.py:391
  (12 shorter events, 0.0 us)
Async XLA Ops:
  0.0 6.0 %copy-start = (bf16[48,128,128]{2,1,0:T(8,128)(2,1)S(1)}, bf16[48,128,128]{2,1,0:T(8,128)(2,1)}, u32[]{:S(2)}) copy-start(bf16[48,128,128]{2,1,0:T(8,128)(2,1)} %state.1) | copy-start | bytes 4718596
  2.6 4.0 %copy-start.1 = (bf16[544,512]{1,0:T(8,128)(2,1)S(1)}, bf16[544,512]{1,0:T(8,128)(2,1)}, u32[]{:S(2)}) copy-start(bf16[544,512]{1,0:T(8,128)(2,1)} %get-tuple-element.48.refs_0_) | copy-start | bytes 1671172
  2.6 6.5 %copy-start.3 = (bf16[272,512]{1,0:T(8,128)(2,1)S(1)}, bf16[272,512]{1,0:T(8,128)(2,1)}, u32[]{:S(2)}) copy-start(bf16[272,512]{1,0:T(8,128)(2,1)} %get-tuple-element.63) | copy-start | bytes 835588
  2.6 6.9 %copy-start.2 = (bf16[272,512]{1,0:T(8,128)(2,1)S(1)}, bf16[272,512]{1,0:T(8,128)(2,1)}, u32[]{:S(2)}) copy-start(bf16[272,512]{1,0:T(8,128)(2,1)} %get-tuple-element.64) | copy-start | bytes 835588
  2.6 4.0 %collective-permute-start.2 = (bf16[544,512]{1,0:T(8,128)(2,1)}, bf16[544,512]{1,0:T(8,128)(2,1)S(1)}, u32[]{:S(2)}, u32[]{:S(2)}) collective-permute-start(bf16[544,512]{1,0:T(8,128)(2,1)} %get-tuple-element.48.refs_0_), channel_id=1, source_target_pairs={{0,1},{1,0},{2,3},{3,2},{4,5},{5,4},{6,7},{7,6},{8,9},{9,8},{10,11... | collective-permute-start | bytes 1671176 | tf_op jit(solution)/shard_map/ppermute | solution.py:41
  2.7 10.7 %collective-permute-start = (bf16[272,512]{1,0:T(8,128)(2,1)}, bf16[272,512]{1,0:T(8,128)(2,1)S(1)}, u32[]{:S(2)}, u32[]{:S(2)}) collective-permute-start(bf16[272,512]{1,0:T(8,128)(2,1)} %get-tuple-element.64), channel_id=1, source_target_pairs={{0,2},{1,3},{2,4},{3,5},{4,6},{5,7},{6,0},{7,1},{8,10},{9,11},{10,... | collective-permute-start | bytes 835592 | tf_op jit(solution)/shard_map/ppermute | solution.py:41
  4.3 9.7 %collective-permute-start.1 = (bf16[272,512]{1,0:T(8,128)(2,1)}, bf16[272,512]{1,0:T(8,128)(2,1)S(1)}, u32[]{:S(2)}, u32[]{:S(2)}) collective-permute-start(bf16[272,512]{1,0:T(8,128)(2,1)} %get-tuple-element.63), channel_id=1, source_target_pairs={{0,6},{1,7},{2,0},{3,1},{4,2},{5,3},{6,4},{7,5},{8,14},{9,15},{10,... | collective-permute-start | bytes 835592 | tf_op jit(solution)/shard_map/ppermute | solution.py:41
  9.2 10.8 %collective-permute-start.7 = (bf16[272,512]{1,0:T(8,128)(2,1)S(1)}, bf16[272,512]{1,0:T(8,128)(2,1)S(1)}, u32[]{:S(2)}, u32[]{:S(2)}) collective-permute-start(bf16[272,512]{1,0:T(8,128)(2,1)S(1)} %copy-done.3), channel_id=1, source_target_pairs={{0,2},{1,3},{2,4},{3,5},{4,6},{5,7},{6,0},{7,1},{8,10},{9,11},{10,... | collective-permute-start | bytes 835592 | tf_op jit(solution)/shard_map/ppermute | solution.py:41
  9.5 10.5 %collective-permute-start.8 = (bf16[272,512]{1,0:T(8,128)(2,1)S(1)}, bf16[272,512]{1,0:T(8,128)(2,1)S(1)}, u32[]{:S(2)}, u32[]{:S(2)}) collective-permute-start(bf16[272,512]{1,0:T(8,128)(2,1)S(1)} %copy-done.2), channel_id=1, source_target_pairs={{0,6},{1,7},{2,0},{3,1},{4,2},{5,3},{6,4},{7,5},{8,14},{9,15},{10,... | collective-permute-start | bytes 835592 | tf_op jit(solution)/shard_map/ppermute | solution.py:41
  14.0 11.2 %collective-permute-start.3 = (bf16[272,512]{1,0:T(8,128)(2,1)S(1)}, bf16[272,512]{1,0:T(8,128)(2,1)S(1)}, u32[]{:S(2)}, u32[]{:S(2)}) collective-permute-start(bf16[272,512]{1,0:T(8,128)(2,1)S(1)} %collective-permute-done.refs_0_), channel_id=1, source_target_pairs={{0,2},{1,3},{2,4},{3,5},{4,6},{5,7},{6,0},{7,1},{8,10},{9,11},{10,... | collective-permute-start | bytes 835592 | tf_op jit(solution)/shard_map/ppermute | solution.py:41
  15.5 9.7 %collective-permute-start.4 = (bf16[272,512]{1,0:T(8,128)(2,1)S(1)}, bf16[272,512]{1,0:T(8,128)(2,1)S(1)}, u32[]{:S(2)}, u32[]{:S(2)}) collective-permute-start(bf16[272,512]{1,0:T(8,128)(2,1)S(1)} %collective-permute-done.1.refs_1_), channel_id=1, source_target_pairs={{0,6},{1,7},{2,0},{3,1},{4,2},{5,3},{6,4},{7,5},{8,14},{9,15},{10,... | collective-permute-start | bytes 835592 | tf_op jit(solution)/shard_map/ppermute | solution.py:41
  18.6 3.5 %collective-permute-start.5 = (bf16[272,512]{1,0:T(8,128)(2,1)S(1)}, bf16[272,512]{1,0:T(8,128)(2,1)S(1)}, u32[]{:S(2)}, u32[]{:S(2)}) collective-permute-start(bf16[272,512]{1,0:T(8,128)(2,1)S(1)} %collective-permute-done.refs_0_), channel_id=1, source_target_pairs={{0,1},{1,0},{2,3},{3,2},{4,5},{5,4},{6,7},{7,6},{8,9},{9,8},{10,11... | collective-permute-start | bytes 835592 | tf_op jit(solution)/shard_map/ppermute | solution.py:41
  20.0 2.3 %collective-permute-start.6 = (bf16[272,512]{1,0:T(8,128)(2,1)S(1)}, bf16[272,512]{1,0:T(8,128)(2,1)S(1)}, u32[]{:S(2)}, u32[]{:S(2)}) collective-permute-start(bf16[272,512]{1,0:T(8,128)(2,1)S(1)} %collective-permute-done.1.refs_1_), channel_id=1, source_target_pairs={{0,1},{1,0},{2,3},{3,2},{4,5},{5,4},{6,7},{7,6},{8,9},{9,8},{10,11... | collective-permute-start | bytes 835592 | tf_op jit(solution)/shard_map/ppermute | solution.py:41
  21.4 2.3 %collective-permute-start.9 = (bf16[272,512]{1,0:T(8,128)(2,1)S(1)}, bf16[272,512]{1,0:T(8,128)(2,1)S(1)}, u32[]{:S(2)}, u32[]{:S(2)}) collective-permute-start(bf16[272,512]{1,0:T(8,128)(2,1)S(1)} %collective-permute-done.7.refs_2_), channel_id=1, source_target_pairs={{0,1},{1,0},{2,3},{3,2},{4,5},{5,4},{6,7},{7,6},{8,9},{9,8},{10,11... | collective-permute-start | bytes 835592 | tf_op jit(solution)/shard_map/ppermute | solution.py:41
  22.1 1.6 %collective-permute-start.10 = (bf16[272,512]{1,0:T(8,128)(2,1)S(1)}, bf16[272,512]{1,0:T(8,128)(2,1)S(1)}, u32[]{:S(2)}, u32[]{:S(2)}) collective-permute-start(bf16[272,512]{1,0:T(8,128)(2,1)S(1)} %collective-permute-done.8.refs_3_), channel_id=1, source_target_pairs={{0,1},{1,0},{2,3},{3,2},{4,5},{5,4},{6,7},{7,6},{8,9},{9,8},{10,11... | collective-permute-start | bytes 835592 | tf_op jit(solution)/shard_map/ppermute | solution.py:41
  25.2 1.9 %collective-permute-start.11 = (bf16[272,512]{1,0:T(8,128)(2,1)S(1)}, bf16[272,512]{1,0:T(8,128)(2,1)S(1)}, u32[]{:S(2)}, u32[]{:S(2)}) collective-permute-start(bf16[272,512]{1,0:T(8,128)(2,1)S(1)} %collective-permute-done.3.refs_0_), channel_id=1, source_target_pairs={{0,1},{1,0},{2,3},{3,2},{4,5},{5,4},{6,7},{7,6},{8,9},{9,8},{10,11... | collective-permute-start | bytes 835592 | tf_op jit(solution)/shard_map/ppermute | solution.py:41
  25.6 1.6 %collective-permute-start.12 = (bf16[272,512]{1,0:T(8,128)(2,1)S(1)}, bf16[272,512]{1,0:T(8,128)(2,1)S(1)}, u32[]{:S(2)}, u32[]{:S(2)}) collective-permute-start(bf16[272,512]{1,0:T(8,128)(2,1)S(1)} %collective-permute-done.4.refs_1_), channel_id=1, source_target_pairs={{0,1},{1,0},{2,3},{3,2},{4,5},{5,4},{6,7},{7,6},{8,9},{9,8},{10,11... | collective-permute-start | bytes 835592 | tf_op jit(solution)/shard_map/ppermute | solution.py:41
  28.2 9.5 %collective-permute-start.13 = (bf16[8,80,128]{2,1,0:T(8,128)(2,1)S(1)}, bf16[8,80,128]{2,1,0:T(8,128)(2,1)S(1)}, u32[]{:S(2)}, u32[]{:S(2)}) collective-permute-start(bf16[8,80,128]{2,1,0:T(8,128)(2,1)S(1)} %shard_map.64), channel_id=1, source_target_pairs={{0,16},{1,17},{2,18},{3,19},{4,20},{5,21},{6,22},{7,23},{8,24},{9,... | collective-permute-start | bytes 491528 | tf_op jit(solution)/shard_map/ppermute | solution.py:41
  33.4 7.5 %collective-permute-start.14 = (bf16[8,80,128]{2,1,0:T(8,128)(2,1)S(1)}, bf16[8,80,128]{2,1,0:T(8,128)(2,1)S(1)}, u32[]{:S(2)}, u32[]{:S(2)}) collective-permute-start(bf16[8,80,128]{2,1,0:T(8,128)(2,1)S(1)} %get-tuple-element.83), channel_id=1, source_target_pairs={{0,8},{1,9},{2,10},{3,11},{4,12},{5,13},{6,14},{7,15},{8,16},{9,17... | collective-permute-start | bytes 491528 | tf_op jit(solution)/shard_map/ppermute | solution.py:41
  34.1 6.7 %collective-permute-start.15 = (bf16[8,80,128]{2,1,0:T(8,128)(2,1)S(1)}, bf16[8,80,128]{2,1,0:T(8,128)(2,1)S(1)}, u32[]{:S(2)}, u32[]{:S(2)}) collective-permute-start(bf16[8,80,128]{2,1,0:T(8,128)(2,1)S(1)} %get-tuple-element.84), channel_id=1, source_target_pairs={{0,24},{1,25},{2,26},{3,27},{4,28},{5,29},{6,30},{7,31},{8,0},{9,1... | collective-permute-start | bytes 491528 | tf_op jit(solution)/shard_map/ppermute | solution.py:41
  59.6 3.8 %collective-permute-start.17 = (bf16[128,128]{1,0:T(8,128)(2,1)S(1)}, bf16[128,128]{1,0:T(8,128)(2,1)S(1)}, u32[]{:S(2)}, u32[]{:S(2)}) collective-permute-start(bf16[128,128]{1,0:T(8,128)(2,1)S(1)} %shard_map.67.own), channel_id=1, source_target_pairs={{0,31},{1,0},{2,1},{3,2},{4,3},{5,4},{6,5},{7,6},{8,7},{9,8},{10,9... | collective-permute-start | bytes 98312 | tf_op jit(solution)/shard_map/ppermute | solution.py:459
  61.8 6.7 %collective-permute-start.16 = (bf16[128,128]{1,0:T(8,128)(2,1)S(1)}, bf16[128,128]{1,0:T(8,128)(2,1)S(1)}, u32[]{:S(2)}, u32[]{:S(2)}) collective-permute-start(bf16[128,128]{1,0:T(8,128)(2,1)S(1)} %shard_map.67.own), channel_id=1, source_target_pairs={{0,1},{1,2},{2,3},{3,4},{4,5},{5,6},{6,7},{7,8},{8,9},{9,10},{10,1... | collective-permute-start | bytes 98312 | tf_op jit(solution)/shard_map/ppermute | solution.py:458

commit v9 on v8

--- a/solution.py
+++ b/solution.py
@@ -200,8 +200,7 @@
     lower = total[64:K]
     upper = jnp.where(lane < row, pltpu.roll(lower, 64, 1), total[0:64])
     diagonal = jnp.sum(jnp.where(lane == row + 64, lower, 0.0), axis=0, keepdims=True)
-    tail = jnp.where(lax.broadcasted_iota(jnp.int32, (16, K), 0) == 0, diagonal, total[K:])
-    return jnp.concatenate([upper, tail], axis=0)
+    return upper, diagonal, total[K : K + 1]
 
 
 def unpack(packed):
@@ -223,6 +222,8 @@
     table = ((0, low[...]), (1, high[...]))
     for out, shift in zip(outs, shifts):
         y = lax.rem(place + shift, Y)
+        tail_row = lax.broadcasted_iota(jnp.int32, (16, K), 0)
+        tail = jnp.zeros((16, K), F32)
         for i in range(2):
             span = slice(i * 256, i * 256 + 256)
             last = pick(table, picks[pl.ds(y, 1), :][:, span])
@@ -236,13 +237,18 @@
                 for side in range(2):
                     rows = jnp.concatenate([pair[side] for pair in pairs], axis=1)
                     total = lax.dot_general(rows, rows[:K], dims(1, 1), preferred_element_type=F32)
-                    out[i + 2 * half + 4 * side] = pack(total).astype(out.dtype)
+                    patch = i + 2 * half + 4 * side
+                    upper, diagonal, pull = pack(total)
+                    out[patch * 64 : patch * 64 + 64, :] = upper.astype(out.dtype)
+                    tail = jnp.where(tail_row == 2 * patch, diagonal, tail)
+                    tail = jnp.where(tail_row == 2 * patch + 1, pull, tail)
+        out[8 * 64 :, :] = tail.astype(out.dtype)
 
 
 def last_grams(shifts, dtype, *args):
     return pl.pallas_call(
         functools.partial(last_kernel, shifts),
-        out_shape=[jax.ShapeDtypeStruct((8, PACK, K), dtype)] * len(shifts),
+        out_shape=[jax.ShapeDtypeStruct((8 * 64 + 16, K), dtype)] * len(shifts),
         in_specs=in_vmem(len(args)),
         out_specs=in_vmem(len(shifts)),
         scratch_shapes=[pltpu.VMEM((Y, LOW), jnp.int32)],
@@ -252,14 +258,21 @@
 
 
 def sum_kernel(own, a, b, c, out):
-    others = a[...].astype(F32) + b[...].astype(F32) + c[...].astype(F32)
-    out[...] = (own[...] + others).astype(BF16)
+    def total(span):
+        return own[span, :] + (a[span, :].astype(F32) + b[span, :].astype(F32) + c[span, :].astype(F32))
+
+    tails = total(slice(8 * 64, 8 * 64 + 16))
+    first = lax.broadcasted_iota(jnp.int32, (16, K), 0) == 0
+    for patch in range(8):
+        out[patch, 0:64, :] = total(slice(patch * 64, patch * 64 + 64)).astype(BF16)
+        tail = jnp.where(first, tails[2 * patch : 2 * patch + 1], tails[2 * patch + 1 : 2 * patch + 2])
+        out[patch, 64:PACK, :] = tail.astype(BF16)
 
 
 def sum_parts(*args):
     return pl.pallas_call(
         sum_kernel,
-        out_shape=jax.ShapeDtypeStruct(args[0].shape, BF16),
+        out_shape=jax.ShapeDtypeStruct((8, PACK, K), BF16),
         in_specs=in_vmem(4),
         out_specs=in_vmem(1)[0],
         compiler_params=params(),
@@ -299,8 +312,9 @@
             both = product(newton, jnp.concatenate([iterate, inverse], axis=1))
             iterate, inverse = both[:, :K], both[:, K:]
         else:
+            shift = product(product(jnp.broadcast_to(pull, (16, K)), inverse), inverse)
+            shift = product(product(shift, newton), newton)[0:1] / frob
             inverse = product(newton, inverse)
-    shift = product(product(jnp.broadcast_to(pull, (16, K)), inverse), inverse)[0:1] / frob
     out[...] = (jnp.sqrt((K - 1.0) / frob) * inverse.T + shift).astype(BF16)
 
 
@@ -336,7 +350,7 @@
         in_specs=in_vmem(1),
         out_specs=in_vmem(2),
         compiler_params=params(),
-        cost_estimate=cost(SHORT),
+        cost_estimate=cost(LONG),
     )(state)
 
 

time: 70.5 us -> 71.2 us (level)
  waiting for transfers between devices: 12.2 us -> 13.1 us
    ppermute x16, waiting for transfers between devices: 6.15 us -> 7.03 us  [hop(): return lax.ppermute(value, 'grid', pairs)]
  transfers between devices with their start and end apart: 18 -> 18, of which waited for: 9 -> 7; matrix products, arithmetic and copies ran while one was open for 0% -> 0% of each run, Pallas kernels for 19% -> 19%
where the time goes in v9:
time: 71.2 us; the launch traced here: 71.1 us
  Pallas kernels  21.3 us (30%)
  starting transfers between devices  20 us (28%)
  blocking collectives  16.3 us (23%)
  waiting for transfers between devices  13.1 us (18%)
    ppermute x16, starting transfers between devices, hop(): return lax.ppermute(value, 'grid', pairs)  18 us
    all_to_all x1, blocking collectives, on_device(): parts = lax.all_to_all(parts, 'obs', 0, 0, tiled=True)  16.3 us
    pallas_call x6, Pallas kernels, pick_rows(): pl.pallas_call(functools.partial(pick_kernel, sources, len(args)), out_sh...  9.34 us
    ppermute x16, waiting for transfers between devices, hop(): return lax.ppermute(value, 'grid', pairs)  7.03 us
    ppermute x1, waiting for transfers between devices, on_device(): lax.ppermute(own, 'grid', [(j, (j + 1) % n_grid) for j in range(n_grid)])  5.06 us
    pallas_call x3, Pallas kernels, last_grams(): pl.pallas_call(functools.partial(last_kernel, shifts), out_shape=[jax.Sha...  4.02 us
    pallas_call x1, Pallas kernels, make_messages(): pl.pallas_call(message_kernel, out_shape=[jax.ShapeDtypeStruct(shape, BF1...  2.58 us
    pallas_call x1, Pallas kernels, transposed_weights(): pl.pallas_call(weights_kernel, out_shape=jax.ShapeDtypeStruct((K, K), BF1...  2.43 us
  transfers between devices with their start and end apart: 18, of which 7 were waited for; matrix products, arithmetic and copies ran while one was open for 0% of the time, Pallas kernels for 19%

profile of v9, /device:TPU:32, one launch (start us, length us, event | category | flops | bytes accessed | tf_op | source)
XLA Modules:
  0.0 71.1 jit_solution(8159515522610529505)
XLA Ops:
  0.0 2.6 %shard_map.55 = (bf16[272,512]{1,0:T(8,128)(2,1)}, bf16[272,512]{1,0:T(8,128)(2,1)}, bf16[544,512]{1,0:T(8,128)(2,1)}) custom-call(bf16[2048,128]{1,0:T(8,128)(2,1)} %departures.1, f32[2048]{0:T(1024)} %innovation.1, f32[2048]{0:T(1024)} %obs_weight.1, s32[64,256]{1,0:T(8,128)} %bitcast.3), custom_call_target="tpu_custom_call" | custom-call | flops 2000000000 | bytes 100000 | tf_op jit(solution)/shard_map/pallas_call | solution.py:131
  2.6 1.6 %collective-permute-start = (bf16[272,512]{1,0:T(8,128)(2,1)}, bf16[272,512]{1,0:T(8,128)(2,1)S(1)}, u32[]{:S(2)}, u32[]{:S(2)}) collective-permute-start(bf16[272,512]{1,0:T(8,128)(2,1)} %get-tuple-element.64), channel_id=1, source_target_pairs={{0,2},{1,3},{2,4},{3,5},{4,6},{5,7},{6,0},{7,1},{8,10},{9,11},{10,... | collective-permute-start | bytes 835592 | tf_op jit(solution)/shard_map/ppermute | solution.py:41
  4.2 1.7 %collective-permute-start.1 = (bf16[272,512]{1,0:T(8,128)(2,1)}, bf16[272,512]{1,0:T(8,128)(2,1)S(1)}, u32[]{:S(2)}, u32[]{:S(2)}) collective-permute-start(bf16[272,512]{1,0:T(8,128)(2,1)} %get-tuple-element.63), channel_id=1, source_target_pairs={{0,6},{1,7},{2,0},{3,1},{4,2},{5,3},{6,4},{7,5},{8,14},{9,15},{10,... | collective-permute-start | bytes 835592 | tf_op jit(solution)/shard_map/ppermute | solution.py:41
  5.9 0.0 collective-permute-start.2
  5.9 0.6 shard_map.57
  6.5 1.6 %collective-permute-done.2.refs_1_ = bf16[544,512]{1,0:T(8,128)(2,1)S(1)} collective-permute-done((bf16[544,512]{1,0:T(8,128)(2,1)}, bf16[544,512]{1,0:T(8,128)(2,1)S(1)}, u32[]{:S(2)}, u32[]{:S(2)}) %collective-permute-start.2) | collective-permute-done | bytes 557088 | tf_op jit(solution)/shard_map/ppermute | solution.py:41
  8.1 2.5 %shard_map.56 = (bf16[8,144,256]{2,1,0:T(8,128)(2,1)S(1)}, bf16[8,144,256]{2,1,0:T(8,128)(2,1)S(1)}) custom-call(bf16[544,512]{1,0:T(8,128)(2,1)S(1)} %copy-done, bf16[544,512]{1,0:T(8,128)(2,1)S(1)} %collective-permute-done.2.refs_1_), custom_call_target="tpu_custom_call" | custom-call | flops 1000000 | bytes 100000 | tf_op jit(solution)/shard_map/pallas_call | solution.py:182
  10.6 0.4 collective-permute-start.7
  11.0 3.0 %collective-permute-start.8 = (bf16[272,512]{1,0:T(8,128)(2,1)S(1)}, bf16[272,512]{1,0:T(8,128)(2,1)S(1)}, u32[]{:S(2)}, u32[]{:S(2)}) collective-permute-start(bf16[272,512]{1,0:T(8,128)(2,1)S(1)} %copy-done.2), channel_id=1, source_target_pairs={{0,6},{1,7},{2,0},{3,1},{4,2},{5,3},{6,4},{7,5},{8,14},{9,15},{10,... | collective-permute-start | bytes 835592 | tf_op jit(solution)/shard_map/ppermute | solution.py:41
  13.9 0.0 collective-permute-done.refs_0_
  13.9 0.0 collective-permute-done.1.refs_1_
  13.9 0.0 collective-permute-start.3
  14.0 3.2 %collective-permute-start.4 = (bf16[272,512]{1,0:T(8,128)(2,1)S(1)}, bf16[272,512]{1,0:T(8,128)(2,1)S(1)}, u32[]{:S(2)}, u32[]{:S(2)}) collective-permute-start(bf16[272,512]{1,0:T(8,128)(2,1)S(1)} %collective-permute-done.1.refs_1_), channel_id=1, source_target_pairs={{0,6},{1,7},{2,0},{3,1},{4,2},{5,3},{6,4},{7,5},{8,14},{9,15},{10,... | collective-permute-start | bytes 835592 | tf_op jit(solution)/shard_map/ppermute | solution.py:41
  17.2 1.4 %shard_map.58 = (bf16[8,144,256]{2,1,0:T(8,128)(2,1)S(1)}, bf16[8,144,256]{2,1,0:T(8,128)(2,1)S(1)}) custom-call(bf16[272,512]{1,0:T(8,128)(2,1)S(1)} %collective-permute-done.refs_0_, bf16[272,512]{1,0:T(8,128)(2,1)S(1)} %collective-permute-done.1.refs_1_), custom_call_target="tpu_custom_call" | custom-call | flops 1000000 | bytes 100000 | tf_op jit(solution)/shard_map/pallas_call | solution.py:182
  18.5 0.1 collective-permute-start.5
  18.6 2.8 %collective-permute-done.7.refs_2_ = bf16[272,512]{1,0:T(8,128)(2,1)S(1)} collective-permute-done((bf16[272,512]{1,0:T(8,128)(2,1)S(1)}, bf16[272,512]{1,0:T(8,128)(2,1)S(1)}, u32[]{:S(2)}, u32[]{:S(2)}) %collective-permute-start.7) | collective-permute-done | bytes 278560 | tf_op jit(solution)/shard_map/ppermute | solution.py:41
  21.4 0.0 collective-permute-start.6
  21.4 1.4 %shard_map.59 = (bf16[8,144,256]{2,1,0:T(8,128)(2,1)S(1)}, bf16[8,144,256]{2,1,0:T(8,128)(2,1)S(1)}) custom-call(bf16[272,512]{1,0:T(8,128)(2,1)S(1)} %collective-permute-done.refs_0_, bf16[272,512]{1,0:T(8,128)(2,1)S(1)} %collective-permute-done.1.refs_1_, bf16[272,512]{1,0:T(8,128)(2,1)S(1)} %collective-permute-done.7.refs_2_, ...), custom_call_target="tpu_custom_call" | custom-call | flops 60000002048 | bytes 100000 | tf_op jit(solution)/shard_map/pallas_call | solution.py:182
  22.8 0.8 %collective-permute-start.9 = (bf16[272,512]{1,0:T(8,128)(2,1)S(1)}, bf16[272,512]{1,0:T(8,128)(2,1)S(1)}, u32[]{:S(2)}, u32[]{:S(2)}) collective-permute-start(bf16[272,512]{1,0:T(8,128)(2,1)S(1)} %collective-permute-done.7.refs_2_), channel_id=1, source_target_pairs={{0,1},{1,0},{2,3},{3,2},{4,5},{5,4},{6,7},{7,6},{8,9},{9,8},{10,11... | collective-permute-start | bytes 835592 | tf_op jit(solution)/shard_map/ppermute | solution.py:41
  23.6 0.0 collective-permute-done.5.refs_0_
  23.6 0.1 collective-permute-start.10
  23.7 0.0 collective-permute-done.6.refs_1_
  23.7 1.4 %shard_map.60 = (bf16[8,144,256]{2,1,0:T(8,128)(2,1)S(1)}, bf16[8,144,256]{2,1,0:T(8,128)(2,1)S(1)}) custom-call(bf16[272,512]{1,0:T(8,128)(2,1)S(1)} %collective-permute-done.5.refs_0_, bf16[272,512]{1,0:T(8,128)(2,1)S(1)} %collective-permute-done.6.refs_1_), custom_call_target="tpu_custom_call" | custom-call | flops 60000002048 | bytes 100000 | tf_op jit(solution)/shard_map/pallas_call | solution.py:182
  25.1 0.1 collective-permute-done.10.refs_3_
  25.2 1.4 %shard_map.61 = (bf16[8,144,256]{2,1,0:T(8,128)(2,1)S(1)}, bf16[8,144,256]{2,1,0:T(8,128)(2,1)S(1)}) custom-call(bf16[272,512]{1,0:T(8,128)(2,1)S(1)} %collective-permute-done.5.refs_0_, bf16[272,512]{1,0:T(8,128)(2,1)S(1)} %collective-permute-done.6.refs_1_, bf16[272,512]{1,0:T(8,128)(2,1)S(1)} %collective-permute-done.9.refs_2_, ...), custom_call_target="tpu_custom_call" | custom-call | flops 1000000 | bytes 100000 | tf_op jit(solution)/shard_map/pallas_call | solution.py:182
  26.5 0.0 collective-permute-done.3.refs_0_
  26.6 0.4 collective-permute-start.11
  27.0 0.1 collective-permute-start.12
  27.2 1.4 %shard_map.62.same = bf16[8,144,256]{2,1,0:T(8,128)(2,1)S(1)} custom-call(bf16[272,512]{1,0:T(8,128)(2,1)S(1)} %collective-permute-done.3.refs_0_, bf16[272,512]{1,0:T(8,128)(2,1)S(1)} %collective-permute-done.4.refs_1_), custom_call_target="tpu_custom_call" | custom-call | flops 1000000 | bytes 100000 | tf_op jit(solution)/shard_map/pallas_call | solution.py:182
  28.5 0.0 collective-permute-done.11.low
  28.5 0.1 collective-permute-done.12.high
  28.6 1.1 %shard_map.64 = bf16[528,128]{1,0:T(8,128)(2,1)S(1)} custom-call(bf16[272,512]{1,0:T(8,128)(2,1)S(1)} %collective-permute-done.11.low, bf16[272,512]{1,0:T(8,128)(2,1)S(1)} %collective-permute-done.12.high, bf16[8,144,256]{2,1,0:T(8,128)(2,1)S(1)} %shard_map.62.same, bf16[8,144,256]{2,1,0:T(8,128)(2,1)S(1)} %get-tuple-element.77.rest_0_, ...), custom_call_target="tpu_custom_call" | custom-call | flops 1000000000 | bytes 100000 | tf_op jit(solution)/shard_map/pallas_call | solution.py:249
  29.7 3.3 %collective-permute-start.13 = (bf16[528,128]{1,0:T(8,128)(2,1)S(1)}, bf16[528,128]{1,0:T(8,128)(2,1)S(1)}, u32[]{:S(2)}, u32[]{:S(2)}) collective-permute-start(bf16[528,128]{1,0:T(8,128)(2,1)S(1)} %shard_map.64), channel_id=1, source_target_pairs={{0,16},{1,17},{2,18},{3,19},{4,20},{5,21},{6,22},{7,23},{8,24},{9,... | collective-permute-start | bytes 405512 | tf_op jit(solution)/shard_map/ppermute | solution.py:41
  33.0 1.9 %shard_map.65 = (bf16[528,128]{1,0:T(8,128)(2,1)S(1)}, bf16[528,128]{1,0:T(8,128)(2,1)S(1)}) custom-call(bf16[272,512]{1,0:T(8,128)(2,1)S(1)} %collective-permute-done.11.low, bf16[272,512]{1,0:T(8,128)(2,1)S(1)} %collective-permute-done.12.high, bf16[8,144,256]{2,1,0:T(8,128)(2,1)S(1)} %shard_map.62.same, ...), custom_call_target="tpu_custom_call" | custom-call | flops 2000000000 | bytes 100000 | tf_op jit(solution)/shard_map/pallas_call | solution.py:249
  34.9 0.8 %collective-permute-start.14 = (bf16[528,128]{1,0:T(8,128)(2,1)S(1)}, bf16[528,128]{1,0:T(8,128)(2,1)S(1)}, u32[]{:S(2)}, u32[]{:S(2)}) collective-permute-start(bf16[528,128]{1,0:T(8,128)(2,1)S(1)} %get-tuple-element.83), channel_id=1, source_target_pairs={{0,8},{1,9},{2,10},{3,11},{4,12},{5,13},{6,14},{7,15},{8,16},{9,17... | collective-permute-start | bytes 405512 | tf_op jit(solution)/shard_map/ppermute | solution.py:41
  35.6 2.6 %collective-permute-start.15 = (bf16[528,128]{1,0:T(8,128)(2,1)S(1)}, bf16[528,128]{1,0:T(8,128)(2,1)S(1)}, u32[]{:S(2)}, u32[]{:S(2)}) collective-permute-start(bf16[528,128]{1,0:T(8,128)(2,1)S(1)} %get-tuple-element.84), channel_id=1, source_target_pairs={{0,24},{1,25},{2,26},{3,27},{4,28},{5,29},{6,30},{7,31},{8,0},{9,1... | collective-permute-start | bytes 405512 | tf_op jit(solution)/shard_map/ppermute | solution.py:41
  38.2 1.1 %shard_map.63.own = f32[528,128]{1,0:T(8,128)S(1)} custom-call(bf16[272,512]{1,0:T(8,128)(2,1)S(1)} %collective-permute-done.11.low, bf16[272,512]{1,0:T(8,128)(2,1)S(1)} %collective-permute-done.12.high, bf16[8,144,256]{2,1,0:T(8,128)(2,1)S(1)} %shard_map.62.same, bf16[8,144,256]{2,1,0:T(8,128)(2,1)S(1)} %get-tuple-element.77.rest_0_, ...), custom_call_target="tpu_custom_call" | custom-call | flops 1000000000 | bytes 100000 | tf_op jit(solution)/shard_map/pallas_call | solution.py:249
  39.3 0.0 collective-permute-done.13.a
  39.3 2.4 %collective-permute-done.14.b = bf16[528,128]{1,0:T(8,128)(2,1)S(1)} collective-permute-done((bf16[528,128]{1,0:T(8,128)(2,1)S(1)}, bf16[528,128]{1,0:T(8,128)(2,1)S(1)}, u32[]{:S(2)}, u32[]{:S(2)}) %collective-permute-start.14) | collective-permute-done | bytes 135200 | tf_op jit(solution)/shard_map/ppermute | solution.py:41
  41.7 0.0 collective-permute-done.15.c
  41.7 0.1 shard_map.66
  41.8 16.3 %all_to_all.5.parts = bf16[8,80,128]{2,1,0:T(8,128)(2,1)S(1)} all-to-all(bf16[8,80,128]{2,1,0:T(8,128)(2,1)S(1)} %shard_map.66), channel_id=1, replica_groups=mesh['obs'=8,'grid'=32] {'obs'}, dimensions={0} | all-to-all | bytes 327680 | tf_op jit(solution)/shard_map/all_to_all | solution.py:469
  58.1 2.4 %shard_map.67.own = bf16[128,128]{1,0:T(8,128)(2,1)S(1)} custom-call(bf16[8,80,128]{2,1,0:T(8,128)(2,1)S(1)} %all_to_all.5.parts), custom_call_target="tpu_custom_call" | custom-call | flops 4000000000 | bytes 100000 | tf_op jit(solution)/shard_map/pallas_call | solution.py:322
  60.6 1.9 %collective-permute-start.17 = (bf16[128,128]{1,0:T(8,128)(2,1)S(1)}, bf16[128,128]{1,0:T(8,128)(2,1)S(1)}, u32[]{:S(2)}, u32[]{:S(2)}) collective-permute-start(bf16[128,128]{1,0:T(8,128)(2,1)S(1)} %shard_map.67.own), channel_id=1, source_target_pairs={{0,31},{1,0},{2,1},{3,2},{4,3},{5,4},{6,5},{7,6},{8,7},{9,8},{10,9... | collective-permute-start | bytes 98312 | tf_op jit(solution)/shard_map/ppermute | solution.py:473
  62.5 0.6 shard_map.68.part
  63.1 1.0 %collective-permute-done.17.right = bf16[128,128]{1,0:T(8,128)(2,1)S(1)} collective-permute-done((bf16[128,128]{1,0:T(8,128)(2,1)S(1)}, bf16[128,128]{1,0:T(8,128)(2,1)S(1)}, u32[]{:S(2)}, u32[]{:S(2)}) %collective-permute-start.17) | collective-permute-done | bytes 32800 | tf_op jit(solution)/shard_map/ppermute | solution.py:473
  64.1 5.1 %collective-permute-done.16.left = bf16[128,128]{1,0:T(8,128)(2,1)S(1)} collective-permute-done((bf16[128,128]{1,0:T(8,128)(2,1)S(1)}, bf16[128,128]{1,0:T(8,128)(2,1)S(1)}, u32[]{:S(2)}, u32[]{:S(2)}) %collective-permute-start.16) | collective-permute-done | bytes 32800 | tf_op jit(solution)/shard_map/ppermute | solution.py:472
  69.2 1.8 %shard_map.69 = bf16[48,128,128]{2,1,0:T(8,128)(2,1)} custom-call(bf16[128,128]{1,0:T(8,128)(2,1)S(1)} %collective-permute-done.16.left, bf16[128,128]{1,0:T(8,128)(2,1)S(1)} %collective-permute-done.17.right, f32[24,128,256]{2,1,0:T(8,128)S(1)} %shard_map.68.part, bf16[24,128,256]{2,1,0:T(8,128)(2,1)S(1)} %get-tuple-element.86.perturb), custom_call_target="tpu_custom_call" | custom-call | flops 2000000000 | bytes 100000 | tf_op jit(solution)/shard_map/pallas_call | solution.py:405
  (12 shorter events, 0.0 us)
Async XLA Ops:
  0.0 5.9 %copy-start.1 = (bf16[48,128,128]{2,1,0:T(8,128)(2,1)S(1)}, bf16[48,128,128]{2,1,0:T(8,128)(2,1)}, u32[]{:S(2)}) copy-start(bf16[48,128,128]{2,1,0:T(8,128)(2,1)} %state.1) | copy-start | bytes 4718596
  2.6 11.4 %collective-permute-start = (bf16[272,512]{1,0:T(8,128)(2,1)}, bf16[272,512]{1,0:T(8,128)(2,1)S(1)}, u32[]{:S(2)}, u32[]{:S(2)}) collective-permute-start(bf16[272,512]{1,0:T(8,128)(2,1)} %get-tuple-element.64), channel_id=1, source_target_pairs={{0,2},{1,3},{2,4},{3,5},{4,6},{5,7},{6,0},{7,1},{8,10},{9,11},{10,... | collective-permute-start | bytes 835592 | tf_op jit(solution)/shard_map/ppermute | solution.py:41
  4.2 9.8 %collective-permute-start.1 = (bf16[272,512]{1,0:T(8,128)(2,1)}, bf16[272,512]{1,0:T(8,128)(2,1)S(1)}, u32[]{:S(2)}, u32[]{:S(2)}) collective-permute-start(bf16[272,512]{1,0:T(8,128)(2,1)} %get-tuple-element.63), channel_id=1, source_target_pairs={{0,6},{1,7},{2,0},{3,1},{4,2},{5,3},{6,4},{7,5},{8,14},{9,15},{10,... | collective-permute-start | bytes 835592 | tf_op jit(solution)/shard_map/ppermute | solution.py:41
  5.9 2.2 %copy-start = (bf16[544,512]{1,0:T(8,128)(2,1)S(1)}, bf16[544,512]{1,0:T(8,128)(2,1)}, u32[]{:S(2)}) copy-start(bf16[544,512]{1,0:T(8,128)(2,1)} %get-tuple-element.48.refs_0_) | copy-start | bytes 1671172
  5.9 4.7 %copy-start.3 = (bf16[272,512]{1,0:T(8,128)(2,1)S(1)}, bf16[272,512]{1,0:T(8,128)(2,1)}, u32[]{:S(2)}) copy-start(bf16[272,512]{1,0:T(8,128)(2,1)} %get-tuple-element.63) | copy-start | bytes 835588
  5.9 5.1 %copy-start.2 = (bf16[272,512]{1,0:T(8,128)(2,1)S(1)}, bf16[272,512]{1,0:T(8,128)(2,1)}, u32[]{:S(2)}) copy-start(bf16[272,512]{1,0:T(8,128)(2,1)} %get-tuple-element.64) | copy-start | bytes 835588
  5.9 2.2 %collective-permute-start.2 = (bf16[544,512]{1,0:T(8,128)(2,1)}, bf16[544,512]{1,0:T(8,128)(2,1)S(1)}, u32[]{:S(2)}, u32[]{:S(2)}) collective-permute-start(bf16[544,512]{1,0:T(8,128)(2,1)} %get-tuple-element.48.refs_0_), channel_id=1, source_target_pairs={{0,1},{1,0},{2,3},{3,2},{4,5},{5,4},{6,7},{7,6},{8,9},{9,8},{10,11... | collective-permute-start | bytes 1671176 | tf_op jit(solution)/shard_map/ppermute | solution.py:41
  10.6 10.8 %collective-permute-start.7 = (bf16[272,512]{1,0:T(8,128)(2,1)S(1)}, bf16[272,512]{1,0:T(8,128)(2,1)S(1)}, u32[]{:S(2)}, u32[]{:S(2)}) collective-permute-start(bf16[272,512]{1,0:T(8,128)(2,1)S(1)} %copy-done.3), channel_id=1, source_target_pairs={{0,2},{1,3},{2,4},{3,5},{4,6},{5,7},{6,0},{7,1},{8,10},{9,11},{10,... | collective-permute-start | bytes 835592 | tf_op jit(solution)/shard_map/ppermute | solution.py:41
  11.0 10.4 %collective-permute-start.8 = (bf16[272,512]{1,0:T(8,128)(2,1)S(1)}, bf16[272,512]{1,0:T(8,128)(2,1)S(1)}, u32[]{:S(2)}, u32[]{:S(2)}) collective-permute-start(bf16[272,512]{1,0:T(8,128)(2,1)S(1)} %copy-done.2), channel_id=1, source_target_pairs={{0,6},{1,7},{2,0},{3,1},{4,2},{5,3},{6,4},{7,5},{8,14},{9,15},{10,... | collective-permute-start | bytes 835592 | tf_op jit(solution)/shard_map/ppermute | solution.py:41
  13.9 12.6 %collective-permute-start.3 = (bf16[272,512]{1,0:T(8,128)(2,1)S(1)}, bf16[272,512]{1,0:T(8,128)(2,1)S(1)}, u32[]{:S(2)}, u32[]{:S(2)}) collective-permute-start(bf16[272,512]{1,0:T(8,128)(2,1)S(1)} %collective-permute-done.refs_0_), channel_id=1, source_target_pairs={{0,2},{1,3},{2,4},{3,5},{4,6},{5,7},{6,0},{7,1},{8,10},{9,11},{10,... | collective-permute-start | bytes 835592 | tf_op jit(solution)/shard_map/ppermute | solution.py:41
  14.0 12.6 %collective-permute-start.4 = (bf16[272,512]{1,0:T(8,128)(2,1)S(1)}, bf16[272,512]{1,0:T(8,128)(2,1)S(1)}, u32[]{:S(2)}, u32[]{:S(2)}) collective-permute-start(bf16[272,512]{1,0:T(8,128)(2,1)S(1)} %collective-permute-done.1.refs_1_), channel_id=1, source_target_pairs={{0,6},{1,7},{2,0},{3,1},{4,2},{5,3},{6,4},{7,5},{8,14},{9,15},{10,... | collective-permute-start | bytes 835592 | tf_op jit(solution)/shard_map/ppermute | solution.py:41
  18.5 5.0 %collective-permute-start.5 = (bf16[272,512]{1,0:T(8,128)(2,1)S(1)}, bf16[272,512]{1,0:T(8,128)(2,1)S(1)}, u32[]{:S(2)}, u32[]{:S(2)}) collective-permute-start(bf16[272,512]{1,0:T(8,128)(2,1)S(1)} %collective-permute-done.refs_0_), channel_id=1, source_target_pairs={{0,1},{1,0},{2,3},{3,2},{4,5},{5,4},{6,7},{7,6},{8,9},{9,8},{10,11... | collective-permute-start | bytes 835592 | tf_op jit(solution)/shard_map/ppermute | solution.py:41
  21.4 2.3 %collective-permute-start.6 = (bf16[272,512]{1,0:T(8,128)(2,1)S(1)}, bf16[272,512]{1,0:T(8,128)(2,1)S(1)}, u32[]{:S(2)}, u32[]{:S(2)}) collective-permute-start(bf16[272,512]{1,0:T(8,128)(2,1)S(1)} %collective-permute-done.1.refs_1_), channel_id=1, source_target_pairs={{0,1},{1,0},{2,3},{3,2},{4,5},{5,4},{6,7},{7,6},{8,9},{9,8},{10,11... | collective-permute-start | bytes 835592 | tf_op jit(solution)/shard_map/ppermute | solution.py:41
  22.8 2.3 %collective-permute-start.9 = (bf16[272,512]{1,0:T(8,128)(2,1)S(1)}, bf16[272,512]{1,0:T(8,128)(2,1)S(1)}, u32[]{:S(2)}, u32[]{:S(2)}) collective-permute-start(bf16[272,512]{1,0:T(8,128)(2,1)S(1)} %collective-permute-done.7.refs_2_), channel_id=1, source_target_pairs={{0,1},{1,0},{2,3},{3,2},{4,5},{5,4},{6,7},{7,6},{8,9},{9,8},{10,11... | collective-permute-start | bytes 835592 | tf_op jit(solution)/shard_map/ppermute | solution.py:41
  23.6 1.6 %collective-permute-start.10 = (bf16[272,512]{1,0:T(8,128)(2,1)S(1)}, bf16[272,512]{1,0:T(8,128)(2,1)S(1)}, u32[]{:S(2)}, u32[]{:S(2)}) collective-permute-start(bf16[272,512]{1,0:T(8,128)(2,1)S(1)} %collective-permute-done.8.refs_3_), channel_id=1, source_target_pairs={{0,1},{1,0},{2,3},{3,2},{4,5},{5,4},{6,7},{7,6},{8,9},{9,8},{10,11... | collective-permute-start | bytes 835592 | tf_op jit(solution)/shard_map/ppermute | solution.py:41
  26.6 1.9 %collective-permute-start.11 = (bf16[272,512]{1,0:T(8,128)(2,1)S(1)}, bf16[272,512]{1,0:T(8,128)(2,1)S(1)}, u32[]{:S(2)}, u32[]{:S(2)}) collective-permute-start(bf16[272,512]{1,0:T(8,128)(2,1)S(1)} %collective-permute-done.3.refs_0_), channel_id=1, source_target_pairs={{0,1},{1,0},{2,3},{3,2},{4,5},{5,4},{6,7},{7,6},{8,9},{9,8},{10,11... | collective-permute-start | bytes 835592 | tf_op jit(solution)/shard_map/ppermute | solution.py:41
  27.0 1.6 %collective-permute-start.12 = (bf16[272,512]{1,0:T(8,128)(2,1)S(1)}, bf16[272,512]{1,0:T(8,128)(2,1)S(1)}, u32[]{:S(2)}, u32[]{:S(2)}) collective-permute-start(bf16[272,512]{1,0:T(8,128)(2,1)S(1)} %collective-permute-done.4.refs_1_), channel_id=1, source_target_pairs={{0,1},{1,0},{2,3},{3,2},{4,5},{5,4},{6,7},{7,6},{8,9},{9,8},{10,11... | collective-permute-start | bytes 835592 | tf_op jit(solution)/shard_map/ppermute | solution.py:41
  29.7 9.6 %collective-permute-start.13 = (bf16[528,128]{1,0:T(8,128)(2,1)S(1)}, bf16[528,128]{1,0:T(8,128)(2,1)S(1)}, u32[]{:S(2)}, u32[]{:S(2)}) collective-permute-start(bf16[528,128]{1,0:T(8,128)(2,1)S(1)} %shard_map.64), channel_id=1, source_target_pairs={{0,16},{1,17},{2,18},{3,19},{4,20},{5,21},{6,22},{7,23},{8,24},{9,... | collective-permute-start | bytes 405512 | tf_op jit(solution)/shard_map/ppermute | solution.py:41
  34.9 6.8 %collective-permute-start.14 = (bf16[528,128]{1,0:T(8,128)(2,1)S(1)}, bf16[528,128]{1,0:T(8,128)(2,1)S(1)}, u32[]{:S(2)}, u32[]{:S(2)}) collective-permute-start(bf16[528,128]{1,0:T(8,128)(2,1)S(1)} %get-tuple-element.83), channel_id=1, source_target_pairs={{0,8},{1,9},{2,10},{3,11},{4,12},{5,13},{6,14},{7,15},{8,16},{9,17... | collective-permute-start | bytes 405512 | tf_op jit(solution)/shard_map/ppermute | solution.py:41
  35.6 6.1 %collective-permute-start.15 = (bf16[528,128]{1,0:T(8,128)(2,1)S(1)}, bf16[528,128]{1,0:T(8,128)(2,1)S(1)}, u32[]{:S(2)}, u32[]{:S(2)}) collective-permute-start(bf16[528,128]{1,0:T(8,128)(2,1)S(1)} %get-tuple-element.84), channel_id=1, source_target_pairs={{0,24},{1,25},{2,26},{3,27},{4,28},{5,29},{6,30},{7,31},{8,0},{9,1... | collective-permute-start | bytes 405512 | tf_op jit(solution)/shard_map/ppermute | solution.py:41
  60.6 3.5 %collective-permute-start.17 = (bf16[128,128]{1,0:T(8,128)(2,1)S(1)}, bf16[128,128]{1,0:T(8,128)(2,1)S(1)}, u32[]{:S(2)}, u32[]{:S(2)}) collective-permute-start(bf16[128,128]{1,0:T(8,128)(2,1)S(1)} %shard_map.67.own), channel_id=1, source_target_pairs={{0,31},{1,0},{2,1},{3,2},{4,3},{5,4},{6,5},{7,6},{8,7},{9,8},{10,9... | collective-permute-start | bytes 98312 | tf_op jit(solution)/shard_map/ppermute | solution.py:473
  62.5 6.7 %collective-permute-start.16 = (bf16[128,128]{1,0:T(8,128)(2,1)S(1)}, bf16[128,128]{1,0:T(8,128)(2,1)S(1)}, u32[]{:S(2)}, u32[]{:S(2)}) collective-permute-start(bf16[128,128]{1,0:T(8,128)(2,1)S(1)} %shard_map.67.own), channel_id=1, source_target_pairs={{0,1},{1,2},{2,3},{3,4},{4,5},{5,6},{6,7},{7,8},{8,9},{9,10},{10,1... | collective-permute-start | bytes 98312 | tf_op jit(solution)/shard_map/ppermute | solution.py:472

commit v10 on v9

--- a/solution.py
+++ b/solution.py
@@ -71,7 +71,7 @@
 
 def message_kernel(departures, innovation, obs_weight, send_rows, *refs):
     outs, (rows, innov, weight, picks, turned) = refs[:3], refs[3:8]
-    built, (in_sems, out_sems) = refs[8:11], refs[11:]
+    built, in_sems = outs, refs[8]
     small = ((send_rows, picks), (obs_weight, weight), (innovation, innov))
     small = [pltpu.make_async_copy(*pair, in_sems.at[i]) for i, pair in enumerate(small)]
     large = []
@@ -96,10 +96,9 @@
     root = jnp.sqrt(weight[...].reshape(1, BLOCKS * LOW))
     scaled = innov[...].reshape(1, BLOCKS * LOW) * root
     blank = jnp.zeros((2, LOW), F32)
-    both, out_both = built[2], outs[2]
-    copies = []
+    both = built[2]
     for half in range(2):
-        one, out_one = built[half], outs[half]
+        one = built[half]
         at = half * HALF
         innovs = []
         for block in range(2):
@@ -114,15 +113,6 @@
         next_one = groups[2:4] if half == 0 else groups[6:8]
         one[2 * K :, :] = jnp.concatenate(top + next_one, axis=0).astype(BF16)
         both[at + 2 * K : at + HALF, :] = jnp.concatenate(top + groups[0:2], axis=0).astype(BF16)
-        copies.append(pltpu.make_async_copy(one, out_one, out_sems.at[half]))
-        span = pl.ds(at, HALF)
-        copies.append(
-            pltpu.make_async_copy(both.at[span], out_both.at[span], out_sems.at[2 + half])
-        )
-        for copy in copies[-2:]:
-            copy.start()
-    for copy in copies:
-        copy.wait()
 
 
 def make_messages(*args):
@@ -132,14 +122,13 @@
         message_kernel,
         out_shape=[jax.ShapeDtypeStruct(shape, BF16) for shape in shapes],
         in_specs=[hbm] * 4,
-        out_specs=[hbm] * 3,
+        out_specs=in_vmem(3),
         scratch_shapes=[pltpu.VMEM(arg.shape, arg.dtype) for arg in args]
         + [pltpu.VMEM(args[3].shape[::-1], jnp.int32)]
-        + [pltpu.VMEM(shape, BF16) for shape in shapes]
-        + [pltpu.SemaphoreType.DMA((3 + BLOCKS,)), pltpu.SemaphoreType.DMA((4,))],
-        compiler_params=pltpu.CompilerParams(vmem_limit_bytes=60 * 1024 * 1024),
+        + [pltpu.SemaphoreType.DMA((3 + BLOCKS,))],
+        compiler_params=pltpu.CompilerParams(vmem_limit_bytes=VMEM),
         cost_estimate=cost(2e9),
-    )(*args)
+    )(*[pltpu.with_memory_space_constraint(arg, pltpu.HBM) for arg in args])
 
 
 def pick(parts, picks):
@@ -312,9 +301,8 @@
             both = product(newton, jnp.concatenate([iterate, inverse], axis=1))
             iterate, inverse = both[:, :K], both[:, K:]
         else:
-            shift = product(product(jnp.broadcast_to(pull, (16, K)), inverse), inverse)
-            shift = product(product(shift, newton), newton)[0:1] / frob
             inverse = product(newton, inverse)
+    shift = product(product(jnp.broadcast_to(pull, (16, K)), inverse), inverse)[0:1] / frob
     out[...] = (jnp.sqrt((K - 1.0) / frob) * inverse.T + shift).astype(BF16)
 
 
@@ -427,8 +415,8 @@
         ((whole(0), (0, 0, 8), None), (whole(1), (1, 0, 12), None)), SHORT, near, other
     )
     mean, perturb = perturbations(state)
-    low_half, high_half, found, mean, perturb = lax.optimization_barrier(
-        (low_half, high_half, found, mean, perturb)
+    low_half, high_half, mean, perturb = lax.optimization_barrier(
+        (low_half, high_half, mean, perturb)
     )
     left_more = hop(high_half, 0, 1, 0)
     right_more = hop(low_half, 0, -1, 0)

time: 71.2 us -> 68.2 us (0.958)
  waiting for transfers between devices: 13.1 us -> 11.2 us
  Pallas kernels: 21.3 us -> 20.4 us
    ppermute x16, waiting for transfers between devices: 7.03 us -> 5.14 us  [hop(): return lax.ppermute(value, 'grid', pairs)]
    pallas_call x1, Pallas kernels: 2.58 us -> 1.75 us  [make_messages(): pl.pallas_call(message_kernel, out_shape=[jax.ShapeDtypeStruct(shape, BF1...]
  transfers between devices with their start and end apart: 18 -> 18, of which waited for: 7 -> 9; matrix products, arithmetic and copies ran while one was open for 0% -> 0% of each run, Pallas kernels for 19% -> 20%
where the time goes in v10:
time: 68.2 us; the launch traced here: 68 us
  Pallas kernels  20.4 us (30%)
  starting transfers between devices  19.7 us (29%)
  blocking collectives  16.3 us (24%)
  waiting for transfers between devices  11.2 us (16%)
    ppermute x16, starting transfers between devices, hop(): return lax.ppermute(value, 'grid', pairs)  17.9 us
    all_to_all x1, blocking collectives, on_device(): parts = lax.all_to_all(parts, 'obs', 0, 0, tiled=True)  16.3 us
    pallas_call x6, Pallas kernels, pick_rows(): pl.pallas_call(functools.partial(pick_kernel, sources, len(args)), out_sh...  9.35 us
    ppermute x16, waiting for transfers between devices, hop(): return lax.ppermute(value, 'grid', pairs)  5.14 us
    ppermute x1, waiting for transfers between devices, on_device(): lax.ppermute(own, 'grid', [(j, (j + 1) % n_grid) for j in range(n_grid)])  5.06 us
    pallas_call x3, Pallas kernels, last_grams(): pl.pallas_call(functools.partial(last_kernel, shifts), out_shape=[jax.Sha...  4.02 us
    pallas_call x1, Pallas kernels, transposed_weights(): pl.pallas_call(weights_kernel, out_shape=jax.ShapeDtypeStruct((K, K), BF1...  2.34 us
    ppermute x1, starting transfers between devices, on_device(): lax.ppermute(own, 'grid', [(j, (j - 1) % n_grid) for j in range(n_grid)])  1.8 us
  transfers between devices with their start and end apart: 18, of which 9 were waited for; matrix products, arithmetic and copies ran while one was open for 0% of the time, Pallas kernels for 20%

profile of v10, /device:TPU:32, one launch (start us, length us, event | category | flops | bytes accessed | tf_op | source)
XLA Modules:
  0.0 68.0 jit_solution(3631737163983456434)
XLA Ops:
  0.0 1.8 %shard_map.55 = (bf16[272,512]{1,0:T(8,128)(2,1)S(1)}, bf16[272,512]{1,0:T(8,128)(2,1)S(1)}, bf16[544,512]{1,0:T(8,128)(2,1)S(1)}) custom-call(bf16[2048,128]{1,0:T(8,128)(2,1)} %departures.1, f32[2048]{0:T(1024)} %innovation.1, f32[2048]{0:T(1024)} %obs_weight.1, s32[64,256]{1,0:T(8,128)} %bitcast.3), custom_call_target="tpu_custom_call" | custom-call | flops 2000000000 | bytes 100000 | tf_op jit(solution)/shard_map/pallas_call | solution.py:121
  1.8 1.6 %collective-permute-start = (bf16[272,512]{1,0:T(8,128)(2,1)S(1)}, bf16[272,512]{1,0:T(8,128)(2,1)S(1)}, u32[]{:S(2)}, u32[]{:S(2)}) collective-permute-start(bf16[272,512]{1,0:T(8,128)(2,1)S(1)} %get-tuple-element.60), channel_id=1, source_target_pairs={{0,2},{1,3},{2,4},{3,5},{4,6},{5,7},{6,0},{7,1},{8,10},{9,11},{10,... | collective-permute-start | bytes 835592 | tf_op jit(solution)/shard_map/ppermute | solution.py:41
  3.3 1.7 %collective-permute-start.1 = (bf16[272,512]{1,0:T(8,128)(2,1)S(1)}, bf16[272,512]{1,0:T(8,128)(2,1)S(1)}, u32[]{:S(2)}, u32[]{:S(2)}) collective-permute-start(bf16[272,512]{1,0:T(8,128)(2,1)S(1)} %get-tuple-element.59), channel_id=1, source_target_pairs={{0,6},{1,7},{2,0},{3,1},{4,2},{5,3},{6,4},{7,5},{8,14},{9,15},{10,... | collective-permute-start | bytes 835592 | tf_op jit(solution)/shard_map/ppermute | solution.py:41
  5.1 0.0 collective-permute-start.2
  5.1 0.6 shard_map.57
  5.6 0.4 collective-permute-start.7
  6.0 3.0 %collective-permute-start.8 = (bf16[272,512]{1,0:T(8,128)(2,1)S(1)}, bf16[272,512]{1,0:T(8,128)(2,1)S(1)}, u32[]{:S(2)}, u32[]{:S(2)}) collective-permute-start(bf16[272,512]{1,0:T(8,128)(2,1)S(1)} %get-tuple-element.60), channel_id=1, source_target_pairs={{0,6},{1,7},{2,0},{3,1},{4,2},{5,3},{6,4},{7,5},{8,14},{9,15},{10,... | collective-permute-start | bytes 835592 | tf_op jit(solution)/shard_map/ppermute | solution.py:41
  9.0 2.5 %shard_map.56 = (bf16[8,144,256]{2,1,0:T(8,128)(2,1)S(1)}, bf16[8,144,256]{2,1,0:T(8,128)(2,1)S(1)}) custom-call(bf16[544,512]{1,0:T(8,128)(2,1)S(1)} %get-tuple-element.46.refs_0_, bf16[544,512]{1,0:T(8,128)(2,1)S(1)} %collective-permute-done.2.refs_1_), custom_call_target="tpu_custom_call" | custom-call | flops 1000000 | bytes 100000 | tf_op jit(solution)/shard_map/pallas_call | solution.py:171
  11.5 1.1 %collective-permute-done.refs_0_ = bf16[272,512]{1,0:T(8,128)(2,1)S(1)} collective-permute-done((bf16[272,512]{1,0:T(8,128)(2,1)S(1)}, bf16[272,512]{1,0:T(8,128)(2,1)S(1)}, u32[]{:S(2)}, u32[]{:S(2)}) %collective-permute-start) | collective-permute-done | bytes 278560 | tf_op jit(solution)/shard_map/ppermute | solution.py:41
  12.6 0.3 collective-permute-done.1.refs_1_
  12.9 1.5 %collective-permute-start.3 = (bf16[272,512]{1,0:T(8,128)(2,1)S(1)}, bf16[272,512]{1,0:T(8,128)(2,1)S(1)}, u32[]{:S(2)}, u32[]{:S(2)}) collective-permute-start(bf16[272,512]{1,0:T(8,128)(2,1)S(1)} %collective-permute-done.refs_0_), channel_id=1, source_target_pairs={{0,2},{1,3},{2,4},{3,5},{4,6},{5,7},{6,0},{7,1},{8,10},{9,11},{10,... | collective-permute-start | bytes 835592 | tf_op jit(solution)/shard_map/ppermute | solution.py:41
  14.4 1.7 %collective-permute-start.4 = (bf16[272,512]{1,0:T(8,128)(2,1)S(1)}, bf16[272,512]{1,0:T(8,128)(2,1)S(1)}, u32[]{:S(2)}, u32[]{:S(2)}) collective-permute-start(bf16[272,512]{1,0:T(8,128)(2,1)S(1)} %collective-permute-done.1.refs_1_), channel_id=1, source_target_pairs={{0,6},{1,7},{2,0},{3,1},{4,2},{5,3},{6,4},{7,5},{8,14},{9,15},{10,... | collective-permute-start | bytes 835592 | tf_op jit(solution)/shard_map/ppermute | solution.py:41
  16.2 1.4 %shard_map.58 = (bf16[8,144,256]{2,1,0:T(8,128)(2,1)S(1)}, bf16[8,144,256]{2,1,0:T(8,128)(2,1)S(1)}) custom-call(bf16[272,512]{1,0:T(8,128)(2,1)S(1)} %collective-permute-done.refs_0_, bf16[272,512]{1,0:T(8,128)(2,1)S(1)} %collective-permute-done.1.refs_1_), custom_call_target="tpu_custom_call" | custom-call | flops 1000000 | bytes 100000 | tf_op jit(solution)/shard_map/pallas_call | solution.py:171
  17.5 0.1 collective-permute-start.5
  17.6 0.9 %collective-permute-done.7.refs_2_ = bf16[272,512]{1,0:T(8,128)(2,1)S(1)} collective-permute-done((bf16[272,512]{1,0:T(8,128)(2,1)S(1)}, bf16[272,512]{1,0:T(8,128)(2,1)S(1)}, u32[]{:S(2)}, u32[]{:S(2)}) %collective-permute-start.7) | collective-permute-done | bytes 278560 | tf_op jit(solution)/shard_map/ppermute | solution.py:41
  18.6 0.0 collective-permute-start.6
  18.6 0.3 collective-permute-done.8.refs_3_
  18.9 1.4 %shard_map.59 = (bf16[8,144,256]{2,1,0:T(8,128)(2,1)S(1)}, bf16[8,144,256]{2,1,0:T(8,128)(2,1)S(1)}) custom-call(bf16[272,512]{1,0:T(8,128)(2,1)S(1)} %collective-permute-done.refs_0_, bf16[272,512]{1,0:T(8,128)(2,1)S(1)} %collective-permute-done.1.refs_1_, bf16[272,512]{1,0:T(8,128)(2,1)S(1)} %collective-permute-done.7.refs_2_, ...), custom_call_target="tpu_custom_call" | custom-call | flops 60000002048 | bytes 100000 | tf_op jit(solution)/shard_map/pallas_call | solution.py:171
  20.3 0.5 collective-permute-start.9
  20.7 0.0 collective-permute-done.5.refs_0_
  20.7 0.3 collective-permute-start.10
  21.1 0.0 collective-permute-done.6.refs_1_
  21.1 1.4 %shard_map.60 = (bf16[8,144,256]{2,1,0:T(8,128)(2,1)S(1)}, bf16[8,144,256]{2,1,0:T(8,128)(2,1)S(1)}) custom-call(bf16[272,512]{1,0:T(8,128)(2,1)S(1)} %collective-permute-done.5.refs_0_, bf16[272,512]{1,0:T(8,128)(2,1)S(1)} %collective-permute-done.6.refs_1_), custom_call_target="tpu_custom_call" | custom-call | flops 60000002048 | bytes 100000 | tf_op jit(solution)/shard_map/pallas_call | solution.py:171
  22.4 0.1 collective-permute-done.10.refs_3_
  22.5 1.4 %shard_map.61 = (bf16[8,144,256]{2,1,0:T(8,128)(2,1)S(1)}, bf16[8,144,256]{2,1,0:T(8,128)(2,1)S(1)}) custom-call(bf16[272,512]{1,0:T(8,128)(2,1)S(1)} %collective-permute-done.5.refs_0_, bf16[272,512]{1,0:T(8,128)(2,1)S(1)} %collective-permute-done.6.refs_1_, bf16[272,512]{1,0:T(8,128)(2,1)S(1)} %collective-permute-done.9.refs_2_, ...), custom_call_target="tpu_custom_call" | custom-call | flops 1000000 | bytes 100000 | tf_op jit(solution)/shard_map/pallas_call | solution.py:171
  23.9 0.0 collective-permute-done.3.refs_0_
  23.9 0.3 collective-permute-start.11
  24.2 0.3 collective-permute-start.12
  24.5 1.4 %shard_map.62.same = bf16[8,144,256]{2,1,0:T(8,128)(2,1)S(1)} custom-call(bf16[272,512]{1,0:T(8,128)(2,1)S(1)} %collective-permute-done.3.refs_0_, bf16[272,512]{1,0:T(8,128)(2,1)S(1)} %collective-permute-done.4.refs_1_), custom_call_target="tpu_custom_call" | custom-call | flops 1000000 | bytes 100000 | tf_op jit(solution)/shard_map/pallas_call | solution.py:171
  25.9 0.0 collective-permute-done.11.low
  25.9 0.1 collective-permute-done.12.high
  25.9 1.1 %shard_map.64 = bf16[528,128]{1,0:T(8,128)(2,1)S(1)} custom-call(bf16[272,512]{1,0:T(8,128)(2,1)S(1)} %collective-permute-done.11.low, bf16[272,512]{1,0:T(8,128)(2,1)S(1)} %collective-permute-done.12.high, bf16[8,144,256]{2,1,0:T(8,128)(2,1)S(1)} %shard_map.62.same, bf16[8,144,256]{2,1,0:T(8,128)(2,1)S(1)} %get-tuple-element.73.rest_0_, ...), custom_call_target="tpu_custom_call" | custom-call | flops 1000000000 | bytes 100000 | tf_op jit(solution)/shard_map/pallas_call | solution.py:238
  27.0 3.3 %collective-permute-start.13 = (bf16[528,128]{1,0:T(8,128)(2,1)S(1)}, bf16[528,128]{1,0:T(8,128)(2,1)S(1)}, u32[]{:S(2)}, u32[]{:S(2)}) collective-permute-start(bf16[528,128]{1,0:T(8,128)(2,1)S(1)} %shard_map.64), channel_id=1, source_target_pairs={{0,16},{1,17},{2,18},{3,19},{4,20},{5,21},{6,22},{7,23},{8,24},{9,... | collective-permute-start | bytes 405512 | tf_op jit(solution)/shard_map/ppermute | solution.py:41
  30.3 1.9 %shard_map.65 = (bf16[528,128]{1,0:T(8,128)(2,1)S(1)}, bf16[528,128]{1,0:T(8,128)(2,1)S(1)}) custom-call(bf16[272,512]{1,0:T(8,128)(2,1)S(1)} %collective-permute-done.11.low, bf16[272,512]{1,0:T(8,128)(2,1)S(1)} %collective-permute-done.12.high, bf16[8,144,256]{2,1,0:T(8,128)(2,1)S(1)} %shard_map.62.same, ...), custom_call_target="tpu_custom_call" | custom-call | flops 2000000000 | bytes 100000 | tf_op jit(solution)/shard_map/pallas_call | solution.py:238
  32.2 0.8 %collective-permute-start.14 = (bf16[528,128]{1,0:T(8,128)(2,1)S(1)}, bf16[528,128]{1,0:T(8,128)(2,1)S(1)}, u32[]{:S(2)}, u32[]{:S(2)}) collective-permute-start(bf16[528,128]{1,0:T(8,128)(2,1)S(1)} %get-tuple-element.79), channel_id=1, source_target_pairs={{0,8},{1,9},{2,10},{3,11},{4,12},{5,13},{6,14},{7,15},{8,16},{9,17... | collective-permute-start | bytes 405512 | tf_op jit(solution)/shard_map/ppermute | solution.py:41
  32.9 2.6 %collective-permute-start.15 = (bf16[528,128]{1,0:T(8,128)(2,1)S(1)}, bf16[528,128]{1,0:T(8,128)(2,1)S(1)}, u32[]{:S(2)}, u32[]{:S(2)}) collective-permute-start(bf16[528,128]{1,0:T(8,128)(2,1)S(1)} %get-tuple-element.80), channel_id=1, source_target_pairs={{0,24},{1,25},{2,26},{3,27},{4,28},{5,29},{6,30},{7,31},{8,0},{9,1... | collective-permute-start | bytes 405512 | tf_op jit(solution)/shard_map/ppermute | solution.py:41
  35.5 1.1 %shard_map.63.own = f32[528,128]{1,0:T(8,128)S(1)} custom-call(bf16[272,512]{1,0:T(8,128)(2,1)S(1)} %collective-permute-done.11.low, bf16[272,512]{1,0:T(8,128)(2,1)S(1)} %collective-permute-done.12.high, bf16[8,144,256]{2,1,0:T(8,128)(2,1)S(1)} %shard_map.62.same, bf16[8,144,256]{2,1,0:T(8,128)(2,1)S(1)} %get-tuple-element.73.rest_0_, ...), custom_call_target="tpu_custom_call" | custom-call | flops 1000000000 | bytes 100000 | tf_op jit(solution)/shard_map/pallas_call | solution.py:238
  36.6 0.0 collective-permute-done.13.a
  36.6 2.3 %collective-permute-done.14.b = bf16[528,128]{1,0:T(8,128)(2,1)S(1)} collective-permute-done((bf16[528,128]{1,0:T(8,128)(2,1)S(1)}, bf16[528,128]{1,0:T(8,128)(2,1)S(1)}, u32[]{:S(2)}, u32[]{:S(2)}) %collective-permute-start.14) | collective-permute-done | bytes 135200 | tf_op jit(solution)/shard_map/ppermute | solution.py:41
  38.9 0.0 collective-permute-done.15.c
  38.9 0.1 shard_map.66
  39.0 16.3 %all_to_all.5.parts = bf16[8,80,128]{2,1,0:T(8,128)(2,1)S(1)} all-to-all(bf16[8,80,128]{2,1,0:T(8,128)(2,1)S(1)} %shard_map.66), channel_id=1, replica_groups=mesh['obs'=8,'grid'=32] {'obs'}, dimensions={0} | all-to-all | bytes 327680 | tf_op jit(solution)/shard_map/all_to_all | solution.py:457
  55.3 2.3 %shard_map.67.own = bf16[128,128]{1,0:T(8,128)(2,1)S(1)} custom-call(bf16[8,80,128]{2,1,0:T(8,128)(2,1)S(1)} %all_to_all.5.parts), custom_call_target="tpu_custom_call" | custom-call | flops 4000000000 | bytes 100000 | tf_op jit(solution)/shard_map/pallas_call | solution.py:310
  57.6 1.8 %collective-permute-start.17 = (bf16[128,128]{1,0:T(8,128)(2,1)S(1)}, bf16[128,128]{1,0:T(8,128)(2,1)S(1)}, u32[]{:S(2)}, u32[]{:S(2)}) collective-permute-start(bf16[128,128]{1,0:T(8,128)(2,1)S(1)} %shard_map.67.own), channel_id=1, source_target_pairs={{0,31},{1,0},{2,1},{3,2},{4,3},{5,4},{6,5},{7,6},{8,7},{9,8},{10,9... | collective-permute-start | bytes 98312 | tf_op jit(solution)/shard_map/ppermute | solution.py:461
  59.4 0.6 shard_map.68.part
  60.0 1.0 %collective-permute-done.17.right = bf16[128,128]{1,0:T(8,128)(2,1)S(1)} collective-permute-done((bf16[128,128]{1,0:T(8,128)(2,1)S(1)}, bf16[128,128]{1,0:T(8,128)(2,1)S(1)}, u32[]{:S(2)}, u32[]{:S(2)}) %collective-permute-start.17) | collective-permute-done | bytes 32800 | tf_op jit(solution)/shard_map/ppermute | solution.py:461
  61.0 5.1 %collective-permute-done.16.left = bf16[128,128]{1,0:T(8,128)(2,1)S(1)} collective-permute-done((bf16[128,128]{1,0:T(8,128)(2,1)S(1)}, bf16[128,128]{1,0:T(8,128)(2,1)S(1)}, u32[]{:S(2)}, u32[]{:S(2)}) %collective-permute-start.16) | collective-permute-done | bytes 32800 | tf_op jit(solution)/shard_map/ppermute | solution.py:460
  66.1 1.8 %shard_map.69 = bf16[48,128,128]{2,1,0:T(8,128)(2,1)} custom-call(bf16[128,128]{1,0:T(8,128)(2,1)S(1)} %collective-permute-done.16.left, bf16[128,128]{1,0:T(8,128)(2,1)S(1)} %collective-permute-done.17.right, f32[24,128,256]{2,1,0:T(8,128)S(1)} %shard_map.68.part, bf16[24,128,256]{2,1,0:T(8,128)(2,1)S(1)} %get-tuple-element.82.perturb), custom_call_target="tpu_custom_call" | custom-call | flops 2000000000 | bytes 100000 | tf_op jit(solution)/shard_map/pallas_call | solution.py:393
  (6 shorter events, 0.0 us)
Async XLA Ops:
  0.0 5.1 %copy-start = (bf16[48,128,128]{2,1,0:T(8,128)(2,1)S(1)}, bf16[48,128,128]{2,1,0:T(8,128)(2,1)}, u32[]{:S(2)}) copy-start(bf16[48,128,128]{2,1,0:T(8,128)(2,1)} %state.1) | copy-start | bytes 4718596
  1.8 10.8 %collective-permute-start = (bf16[272,512]{1,0:T(8,128)(2,1)S(1)}, bf16[272,512]{1,0:T(8,128)(2,1)S(1)}, u32[]{:S(2)}, u32[]{:S(2)}) collective-permute-start(bf16[272,512]{1,0:T(8,128)(2,1)S(1)} %get-tuple-element.60), channel_id=1, source_target_pairs={{0,2},{1,3},{2,4},{3,5},{4,6},{5,7},{6,0},{7,1},{8,10},{9,11},{10,... | collective-permute-start | bytes 835592 | tf_op jit(solution)/shard_map/ppermute | solution.py:41
  3.3 9.6 %collective-permute-start.1 = (bf16[272,512]{1,0:T(8,128)(2,1)S(1)}, bf16[272,512]{1,0:T(8,128)(2,1)S(1)}, u32[]{:S(2)}, u32[]{:S(2)}) collective-permute-start(bf16[272,512]{1,0:T(8,128)(2,1)S(1)} %get-tuple-element.59), channel_id=1, source_target_pairs={{0,6},{1,7},{2,0},{3,1},{4,2},{5,3},{6,4},{7,5},{8,14},{9,15},{10,... | collective-permute-start | bytes 835592 | tf_op jit(solution)/shard_map/ppermute | solution.py:41
  5.1 3.9 %collective-permute-start.2 = (bf16[544,512]{1,0:T(8,128)(2,1)S(1)}, bf16[544,512]{1,0:T(8,128)(2,1)S(1)}, u32[]{:S(2)}, u32[]{:S(2)}) collective-permute-start(bf16[544,512]{1,0:T(8,128)(2,1)S(1)} %get-tuple-element.46.refs_0_), channel_id=1, source_target_pairs={{0,1},{1,0},{2,3},{3,2},{4,5},{5,4},{6,7},{7,6},{8,9},{9,8},{10,11... | collective-permute-start | bytes 1671176 | tf_op jit(solution)/shard_map/ppermute | solution.py:41
  5.6 12.9 %collective-permute-start.7 = (bf16[272,512]{1,0:T(8,128)(2,1)S(1)}, bf16[272,512]{1,0:T(8,128)(2,1)S(1)}, u32[]{:S(2)}, u32[]{:S(2)}) collective-permute-start(bf16[272,512]{1,0:T(8,128)(2,1)S(1)} %get-tuple-element.59), channel_id=1, source_target_pairs={{0,2},{1,3},{2,4},{3,5},{4,6},{5,7},{6,0},{7,1},{8,10},{9,11},{10,... | collective-permute-start | bytes 835592 | tf_op jit(solution)/shard_map/ppermute | solution.py:41
  6.0 12.9 %collective-permute-start.8 = (bf16[272,512]{1,0:T(8,128)(2,1)S(1)}, bf16[272,512]{1,0:T(8,128)(2,1)S(1)}, u32[]{:S(2)}, u32[]{:S(2)}) collective-permute-start(bf16[272,512]{1,0:T(8,128)(2,1)S(1)} %get-tuple-element.60), channel_id=1, source_target_pairs={{0,6},{1,7},{2,0},{3,1},{4,2},{5,3},{6,4},{7,5},{8,14},{9,15},{10,... | collective-permute-start | bytes 835592 | tf_op jit(solution)/shard_map/ppermute | solution.py:41
  12.9 11.0 %collective-permute-start.3 = (bf16[272,512]{1,0:T(8,128)(2,1)S(1)}, bf16[272,512]{1,0:T(8,128)(2,1)S(1)}, u32[]{:S(2)}, u32[]{:S(2)}) collective-permute-start(bf16[272,512]{1,0:T(8,128)(2,1)S(1)} %collective-permute-done.refs_0_), channel_id=1, source_target_pairs={{0,2},{1,3},{2,4},{3,5},{4,6},{5,7},{6,0},{7,1},{8,10},{9,11},{10,... | collective-permute-start | bytes 835592 | tf_op jit(solution)/shard_map/ppermute | solution.py:41
  14.4 9.5 %collective-permute-start.4 = (bf16[272,512]{1,0:T(8,128)(2,1)S(1)}, bf16[272,512]{1,0:T(8,128)(2,1)S(1)}, u32[]{:S(2)}, u32[]{:S(2)}) collective-permute-start(bf16[272,512]{1,0:T(8,128)(2,1)S(1)} %collective-permute-done.1.refs_1_), channel_id=1, source_target_pairs={{0,6},{1,7},{2,0},{3,1},{4,2},{5,3},{6,4},{7,5},{8,14},{9,15},{10,... | collective-permute-start | bytes 835592 | tf_op jit(solution)/shard_map/ppermute | solution.py:41
  17.5 3.2 %collective-permute-start.5 = (bf16[272,512]{1,0:T(8,128)(2,1)S(1)}, bf16[272,512]{1,0:T(8,128)(2,1)S(1)}, u32[]{:S(2)}, u32[]{:S(2)}) collective-permute-start(bf16[272,512]{1,0:T(8,128)(2,1)S(1)} %collective-permute-done.refs_0_), channel_id=1, source_target_pairs={{0,1},{1,0},{2,3},{3,2},{4,5},{5,4},{6,7},{7,6},{8,9},{9,8},{10,11... | collective-permute-start | bytes 835592 | tf_op jit(solution)/shard_map/ppermute | solution.py:41
  18.6 2.5 %collective-permute-start.6 = (bf16[272,512]{1,0:T(8,128)(2,1)S(1)}, bf16[272,512]{1,0:T(8,128)(2,1)S(1)}, u32[]{:S(2)}, u32[]{:S(2)}) collective-permute-start(bf16[272,512]{1,0:T(8,128)(2,1)S(1)} %collective-permute-done.1.refs_1_), channel_id=1, source_target_pairs={{0,1},{1,0},{2,3},{3,2},{4,5},{5,4},{6,7},{7,6},{8,9},{9,8},{10,11... | collective-permute-start | bytes 835592 | tf_op jit(solution)/shard_map/ppermute | solution.py:41
  20.3 2.2 %collective-permute-start.9 = (bf16[272,512]{1,0:T(8,128)(2,1)S(1)}, bf16[272,512]{1,0:T(8,128)(2,1)S(1)}, u32[]{:S(2)}, u32[]{:S(2)}) collective-permute-start(bf16[272,512]{1,0:T(8,128)(2,1)S(1)} %collective-permute-done.7.refs_2_), channel_id=1, source_target_pairs={{0,1},{1,0},{2,3},{3,2},{4,5},{5,4},{6,7},{7,6},{8,9},{9,8},{10,11... | collective-permute-start | bytes 835592 | tf_op jit(solution)/shard_map/ppermute | solution.py:41
  20.7 1.8 %collective-permute-start.10 = (bf16[272,512]{1,0:T(8,128)(2,1)S(1)}, bf16[272,512]{1,0:T(8,128)(2,1)S(1)}, u32[]{:S(2)}, u32[]{:S(2)}) collective-permute-start(bf16[272,512]{1,0:T(8,128)(2,1)S(1)} %collective-permute-done.8.refs_3_), channel_id=1, source_target_pairs={{0,1},{1,0},{2,3},{3,2},{4,5},{5,4},{6,7},{7,6},{8,9},{9,8},{10,11... | collective-permute-start | bytes 835592 | tf_op jit(solution)/shard_map/ppermute | solution.py:41
  23.9 2.0 %collective-permute-start.11 = (bf16[272,512]{1,0:T(8,128)(2,1)S(1)}, bf16[272,512]{1,0:T(8,128)(2,1)S(1)}, u32[]{:S(2)}, u32[]{:S(2)}) collective-permute-start(bf16[272,512]{1,0:T(8,128)(2,1)S(1)} %collective-permute-done.3.refs_0_), channel_id=1, source_target_pairs={{0,1},{1,0},{2,3},{3,2},{4,5},{5,4},{6,7},{7,6},{8,9},{9,8},{10,11... | collective-permute-start | bytes 835592 | tf_op jit(solution)/shard_map/ppermute | solution.py:41
  24.2 1.8 %collective-permute-start.12 = (bf16[272,512]{1,0:T(8,128)(2,1)S(1)}, bf16[272,512]{1,0:T(8,128)(2,1)S(1)}, u32[]{:S(2)}, u32[]{:S(2)}) collective-permute-start(bf16[272,512]{1,0:T(8,128)(2,1)S(1)} %collective-permute-done.4.refs_1_), channel_id=1, source_target_pairs={{0,1},{1,0},{2,3},{3,2},{4,5},{5,4},{6,7},{7,6},{8,9},{9,8},{10,11... | collective-permute-start | bytes 835592 | tf_op jit(solution)/shard_map/ppermute | solution.py:41
  27.0 9.6 %collective-permute-start.13 = (bf16[528,128]{1,0:T(8,128)(2,1)S(1)}, bf16[528,128]{1,0:T(8,128)(2,1)S(1)}, u32[]{:S(2)}, u32[]{:S(2)}) collective-permute-start(bf16[528,128]{1,0:T(8,128)(2,1)S(1)} %shard_map.64), channel_id=1, source_target_pairs={{0,16},{1,17},{2,18},{3,19},{4,20},{5,21},{6,22},{7,23},{8,24},{9,... | collective-permute-start | bytes 405512 | tf_op jit(solution)/shard_map/ppermute | solution.py:41
  32.2 6.7 %collective-permute-start.14 = (bf16[528,128]{1,0:T(8,128)(2,1)S(1)}, bf16[528,128]{1,0:T(8,128)(2,1)S(1)}, u32[]{:S(2)}, u32[]{:S(2)}) collective-permute-start(bf16[528,128]{1,0:T(8,128)(2,1)S(1)} %get-tuple-element.79), channel_id=1, source_target_pairs={{0,8},{1,9},{2,10},{3,11},{4,12},{5,13},{6,14},{7,15},{8,16},{9,17... | collective-permute-start | bytes 405512 | tf_op jit(solution)/shard_map/ppermute | solution.py:41
  32.9 5.9 %collective-permute-start.15 = (bf16[528,128]{1,0:T(8,128)(2,1)S(1)}, bf16[528,128]{1,0:T(8,128)(2,1)S(1)}, u32[]{:S(2)}, u32[]{:S(2)}) collective-permute-start(bf16[528,128]{1,0:T(8,128)(2,1)S(1)} %get-tuple-element.80), channel_id=1, source_target_pairs={{0,24},{1,25},{2,26},{3,27},{4,28},{5,29},{6,30},{7,31},{8,0},{9,1... | collective-permute-start | bytes 405512 | tf_op jit(solution)/shard_map/ppermute | solution.py:41
  57.6 3.4 %collective-permute-start.17 = (bf16[128,128]{1,0:T(8,128)(2,1)S(1)}, bf16[128,128]{1,0:T(8,128)(2,1)S(1)}, u32[]{:S(2)}, u32[]{:S(2)}) collective-permute-start(bf16[128,128]{1,0:T(8,128)(2,1)S(1)} %shard_map.67.own), channel_id=1, source_target_pairs={{0,31},{1,0},{2,1},{3,2},{4,3},{5,4},{6,5},{7,6},{8,7},{9,8},{10,9... | collective-permute-start | bytes 98312 | tf_op jit(solution)/shard_map/ppermute | solution.py:461
  59.4 6.7 %collective-permute-start.16 = (bf16[128,128]{1,0:T(8,128)(2,1)S(1)}, bf16[128,128]{1,0:T(8,128)(2,1)S(1)}, u32[]{:S(2)}, u32[]{:S(2)}) collective-permute-start(bf16[128,128]{1,0:T(8,128)(2,1)S(1)} %shard_map.67.own), channel_id=1, source_target_pairs={{0,1},{1,2},{2,3},{3,4},{4,5},{5,6},{6,7},{7,8},{8,9},{9,10},{10,1... | collective-permute-start | bytes 98312 | tf_op jit(solution)/shard_map/ppermute | solution.py:460

commit v11 on v10

--- a/solution.py
+++ b/solution.py
@@ -317,14 +317,24 @@
     )(parts)
 
 
-def perturb_kernel(state, mean, perturb):
+def column_coefs():
+    position = lax.broadcasted_iota(jnp.int32, (1, 2 * K), 1) % K
+    position = (position.astype(F32) + 0.5) / K
+    return jnp.maximum(0.5 - position, 0.0), jnp.maximum(position - 0.5, 0.0)
+
+
+def perturb_kernel(state, mean, perturb, sides):
     for pair in range(mean.shape[0]):
         for i in range(2):
             span = slice(i * K, (i + 1) * K)
             values = state[2 * pair + i].astype(F32)
             average = jnp.mean(values, axis=0, keepdims=True)
             mean[pair : pair + 1, span] = average
-            perturb[pair, :, span] = (values - average).astype(BF16)
+            rounded = (values - average).astype(BF16)
+            perturb[pair, :, span] = rounded
+            for side, coef in enumerate(column_coefs()):
+                scaled = coef[:, span] * rounded.astype(F32)
+                sides[pair, side * K : (side + 1) * K, span] = scaled.astype(BF16)
 
 
 def perturbations(state):
@@ -334,22 +344,17 @@
         out_shape=[
             jax.ShapeDtypeStruct((pairs, 2 * K), F32),
             jax.ShapeDtypeStruct((pairs, K, 2 * K), BF16),
+            jax.ShapeDtypeStruct((pairs, 2 * K, 2 * K), BF16),
         ],
         in_specs=in_vmem(1),
-        out_specs=in_vmem(2),
+        out_specs=in_vmem(3),
         compiler_params=params(),
         cost_estimate=cost(LONG),
     )(state)
 
 
-def column_coefs():
-    lane = lax.broadcasted_iota(jnp.int32, (1, 2 * K), 1) % K
-    position = (lane.astype(F32) + 0.5) / K
-    return lane, jnp.maximum(0.5 - position, 0.0), jnp.maximum(position - 0.5, 0.0)
-
-
 def own_kernel(own, mean, perturb, out):
-    _, left_coef, right_coef = column_coefs()
+    left_coef, right_coef = column_coefs()
     own_coef = 1.0 - left_coef - right_coef
     for pair in range(mean.shape[0]):
         sums = jnp.dot(own[...], perturb[pair], preferred_element_type=F32)
@@ -367,18 +372,15 @@
     )(own, mean, perturb)
 
 
-def side_kernel(left, right, part, perturb, out, held, sems):
-    lane, left_coef, right_coef = column_coefs()
-    coef = left_coef + right_coef
-    weights = jnp.concatenate([left[...], right[...]], axis=0)
+def side_kernel(left, right, part, sides, out, held, sems):
+    weights = jnp.concatenate([left[...], right[...]], axis=1)
     chunks = sems.shape[0]
-    pairs = perturb.shape[0] // chunks
+    pairs = sides.shape[0] // chunks
     copies = []
     for chunk in range(chunks):
         for pair in range(chunk * pairs, (chunk + 1) * pairs):
-            sums = jnp.dot(weights, perturb[pair], preferred_element_type=F32)
-            side = jnp.where(lane < K // 2, sums[:K], sums[K:])
-            total = (part[pair] + coef * side).astype(BF16)
+            total = part[pair] + jnp.dot(weights, sides[pair], preferred_element_type=F32)
+            total = total.astype(BF16)
             for i in range(2):
                 held[2 * pair + i] = total[:, i * K : (i + 1) * K]
         rows = pl.ds(2 * chunk * pairs, 2 * pairs)
@@ -388,17 +390,17 @@
         copy.wait()
 
 
-def add_sides(left, right, part, perturb):
-    shape = (2 * perturb.shape[0], K, K)
+def add_sides(left, right, part, sides):
+    shape = (2 * sides.shape[0], K, K)
     return pl.pallas_call(
         side_kernel,
         out_shape=jax.ShapeDtypeStruct(shape, BF16),
         in_specs=in_vmem(4),
         out_specs=pl.BlockSpec(memory_space=pltpu.HBM),
-        scratch_shapes=[pltpu.VMEM(shape, BF16), pltpu.SemaphoreType.DMA((6,))],
+        scratch_shapes=[pltpu.VMEM(shape, BF16), pltpu.SemaphoreType.DMA((8,))],
         compiler_params=params(),
         cost_estimate=cost(2e9),
-    )(left, right, part, perturb)
+    )(left, right, part, sides)
 
 
 def on_device(departures, innovation, obs_weight, send_rows, send_counts, state):
@@ -414,9 +416,9 @@
     found = pick_rows(
         ((whole(0), (0, 0, 8), None), (whole(1), (1, 0, 12), None)), SHORT, near, other
     )
-    mean, perturb = perturbations(state)
-    low_half, high_half, mean, perturb = lax.optimization_barrier(
-        (low_half, high_half, mean, perturb)
+    mean, perturb, sides = perturbations(state)
+    low_half, high_half, mean, perturb, sides = lax.optimization_barrier(
+        (low_half, high_half, mean, perturb, sides)
     )
     left_more = hop(high_half, 0, 1, 0)
     right_more = hop(low_half, 0, -1, 0)
@@ -450,8 +452,8 @@
 
     across = last_grams((2,), BF16, *last)[0]
     from_across = hop(across, 2, 0, 0)
-    up, down = last_grams((1, 3), BF16, *last)
-    from_up, from_down = hop(up, 1, 0, 0), hop(down, -1, 0, 0)
+    from_up = hop(last_grams((1,), BF16, *last)[0], 1, 0, 0)
+    from_down = hop(last_grams((3,), BF16, *last)[0], -1, 0, 0)
     own = last_grams((0,), F32, *last)[0]
     parts = sum_parts(own, from_across, from_up, from_down)
     parts = lax.all_to_all(parts, "obs", 0, 0, tiled=True)
@@ -460,7 +462,7 @@
     low = lax.ppermute(own, "grid", [(j, (j + 1) % n_grid) for j in range(n_grid)])
     high = lax.ppermute(own, "grid", [(j, (j - 1) % n_grid) for j in range(n_grid)])
     part = own_part(own, mean, perturb)
-    return add_sides(low, high, part, perturb)
+    return add_sides(low, high, part, sides)
 
 
 def solution(mesh):

time: 68.2 us -> 68 us (level)
  waiting for transfers between devices: 11.2 us -> 9.83 us
  starting transfers between devices: 19.7 us -> 20.4 us
    ppermute x16, waiting for transfers between devices: 5.14 us -> 3.73 us  [hop(): return lax.ppermute(value, 'grid', pairs)]
    ppermute x1, starting transfers between devices: 1.8 us -> 2.61 us  [on_device(): lax.ppermute(own, 'grid', [(j, (j - 1) % n_grid) for j in range(n_grid)])]
    pallas_call x3 -> x4, Pallas kernels: 4.02 us -> 4.27 us  [last_grams(): pl.pallas_call(functools.partial(last_kernel, shifts), out_shape=[jax.Sha...]
  transfers between devices with their start and end apart: 18 -> 18, of which waited for: 9 -> 10; matrix products, arithmetic and copies ran while one was open for 0% -> 0% of each run, Pallas kernels for 20% -> 21%
where the time goes in v11:
time: 68 us; the launch traced here: 67.9 us
  Pallas kernels  20.9 us (31%)
  starting transfers between devices  20.4 us (30%)
  blocking collectives  16.4 us (24%)
  waiting for transfers between devices  9.83 us (14%)
    ppermute x16, starting transfers between devices, hop(): return lax.ppermute(value, 'grid', pairs)  17.8 us
    all_to_all x1, blocking collectives, on_device(): parts = lax.all_to_all(parts, 'obs', 0, 0, tiled=True)  16.4 us
    pallas_call x6, Pallas kernels, pick_rows(): pl.pallas_call(functools.partial(pick_kernel, sources, len(args)), out_sh...  9.32 us
    ppermute x1, waiting for transfers between devices, on_device(): lax.ppermute(own, 'grid', [(j, (j + 1) % n_grid) for j in range(n_grid)])  5.06 us
    pallas_call x4, Pallas kernels, last_grams(): pl.pallas_call(functools.partial(last_kernel, shifts), out_shape=[jax.Sha...  4.27 us
    ppermute x16, waiting for transfers between devices, hop(): return lax.ppermute(value, 'grid', pairs)  3.73 us
    ppermute x1, starting transfers between devices, on_device(): lax.ppermute(own, 'grid', [(j, (j - 1) % n_grid) for j in range(n_grid)])  2.61 us
    pallas_call x1, Pallas kernels, transposed_weights(): pl.pallas_call(weights_kernel, out_shape=jax.ShapeDtypeStruct((K, K), BF1...  2.34 us
  transfers between devices with their start and end apart: 18, of which 10 were waited for; matrix products, arithmetic and copies ran while one was open for 0% of the time, Pallas kernels for 21%

profile of v11, /device:TPU:32, one launch (start us, length us, event | category | flops | bytes accessed | tf_op | source)
XLA Modules:
  0.0 67.9 jit_solution(9323753158556693767)
XLA Ops:
  0.0 1.8 %shard_map.55 = (bf16[272,512]{1,0:T(8,128)(2,1)S(1)}, bf16[272,512]{1,0:T(8,128)(2,1)S(1)}, bf16[544,512]{1,0:T(8,128)(2,1)S(1)}) custom-call(bf16[2048,128]{1,0:T(8,128)(2,1)} %departures.1, f32[2048]{0:T(1024)} %innovation.1, f32[2048]{0:T(1024)} %obs_weight.1, s32[64,256]{1,0:T(8,128)} %bitcast.3), custom_call_target="tpu_custom_call" | custom-call | flops 2000000000 | bytes 100000 | tf_op jit(solution)/shard_map/pallas_call | solution.py:121
  1.8 1.6 %collective-permute-start = (bf16[272,512]{1,0:T(8,128)(2,1)S(1)}, bf16[272,512]{1,0:T(8,128)(2,1)S(1)}, u32[]{:S(2)}, u32[]{:S(2)}) collective-permute-start(bf16[272,512]{1,0:T(8,128)(2,1)S(1)} %get-tuple-element.61), channel_id=1, source_target_pairs={{0,2},{1,3},{2,4},{3,5},{4,6},{5,7},{6,0},{7,1},{8,10},{9,11},{10,... | collective-permute-start | bytes 835592 | tf_op jit(solution)/shard_map/ppermute | solution.py:41
  3.3 1.7 %collective-permute-start.1 = (bf16[272,512]{1,0:T(8,128)(2,1)S(1)}, bf16[272,512]{1,0:T(8,128)(2,1)S(1)}, u32[]{:S(2)}, u32[]{:S(2)}) collective-permute-start(bf16[272,512]{1,0:T(8,128)(2,1)S(1)} %get-tuple-element.60), channel_id=1, source_target_pairs={{0,6},{1,7},{2,0},{3,1},{4,2},{5,3},{6,4},{7,5},{8,14},{9,15},{10,... | collective-permute-start | bytes 835592 | tf_op jit(solution)/shard_map/ppermute | solution.py:41
  5.1 1.2 %shard_map.57 = (f32[24,256]{1,0:T(8,128)S(1)}, bf16[24,128,256]{2,1,0:T(8,128)(2,1)S(1)}, bf16[24,256,256]{2,1,0:T(8,128)(2,1)S(1)}) custom-call(bf16[48,128,128]{2,1,0:T(8,128)(2,1)S(1)} %copy-done), custom_call_target="tpu_custom_call" | custom-call | flops 60000002048 | bytes 100000 | tf_op jit(solution)/shard_map/pallas_call | solution.py:342
  6.3 0.4 collective-permute-start.7
  6.6 3.0 %collective-permute-start.8 = (bf16[272,512]{1,0:T(8,128)(2,1)S(1)}, bf16[272,512]{1,0:T(8,128)(2,1)S(1)}, u32[]{:S(2)}, u32[]{:S(2)}) collective-permute-start(bf16[272,512]{1,0:T(8,128)(2,1)S(1)} %get-tuple-element.61), channel_id=1, source_target_pairs={{0,6},{1,7},{2,0},{3,1},{4,2},{5,3},{6,4},{7,5},{8,14},{9,15},{10,... | collective-permute-start | bytes 835592 | tf_op jit(solution)/shard_map/ppermute | solution.py:41
  9.6 2.5 %shard_map.56 = (bf16[8,144,256]{2,1,0:T(8,128)(2,1)S(1)}, bf16[8,144,256]{2,1,0:T(8,128)(2,1)S(1)}) custom-call(bf16[544,512]{1,0:T(8,128)(2,1)S(1)} %get-tuple-element.46.refs_0_, bf16[544,512]{1,0:T(8,128)(2,1)S(1)} %collective-permute-done.2.refs_1_), custom_call_target="tpu_custom_call" | custom-call | flops 1000000 | bytes 100000 | tf_op jit(solution)/shard_map/pallas_call | solution.py:171
  12.1 0.1 collective-permute-done.refs_0_
  12.2 0.7 %collective-permute-done.1.refs_1_ = bf16[272,512]{1,0:T(8,128)(2,1)S(1)} collective-permute-done((bf16[272,512]{1,0:T(8,128)(2,1)S(1)}, bf16[272,512]{1,0:T(8,128)(2,1)S(1)}, u32[]{:S(2)}, u32[]{:S(2)}) %collective-permute-start.1) | collective-permute-done | bytes 278560 | tf_op jit(solution)/shard_map/ppermute | solution.py:41
  12.9 1.5 %collective-permute-start.3 = (bf16[272,512]{1,0:T(8,128)(2,1)S(1)}, bf16[272,512]{1,0:T(8,128)(2,1)S(1)}, u32[]{:S(2)}, u32[]{:S(2)}) collective-permute-start(bf16[272,512]{1,0:T(8,128)(2,1)S(1)} %collective-permute-done.refs_0_), channel_id=1, source_target_pairs={{0,2},{1,3},{2,4},{3,5},{4,6},{5,7},{6,0},{7,1},{8,10},{9,11},{10,... | collective-permute-start | bytes 835592 | tf_op jit(solution)/shard_map/ppermute | solution.py:41
  14.4 1.7 %collective-permute-start.4 = (bf16[272,512]{1,0:T(8,128)(2,1)S(1)}, bf16[272,512]{1,0:T(8,128)(2,1)S(1)}, u32[]{:S(2)}, u32[]{:S(2)}) collective-permute-start(bf16[272,512]{1,0:T(8,128)(2,1)S(1)} %collective-permute-done.1.refs_1_), channel_id=1, source_target_pairs={{0,6},{1,7},{2,0},{3,1},{4,2},{5,3},{6,4},{7,5},{8,14},{9,15},{10,... | collective-permute-start | bytes 835592 | tf_op jit(solution)/shard_map/ppermute | solution.py:41
  16.2 1.4 %shard_map.58 = (bf16[8,144,256]{2,1,0:T(8,128)(2,1)S(1)}, bf16[8,144,256]{2,1,0:T(8,128)(2,1)S(1)}) custom-call(bf16[272,512]{1,0:T(8,128)(2,1)S(1)} %collective-permute-done.refs_0_, bf16[272,512]{1,0:T(8,128)(2,1)S(1)} %collective-permute-done.1.refs_1_), custom_call_target="tpu_custom_call" | custom-call | flops 1000000 | bytes 100000 | tf_op jit(solution)/shard_map/pallas_call | solution.py:171
  17.5 0.1 collective-permute-start.5
  17.6 0.5 collective-permute-done.7.refs_2_
  18.2 0.0 collective-permute-start.6
  18.2 0.7 %collective-permute-done.8.refs_3_ = bf16[272,512]{1,0:T(8,128)(2,1)S(1)} collective-permute-done((bf16[272,512]{1,0:T(8,128)(2,1)S(1)}, bf16[272,512]{1,0:T(8,128)(2,1)S(1)}, u32[]{:S(2)}, u32[]{:S(2)}) %collective-permute-start.8) | collective-permute-done | bytes 278560 | tf_op jit(solution)/shard_map/ppermute | solution.py:41
  18.9 1.4 %shard_map.59 = (bf16[8,144,256]{2,1,0:T(8,128)(2,1)S(1)}, bf16[8,144,256]{2,1,0:T(8,128)(2,1)S(1)}) custom-call(bf16[272,512]{1,0:T(8,128)(2,1)S(1)} %collective-permute-done.refs_0_, bf16[272,512]{1,0:T(8,128)(2,1)S(1)} %collective-permute-done.1.refs_1_, bf16[272,512]{1,0:T(8,128)(2,1)S(1)} %collective-permute-done.7.refs_2_, ...), custom_call_target="tpu_custom_call" | custom-call | flops 60000002048 | bytes 100000 | tf_op jit(solution)/shard_map/pallas_call | solution.py:171
  20.3 0.1 collective-permute-start.9
  20.4 0.0 collective-permute-done.5.refs_0_
  20.4 0.5 collective-permute-start.10
  20.9 0.0 collective-permute-done.6.refs_1_
  20.9 1.4 %shard_map.60 = (bf16[8,144,256]{2,1,0:T(8,128)(2,1)S(1)}, bf16[8,144,256]{2,1,0:T(8,128)(2,1)S(1)}) custom-call(bf16[272,512]{1,0:T(8,128)(2,1)S(1)} %collective-permute-done.5.refs_0_, bf16[272,512]{1,0:T(8,128)(2,1)S(1)} %collective-permute-done.6.refs_1_), custom_call_target="tpu_custom_call" | custom-call | flops 60000002048 | bytes 100000 | tf_op jit(solution)/shard_map/pallas_call | solution.py:171
  22.2 0.1 collective-permute-done.10.refs_3_
  22.3 1.4 %shard_map.61 = (bf16[8,144,256]{2,1,0:T(8,128)(2,1)S(1)}, bf16[8,144,256]{2,1,0:T(8,128)(2,1)S(1)}) custom-call(bf16[272,512]{1,0:T(8,128)(2,1)S(1)} %collective-permute-done.5.refs_0_, bf16[272,512]{1,0:T(8,128)(2,1)S(1)} %collective-permute-done.6.refs_1_, bf16[272,512]{1,0:T(8,128)(2,1)S(1)} %collective-permute-done.9.refs_2_, ...), custom_call_target="tpu_custom_call" | custom-call | flops 1000000 | bytes 100000 | tf_op jit(solution)/shard_map/pallas_call | solution.py:171
  23.7 0.0 collective-permute-done.4.refs_1_
  23.7 0.2 collective-permute-start.11
  23.9 0.4 collective-permute-start.12
  24.3 1.4 %shard_map.62.same = bf16[8,144,256]{2,1,0:T(8,128)(2,1)S(1)} custom-call(bf16[272,512]{1,0:T(8,128)(2,1)S(1)} %collective-permute-done.3.refs_0_, bf16[272,512]{1,0:T(8,128)(2,1)S(1)} %collective-permute-done.4.refs_1_), custom_call_target="tpu_custom_call" | custom-call | flops 1000000 | bytes 100000 | tf_op jit(solution)/shard_map/pallas_call | solution.py:171
  25.7 0.1 collective-permute-done.12.high
  25.7 1.1 %shard_map.64 = bf16[528,128]{1,0:T(8,128)(2,1)S(1)} custom-call(bf16[272,512]{1,0:T(8,128)(2,1)S(1)} %collective-permute-done.11.low, bf16[272,512]{1,0:T(8,128)(2,1)S(1)} %collective-permute-done.12.high, bf16[8,144,256]{2,1,0:T(8,128)(2,1)S(1)} %shard_map.62.same, bf16[8,144,256]{2,1,0:T(8,128)(2,1)S(1)} %get-tuple-element.74.rest_0_, ...), custom_call_target="tpu_custom_call" | custom-call | flops 1000000000 | bytes 100000 | tf_op jit(solution)/shard_map/pallas_call | solution.py:238
  26.8 3.3 %collective-permute-start.13 = (bf16[528,128]{1,0:T(8,128)(2,1)S(1)}, bf16[528,128]{1,0:T(8,128)(2,1)S(1)}, u32[]{:S(2)}, u32[]{:S(2)}) collective-permute-start(bf16[528,128]{1,0:T(8,128)(2,1)S(1)} %shard_map.64), channel_id=1, source_target_pairs={{0,16},{1,17},{2,18},{3,19},{4,20},{5,21},{6,22},{7,23},{8,24},{9,... | collective-permute-start | bytes 405512 | tf_op jit(solution)/shard_map/ppermute | solution.py:41
  30.1 1.1 %shard_map.65 = bf16[528,128]{1,0:T(8,128)(2,1)S(1)} custom-call(bf16[272,512]{1,0:T(8,128)(2,1)S(1)} %collective-permute-done.11.low, bf16[272,512]{1,0:T(8,128)(2,1)S(1)} %collective-permute-done.12.high, bf16[8,144,256]{2,1,0:T(8,128)(2,1)S(1)} %shard_map.62.same, bf16[8,144,256]{2,1,0:T(8,128)(2,1)S(1)} %get-tuple-element.74.rest_0_, ...), custom_call_target="tpu_custom_call" | custom-call | flops 1000000000 | bytes 100000 | tf_op jit(solution)/shard_map/pallas_call | solution.py:238
  31.2 0.8 %collective-permute-start.14 = (bf16[528,128]{1,0:T(8,128)(2,1)S(1)}, bf16[528,128]{1,0:T(8,128)(2,1)S(1)}, u32[]{:S(2)}, u32[]{:S(2)}) collective-permute-start(bf16[528,128]{1,0:T(8,128)(2,1)S(1)} %shard_map.65), channel_id=1, source_target_pairs={{0,8},{1,9},{2,10},{3,11},{4,12},{5,13},{6,14},{7,15},{8,16},{9,17... | collective-permute-start | bytes 405512 | tf_op jit(solution)/shard_map/ppermute | solution.py:41
  31.9 1.1 %shard_map.66 = bf16[528,128]{1,0:T(8,128)(2,1)S(1)} custom-call(bf16[272,512]{1,0:T(8,128)(2,1)S(1)} %collective-permute-done.11.low, bf16[272,512]{1,0:T(8,128)(2,1)S(1)} %collective-permute-done.12.high, bf16[8,144,256]{2,1,0:T(8,128)(2,1)S(1)} %shard_map.62.same, bf16[8,144,256]{2,1,0:T(8,128)(2,1)S(1)} %get-tuple-element.74.rest_0_, ...), custom_call_target="tpu_custom_call" | custom-call | flops 1000000000 | bytes 100000 | tf_op jit(solution)/shard_map/pallas_call | solution.py:238
  33.0 2.6 %collective-permute-start.15 = (bf16[528,128]{1,0:T(8,128)(2,1)S(1)}, bf16[528,128]{1,0:T(8,128)(2,1)S(1)}, u32[]{:S(2)}, u32[]{:S(2)}) collective-permute-start(bf16[528,128]{1,0:T(8,128)(2,1)S(1)} %shard_map.66), channel_id=1, source_target_pairs={{0,24},{1,25},{2,26},{3,27},{4,28},{5,29},{6,30},{7,31},{8,0},{9,1... | collective-permute-start | bytes 405512 | tf_op jit(solution)/shard_map/ppermute | solution.py:41
  35.6 1.1 %shard_map.63.own = f32[528,128]{1,0:T(8,128)S(1)} custom-call(bf16[272,512]{1,0:T(8,128)(2,1)S(1)} %collective-permute-done.11.low, bf16[272,512]{1,0:T(8,128)(2,1)S(1)} %collective-permute-done.12.high, bf16[8,144,256]{2,1,0:T(8,128)(2,1)S(1)} %shard_map.62.same, bf16[8,144,256]{2,1,0:T(8,128)(2,1)S(1)} %get-tuple-element.74.rest_0_, ...), custom_call_target="tpu_custom_call" | custom-call | flops 1000000000 | bytes 100000 | tf_op jit(solution)/shard_map/pallas_call | solution.py:238
  36.7 0.0 collective-permute-done.13.a
  36.7 1.1 %collective-permute-done.14.b = bf16[528,128]{1,0:T(8,128)(2,1)S(1)} collective-permute-done((bf16[528,128]{1,0:T(8,128)(2,1)S(1)}, bf16[528,128]{1,0:T(8,128)(2,1)S(1)}, u32[]{:S(2)}, u32[]{:S(2)}) %collective-permute-start.14) | collective-permute-done | bytes 135200 | tf_op jit(solution)/shard_map/ppermute | solution.py:41
  37.8 0.4 collective-permute-done.15.c
  38.2 0.1 shard_map.67
  38.3 16.4 %all_to_all.5.parts = bf16[8,80,128]{2,1,0:T(8,128)(2,1)S(1)} all-to-all(bf16[8,80,128]{2,1,0:T(8,128)(2,1)S(1)} %shard_map.67), channel_id=1, replica_groups=mesh['obs'=8,'grid'=32] {'obs'}, dimensions={0} | all-to-all | bytes 327680 | tf_op jit(solution)/shard_map/all_to_all | solution.py:459
  54.7 2.3 %shard_map.68.own = bf16[128,128]{1,0:T(8,128)(2,1)S(1)} custom-call(bf16[8,80,128]{2,1,0:T(8,128)(2,1)S(1)} %all_to_all.5.parts), custom_call_target="tpu_custom_call" | custom-call | flops 4000000000 | bytes 100000 | tf_op jit(solution)/shard_map/pallas_call | solution.py:310
  57.0 2.6 %collective-permute-start.17 = (bf16[128,128]{1,0:T(8,128)(2,1)S(1)}, bf16[128,128]{1,0:T(8,128)(2,1)S(1)}, u32[]{:S(2)}, u32[]{:S(2)}) collective-permute-start(bf16[128,128]{1,0:T(8,128)(2,1)S(1)} %shard_map.68.own), channel_id=1, source_target_pairs={{0,31},{1,0},{2,1},{3,2},{4,3},{5,4},{6,5},{7,6},{8,7},{9,8},{10,9... | collective-permute-start | bytes 98312 | tf_op jit(solution)/shard_map/ppermute | solution.py:463
  59.6 0.0 collective-permute-start.16
  59.6 0.6 shard_map.69.part
  60.2 1.0 %collective-permute-done.17.right = bf16[128,128]{1,0:T(8,128)(2,1)S(1)} collective-permute-done((bf16[128,128]{1,0:T(8,128)(2,1)S(1)}, bf16[128,128]{1,0:T(8,128)(2,1)S(1)}, u32[]{:S(2)}, u32[]{:S(2)}) %collective-permute-start.17) | collective-permute-done | bytes 32800 | tf_op jit(solution)/shard_map/ppermute | solution.py:463
  61.2 5.1 %collective-permute-done.16.left = bf16[128,128]{1,0:T(8,128)(2,1)S(1)} collective-permute-done((bf16[128,128]{1,0:T(8,128)(2,1)S(1)}, bf16[128,128]{1,0:T(8,128)(2,1)S(1)}, u32[]{:S(2)}, u32[]{:S(2)}) %collective-permute-start.16) | collective-permute-done | bytes 32800 | tf_op jit(solution)/shard_map/ppermute | solution.py:462
  66.3 1.4 %shard_map.70 = bf16[48,128,128]{2,1,0:T(8,128)(2,1)} custom-call(bf16[128,128]{1,0:T(8,128)(2,1)S(1)} %collective-permute-done.16.left, bf16[128,128]{1,0:T(8,128)(2,1)S(1)} %collective-permute-done.17.right, f32[24,128,256]{2,1,0:T(8,128)S(1)} %shard_map.69.part, bf16[24,256,256]{2,1,0:T(8,128)(2,1)S(1)} %get-tuple-element.82.sides), custom_call_target="tpu_custom_call" | custom-call | flops 2000000000 | bytes 100000 | tf_op jit(solution)/shard_map/pallas_call | solution.py:395
  (7 shorter events, 0.0 us)
Async XLA Ops:
  0.0 5.1 %copy-start = (bf16[48,128,128]{2,1,0:T(8,128)(2,1)S(1)}, bf16[48,128,128]{2,1,0:T(8,128)(2,1)}, u32[]{:S(2)}) copy-start(bf16[48,128,128]{2,1,0:T(8,128)(2,1)} %state.1) | copy-start | bytes 4718596
  1.8 10.4 %collective-permute-start = (bf16[272,512]{1,0:T(8,128)(2,1)S(1)}, bf16[272,512]{1,0:T(8,128)(2,1)S(1)}, u32[]{:S(2)}, u32[]{:S(2)}) collective-permute-start(bf16[272,512]{1,0:T(8,128)(2,1)S(1)} %get-tuple-element.61), channel_id=1, source_target_pairs={{0,2},{1,3},{2,4},{3,5},{4,6},{5,7},{6,0},{7,1},{8,10},{9,11},{10,... | collective-permute-start | bytes 835592 | tf_op jit(solution)/shard_map/ppermute | solution.py:41
  3.3 9.6 %collective-permute-start.1 = (bf16[272,512]{1,0:T(8,128)(2,1)S(1)}, bf16[272,512]{1,0:T(8,128)(2,1)S(1)}, u32[]{:S(2)}, u32[]{:S(2)}) collective-permute-start(bf16[272,512]{1,0:T(8,128)(2,1)S(1)} %get-tuple-element.60), channel_id=1, source_target_pairs={{0,6},{1,7},{2,0},{3,1},{4,2},{5,3},{6,4},{7,5},{8,14},{9,15},{10,... | collective-permute-start | bytes 835592 | tf_op jit(solution)/shard_map/ppermute | solution.py:41
  5.1 4.5 %collective-permute-start.2 = (bf16[544,512]{1,0:T(8,128)(2,1)S(1)}, bf16[544,512]{1,0:T(8,128)(2,1)S(1)}, u32[]{:S(2)}, u32[]{:S(2)}) collective-permute-start(bf16[544,512]{1,0:T(8,128)(2,1)S(1)} %get-tuple-element.46.refs_0_), channel_id=1, source_target_pairs={{0,1},{1,0},{2,3},{3,2},{4,5},{5,4},{6,7},{7,6},{8,9},{9,8},{10,11... | collective-permute-start | bytes 1671176 | tf_op jit(solution)/shard_map/ppermute | solution.py:41
  6.3 11.9 %collective-permute-start.7 = (bf16[272,512]{1,0:T(8,128)(2,1)S(1)}, bf16[272,512]{1,0:T(8,128)(2,1)S(1)}, u32[]{:S(2)}, u32[]{:S(2)}) collective-permute-start(bf16[272,512]{1,0:T(8,128)(2,1)S(1)} %get-tuple-element.60), channel_id=1, source_target_pairs={{0,2},{1,3},{2,4},{3,5},{4,6},{5,7},{6,0},{7,1},{8,10},{9,11},{10,... | collective-permute-start | bytes 835592 | tf_op jit(solution)/shard_map/ppermute | solution.py:41
  6.6 12.3 %collective-permute-start.8 = (bf16[272,512]{1,0:T(8,128)(2,1)S(1)}, bf16[272,512]{1,0:T(8,128)(2,1)S(1)}, u32[]{:S(2)}, u32[]{:S(2)}) collective-permute-start(bf16[272,512]{1,0:T(8,128)(2,1)S(1)} %get-tuple-element.61), channel_id=1, source_target_pairs={{0,6},{1,7},{2,0},{3,1},{4,2},{5,3},{6,4},{7,5},{8,14},{9,15},{10,... | collective-permute-start | bytes 835592 | tf_op jit(solution)/shard_map/ppermute | solution.py:41
  12.9 10.8 %collective-permute-start.3 = (bf16[272,512]{1,0:T(8,128)(2,1)S(1)}, bf16[272,512]{1,0:T(8,128)(2,1)S(1)}, u32[]{:S(2)}, u32[]{:S(2)}) collective-permute-start(bf16[272,512]{1,0:T(8,128)(2,1)S(1)} %collective-permute-done.refs_0_), channel_id=1, source_target_pairs={{0,2},{1,3},{2,4},{3,5},{4,6},{5,7},{6,0},{7,1},{8,10},{9,11},{10,... | collective-permute-start | bytes 835592 | tf_op jit(solution)/shard_map/ppermute | solution.py:41
  14.4 9.3 %collective-permute-start.4 = (bf16[272,512]{1,0:T(8,128)(2,1)S(1)}, bf16[272,512]{1,0:T(8,128)(2,1)S(1)}, u32[]{:S(2)}, u32[]{:S(2)}) collective-permute-start(bf16[272,512]{1,0:T(8,128)(2,1)S(1)} %collective-permute-done.1.refs_1_), channel_id=1, source_target_pairs={{0,6},{1,7},{2,0},{3,1},{4,2},{5,3},{6,4},{7,5},{8,14},{9,15},{10,... | collective-permute-start | bytes 835592 | tf_op jit(solution)/shard_map/ppermute | solution.py:41
  17.5 2.9 %collective-permute-start.5 = (bf16[272,512]{1,0:T(8,128)(2,1)S(1)}, bf16[272,512]{1,0:T(8,128)(2,1)S(1)}, u32[]{:S(2)}, u32[]{:S(2)}) collective-permute-start(bf16[272,512]{1,0:T(8,128)(2,1)S(1)} %collective-permute-done.refs_0_), channel_id=1, source_target_pairs={{0,1},{1,0},{2,3},{3,2},{4,5},{5,4},{6,7},{7,6},{8,9},{9,8},{10,11... | collective-permute-start | bytes 835592 | tf_op jit(solution)/shard_map/ppermute | solution.py:41
  18.2 2.7 %collective-permute-start.6 = (bf16[272,512]{1,0:T(8,128)(2,1)S(1)}, bf16[272,512]{1,0:T(8,128)(2,1)S(1)}, u32[]{:S(2)}, u32[]{:S(2)}) collective-permute-start(bf16[272,512]{1,0:T(8,128)(2,1)S(1)} %collective-permute-done.1.refs_1_), channel_id=1, source_target_pairs={{0,1},{1,0},{2,3},{3,2},{4,5},{5,4},{6,7},{7,6},{8,9},{9,8},{10,11... | collective-permute-start | bytes 835592 | tf_op jit(solution)/shard_map/ppermute | solution.py:41
  20.3 2.0 %collective-permute-start.9 = (bf16[272,512]{1,0:T(8,128)(2,1)S(1)}, bf16[272,512]{1,0:T(8,128)(2,1)S(1)}, u32[]{:S(2)}, u32[]{:S(2)}) collective-permute-start(bf16[272,512]{1,0:T(8,128)(2,1)S(1)} %collective-permute-done.7.refs_2_), channel_id=1, source_target_pairs={{0,1},{1,0},{2,3},{3,2},{4,5},{5,4},{6,7},{7,6},{8,9},{9,8},{10,11... | collective-permute-start | bytes 835592 | tf_op jit(solution)/shard_map/ppermute | solution.py:41
  20.4 1.9 %collective-permute-start.10 = (bf16[272,512]{1,0:T(8,128)(2,1)S(1)}, bf16[272,512]{1,0:T(8,128)(2,1)S(1)}, u32[]{:S(2)}, u32[]{:S(2)}) collective-permute-start(bf16[272,512]{1,0:T(8,128)(2,1)S(1)} %collective-permute-done.8.refs_3_), channel_id=1, source_target_pairs={{0,1},{1,0},{2,3},{3,2},{4,5},{5,4},{6,7},{7,6},{8,9},{9,8},{10,11... | collective-permute-start | bytes 835592 | tf_op jit(solution)/shard_map/ppermute | solution.py:41
  23.7 2.0 %collective-permute-start.11 = (bf16[272,512]{1,0:T(8,128)(2,1)S(1)}, bf16[272,512]{1,0:T(8,128)(2,1)S(1)}, u32[]{:S(2)}, u32[]{:S(2)}) collective-permute-start(bf16[272,512]{1,0:T(8,128)(2,1)S(1)} %collective-permute-done.3.refs_0_), channel_id=1, source_target_pairs={{0,1},{1,0},{2,3},{3,2},{4,5},{5,4},{6,7},{7,6},{8,9},{9,8},{10,11... | collective-permute-start | bytes 835592 | tf_op jit(solution)/shard_map/ppermute | solution.py:41
  23.9 1.8 %collective-permute-start.12 = (bf16[272,512]{1,0:T(8,128)(2,1)S(1)}, bf16[272,512]{1,0:T(8,128)(2,1)S(1)}, u32[]{:S(2)}, u32[]{:S(2)}) collective-permute-start(bf16[272,512]{1,0:T(8,128)(2,1)S(1)} %collective-permute-done.4.refs_1_), channel_id=1, source_target_pairs={{0,1},{1,0},{2,3},{3,2},{4,5},{5,4},{6,7},{7,6},{8,9},{9,8},{10,11... | collective-permute-start | bytes 835592 | tf_op jit(solution)/shard_map/ppermute | solution.py:41
  26.8 9.9 %collective-permute-start.13 = (bf16[528,128]{1,0:T(8,128)(2,1)S(1)}, bf16[528,128]{1,0:T(8,128)(2,1)S(1)}, u32[]{:S(2)}, u32[]{:S(2)}) collective-permute-start(bf16[528,128]{1,0:T(8,128)(2,1)S(1)} %shard_map.64), channel_id=1, source_target_pairs={{0,16},{1,17},{2,18},{3,19},{4,20},{5,21},{6,22},{7,23},{8,24},{9,... | collective-permute-start | bytes 405512 | tf_op jit(solution)/shard_map/ppermute | solution.py:41
  31.2 6.6 %collective-permute-start.14 = (bf16[528,128]{1,0:T(8,128)(2,1)S(1)}, bf16[528,128]{1,0:T(8,128)(2,1)S(1)}, u32[]{:S(2)}, u32[]{:S(2)}) collective-permute-start(bf16[528,128]{1,0:T(8,128)(2,1)S(1)} %shard_map.65), channel_id=1, source_target_pairs={{0,8},{1,9},{2,10},{3,11},{4,12},{5,13},{6,14},{7,15},{8,16},{9,17... | collective-permute-start | bytes 405512 | tf_op jit(solution)/shard_map/ppermute | solution.py:41
  33.0 5.2 %collective-permute-start.15 = (bf16[528,128]{1,0:T(8,128)(2,1)S(1)}, bf16[528,128]{1,0:T(8,128)(2,1)S(1)}, u32[]{:S(2)}, u32[]{:S(2)}) collective-permute-start(bf16[528,128]{1,0:T(8,128)(2,1)S(1)} %shard_map.66), channel_id=1, source_target_pairs={{0,24},{1,25},{2,26},{3,27},{4,28},{5,29},{6,30},{7,31},{8,0},{9,1... | collective-permute-start | bytes 405512 | tf_op jit(solution)/shard_map/ppermute | solution.py:41
  57.0 4.2 %collective-permute-start.17 = (bf16[128,128]{1,0:T(8,128)(2,1)S(1)}, bf16[128,128]{1,0:T(8,128)(2,1)S(1)}, u32[]{:S(2)}, u32[]{:S(2)}) collective-permute-start(bf16[128,128]{1,0:T(8,128)(2,1)S(1)} %shard_map.68.own), channel_id=1, source_target_pairs={{0,31},{1,0},{2,1},{3,2},{4,3},{5,4},{6,5},{7,6},{8,7},{9,8},{10,9... | collective-permute-start | bytes 98312 | tf_op jit(solution)/shard_map/ppermute | solution.py:463
  59.6 6.7 %collective-permute-start.16 = (bf16[128,128]{1,0:T(8,128)(2,1)S(1)}, bf16[128,128]{1,0:T(8,128)(2,1)S(1)}, u32[]{:S(2)}, u32[]{:S(2)}) collective-permute-start(bf16[128,128]{1,0:T(8,128)(2,1)S(1)} %shard_map.68.own), channel_id=1, source_target_pairs={{0,1},{1,2},{2,3},{3,4},{4,5},{5,6},{6,7},{7,8},{8,9},{9,10},{10,1... | collective-permute-start | bytes 98312 | tf_op jit(solution)/shard_map/ppermute | solution.py:462

commit v12 on v11

--- a/solution.py
+++ b/solution.py
@@ -37,7 +37,7 @@
     pairs = []
     for place in range(Y * X * CORES):
         y, x, c = place // (X * CORES), place // CORES % X, place % CORES
-        pairs.append((place, ((y + dy) % Y * X + (x + dx) % X) * CORES + (c ^ dc)))
+        pairs.append((place, ((y ^ dy) * X + (x ^ dx)) * CORES + (c ^ dc)))
     return lax.ppermute(value, "grid", pairs)
 
 
@@ -89,7 +89,7 @@
     groups = []
     for dx in range(X):
         for dc in range(CORES):
-            cx = lax.rem(x + dx, X) * CORES + lax.rem(c + dc, CORES)
+            cx = jnp.bitwise_xor(x, dx) * CORES + jnp.bitwise_xor(c, dc)
             groups.append(send_picks(turned, cx, dc == 1))
     small[1].wait()
     small[2].wait()
@@ -210,7 +210,7 @@
     picks[...] = tail_picks(high, 0, 4)
     table = ((0, low[...]), (1, high[...]))
     for out, shift in zip(outs, shifts):
-        y = lax.rem(place + shift, Y)
+        y = jnp.bitwise_xor(place, shift)
         tail_row = lax.broadcasted_iota(jnp.int32, (16, K), 0)
         tail = jnp.zeros((16, K), F32)
         for i in range(2):
@@ -372,8 +372,11 @@
     )(own, mean, perturb)
 
 
-def side_kernel(left, right, part, sides, out, held, sems):
-    weights = jnp.concatenate([left[...], right[...]], axis=1)
+def side_kernel(beyond, beside, part, sides, out, held, sems):
+    first_core = lax.rem(lax.axis_index("grid"), CORES) == 0
+    left = jnp.where(first_core, beyond[...], beside[...])
+    right = jnp.where(first_core, beside[...], beyond[...])
+    weights = jnp.concatenate([left, right], axis=1)
     chunks = sems.shape[0]
     pairs = sides.shape[0] // chunks
     copies = []
@@ -390,7 +393,7 @@
         copy.wait()
 
 
-def add_sides(left, right, part, sides):
+def add_sides(beyond, beside, part, sides):
     shape = (2 * sides.shape[0], K, K)
     return pl.pallas_call(
         side_kernel,
@@ -400,7 +403,7 @@
         scratch_shapes=[pltpu.VMEM(shape, BF16), pltpu.SemaphoreType.DMA((8,))],
         compiler_params=params(),
         cost_estimate=cost(2e9),
-    )(left, right, part, sides)
+    )(beyond, beside, part, sides)
 
 
 def on_device(departures, innovation, obs_weight, send_rows, send_counts, state):
@@ -409,7 +412,7 @@
         departures, innovation, obs_weight, send_rows[0].T
     )
     left = hop(low_half, 0, 1, 0)
-    right = hop(high_half, 0, -1, 0)
+    right = hop(high_half, 0, 3, 0)
     other = hop(near, 0, 0, 1)
 
     whole = lambda which: ((0, which, 0), (1, which, HALF))
@@ -421,11 +424,11 @@
         (low_half, high_half, mean, perturb, sides)
     )
     left_more = hop(high_half, 0, 1, 0)
-    right_more = hop(low_half, 0, -1, 0)
+    right_more = hop(low_half, 0, 3, 0)
     left, right, found, mean, perturb = lax.optimization_barrier(
         (left, right, found, mean, perturb)
     )
-    far_low, far_high = hop(left, 0, 1, 0), hop(right, 0, -1, 0)
+    far_low, far_high = hop(left, 0, 3, 0), hop(right, 0, 1, 0)
 
     def firsts(core):
         row = 8 + 4 * core
@@ -453,16 +456,16 @@
     across = last_grams((2,), BF16, *last)[0]
     from_across = hop(across, 2, 0, 0)
     from_up = hop(last_grams((1,), BF16, *last)[0], 1, 0, 0)
-    from_down = hop(last_grams((3,), BF16, *last)[0], -1, 0, 0)
+    from_down = hop(last_grams((3,), BF16, *last)[0], 3, 0, 0)
     own = last_grams((0,), F32, *last)[0]
     parts = sum_parts(own, from_across, from_up, from_down)
     parts = lax.all_to_all(parts, "obs", 0, 0, tiled=True)
 
     own = transposed_weights(parts)
-    low = lax.ppermute(own, "grid", [(j, (j + 1) % n_grid) for j in range(n_grid)])
-    high = lax.ppermute(own, "grid", [(j, (j - 1) % n_grid) for j in range(n_grid)])
+    beyond = lax.ppermute(own, "grid", [(j, (j + 2 * (j % 2) - 1) % n_grid) for j in range(n_grid)])
+    beside = hop(own, 0, 0, 1)
     part = own_part(own, mean, perturb)
-    return add_sides(low, high, part, sides)
+    return add_sides(beyond, beside, part, sides)
 
 
 def solution(mesh):

time: 68 us -> 68.1 us (level)
  starting transfers between devices: 20.4 us -> 16.4 us
  waiting for transfers between devices: 9.83 us -> 13.7 us
    ppermute x16 -> x17, waiting for transfers between devices: 3.73 us -> 10.2 us  [hop(): return lax.ppermute(value, 'grid', pairs)]
    ppermute x16 -> x17, starting transfers between devices: 17.8 us -> 13.7 us  [hop(): return lax.ppermute(value, 'grid', pairs)]
    ppermute x2 -> x1, waiting for transfers between devices: 6.09 us -> 3.43 us  [on_device(): lax.ppermute(own, 'grid', [(j, (j + 2 * (j % 2) - 1) % n_grid) for j in r...]
    ppermute x2 -> x1, starting transfers between devices: 2.61 us -> 2.75 us  [on_device(): lax.ppermute(own, 'grid', [(j, (j + 2 * (j % 2) - 1) % n_grid) for j in r...]
  transfers between devices with their start and end apart: 18 -> 18, of which waited for: 10 -> 8; matrix products, arithmetic and copies ran while one was open for 0% -> 0% of each run, Pallas kernels for 21% -> 21%
where the time goes in v12:
time: 68.1 us; the launch traced here: 67.7 us
  Pallas kernels  20.9 us (31%)
  starting transfers between devices  16.4 us (24%)
  blocking collectives  16.3 us (24%)
  waiting for transfers between devices  13.7 us (20%)
    all_to_all x1, blocking collectives, on_device(): parts = lax.all_to_all(parts, 'obs', 0, 0, tiled=True)  16.3 us
    ppermute x17, starting transfers between devices, hop(): return lax.ppermute(value, 'grid', pairs)  13.7 us
    ppermute x17, waiting for transfers between devices, hop(): return lax.ppermute(value, 'grid', pairs)  10.2 us
    pallas_call x6, Pallas kernels, pick_rows(): pl.pallas_call(functools.partial(pick_kernel, sources, len(args)), out_sh...  9.34 us
    pallas_call x4, Pallas kernels, last_grams(): pl.pallas_call(functools.partial(last_kernel, shifts), out_shape=[jax.Sha...  4.26 us
    ppermute x1, waiting for transfers between devices, on_device(): lax.ppermute(own, 'grid', [(j, (j + 2 * (j % 2) - 1) % n_grid) for j in r...  3.43 us
    ppermute x1, starting transfers between devices, on_device(): lax.ppermute(own, 'grid', [(j, (j + 2 * (j % 2) - 1) % n_grid) for j in r...  2.75 us
    pallas_call x1, Pallas kernels, transposed_weights(): pl.pallas_call(weights_kernel, out_shape=jax.ShapeDtypeStruct((K, K), BF1...  2.34 us
  transfers between devices with their start and end apart: 18, of which 8 were waited for; matrix products, arithmetic and copies ran while one was open for 0% of the time, Pallas kernels for 21%

profile of v12, /device:TPU:32, one launch (start us, length us, event | category | flops | bytes accessed | tf_op | source)
XLA Modules:
  0.0 67.7 jit_solution(14012546955476434809)
XLA Ops:
  0.0 1.8 %shard_map.55 = (bf16[272,512]{1,0:T(8,128)(2,1)S(1)}, bf16[272,512]{1,0:T(8,128)(2,1)S(1)}, bf16[544,512]{1,0:T(8,128)(2,1)S(1)}) custom-call(bf16[2048,128]{1,0:T(8,128)(2,1)} %departures.1, f32[2048]{0:T(1024)} %innovation.1, f32[2048]{0:T(1024)} %obs_weight.1, s32[64,256]{1,0:T(8,128)} %bitcast.3), custom_call_target="tpu_custom_call" | custom-call | flops 2000000000 | bytes 100000 | tf_op jit(solution)/shard_map/pallas_call | solution.py:121
  1.8 1.6 %collective-permute-start = (bf16[272,512]{1,0:T(8,128)(2,1)S(1)}, bf16[272,512]{1,0:T(8,128)(2,1)S(1)}, u32[]{:S(2)}, u32[]{:S(2)}) collective-permute-start(bf16[272,512]{1,0:T(8,128)(2,1)S(1)} %get-tuple-element.61), channel_id=1, source_target_pairs={{0,2},{1,3},{2,0},{3,1},{4,6},{5,7},{6,4},{7,5},{8,10},{9,11},{10,... | collective-permute-start | bytes 835592 | tf_op jit(solution)/shard_map/ppermute | solution.py:41
  3.3 2.1 %collective-permute-start.1 = (bf16[272,512]{1,0:T(8,128)(2,1)S(1)}, bf16[272,512]{1,0:T(8,128)(2,1)S(1)}, u32[]{:S(2)}, u32[]{:S(2)}) collective-permute-start(bf16[272,512]{1,0:T(8,128)(2,1)S(1)} %get-tuple-element.60), channel_id=1, source_target_pairs={{0,6},{1,7},{2,4},{3,5},{4,2},{5,3},{6,0},{7,1},{8,14},{9,15},{10,... | collective-permute-start | bytes 835592 | tf_op jit(solution)/shard_map/ppermute | solution.py:41
  5.4 0.0 collective-permute-start.2
  5.4 1.2 %shard_map.57 = (f32[24,256]{1,0:T(8,128)S(1)}, bf16[24,128,256]{2,1,0:T(8,128)(2,1)S(1)}, bf16[24,256,256]{2,1,0:T(8,128)(2,1)S(1)}) custom-call(bf16[48,128,128]{2,1,0:T(8,128)(2,1)S(1)} %copy-done), custom_call_target="tpu_custom_call" | custom-call | flops 60000002048 | bytes 100000 | tf_op jit(solution)/shard_map/pallas_call | solution.py:342
  6.6 0.7 %collective-permute-start.7 = (bf16[272,512]{1,0:T(8,128)(2,1)S(1)}, bf16[272,512]{1,0:T(8,128)(2,1)S(1)}, u32[]{:S(2)}, u32[]{:S(2)}) collective-permute-start(bf16[272,512]{1,0:T(8,128)(2,1)S(1)} %get-tuple-element.60), channel_id=1, source_target_pairs={{0,2},{1,3},{2,0},{3,1},{4,6},{5,7},{6,4},{7,5},{8,10},{9,11},{10,... | collective-permute-start | bytes 835592 | tf_op jit(solution)/shard_map/ppermute | solution.py:41
  7.3 0.6 collective-permute-start.8
  7.9 0.0 collective-permute-done.2.refs_1_
  7.9 2.5 %shard_map.56 = (bf16[8,144,256]{2,1,0:T(8,128)(2,1)S(1)}, bf16[8,144,256]{2,1,0:T(8,128)(2,1)S(1)}) custom-call(bf16[544,512]{1,0:T(8,128)(2,1)S(1)} %get-tuple-element.46.refs_0_, bf16[544,512]{1,0:T(8,128)(2,1)S(1)} %collective-permute-done.2.refs_1_), custom_call_target="tpu_custom_call" | custom-call | flops 1000000 | bytes 100000 | tf_op jit(solution)/shard_map/pallas_call | solution.py:171
  10.5 0.1 collective-permute-done.refs_0_
  10.6 3.3 %collective-permute-done.1.refs_1_ = bf16[272,512]{1,0:T(8,128)(2,1)S(1)} collective-permute-done((bf16[272,512]{1,0:T(8,128)(2,1)S(1)}, bf16[272,512]{1,0:T(8,128)(2,1)S(1)}, u32[]{:S(2)}, u32[]{:S(2)}) %collective-permute-start.1) | collective-permute-done | bytes 278560 | tf_op jit(solution)/shard_map/ppermute | solution.py:41
  13.9 2.3 %collective-permute-start.3 = (bf16[272,512]{1,0:T(8,128)(2,1)S(1)}, bf16[272,512]{1,0:T(8,128)(2,1)S(1)}, u32[]{:S(2)}, u32[]{:S(2)}) collective-permute-start(bf16[272,512]{1,0:T(8,128)(2,1)S(1)} %collective-permute-done.refs_0_), channel_id=1, source_target_pairs={{0,6},{1,7},{2,4},{3,5},{4,2},{5,3},{6,0},{7,1},{8,14},{9,15},{10,... | collective-permute-start | bytes 835592 | tf_op jit(solution)/shard_map/ppermute | solution.py:41
  16.2 0.0 collective-permute-start.4
  16.2 1.4 %shard_map.58 = (bf16[8,144,256]{2,1,0:T(8,128)(2,1)S(1)}, bf16[8,144,256]{2,1,0:T(8,128)(2,1)S(1)}) custom-call(bf16[272,512]{1,0:T(8,128)(2,1)S(1)} %collective-permute-done.refs_0_, bf16[272,512]{1,0:T(8,128)(2,1)S(1)} %collective-permute-done.1.refs_1_), custom_call_target="tpu_custom_call" | custom-call | flops 1000000 | bytes 100000 | tf_op jit(solution)/shard_map/pallas_call | solution.py:171
  17.6 0.1 collective-permute-start.5
  17.7 0.5 collective-permute-start.6
  18.2 1.7 %collective-permute-done.8.refs_3_ = bf16[272,512]{1,0:T(8,128)(2,1)S(1)} collective-permute-done((bf16[272,512]{1,0:T(8,128)(2,1)S(1)}, bf16[272,512]{1,0:T(8,128)(2,1)S(1)}, u32[]{:S(2)}, u32[]{:S(2)}) %collective-permute-start.8) | collective-permute-done | bytes 278560 | tf_op jit(solution)/shard_map/ppermute | solution.py:41
  19.9 1.4 %shard_map.59 = (bf16[8,144,256]{2,1,0:T(8,128)(2,1)S(1)}, bf16[8,144,256]{2,1,0:T(8,128)(2,1)S(1)}) custom-call(bf16[272,512]{1,0:T(8,128)(2,1)S(1)} %collective-permute-done.refs_0_, bf16[272,512]{1,0:T(8,128)(2,1)S(1)} %collective-permute-done.1.refs_1_, bf16[272,512]{1,0:T(8,128)(2,1)S(1)} %collective-permute-done.7.refs_2_, ...), custom_call_target="tpu_custom_call" | custom-call | flops 60000002048 | bytes 100000 | tf_op jit(solution)/shard_map/pallas_call | solution.py:171
  21.3 0.1 collective-permute-start.9
  21.4 0.5 collective-permute-start.10
  21.9 1.4 %shard_map.60 = (bf16[8,144,256]{2,1,0:T(8,128)(2,1)S(1)}, bf16[8,144,256]{2,1,0:T(8,128)(2,1)S(1)}) custom-call(bf16[272,512]{1,0:T(8,128)(2,1)S(1)} %collective-permute-done.5.refs_0_, bf16[272,512]{1,0:T(8,128)(2,1)S(1)} %collective-permute-done.6.refs_1_), custom_call_target="tpu_custom_call" | custom-call | flops 60000002048 | bytes 100000 | tf_op jit(solution)/shard_map/pallas_call | solution.py:171
  23.3 0.0 collective-permute-done.9.refs_2_
  23.3 0.1 collective-permute-done.10.refs_3_
  23.3 1.4 %shard_map.61 = (bf16[8,144,256]{2,1,0:T(8,128)(2,1)S(1)}, bf16[8,144,256]{2,1,0:T(8,128)(2,1)S(1)}) custom-call(bf16[272,512]{1,0:T(8,128)(2,1)S(1)} %collective-permute-done.5.refs_0_, bf16[272,512]{1,0:T(8,128)(2,1)S(1)} %collective-permute-done.6.refs_1_, bf16[272,512]{1,0:T(8,128)(2,1)S(1)} %collective-permute-done.9.refs_2_, ...), custom_call_target="tpu_custom_call" | custom-call | flops 1000000 | bytes 100000 | tf_op jit(solution)/shard_map/pallas_call | solution.py:171
  24.7 0.0 collective-permute-done.3.refs_0_
  24.7 0.3 collective-permute-start.11
  25.1 0.3 collective-permute-start.12
  25.3 1.4 %shard_map.62.same = bf16[8,144,256]{2,1,0:T(8,128)(2,1)S(1)} custom-call(bf16[272,512]{1,0:T(8,128)(2,1)S(1)} %collective-permute-done.3.refs_0_, bf16[272,512]{1,0:T(8,128)(2,1)S(1)} %collective-permute-done.4.refs_1_), custom_call_target="tpu_custom_call" | custom-call | flops 1000000 | bytes 100000 | tf_op jit(solution)/shard_map/pallas_call | solution.py:171
  26.7 0.0 collective-permute-done.11.low
  26.7 0.1 collective-permute-done.12.high
  26.8 1.1 %shard_map.64 = bf16[528,128]{1,0:T(8,128)(2,1)S(1)} custom-call(bf16[272,512]{1,0:T(8,128)(2,1)S(1)} %collective-permute-done.11.low, bf16[272,512]{1,0:T(8,128)(2,1)S(1)} %collective-permute-done.12.high, bf16[8,144,256]{2,1,0:T(8,128)(2,1)S(1)} %shard_map.62.same, bf16[8,144,256]{2,1,0:T(8,128)(2,1)S(1)} %get-tuple-element.74.rest_0_, ...), custom_call_target="tpu_custom_call" | custom-call | flops 1000000000 | bytes 100000 | tf_op jit(solution)/shard_map/pallas_call | solution.py:238
  27.9 3.3 %collective-permute-start.13 = (bf16[528,128]{1,0:T(8,128)(2,1)S(1)}, bf16[528,128]{1,0:T(8,128)(2,1)S(1)}, u32[]{:S(2)}, u32[]{:S(2)}) collective-permute-start(bf16[528,128]{1,0:T(8,128)(2,1)S(1)} %shard_map.64), channel_id=1, source_target_pairs={{0,16},{1,17},{2,18},{3,19},{4,20},{5,21},{6,22},{7,23},{8,24},{9,... | collective-permute-start | bytes 405512 | tf_op jit(solution)/shard_map/ppermute | solution.py:41
  31.1 1.1 %shard_map.65 = bf16[528,128]{1,0:T(8,128)(2,1)S(1)} custom-call(bf16[272,512]{1,0:T(8,128)(2,1)S(1)} %collective-permute-done.11.low, bf16[272,512]{1,0:T(8,128)(2,1)S(1)} %collective-permute-done.12.high, bf16[8,144,256]{2,1,0:T(8,128)(2,1)S(1)} %shard_map.62.same, bf16[8,144,256]{2,1,0:T(8,128)(2,1)S(1)} %get-tuple-element.74.rest_0_, ...), custom_call_target="tpu_custom_call" | custom-call | flops 1000000000 | bytes 100000 | tf_op jit(solution)/shard_map/pallas_call | solution.py:238
  32.2 0.8 %collective-permute-start.14 = (bf16[528,128]{1,0:T(8,128)(2,1)S(1)}, bf16[528,128]{1,0:T(8,128)(2,1)S(1)}, u32[]{:S(2)}, u32[]{:S(2)}) collective-permute-start(bf16[528,128]{1,0:T(8,128)(2,1)S(1)} %shard_map.65), channel_id=1, source_target_pairs={{0,8},{1,9},{2,10},{3,11},{4,12},{5,13},{6,14},{7,15},{8,0},{9,1},... | collective-permute-start | bytes 405512 | tf_op jit(solution)/shard_map/ppermute | solution.py:41
  33.0 1.1 %shard_map.66 = bf16[528,128]{1,0:T(8,128)(2,1)S(1)} custom-call(bf16[272,512]{1,0:T(8,128)(2,1)S(1)} %collective-permute-done.11.low, bf16[272,512]{1,0:T(8,128)(2,1)S(1)} %collective-permute-done.12.high, bf16[8,144,256]{2,1,0:T(8,128)(2,1)S(1)} %shard_map.62.same, bf16[8,144,256]{2,1,0:T(8,128)(2,1)S(1)} %get-tuple-element.74.rest_0_, ...), custom_call_target="tpu_custom_call" | custom-call | flops 1000000000 | bytes 100000 | tf_op jit(solution)/shard_map/pallas_call | solution.py:238
  34.0 0.5 collective-permute-start.15
  34.5 1.1 %shard_map.63.own = f32[528,128]{1,0:T(8,128)S(1)} custom-call(bf16[272,512]{1,0:T(8,128)(2,1)S(1)} %collective-permute-done.11.low, bf16[272,512]{1,0:T(8,128)(2,1)S(1)} %collective-permute-done.12.high, bf16[8,144,256]{2,1,0:T(8,128)(2,1)S(1)} %shard_map.62.same, bf16[8,144,256]{2,1,0:T(8,128)(2,1)S(1)} %get-tuple-element.74.rest_0_, ...), custom_call_target="tpu_custom_call" | custom-call | flops 1000000000 | bytes 100000 | tf_op jit(solution)/shard_map/pallas_call | solution.py:238
  35.6 2.8 %collective-permute-done.14.b = bf16[528,128]{1,0:T(8,128)(2,1)S(1)} collective-permute-done((bf16[528,128]{1,0:T(8,128)(2,1)S(1)}, bf16[528,128]{1,0:T(8,128)(2,1)S(1)}, u32[]{:S(2)}, u32[]{:S(2)}) %collective-permute-start.14) | collective-permute-done | bytes 135200 | tf_op jit(solution)/shard_map/ppermute | solution.py:41
  38.4 2.1 %collective-permute-done.15.c = bf16[528,128]{1,0:T(8,128)(2,1)S(1)} collective-permute-done((bf16[528,128]{1,0:T(8,128)(2,1)S(1)}, bf16[528,128]{1,0:T(8,128)(2,1)S(1)}, u32[]{:S(2)}, u32[]{:S(2)}) %collective-permute-start.15) | collective-permute-done | bytes 135200 | tf_op jit(solution)/shard_map/ppermute | solution.py:41
  40.5 0.1 shard_map.67
  40.6 16.3 %all_to_all.5.parts = bf16[8,80,128]{2,1,0:T(8,128)(2,1)S(1)} all-to-all(bf16[8,80,128]{2,1,0:T(8,128)(2,1)S(1)} %shard_map.67), channel_id=1, replica_groups=mesh['obs'=8,'grid'=32] {'obs'}, dimensions={0} | all-to-all | bytes 327680 | tf_op jit(solution)/shard_map/all_to_all | solution.py:462
  56.9 2.3 %shard_map.68.own = bf16[128,128]{1,0:T(8,128)(2,1)S(1)} custom-call(bf16[8,80,128]{2,1,0:T(8,128)(2,1)S(1)} %all_to_all.5.parts), custom_call_target="tpu_custom_call" | custom-call | flops 4000000000 | bytes 100000 | tf_op jit(solution)/shard_map/pallas_call | solution.py:310
  59.3 0.1 collective-permute-start.17
  59.4 2.7 %collective-permute-start.16 = (bf16[128,128]{1,0:T(8,128)(2,1)S(1)}, bf16[128,128]{1,0:T(8,128)(2,1)S(1)}, u32[]{:S(2)}, u32[]{:S(2)}) collective-permute-start(bf16[128,128]{1,0:T(8,128)(2,1)S(1)} %shard_map.68.own), channel_id=1, source_target_pairs={{0,31},{1,2},{2,1},{3,4},{4,3},{5,6},{6,5},{7,8},{8,7},{9,10},{10,... | collective-permute-start | bytes 98312 | tf_op jit(solution)/shard_map/ppermute | solution.py:465
  62.1 0.6 shard_map.69.part
  62.7 0.0 collective-permute-done.17.beside
  62.7 3.4 %collective-permute-done.16.beyond = bf16[128,128]{1,0:T(8,128)(2,1)S(1)} collective-permute-done((bf16[128,128]{1,0:T(8,128)(2,1)S(1)}, bf16[128,128]{1,0:T(8,128)(2,1)S(1)}, u32[]{:S(2)}, u32[]{:S(2)}) %collective-permute-start.16) | collective-permute-done | bytes 32800 | tf_op jit(solution)/shard_map/ppermute | solution.py:465
  66.1 1.4 %shard_map.70 = bf16[48,128,128]{2,1,0:T(8,128)(2,1)} custom-call(bf16[128,128]{1,0:T(8,128)(2,1)S(1)} %collective-permute-done.16.beyond, bf16[128,128]{1,0:T(8,128)(2,1)S(1)} %collective-permute-done.17.beside, f32[24,128,256]{2,1,0:T(8,128)S(1)} %shard_map.69.part, bf16[24,256,256]{2,1,0:T(8,128)(2,1)S(1)} %get-tuple-element.82.sides), custom_call_target="tpu_custom_call" | custom-call | flops 2000000000 | bytes 100000 | tf_op jit(solution)/shard_map/pallas_call | solution.py:398
  (7 shorter events, 0.0 us)
Async XLA Ops:
  0.0 5.4 %copy-start = (bf16[48,128,128]{2,1,0:T(8,128)(2,1)S(1)}, bf16[48,128,128]{2,1,0:T(8,128)(2,1)}, u32[]{:S(2)}) copy-start(bf16[48,128,128]{2,1,0:T(8,128)(2,1)} %state.1) | copy-start | bytes 4718596
  1.8 8.9 %collective-permute-start = (bf16[272,512]{1,0:T(8,128)(2,1)S(1)}, bf16[272,512]{1,0:T(8,128)(2,1)S(1)}, u32[]{:S(2)}, u32[]{:S(2)}) collective-permute-start(bf16[272,512]{1,0:T(8,128)(2,1)S(1)} %get-tuple-element.61), channel_id=1, source_target_pairs={{0,2},{1,3},{2,0},{3,1},{4,6},{5,7},{6,4},{7,5},{8,10},{9,11},{10,... | collective-permute-start | bytes 835592 | tf_op jit(solution)/shard_map/ppermute | solution.py:41
  3.3 10.6 %collective-permute-start.1 = (bf16[272,512]{1,0:T(8,128)(2,1)S(1)}, bf16[272,512]{1,0:T(8,128)(2,1)S(1)}, u32[]{:S(2)}, u32[]{:S(2)}) collective-permute-start(bf16[272,512]{1,0:T(8,128)(2,1)S(1)} %get-tuple-element.60), channel_id=1, source_target_pairs={{0,6},{1,7},{2,4},{3,5},{4,2},{5,3},{6,0},{7,1},{8,14},{9,15},{10,... | collective-permute-start | bytes 835592 | tf_op jit(solution)/shard_map/ppermute | solution.py:41
  5.4 2.5 %collective-permute-start.2 = (bf16[544,512]{1,0:T(8,128)(2,1)S(1)}, bf16[544,512]{1,0:T(8,128)(2,1)S(1)}, u32[]{:S(2)}, u32[]{:S(2)}) collective-permute-start(bf16[544,512]{1,0:T(8,128)(2,1)S(1)} %get-tuple-element.46.refs_0_), channel_id=1, source_target_pairs={{0,1},{1,0},{2,3},{3,2},{4,5},{5,4},{6,7},{7,6},{8,9},{9,8},{10,11... | collective-permute-start | bytes 1671176 | tf_op jit(solution)/shard_map/ppermute | solution.py:41
  6.6 11.1 %collective-permute-start.7 = (bf16[272,512]{1,0:T(8,128)(2,1)S(1)}, bf16[272,512]{1,0:T(8,128)(2,1)S(1)}, u32[]{:S(2)}, u32[]{:S(2)}) collective-permute-start(bf16[272,512]{1,0:T(8,128)(2,1)S(1)} %get-tuple-element.60), channel_id=1, source_target_pairs={{0,2},{1,3},{2,0},{3,1},{4,6},{5,7},{6,4},{7,5},{8,10},{9,11},{10,... | collective-permute-start | bytes 835592 | tf_op jit(solution)/shard_map/ppermute | solution.py:41
  7.3 12.6 %collective-permute-start.8 = (bf16[272,512]{1,0:T(8,128)(2,1)S(1)}, bf16[272,512]{1,0:T(8,128)(2,1)S(1)}, u32[]{:S(2)}, u32[]{:S(2)}) collective-permute-start(bf16[272,512]{1,0:T(8,128)(2,1)S(1)} %get-tuple-element.61), channel_id=1, source_target_pairs={{0,6},{1,7},{2,4},{3,5},{4,2},{5,3},{6,0},{7,1},{8,14},{9,15},{10,... | collective-permute-start | bytes 835592 | tf_op jit(solution)/shard_map/ppermute | solution.py:41
  13.9 10.8 %collective-permute-start.3 = (bf16[272,512]{1,0:T(8,128)(2,1)S(1)}, bf16[272,512]{1,0:T(8,128)(2,1)S(1)}, u32[]{:S(2)}, u32[]{:S(2)}) collective-permute-start(bf16[272,512]{1,0:T(8,128)(2,1)S(1)} %collective-permute-done.refs_0_), channel_id=1, source_target_pairs={{0,6},{1,7},{2,4},{3,5},{4,2},{5,3},{6,0},{7,1},{8,14},{9,15},{10,... | collective-permute-start | bytes 835592 | tf_op jit(solution)/shard_map/ppermute | solution.py:41
  16.2 8.5 %collective-permute-start.4 = (bf16[272,512]{1,0:T(8,128)(2,1)S(1)}, bf16[272,512]{1,0:T(8,128)(2,1)S(1)}, u32[]{:S(2)}, u32[]{:S(2)}) collective-permute-start(bf16[272,512]{1,0:T(8,128)(2,1)S(1)} %collective-permute-done.1.refs_1_), channel_id=1, source_target_pairs={{0,2},{1,3},{2,0},{3,1},{4,6},{5,7},{6,4},{7,5},{8,10},{9,11},{10,... | collective-permute-start | bytes 835592 | tf_op jit(solution)/shard_map/ppermute | solution.py:41
  17.6 3.8 %collective-permute-start.5 = (bf16[272,512]{1,0:T(8,128)(2,1)S(1)}, bf16[272,512]{1,0:T(8,128)(2,1)S(1)}, u32[]{:S(2)}, u32[]{:S(2)}) collective-permute-start(bf16[272,512]{1,0:T(8,128)(2,1)S(1)} %collective-permute-done.refs_0_), channel_id=1, source_target_pairs={{0,1},{1,0},{2,3},{3,2},{4,5},{5,4},{6,7},{7,6},{8,9},{9,8},{10,11... | collective-permute-start | bytes 835592 | tf_op jit(solution)/shard_map/ppermute | solution.py:41
  17.7 4.2 %collective-permute-start.6 = (bf16[272,512]{1,0:T(8,128)(2,1)S(1)}, bf16[272,512]{1,0:T(8,128)(2,1)S(1)}, u32[]{:S(2)}, u32[]{:S(2)}) collective-permute-start(bf16[272,512]{1,0:T(8,128)(2,1)S(1)} %collective-permute-done.1.refs_1_), channel_id=1, source_target_pairs={{0,1},{1,0},{2,3},{3,2},{4,5},{5,4},{6,7},{7,6},{8,9},{9,8},{10,11... | collective-permute-start | bytes 835592 | tf_op jit(solution)/shard_map/ppermute | solution.py:41
  21.3 2.0 %collective-permute-start.9 = (bf16[272,512]{1,0:T(8,128)(2,1)S(1)}, bf16[272,512]{1,0:T(8,128)(2,1)S(1)}, u32[]{:S(2)}, u32[]{:S(2)}) collective-permute-start(bf16[272,512]{1,0:T(8,128)(2,1)S(1)} %collective-permute-done.7.refs_2_), channel_id=1, source_target_pairs={{0,1},{1,0},{2,3},{3,2},{4,5},{5,4},{6,7},{7,6},{8,9},{9,8},{10,11... | collective-permute-start | bytes 835592 | tf_op jit(solution)/shard_map/ppermute | solution.py:41
  21.4 1.9 %collective-permute-start.10 = (bf16[272,512]{1,0:T(8,128)(2,1)S(1)}, bf16[272,512]{1,0:T(8,128)(2,1)S(1)}, u32[]{:S(2)}, u32[]{:S(2)}) collective-permute-start(bf16[272,512]{1,0:T(8,128)(2,1)S(1)} %collective-permute-done.8.refs_3_), channel_id=1, source_target_pairs={{0,1},{1,0},{2,3},{3,2},{4,5},{5,4},{6,7},{7,6},{8,9},{9,8},{10,11... | collective-permute-start | bytes 835592 | tf_op jit(solution)/shard_map/ppermute | solution.py:41
  24.7 2.0 %collective-permute-start.11 = (bf16[272,512]{1,0:T(8,128)(2,1)S(1)}, bf16[272,512]{1,0:T(8,128)(2,1)S(1)}, u32[]{:S(2)}, u32[]{:S(2)}) collective-permute-start(bf16[272,512]{1,0:T(8,128)(2,1)S(1)} %collective-permute-done.3.refs_0_), channel_id=1, source_target_pairs={{0,1},{1,0},{2,3},{3,2},{4,5},{5,4},{6,7},{7,6},{8,9},{9,8},{10,11... | collective-permute-start | bytes 835592 | tf_op jit(solution)/shard_map/ppermute | solution.py:41
  25.1 1.7 %collective-permute-start.12 = (bf16[272,512]{1,0:T(8,128)(2,1)S(1)}, bf16[272,512]{1,0:T(8,128)(2,1)S(1)}, u32[]{:S(2)}, u32[]{:S(2)}) collective-permute-start(bf16[272,512]{1,0:T(8,128)(2,1)S(1)} %collective-permute-done.4.refs_1_), channel_id=1, source_target_pairs={{0,1},{1,0},{2,3},{3,2},{4,5},{5,4},{6,7},{7,6},{8,9},{9,8},{10,11... | collective-permute-start | bytes 835592 | tf_op jit(solution)/shard_map/ppermute | solution.py:41
  27.9 7.7 %collective-permute-start.13 = (bf16[528,128]{1,0:T(8,128)(2,1)S(1)}, bf16[528,128]{1,0:T(8,128)(2,1)S(1)}, u32[]{:S(2)}, u32[]{:S(2)}) collective-permute-start(bf16[528,128]{1,0:T(8,128)(2,1)S(1)} %shard_map.64), channel_id=1, source_target_pairs={{0,16},{1,17},{2,18},{3,19},{4,20},{5,21},{6,22},{7,23},{8,24},{9,... | collective-permute-start | bytes 405512 | tf_op jit(solution)/shard_map/ppermute | solution.py:41
  32.2 6.2 %collective-permute-start.14 = (bf16[528,128]{1,0:T(8,128)(2,1)S(1)}, bf16[528,128]{1,0:T(8,128)(2,1)S(1)}, u32[]{:S(2)}, u32[]{:S(2)}) collective-permute-start(bf16[528,128]{1,0:T(8,128)(2,1)S(1)} %shard_map.65), channel_id=1, source_target_pairs={{0,8},{1,9},{2,10},{3,11},{4,12},{5,13},{6,14},{7,15},{8,0},{9,1},... | collective-permute-start | bytes 405512 | tf_op jit(solution)/shard_map/ppermute | solution.py:41
  34.0 6.5 %collective-permute-start.15 = (bf16[528,128]{1,0:T(8,128)(2,1)S(1)}, bf16[528,128]{1,0:T(8,128)(2,1)S(1)}, u32[]{:S(2)}, u32[]{:S(2)}) collective-permute-start(bf16[528,128]{1,0:T(8,128)(2,1)S(1)} %shard_map.66), channel_id=1, source_target_pairs={{0,24},{1,25},{2,26},{3,27},{4,28},{5,29},{6,30},{7,31},{8,16},{9,... | collective-permute-start | bytes 405512 | tf_op jit(solution)/shard_map/ppermute | solution.py:41
  59.3 3.4 %collective-permute-start.17 = (bf16[128,128]{1,0:T(8,128)(2,1)S(1)}, bf16[128,128]{1,0:T(8,128)(2,1)S(1)}, u32[]{:S(2)}, u32[]{:S(2)}) collective-permute-start(bf16[128,128]{1,0:T(8,128)(2,1)S(1)} %shard_map.68.own), channel_id=1, source_target_pairs={{0,1},{1,0},{2,3},{3,2},{4,5},{5,4},{6,7},{7,6},{8,9},{9,8},{10,11... | collective-permute-start | bytes 98312 | tf_op jit(solution)/shard_map/ppermute | solution.py:41
  59.4 6.7 %collective-permute-start.16 = (bf16[128,128]{1,0:T(8,128)(2,1)S(1)}, bf16[128,128]{1,0:T(8,128)(2,1)S(1)}, u32[]{:S(2)}, u32[]{:S(2)}) collective-permute-start(bf16[128,128]{1,0:T(8,128)(2,1)S(1)} %shard_map.68.own), channel_id=1, source_target_pairs={{0,31},{1,2},{2,1},{3,4},{4,3},{5,6},{6,5},{7,8},{8,7},{9,10},{10,... | collective-permute-start | bytes 98312 | tf_op jit(solution)/shard_map/ppermute | solution.py:465

commit v13 on v12

--- a/solution.py
+++ b/solution.py
@@ -37,7 +37,7 @@
     pairs = []
     for place in range(Y * X * CORES):
         y, x, c = place // (X * CORES), place // CORES % X, place % CORES
-        pairs.append((place, ((y ^ dy) * X + (x ^ dx)) * CORES + (c ^ dc)))
+        pairs.append((place, ((y + dy) % Y * X + (x + dx) % X) * CORES + (c ^ dc)))
     return lax.ppermute(value, "grid", pairs)
 
 
@@ -89,7 +89,7 @@
     groups = []
     for dx in range(X):
         for dc in range(CORES):
-            cx = jnp.bitwise_xor(x, dx) * CORES + jnp.bitwise_xor(c, dc)
+            cx = lax.rem(x + dx, X) * CORES + lax.rem(c + dc, CORES)
             groups.append(send_picks(turned, cx, dc == 1))
     small[1].wait()
     small[2].wait()
@@ -210,7 +210,7 @@
     picks[...] = tail_picks(high, 0, 4)
     table = ((0, low[...]), (1, high[...]))
     for out, shift in zip(outs, shifts):
-        y = jnp.bitwise_xor(place, shift)
+        y = lax.rem(place + shift, Y)
         tail_row = lax.broadcasted_iota(jnp.int32, (16, K), 0)
         tail = jnp.zeros((16, K), F32)
         for i in range(2):
@@ -412,7 +412,7 @@
         departures, innovation, obs_weight, send_rows[0].T
     )
     left = hop(low_half, 0, 1, 0)
-    right = hop(high_half, 0, 3, 0)
+    right = hop(high_half, 0, -1, 0)
     other = hop(near, 0, 0, 1)
 
     whole = lambda which: ((0, which, 0), (1, which, HALF))
@@ -424,11 +424,11 @@
         (low_half, high_half, mean, perturb, sides)
     )
     left_more = hop(high_half, 0, 1, 0)
-    right_more = hop(low_half, 0, 3, 0)
+    right_more = hop(low_half, 0, -1, 0)
     left, right, found, mean, perturb = lax.optimization_barrier(
         (left, right, found, mean, perturb)
     )
-    far_low, far_high = hop(left, 0, 3, 0), hop(right, 0, 1, 0)
+    far_low, far_high = hop(left, 0, 1, 0), hop(right, 0, -1, 0)
 
     def firsts(core):
         row = 8 + 4 * core
@@ -456,15 +456,16 @@
     across = last_grams((2,), BF16, *last)[0]
     from_across = hop(across, 2, 0, 0)
     from_up = hop(last_grams((1,), BF16, *last)[0], 1, 0, 0)
-    from_down = hop(last_grams((3,), BF16, *last)[0], 3, 0, 0)
+    from_down = hop(last_grams((3,), BF16, *last)[0], -1, 0, 0)
     own = last_grams((0,), F32, *last)[0]
     parts = sum_parts(own, from_across, from_up, from_down)
     parts = lax.all_to_all(parts, "obs", 0, 0, tiled=True)
 
     own = transposed_weights(parts)
     beyond = lax.ppermute(own, "grid", [(j, (j + 2 * (j % 2) - 1) % n_grid) for j in range(n_grid)])
+    part = own_part(own, mean, perturb)
+    own, part = lax.optimization_barrier((own, part))
     beside = hop(own, 0, 0, 1)
-    part = own_part(own, mean, perturb)
     return add_sides(beyond, beside, part, sides)
 
 

time: 68.1 us -> 66.3 us (0.974)
  waiting for transfers between devices: 13.7 us -> 7.2 us
  starting transfers between devices: 16.4 us -> 20.5 us
    ppermute x17, waiting for transfers between devices: 10.2 us -> 3.74 us  [hop(): return lax.ppermute(value, 'grid', pairs)]
    ppermute x17, starting transfers between devices: 13.7 us -> 17.9 us  [hop(): return lax.ppermute(value, 'grid', pairs)]
  transfers between devices with their start and end apart: 18 -> 18, of which waited for: 8 -> 9; matrix products, arithmetic and copies ran while one was open for 0% -> 0% of each run, Pallas kernels for 21% -> 22%
where the time goes in v13:
time: 66.3 us; the launch traced here: 65.4 us
  Pallas kernels  20.9 us (32%)
  starting transfers between devices  20.5 us (31%)
  blocking collectives  16.4 us (25%)
  waiting for transfers between devices  7.2 us (11%)
    ppermute x17, starting transfers between devices, hop(): return lax.ppermute(value, 'grid', pairs)  17.9 us
    all_to_all x1, blocking collectives, on_device(): parts = lax.all_to_all(parts, 'obs', 0, 0, tiled=True)  16.4 us
    pallas_call x6, Pallas kernels, pick_rows(): pl.pallas_call(functools.partial(pick_kernel, sources, len(args)), out_sh...  9.32 us
    pallas_call x4, Pallas kernels, last_grams(): pl.pallas_call(functools.partial(last_kernel, shifts), out_shape=[jax.Sha...  4.27 us
    ppermute x17, waiting for transfers between devices, hop(): return lax.ppermute(value, 'grid', pairs)  3.74 us
    ppermute x1, waiting for transfers between devices, on_device(): lax.ppermute(own, 'grid', [(j, (j + 2 * (j % 2) - 1) % n_grid) for j in r...  3.46 us
    ppermute x1, starting transfers between devices, on_device(): lax.ppermute(own, 'grid', [(j, (j + 2 * (j % 2) - 1) % n_grid) for j in r...  2.62 us
    pallas_call x1, Pallas kernels, transposed_weights(): pl.pallas_call(weights_kernel, out_shape=jax.ShapeDtypeStruct((K, K), BF1...  2.34 us
  transfers between devices with their start and end apart: 18, of which 9 were waited for; matrix products, arithmetic and copies ran while one was open for 0% of the time, Pallas kernels for 22%

profile of v13, /device:TPU:32, one launch (start us, length us, event | category | flops | bytes accessed | tf_op | source)
XLA Modules:
  0.0 65.4 jit_solution(8047038919261182752)
XLA Ops:
  0.0 1.8 %shard_map.55 = (bf16[272,512]{1,0:T(8,128)(2,1)S(1)}, bf16[272,512]{1,0:T(8,128)(2,1)S(1)}, bf16[544,512]{1,0:T(8,128)(2,1)S(1)}) custom-call(bf16[2048,128]{1,0:T(8,128)(2,1)} %departures.1, f32[2048]{0:T(1024)} %innovation.1, f32[2048]{0:T(1024)} %obs_weight.1, s32[64,256]{1,0:T(8,128)} %bitcast.3), custom_call_target="tpu_custom_call" | custom-call | flops 2000000000 | bytes 100000 | tf_op jit(solution)/shard_map/pallas_call | solution.py:121
  1.8 1.6 %collective-permute-start = (bf16[272,512]{1,0:T(8,128)(2,1)S(1)}, bf16[272,512]{1,0:T(8,128)(2,1)S(1)}, u32[]{:S(2)}, u32[]{:S(2)}) collective-permute-start(bf16[272,512]{1,0:T(8,128)(2,1)S(1)} %get-tuple-element.63), channel_id=1, source_target_pairs={{0,2},{1,3},{2,4},{3,5},{4,6},{5,7},{6,0},{7,1},{8,10},{9,11},{10,... | collective-permute-start | bytes 835592 | tf_op jit(solution)/shard_map/ppermute | solution.py:41
  3.3 1.7 %collective-permute-start.1 = (bf16[272,512]{1,0:T(8,128)(2,1)S(1)}, bf16[272,512]{1,0:T(8,128)(2,1)S(1)}, u32[]{:S(2)}, u32[]{:S(2)}) collective-permute-start(bf16[272,512]{1,0:T(8,128)(2,1)S(1)} %get-tuple-element.62), channel_id=1, source_target_pairs={{0,6},{1,7},{2,0},{3,1},{4,2},{5,3},{6,4},{7,5},{8,14},{9,15},{10,... | collective-permute-start | bytes 835592 | tf_op jit(solution)/shard_map/ppermute | solution.py:41
  5.1 1.2 %shard_map.57 = (f32[24,256]{1,0:T(8,128)S(1)}, bf16[24,128,256]{2,1,0:T(8,128)(2,1)S(1)}, bf16[24,256,256]{2,1,0:T(8,128)(2,1)S(1)}) custom-call(bf16[48,128,128]{2,1,0:T(8,128)(2,1)S(1)} %copy-done), custom_call_target="tpu_custom_call" | custom-call | flops 60000002048 | bytes 100000 | tf_op jit(solution)/shard_map/pallas_call | solution.py:342
  6.3 0.4 collective-permute-start.7
  6.6 3.0 %collective-permute-start.8 = (bf16[272,512]{1,0:T(8,128)(2,1)S(1)}, bf16[272,512]{1,0:T(8,128)(2,1)S(1)}, u32[]{:S(2)}, u32[]{:S(2)}) collective-permute-start(bf16[272,512]{1,0:T(8,128)(2,1)S(1)} %get-tuple-element.63), channel_id=1, source_target_pairs={{0,6},{1,7},{2,0},{3,1},{4,2},{5,3},{6,4},{7,5},{8,14},{9,15},{10,... | collective-permute-start | bytes 835592 | tf_op jit(solution)/shard_map/ppermute | solution.py:41
  9.6 2.5 %shard_map.56 = (bf16[8,144,256]{2,1,0:T(8,128)(2,1)S(1)}, bf16[8,144,256]{2,1,0:T(8,128)(2,1)S(1)}) custom-call(bf16[544,512]{1,0:T(8,128)(2,1)S(1)} %get-tuple-element.48.refs_0_, bf16[544,512]{1,0:T(8,128)(2,1)S(1)} %collective-permute-done.2.refs_1_), custom_call_target="tpu_custom_call" | custom-call | flops 1000000 | bytes 100000 | tf_op jit(solution)/shard_map/pallas_call | solution.py:171
  12.1 0.1 collective-permute-done.refs_0_
  12.2 0.7 %collective-permute-done.1.refs_1_ = bf16[272,512]{1,0:T(8,128)(2,1)S(1)} collective-permute-done((bf16[272,512]{1,0:T(8,128)(2,1)S(1)}, bf16[272,512]{1,0:T(8,128)(2,1)S(1)}, u32[]{:S(2)}, u32[]{:S(2)}) %collective-permute-start.1) | collective-permute-done | bytes 278560 | tf_op jit(solution)/shard_map/ppermute | solution.py:41
  12.9 1.5 %collective-permute-start.3 = (bf16[272,512]{1,0:T(8,128)(2,1)S(1)}, bf16[272,512]{1,0:T(8,128)(2,1)S(1)}, u32[]{:S(2)}, u32[]{:S(2)}) collective-permute-start(bf16[272,512]{1,0:T(8,128)(2,1)S(1)} %collective-permute-done.refs_0_), channel_id=1, source_target_pairs={{0,2},{1,3},{2,4},{3,5},{4,6},{5,7},{6,0},{7,1},{8,10},{9,11},{10,... | collective-permute-start | bytes 835592 | tf_op jit(solution)/shard_map/ppermute | solution.py:41
  14.4 1.7 %collective-permute-start.4 = (bf16[272,512]{1,0:T(8,128)(2,1)S(1)}, bf16[272,512]{1,0:T(8,128)(2,1)S(1)}, u32[]{:S(2)}, u32[]{:S(2)}) collective-permute-start(bf16[272,512]{1,0:T(8,128)(2,1)S(1)} %collective-permute-done.1.refs_1_), channel_id=1, source_target_pairs={{0,6},{1,7},{2,0},{3,1},{4,2},{5,3},{6,4},{7,5},{8,14},{9,15},{10,... | collective-permute-start | bytes 835592 | tf_op jit(solution)/shard_map/ppermute | solution.py:41
  16.2 1.4 %shard_map.58 = (bf16[8,144,256]{2,1,0:T(8,128)(2,1)S(1)}, bf16[8,144,256]{2,1,0:T(8,128)(2,1)S(1)}) custom-call(bf16[272,512]{1,0:T(8,128)(2,1)S(1)} %collective-permute-done.refs_0_, bf16[272,512]{1,0:T(8,128)(2,1)S(1)} %collective-permute-done.1.refs_1_), custom_call_target="tpu_custom_call" | custom-call | flops 1000000 | bytes 100000 | tf_op jit(solution)/shard_map/pallas_call | solution.py:171
  17.5 0.1 collective-permute-start.5
  17.6 0.5 collective-permute-done.7.refs_2_
  18.2 0.0 collective-permute-start.6
  18.2 0.7 %collective-permute-done.8.refs_3_ = bf16[272,512]{1,0:T(8,128)(2,1)S(1)} collective-permute-done((bf16[272,512]{1,0:T(8,128)(2,1)S(1)}, bf16[272,512]{1,0:T(8,128)(2,1)S(1)}, u32[]{:S(2)}, u32[]{:S(2)}) %collective-permute-start.8) | collective-permute-done | bytes 278560 | tf_op jit(solution)/shard_map/ppermute | solution.py:41
  18.9 1.4 %shard_map.59 = (bf16[8,144,256]{2,1,0:T(8,128)(2,1)S(1)}, bf16[8,144,256]{2,1,0:T(8,128)(2,1)S(1)}) custom-call(bf16[272,512]{1,0:T(8,128)(2,1)S(1)} %collective-permute-done.refs_0_, bf16[272,512]{1,0:T(8,128)(2,1)S(1)} %collective-permute-done.1.refs_1_, bf16[272,512]{1,0:T(8,128)(2,1)S(1)} %collective-permute-done.7.refs_2_, ...), custom_call_target="tpu_custom_call" | custom-call | flops 60000002048 | bytes 100000 | tf_op jit(solution)/shard_map/pallas_call | solution.py:171
  20.3 0.1 collective-permute-start.9
  20.4 0.0 collective-permute-done.5.refs_0_
  20.4 0.5 collective-permute-start.10
  20.9 0.0 collective-permute-done.6.refs_1_
  20.9 1.4 %shard_map.60 = (bf16[8,144,256]{2,1,0:T(8,128)(2,1)S(1)}, bf16[8,144,256]{2,1,0:T(8,128)(2,1)S(1)}) custom-call(bf16[272,512]{1,0:T(8,128)(2,1)S(1)} %collective-permute-done.5.refs_0_, bf16[272,512]{1,0:T(8,128)(2,1)S(1)} %collective-permute-done.6.refs_1_), custom_call_target="tpu_custom_call" | custom-call | flops 60000002048 | bytes 100000 | tf_op jit(solution)/shard_map/pallas_call | solution.py:171
  22.2 0.1 collective-permute-done.10.refs_3_
  22.3 1.4 %shard_map.61 = (bf16[8,144,256]{2,1,0:T(8,128)(2,1)S(1)}, bf16[8,144,256]{2,1,0:T(8,128)(2,1)S(1)}) custom-call(bf16[272,512]{1,0:T(8,128)(2,1)S(1)} %collective-permute-done.5.refs_0_, bf16[272,512]{1,0:T(8,128)(2,1)S(1)} %collective-permute-done.6.refs_1_, bf16[272,512]{1,0:T(8,128)(2,1)S(1)} %collective-permute-done.9.refs_2_, ...), custom_call_target="tpu_custom_call" | custom-call | flops 1000000 | bytes 100000 | tf_op jit(solution)/shard_map/pallas_call | solution.py:171
  23.7 0.0 collective-permute-done.4.refs_1_
  23.7 0.2 collective-permute-start.11
  23.9 0.4 collective-permute-start.12
  24.3 1.4 %shard_map.62.same = bf16[8,144,256]{2,1,0:T(8,128)(2,1)S(1)} custom-call(bf16[272,512]{1,0:T(8,128)(2,1)S(1)} %collective-permute-done.3.refs_0_, bf16[272,512]{1,0:T(8,128)(2,1)S(1)} %collective-permute-done.4.refs_1_), custom_call_target="tpu_custom_call" | custom-call | flops 1000000 | bytes 100000 | tf_op jit(solution)/shard_map/pallas_call | solution.py:171
  25.7 0.1 collective-permute-done.12.high
  25.7 1.1 %shard_map.64 = bf16[528,128]{1,0:T(8,128)(2,1)S(1)} custom-call(bf16[272,512]{1,0:T(8,128)(2,1)S(1)} %collective-permute-done.11.low, bf16[272,512]{1,0:T(8,128)(2,1)S(1)} %collective-permute-done.12.high, bf16[8,144,256]{2,1,0:T(8,128)(2,1)S(1)} %shard_map.62.same, bf16[8,144,256]{2,1,0:T(8,128)(2,1)S(1)} %get-tuple-element.76.rest_0_, ...), custom_call_target="tpu_custom_call" | custom-call | flops 1000000000 | bytes 100000 | tf_op jit(solution)/shard_map/pallas_call | solution.py:238
  26.8 3.3 %collective-permute-start.13 = (bf16[528,128]{1,0:T(8,128)(2,1)S(1)}, bf16[528,128]{1,0:T(8,128)(2,1)S(1)}, u32[]{:S(2)}, u32[]{:S(2)}) collective-permute-start(bf16[528,128]{1,0:T(8,128)(2,1)S(1)} %shard_map.64), channel_id=1, source_target_pairs={{0,16},{1,17},{2,18},{3,19},{4,20},{5,21},{6,22},{7,23},{8,24},{9,... | collective-permute-start | bytes 405512 | tf_op jit(solution)/shard_map/ppermute | solution.py:41
  30.1 1.1 %shard_map.65 = bf16[528,128]{1,0:T(8,128)(2,1)S(1)} custom-call(bf16[272,512]{1,0:T(8,128)(2,1)S(1)} %collective-permute-done.11.low, bf16[272,512]{1,0:T(8,128)(2,1)S(1)} %collective-permute-done.12.high, bf16[8,144,256]{2,1,0:T(8,128)(2,1)S(1)} %shard_map.62.same, bf16[8,144,256]{2,1,0:T(8,128)(2,1)S(1)} %get-tuple-element.76.rest_0_, ...), custom_call_target="tpu_custom_call" | custom-call | flops 1000000000 | bytes 100000 | tf_op jit(solution)/shard_map/pallas_call | solution.py:238
  31.2 0.8 %collective-permute-start.14 = (bf16[528,128]{1,0:T(8,128)(2,1)S(1)}, bf16[528,128]{1,0:T(8,128)(2,1)S(1)}, u32[]{:S(2)}, u32[]{:S(2)}) collective-permute-start(bf16[528,128]{1,0:T(8,128)(2,1)S(1)} %shard_map.65), channel_id=1, source_target_pairs={{0,8},{1,9},{2,10},{3,11},{4,12},{5,13},{6,14},{7,15},{8,16},{9,17... | collective-permute-start | bytes 405512 | tf_op jit(solution)/shard_map/ppermute | solution.py:41
  31.9 1.1 %shard_map.66 = bf16[528,128]{1,0:T(8,128)(2,1)S(1)} custom-call(bf16[272,512]{1,0:T(8,128)(2,1)S(1)} %collective-permute-done.11.low, bf16[272,512]{1,0:T(8,128)(2,1)S(1)} %collective-permute-done.12.high, bf16[8,144,256]{2,1,0:T(8,128)(2,1)S(1)} %shard_map.62.same, bf16[8,144,256]{2,1,0:T(8,128)(2,1)S(1)} %get-tuple-element.76.rest_0_, ...), custom_call_target="tpu_custom_call" | custom-call | flops 1000000000 | bytes 100000 | tf_op jit(solution)/shard_map/pallas_call | solution.py:238
  33.0 2.6 %collective-permute-start.15 = (bf16[528,128]{1,0:T(8,128)(2,1)S(1)}, bf16[528,128]{1,0:T(8,128)(2,1)S(1)}, u32[]{:S(2)}, u32[]{:S(2)}) collective-permute-start(bf16[528,128]{1,0:T(8,128)(2,1)S(1)} %shard_map.66), channel_id=1, source_target_pairs={{0,24},{1,25},{2,26},{3,27},{4,28},{5,29},{6,30},{7,31},{8,0},{9,1... | collective-permute-start | bytes 405512 | tf_op jit(solution)/shard_map/ppermute | solution.py:41
  35.6 1.1 %shard_map.63.own = f32[528,128]{1,0:T(8,128)S(1)} custom-call(bf16[272,512]{1,0:T(8,128)(2,1)S(1)} %collective-permute-done.11.low, bf16[272,512]{1,0:T(8,128)(2,1)S(1)} %collective-permute-done.12.high, bf16[8,144,256]{2,1,0:T(8,128)(2,1)S(1)} %shard_map.62.same, bf16[8,144,256]{2,1,0:T(8,128)(2,1)S(1)} %get-tuple-element.76.rest_0_, ...), custom_call_target="tpu_custom_call" | custom-call | flops 1000000000 | bytes 100000 | tf_op jit(solution)/shard_map/pallas_call | solution.py:238
  36.7 0.0 collective-permute-done.13.a
  36.7 1.1 %collective-permute-done.14.b = bf16[528,128]{1,0:T(8,128)(2,1)S(1)} collective-permute-done((bf16[528,128]{1,0:T(8,128)(2,1)S(1)}, bf16[528,128]{1,0:T(8,128)(2,1)S(1)}, u32[]{:S(2)}, u32[]{:S(2)}) %collective-permute-start.14) | collective-permute-done | bytes 135200 | tf_op jit(solution)/shard_map/ppermute | solution.py:41
  37.8 0.4 collective-permute-done.15.c
  38.2 0.1 shard_map.67
  38.3 16.4 %all_to_all.5.parts = bf16[8,80,128]{2,1,0:T(8,128)(2,1)S(1)} all-to-all(bf16[8,80,128]{2,1,0:T(8,128)(2,1)S(1)} %shard_map.67), channel_id=1, replica_groups=mesh['obs'=8,'grid'=32] {'obs'}, dimensions={0} | all-to-all | bytes 327680 | tf_op jit(solution)/shard_map/all_to_all | solution.py:462
  54.7 2.3 %shard_map.68.own = bf16[128,128]{1,0:T(8,128)(2,1)S(1)} custom-call(bf16[8,80,128]{2,1,0:T(8,128)(2,1)S(1)} %all_to_all.5.parts), custom_call_target="tpu_custom_call" | custom-call | flops 4000000000 | bytes 100000 | tf_op jit(solution)/shard_map/pallas_call | solution.py:310
  57.0 2.6 %collective-permute-start.16 = (bf16[128,128]{1,0:T(8,128)(2,1)S(1)}, bf16[128,128]{1,0:T(8,128)(2,1)S(1)}, u32[]{:S(2)}, u32[]{:S(2)}) collective-permute-start(bf16[128,128]{1,0:T(8,128)(2,1)S(1)} %shard_map.68.own), channel_id=1, source_target_pairs={{0,31},{1,2},{2,1},{3,4},{4,3},{5,6},{6,5},{7,8},{8,7},{9,10},{10,... | collective-permute-start | bytes 98312 | tf_op jit(solution)/shard_map/ppermute | solution.py:465
  59.6 0.6 shard_map.69.part
  60.2 0.1 collective-permute-start.17
  60.3 3.5 %collective-permute-done.16.beyond = bf16[128,128]{1,0:T(8,128)(2,1)S(1)} collective-permute-done((bf16[128,128]{1,0:T(8,128)(2,1)S(1)}, bf16[128,128]{1,0:T(8,128)(2,1)S(1)}, u32[]{:S(2)}, u32[]{:S(2)}) %collective-permute-start.16) | collective-permute-done | bytes 32800 | tf_op jit(solution)/shard_map/ppermute | solution.py:465
  63.7 0.0 collective-permute-done.17.beside
  63.7 1.4 %shard_map.70 = bf16[48,128,128]{2,1,0:T(8,128)(2,1)} custom-call(bf16[128,128]{1,0:T(8,128)(2,1)S(1)} %collective-permute-done.16.beyond, bf16[128,128]{1,0:T(8,128)(2,1)S(1)} %collective-permute-done.17.beside, f32[24,128,256]{2,1,0:T(8,128)S(1)} %shard_map.69.part, bf16[24,256,256]{2,1,0:T(8,128)(2,1)S(1)} %get-tuple-element.86.sides), custom_call_target="tpu_custom_call" | custom-call | flops 2000000000 | bytes 100000 | tf_op jit(solution)/shard_map/pallas_call | solution.py:398
  (7 shorter events, 0.0 us)
Async XLA Ops:
  0.0 5.1 %copy-start = (bf16[48,128,128]{2,1,0:T(8,128)(2,1)S(1)}, bf16[48,128,128]{2,1,0:T(8,128)(2,1)}, u32[]{:S(2)}) copy-start(bf16[48,128,128]{2,1,0:T(8,128)(2,1)} %state.1) | copy-start | bytes 4718596
  1.8 10.4 %collective-permute-start = (bf16[272,512]{1,0:T(8,128)(2,1)S(1)}, bf16[272,512]{1,0:T(8,128)(2,1)S(1)}, u32[]{:S(2)}, u32[]{:S(2)}) collective-permute-start(bf16[272,512]{1,0:T(8,128)(2,1)S(1)} %get-tuple-element.63), channel_id=1, source_target_pairs={{0,2},{1,3},{2,4},{3,5},{4,6},{5,7},{6,0},{7,1},{8,10},{9,11},{10,... | collective-permute-start | bytes 835592 | tf_op jit(solution)/shard_map/ppermute | solution.py:41
  3.3 9.6 %collective-permute-start.1 = (bf16[272,512]{1,0:T(8,128)(2,1)S(1)}, bf16[272,512]{1,0:T(8,128)(2,1)S(1)}, u32[]{:S(2)}, u32[]{:S(2)}) collective-permute-start(bf16[272,512]{1,0:T(8,128)(2,1)S(1)} %get-tuple-element.62), channel_id=1, source_target_pairs={{0,6},{1,7},{2,0},{3,1},{4,2},{5,3},{6,4},{7,5},{8,14},{9,15},{10,... | collective-permute-start | bytes 835592 | tf_op jit(solution)/shard_map/ppermute | solution.py:41
  5.1 4.5 %collective-permute-start.2 = (bf16[544,512]{1,0:T(8,128)(2,1)S(1)}, bf16[544,512]{1,0:T(8,128)(2,1)S(1)}, u32[]{:S(2)}, u32[]{:S(2)}) collective-permute-start(bf16[544,512]{1,0:T(8,128)(2,1)S(1)} %get-tuple-element.48.refs_0_), channel_id=1, source_target_pairs={{0,1},{1,0},{2,3},{3,2},{4,5},{5,4},{6,7},{7,6},{8,9},{9,8},{10,11... | collective-permute-start | bytes 1671176 | tf_op jit(solution)/shard_map/ppermute | solution.py:41
  6.3 11.9 %collective-permute-start.7 = (bf16[272,512]{1,0:T(8,128)(2,1)S(1)}, bf16[272,512]{1,0:T(8,128)(2,1)S(1)}, u32[]{:S(2)}, u32[]{:S(2)}) collective-permute-start(bf16[272,512]{1,0:T(8,128)(2,1)S(1)} %get-tuple-element.62), channel_id=1, source_target_pairs={{0,2},{1,3},{2,4},{3,5},{4,6},{5,7},{6,0},{7,1},{8,10},{9,11},{10,... | collective-permute-start | bytes 835592 | tf_op jit(solution)/shard_map/ppermute | solution.py:41
  6.6 12.3 %collective-permute-start.8 = (bf16[272,512]{1,0:T(8,128)(2,1)S(1)}, bf16[272,512]{1,0:T(8,128)(2,1)S(1)}, u32[]{:S(2)}, u32[]{:S(2)}) collective-permute-start(bf16[272,512]{1,0:T(8,128)(2,1)S(1)} %get-tuple-element.63), channel_id=1, source_target_pairs={{0,6},{1,7},{2,0},{3,1},{4,2},{5,3},{6,4},{7,5},{8,14},{9,15},{10,... | collective-permute-start | bytes 835592 | tf_op jit(solution)/shard_map/ppermute | solution.py:41
  12.9 10.8 %collective-permute-start.3 = (bf16[272,512]{1,0:T(8,128)(2,1)S(1)}, bf16[272,512]{1,0:T(8,128)(2,1)S(1)}, u32[]{:S(2)}, u32[]{:S(2)}) collective-permute-start(bf16[272,512]{1,0:T(8,128)(2,1)S(1)} %collective-permute-done.refs_0_), channel_id=1, source_target_pairs={{0,2},{1,3},{2,4},{3,5},{4,6},{5,7},{6,0},{7,1},{8,10},{9,11},{10,... | collective-permute-start | bytes 835592 | tf_op jit(solution)/shard_map/ppermute | solution.py:41
  14.4 9.3 %collective-permute-start.4 = (bf16[272,512]{1,0:T(8,128)(2,1)S(1)}, bf16[272,512]{1,0:T(8,128)(2,1)S(1)}, u32[]{:S(2)}, u32[]{:S(2)}) collective-permute-start(bf16[272,512]{1,0:T(8,128)(2,1)S(1)} %collective-permute-done.1.refs_1_), channel_id=1, source_target_pairs={{0,6},{1,7},{2,0},{3,1},{4,2},{5,3},{6,4},{7,5},{8,14},{9,15},{10,... | collective-permute-start | bytes 835592 | tf_op jit(solution)/shard_map/ppermute | solution.py:41
  17.5 2.9 %collective-permute-start.5 = (bf16[272,512]{1,0:T(8,128)(2,1)S(1)}, bf16[272,512]{1,0:T(8,128)(2,1)S(1)}, u32[]{:S(2)}, u32[]{:S(2)}) collective-permute-start(bf16[272,512]{1,0:T(8,128)(2,1)S(1)} %collective-permute-done.refs_0_), channel_id=1, source_target_pairs={{0,1},{1,0},{2,3},{3,2},{4,5},{5,4},{6,7},{7,6},{8,9},{9,8},{10,11... | collective-permute-start | bytes 835592 | tf_op jit(solution)/shard_map/ppermute | solution.py:41
  18.2 2.7 %collective-permute-start.6 = (bf16[272,512]{1,0:T(8,128)(2,1)S(1)}, bf16[272,512]{1,0:T(8,128)(2,1)S(1)}, u32[]{:S(2)}, u32[]{:S(2)}) collective-permute-start(bf16[272,512]{1,0:T(8,128)(2,1)S(1)} %collective-permute-done.1.refs_1_), channel_id=1, source_target_pairs={{0,1},{1,0},{2,3},{3,2},{4,5},{5,4},{6,7},{7,6},{8,9},{9,8},{10,11... | collective-permute-start | bytes 835592 | tf_op jit(solution)/shard_map/ppermute | solution.py:41
  20.3 2.0 %collective-permute-start.9 = (bf16[272,512]{1,0:T(8,128)(2,1)S(1)}, bf16[272,512]{1,0:T(8,128)(2,1)S(1)}, u32[]{:S(2)}, u32[]{:S(2)}) collective-permute-start(bf16[272,512]{1,0:T(8,128)(2,1)S(1)} %collective-permute-done.7.refs_2_), channel_id=1, source_target_pairs={{0,1},{1,0},{2,3},{3,2},{4,5},{5,4},{6,7},{7,6},{8,9},{9,8},{10,11... | collective-permute-start | bytes 835592 | tf_op jit(solution)/shard_map/ppermute | solution.py:41
  20.4 1.9 %collective-permute-start.10 = (bf16[272,512]{1,0:T(8,128)(2,1)S(1)}, bf16[272,512]{1,0:T(8,128)(2,1)S(1)}, u32[]{:S(2)}, u32[]{:S(2)}) collective-permute-start(bf16[272,512]{1,0:T(8,128)(2,1)S(1)} %collective-permute-done.8.refs_3_), channel_id=1, source_target_pairs={{0,1},{1,0},{2,3},{3,2},{4,5},{5,4},{6,7},{7,6},{8,9},{9,8},{10,11... | collective-permute-start | bytes 835592 | tf_op jit(solution)/shard_map/ppermute | solution.py:41
  23.7 2.0 %collective-permute-start.11 = (bf16[272,512]{1,0:T(8,128)(2,1)S(1)}, bf16[272,512]{1,0:T(8,128)(2,1)S(1)}, u32[]{:S(2)}, u32[]{:S(2)}) collective-permute-start(bf16[272,512]{1,0:T(8,128)(2,1)S(1)} %collective-permute-done.3.refs_0_), channel_id=1, source_target_pairs={{0,1},{1,0},{2,3},{3,2},{4,5},{5,4},{6,7},{7,6},{8,9},{9,8},{10,11... | collective-permute-start | bytes 835592 | tf_op jit(solution)/shard_map/ppermute | solution.py:41
  23.9 1.8 %collective-permute-start.12 = (bf16[272,512]{1,0:T(8,128)(2,1)S(1)}, bf16[272,512]{1,0:T(8,128)(2,1)S(1)}, u32[]{:S(2)}, u32[]{:S(2)}) collective-permute-start(bf16[272,512]{1,0:T(8,128)(2,1)S(1)} %collective-permute-done.4.refs_1_), channel_id=1, source_target_pairs={{0,1},{1,0},{2,3},{3,2},{4,5},{5,4},{6,7},{7,6},{8,9},{9,8},{10,11... | collective-permute-start | bytes 835592 | tf_op jit(solution)/shard_map/ppermute | solution.py:41
  26.8 9.9 %collective-permute-start.13 = (bf16[528,128]{1,0:T(8,128)(2,1)S(1)}, bf16[528,128]{1,0:T(8,128)(2,1)S(1)}, u32[]{:S(2)}, u32[]{:S(2)}) collective-permute-start(bf16[528,128]{1,0:T(8,128)(2,1)S(1)} %shard_map.64), channel_id=1, source_target_pairs={{0,16},{1,17},{2,18},{3,19},{4,20},{5,21},{6,22},{7,23},{8,24},{9,... | collective-permute-start | bytes 405512 | tf_op jit(solution)/shard_map/ppermute | solution.py:41
  31.2 6.6 %collective-permute-start.14 = (bf16[528,128]{1,0:T(8,128)(2,1)S(1)}, bf16[528,128]{1,0:T(8,128)(2,1)S(1)}, u32[]{:S(2)}, u32[]{:S(2)}) collective-permute-start(bf16[528,128]{1,0:T(8,128)(2,1)S(1)} %shard_map.65), channel_id=1, source_target_pairs={{0,8},{1,9},{2,10},{3,11},{4,12},{5,13},{6,14},{7,15},{8,16},{9,17... | collective-permute-start | bytes 405512 | tf_op jit(solution)/shard_map/ppermute | solution.py:41
  33.0 5.2 %collective-permute-start.15 = (bf16[528,128]{1,0:T(8,128)(2,1)S(1)}, bf16[528,128]{1,0:T(8,128)(2,1)S(1)}, u32[]{:S(2)}, u32[]{:S(2)}) collective-permute-start(bf16[528,128]{1,0:T(8,128)(2,1)S(1)} %shard_map.66), channel_id=1, source_target_pairs={{0,24},{1,25},{2,26},{3,27},{4,28},{5,29},{6,30},{7,31},{8,0},{9,1... | collective-permute-start | bytes 405512 | tf_op jit(solution)/shard_map/ppermute | solution.py:41
  57.0 6.7 %collective-permute-start.16 = (bf16[128,128]{1,0:T(8,128)(2,1)S(1)}, bf16[128,128]{1,0:T(8,128)(2,1)S(1)}, u32[]{:S(2)}, u32[]{:S(2)}) collective-permute-start(bf16[128,128]{1,0:T(8,128)(2,1)S(1)} %shard_map.68.own), channel_id=1, source_target_pairs={{0,31},{1,2},{2,1},{3,4},{4,3},{5,6},{6,5},{7,8},{8,7},{9,10},{10,... | collective-permute-start | bytes 98312 | tf_op jit(solution)/shard_map/ppermute | solution.py:465
  60.2 3.6 %collective-permute-start.17 = (bf16[128,128]{1,0:T(8,128)(2,1)S(1)}, bf16[128,128]{1,0:T(8,128)(2,1)S(1)}, u32[]{:S(2)}, u32[]{:S(2)}) collective-permute-start(bf16[128,128]{1,0:T(8,128)(2,1)S(1)} %shard_map.68.own), channel_id=1, source_target_pairs={{0,1},{1,0},{2,3},{3,2},{4,5},{5,4},{6,7},{7,6},{8,9},{9,8},{10,11... | collective-permute-start | bytes 98312 | tf_op jit(solution)/shard_map/ppermute | solution.py:41

commit v14 on v13

--- a/solution.py
+++ b/solution.py
@@ -400,7 +400,7 @@
         out_shape=jax.ShapeDtypeStruct(shape, BF16),
         in_specs=in_vmem(4),
         out_specs=pl.BlockSpec(memory_space=pltpu.HBM),
-        scratch_shapes=[pltpu.VMEM(shape, BF16), pltpu.SemaphoreType.DMA((8,))],
+        scratch_shapes=[pltpu.VMEM(shape, BF16), pltpu.SemaphoreType.DMA((12,))],
         compiler_params=params(),
         cost_estimate=cost(2e9),
     )(beyond, beside, part, sides)
@@ -425,10 +425,10 @@
     )
     left_more = hop(high_half, 0, 1, 0)
     right_more = hop(low_half, 0, -1, 0)
-    left, right, found, mean, perturb = lax.optimization_barrier(
-        (left, right, found, mean, perturb)
-    )
-    far_low, far_high = hop(left, 0, 1, 0), hop(right, 0, -1, 0)
+    left, found, mean, perturb = lax.optimization_barrier((left, found, mean, perturb))
+    far_low = hop(left, 0, 1, 0)
+    left, right, found = lax.optimization_barrier((left, right, found))
+    far_high = hop(right, 0, -1, 0)
 
     def firsts(core):
         row = 8 + 4 * core

time: 66.3 us -> 66.3 us (level)
  transfers between devices with their start and end apart: 18 -> 18, of which waited for: 9 -> 8; matrix products, arithmetic and copies ran while one was open for 0% -> 0% of each run, Pallas kernels for 22% -> 22%
where the time goes in v14:
time: 66.3 us; the launch traced here: 65.4 us
  Pallas kernels  20.9 us (32%)
  starting transfers between devices  20.2 us (30%)
  blocking collectives  16.4 us (25%)
  waiting for transfers between devices  7.54 us (11%)
    ppermute x17, starting transfers between devices, hop(): return lax.ppermute(value, 'grid', pairs)  17.9 us
    all_to_all x1, blocking collectives, on_device(): parts = lax.all_to_all(parts, 'obs', 0, 0, tiled=True)  16.4 us
    pallas_call x6, Pallas kernels, pick_rows(): pl.pallas_call(functools.partial(pick_kernel, sources, len(args)), out_sh...  9.32 us
    pallas_call x4, Pallas kernels, last_grams(): pl.pallas_call(functools.partial(last_kernel, shifts), out_shape=[jax.Sha...  4.27 us
    ppermute x17, waiting for transfers between devices, hop(): return lax.ppermute(value, 'grid', pairs)  3.77 us
    ppermute x1, waiting for transfers between devices, on_device(): lax.ppermute(own, 'grid', [(j, (j + 2 * (j % 2) - 1) % n_grid) for j in r...  3.77 us
    pallas_call x1, Pallas kernels, transposed_weights(): pl.pallas_call(weights_kernel, out_shape=jax.ShapeDtypeStruct((K, K), BF1...  2.34 us
    ppermute x1, starting transfers between devices, on_device(): lax.ppermute(own, 'grid', [(j, (j + 2 * (j % 2) - 1) % n_grid) for j in r...  2.31 us
  transfers between devices with their start and end apart: 18, of which 8 were waited for; matrix products, arithmetic and copies ran while one was open for 0% of the time, Pallas kernels for 22%

profile of v14, /device:TPU:32, one launch (start us, length us, event | category | flops | bytes accessed | tf_op | source)
XLA Modules:
  0.0 65.4 jit_solution(9887209588020814450)
XLA Ops:
  0.0 1.8 %shard_map.55 = (bf16[272,512]{1,0:T(8,128)(2,1)S(1)}, bf16[272,512]{1,0:T(8,128)(2,1)S(1)}, bf16[544,512]{1,0:T(8,128)(2,1)S(1)}) custom-call(bf16[2048,128]{1,0:T(8,128)(2,1)} %departures.1, f32[2048]{0:T(1024)} %innovation.1, f32[2048]{0:T(1024)} %obs_weight.1, s32[64,256]{1,0:T(8,128)} %bitcast.3), custom_call_target="tpu_custom_call" | custom-call | flops 2000000000 | bytes 100000 | tf_op jit(solution)/shard_map/pallas_call | solution.py:121
  1.8 1.6 %collective-permute-start = (bf16[272,512]{1,0:T(8,128)(2,1)S(1)}, bf16[272,512]{1,0:T(8,128)(2,1)S(1)}, u32[]{:S(2)}, u32[]{:S(2)}) collective-permute-start(bf16[272,512]{1,0:T(8,128)(2,1)S(1)} %get-tuple-element.69), channel_id=1, source_target_pairs={{0,2},{1,3},{2,4},{3,5},{4,6},{5,7},{6,0},{7,1},{8,10},{9,11},{10,... | collective-permute-start | bytes 835592 | tf_op jit(solution)/shard_map/ppermute | solution.py:41
  3.3 1.7 %collective-permute-start.3 = (bf16[272,512]{1,0:T(8,128)(2,1)S(1)}, bf16[272,512]{1,0:T(8,128)(2,1)S(1)}, u32[]{:S(2)}, u32[]{:S(2)}) collective-permute-start(bf16[272,512]{1,0:T(8,128)(2,1)S(1)} %get-tuple-element.68), channel_id=1, source_target_pairs={{0,6},{1,7},{2,0},{3,1},{4,2},{5,3},{6,4},{7,5},{8,14},{9,15},{10,... | collective-permute-start | bytes 835592 | tf_op jit(solution)/shard_map/ppermute | solution.py:41
  5.1 1.2 %shard_map.57 = (f32[24,256]{1,0:T(8,128)S(1)}, bf16[24,128,256]{2,1,0:T(8,128)(2,1)S(1)}, bf16[24,256,256]{2,1,0:T(8,128)(2,1)S(1)}) custom-call(bf16[48,128,128]{2,1,0:T(8,128)(2,1)S(1)} %copy-done), custom_call_target="tpu_custom_call" | custom-call | flops 60000002048 | bytes 100000 | tf_op jit(solution)/shard_map/pallas_call | solution.py:342
  6.3 0.4 collective-permute-start.7
  6.6 3.0 %collective-permute-start.8 = (bf16[272,512]{1,0:T(8,128)(2,1)S(1)}, bf16[272,512]{1,0:T(8,128)(2,1)S(1)}, u32[]{:S(2)}, u32[]{:S(2)}) collective-permute-start(bf16[272,512]{1,0:T(8,128)(2,1)S(1)} %get-tuple-element.69), channel_id=1, source_target_pairs={{0,6},{1,7},{2,0},{3,1},{4,2},{5,3},{6,4},{7,5},{8,14},{9,15},{10,... | collective-permute-start | bytes 835592 | tf_op jit(solution)/shard_map/ppermute | solution.py:41
  9.6 2.5 %shard_map.56 = (bf16[8,144,256]{2,1,0:T(8,128)(2,1)S(1)}, bf16[8,144,256]{2,1,0:T(8,128)(2,1)S(1)}) custom-call(bf16[544,512]{1,0:T(8,128)(2,1)S(1)} %get-tuple-element.50.refs_0_, bf16[544,512]{1,0:T(8,128)(2,1)S(1)} %collective-permute-done.1.refs_1_), custom_call_target="tpu_custom_call" | custom-call | flops 1000000 | bytes 100000 | tf_op jit(solution)/shard_map/pallas_call | solution.py:171
  12.1 0.1 collective-permute-done.refs_0_
  12.2 0.7 %collective-permute-start.2 = (bf16[272,512]{1,0:T(8,128)(2,1)S(1)}, bf16[272,512]{1,0:T(8,128)(2,1)S(1)}, u32[]{:S(2)}, u32[]{:S(2)}) collective-permute-start(bf16[272,512]{1,0:T(8,128)(2,1)S(1)} %collective-permute-done.refs_0_), channel_id=1, source_target_pairs={{0,2},{1,3},{2,4},{3,5},{4,6},{5,7},{6,0},{7,1},{8,10},{9,11},{10,... | collective-permute-start | bytes 835592 | tf_op jit(solution)/shard_map/ppermute | solution.py:41
  12.9 0.0 collective-permute-done.3.refs_1_
  12.9 2.5 %collective-permute-start.4 = (bf16[272,512]{1,0:T(8,128)(2,1)S(1)}, bf16[272,512]{1,0:T(8,128)(2,1)S(1)}, u32[]{:S(2)}, u32[]{:S(2)}) collective-permute-start(bf16[272,512]{1,0:T(8,128)(2,1)S(1)} %collective-permute-done.3.refs_1_), channel_id=1, source_target_pairs={{0,6},{1,7},{2,0},{3,1},{4,2},{5,3},{6,4},{7,5},{8,14},{9,15},{10,... | collective-permute-start | bytes 835592 | tf_op jit(solution)/shard_map/ppermute | solution.py:41
  15.4 1.4 %shard_map.58 = (bf16[8,144,256]{2,1,0:T(8,128)(2,1)S(1)}, bf16[8,144,256]{2,1,0:T(8,128)(2,1)S(1)}) custom-call(bf16[272,512]{1,0:T(8,128)(2,1)S(1)} %collective-permute-done.refs_0_, bf16[272,512]{1,0:T(8,128)(2,1)S(1)} %collective-permute-done.3.refs_1_), custom_call_target="tpu_custom_call" | custom-call | flops 1000000 | bytes 100000 | tf_op jit(solution)/shard_map/pallas_call | solution.py:171
  16.8 0.1 collective-permute-start.5
  16.9 1.3 %collective-permute-done.7.refs_2_ = bf16[272,512]{1,0:T(8,128)(2,1)S(1)} collective-permute-done((bf16[272,512]{1,0:T(8,128)(2,1)S(1)}, bf16[272,512]{1,0:T(8,128)(2,1)S(1)}, u32[]{:S(2)}, u32[]{:S(2)}) %collective-permute-start.7) | collective-permute-done | bytes 278560 | tf_op jit(solution)/shard_map/ppermute | solution.py:41
  18.2 0.0 collective-permute-start.6
  18.2 0.7 %collective-permute-done.8.refs_3_ = bf16[272,512]{1,0:T(8,128)(2,1)S(1)} collective-permute-done((bf16[272,512]{1,0:T(8,128)(2,1)S(1)}, bf16[272,512]{1,0:T(8,128)(2,1)S(1)}, u32[]{:S(2)}, u32[]{:S(2)}) %collective-permute-start.8) | collective-permute-done | bytes 278560 | tf_op jit(solution)/shard_map/ppermute | solution.py:41
  18.9 1.4 %shard_map.59 = (bf16[8,144,256]{2,1,0:T(8,128)(2,1)S(1)}, bf16[8,144,256]{2,1,0:T(8,128)(2,1)S(1)}) custom-call(bf16[272,512]{1,0:T(8,128)(2,1)S(1)} %collective-permute-done.refs_0_, bf16[272,512]{1,0:T(8,128)(2,1)S(1)} %collective-permute-done.3.refs_1_, bf16[272,512]{1,0:T(8,128)(2,1)S(1)} %collective-permute-done.7.refs_2_, ...), custom_call_target="tpu_custom_call" | custom-call | flops 60000002048 | bytes 100000 | tf_op jit(solution)/shard_map/pallas_call | solution.py:171
  20.3 0.1 collective-permute-start.9
  20.4 0.0 collective-permute-done.5.refs_0_
  20.4 0.5 collective-permute-start.10
  20.9 0.0 collective-permute-done.6.refs_1_
  20.9 1.4 %shard_map.60 = (bf16[8,144,256]{2,1,0:T(8,128)(2,1)S(1)}, bf16[8,144,256]{2,1,0:T(8,128)(2,1)S(1)}) custom-call(bf16[272,512]{1,0:T(8,128)(2,1)S(1)} %collective-permute-done.5.refs_0_, bf16[272,512]{1,0:T(8,128)(2,1)S(1)} %collective-permute-done.6.refs_1_), custom_call_target="tpu_custom_call" | custom-call | flops 60000002048 | bytes 100000 | tf_op jit(solution)/shard_map/pallas_call | solution.py:171
  22.2 0.1 collective-permute-done.10.refs_3_
  22.3 1.4 %shard_map.61 = (bf16[8,144,256]{2,1,0:T(8,128)(2,1)S(1)}, bf16[8,144,256]{2,1,0:T(8,128)(2,1)S(1)}) custom-call(bf16[272,512]{1,0:T(8,128)(2,1)S(1)} %collective-permute-done.5.refs_0_, bf16[272,512]{1,0:T(8,128)(2,1)S(1)} %collective-permute-done.6.refs_1_, bf16[272,512]{1,0:T(8,128)(2,1)S(1)} %collective-permute-done.9.refs_2_, ...), custom_call_target="tpu_custom_call" | custom-call | flops 1000000 | bytes 100000 | tf_op jit(solution)/shard_map/pallas_call | solution.py:171
  23.7 0.0 collective-permute-done.2.refs_0_
  23.7 0.2 collective-permute-start.11
  23.9 0.4 collective-permute-start.12
  24.3 1.4 %shard_map.62.same = bf16[8,144,256]{2,1,0:T(8,128)(2,1)S(1)} custom-call(bf16[272,512]{1,0:T(8,128)(2,1)S(1)} %collective-permute-done.2.refs_0_, bf16[272,512]{1,0:T(8,128)(2,1)S(1)} %collective-permute-done.4.refs_1_), custom_call_target="tpu_custom_call" | custom-call | flops 1000000 | bytes 100000 | tf_op jit(solution)/shard_map/pallas_call | solution.py:171
  25.7 0.1 collective-permute-done.12.high
  25.7 1.1 %shard_map.64 = bf16[528,128]{1,0:T(8,128)(2,1)S(1)} custom-call(bf16[272,512]{1,0:T(8,128)(2,1)S(1)} %collective-permute-done.11.low, bf16[272,512]{1,0:T(8,128)(2,1)S(1)} %collective-permute-done.12.high, bf16[8,144,256]{2,1,0:T(8,128)(2,1)S(1)} %shard_map.62.same, bf16[8,144,256]{2,1,0:T(8,128)(2,1)S(1)} %get-tuple-element.82.rest_0_, ...), custom_call_target="tpu_custom_call" | custom-call | flops 1000000000 | bytes 100000 | tf_op jit(solution)/shard_map/pallas_call | solution.py:238
  26.8 3.3 %collective-permute-start.13 = (bf16[528,128]{1,0:T(8,128)(2,1)S(1)}, bf16[528,128]{1,0:T(8,128)(2,1)S(1)}, u32[]{:S(2)}, u32[]{:S(2)}) collective-permute-start(bf16[528,128]{1,0:T(8,128)(2,1)S(1)} %shard_map.64), channel_id=1, source_target_pairs={{0,16},{1,17},{2,18},{3,19},{4,20},{5,21},{6,22},{7,23},{8,24},{9,... | collective-permute-start | bytes 405512 | tf_op jit(solution)/shard_map/ppermute | solution.py:41
  30.1 1.1 %shard_map.65 = bf16[528,128]{1,0:T(8,128)(2,1)S(1)} custom-call(bf16[272,512]{1,0:T(8,128)(2,1)S(1)} %collective-permute-done.11.low, bf16[272,512]{1,0:T(8,128)(2,1)S(1)} %collective-permute-done.12.high, bf16[8,144,256]{2,1,0:T(8,128)(2,1)S(1)} %shard_map.62.same, bf16[8,144,256]{2,1,0:T(8,128)(2,1)S(1)} %get-tuple-element.82.rest_0_, ...), custom_call_target="tpu_custom_call" | custom-call | flops 1000000000 | bytes 100000 | tf_op jit(solution)/shard_map/pallas_call | solution.py:238
  31.2 0.8 %collective-permute-start.14 = (bf16[528,128]{1,0:T(8,128)(2,1)S(1)}, bf16[528,128]{1,0:T(8,128)(2,1)S(1)}, u32[]{:S(2)}, u32[]{:S(2)}) collective-permute-start(bf16[528,128]{1,0:T(8,128)(2,1)S(1)} %shard_map.65), channel_id=1, source_target_pairs={{0,8},{1,9},{2,10},{3,11},{4,12},{5,13},{6,14},{7,15},{8,16},{9,17... | collective-permute-start | bytes 405512 | tf_op jit(solution)/shard_map/ppermute | solution.py:41
  31.9 1.1 %shard_map.66 = bf16[528,128]{1,0:T(8,128)(2,1)S(1)} custom-call(bf16[272,512]{1,0:T(8,128)(2,1)S(1)} %collective-permute-done.11.low, bf16[272,512]{1,0:T(8,128)(2,1)S(1)} %collective-permute-done.12.high, bf16[8,144,256]{2,1,0:T(8,128)(2,1)S(1)} %shard_map.62.same, bf16[8,144,256]{2,1,0:T(8,128)(2,1)S(1)} %get-tuple-element.82.rest_0_, ...), custom_call_target="tpu_custom_call" | custom-call | flops 1000000000 | bytes 100000 | tf_op jit(solution)/shard_map/pallas_call | solution.py:238
  33.0 2.6 %collective-permute-start.15 = (bf16[528,128]{1,0:T(8,128)(2,1)S(1)}, bf16[528,128]{1,0:T(8,128)(2,1)S(1)}, u32[]{:S(2)}, u32[]{:S(2)}) collective-permute-start(bf16[528,128]{1,0:T(8,128)(2,1)S(1)} %shard_map.66), channel_id=1, source_target_pairs={{0,24},{1,25},{2,26},{3,27},{4,28},{5,29},{6,30},{7,31},{8,0},{9,1... | collective-permute-start | bytes 405512 | tf_op jit(solution)/shard_map/ppermute | solution.py:41
  35.6 1.1 %shard_map.63.own = f32[528,128]{1,0:T(8,128)S(1)} custom-call(bf16[272,512]{1,0:T(8,128)(2,1)S(1)} %collective-permute-done.11.low, bf16[272,512]{1,0:T(8,128)(2,1)S(1)} %collective-permute-done.12.high, bf16[8,144,256]{2,1,0:T(8,128)(2,1)S(1)} %shard_map.62.same, bf16[8,144,256]{2,1,0:T(8,128)(2,1)S(1)} %get-tuple-element.82.rest_0_, ...), custom_call_target="tpu_custom_call" | custom-call | flops 1000000000 | bytes 100000 | tf_op jit(solution)/shard_map/pallas_call | solution.py:238
  36.7 0.0 collective-permute-done.13.a
  36.7 1.1 %collective-permute-done.14.b = bf16[528,128]{1,0:T(8,128)(2,1)S(1)} collective-permute-done((bf16[528,128]{1,0:T(8,128)(2,1)S(1)}, bf16[528,128]{1,0:T(8,128)(2,1)S(1)}, u32[]{:S(2)}, u32[]{:S(2)}) %collective-permute-start.14) | collective-permute-done | bytes 135200 | tf_op jit(solution)/shard_map/ppermute | solution.py:41
  37.8 0.4 collective-permute-done.15.c
  38.2 0.1 shard_map.67
  38.3 16.4 %all_to_all.5.parts = bf16[8,80,128]{2,1,0:T(8,128)(2,1)S(1)} all-to-all(bf16[8,80,128]{2,1,0:T(8,128)(2,1)S(1)} %shard_map.67), channel_id=1, replica_groups=mesh['obs'=8,'grid'=32] {'obs'}, dimensions={0} | all-to-all | bytes 327680 | tf_op jit(solution)/shard_map/all_to_all | solution.py:462
  54.7 2.3 %shard_map.68.own = bf16[128,128]{1,0:T(8,128)(2,1)S(1)} custom-call(bf16[8,80,128]{2,1,0:T(8,128)(2,1)S(1)} %all_to_all.5.parts), custom_call_target="tpu_custom_call" | custom-call | flops 4000000000 | bytes 100000 | tf_op jit(solution)/shard_map/pallas_call | solution.py:310
  57.0 2.3 %collective-permute-start.16 = (bf16[128,128]{1,0:T(8,128)(2,1)S(1)}, bf16[128,128]{1,0:T(8,128)(2,1)S(1)}, u32[]{:S(2)}, u32[]{:S(2)}) collective-permute-start(bf16[128,128]{1,0:T(8,128)(2,1)S(1)} %shard_map.68.own), channel_id=1, source_target_pairs={{0,31},{1,2},{2,1},{3,4},{4,3},{5,6},{6,5},{7,8},{8,7},{9,10},{10,... | collective-permute-start | bytes 98312 | tf_op jit(solution)/shard_map/ppermute | solution.py:465
  59.3 0.6 shard_map.69.part
  59.9 0.1 collective-permute-start.17
  60.0 3.8 %collective-permute-done.16.beyond = bf16[128,128]{1,0:T(8,128)(2,1)S(1)} collective-permute-done((bf16[128,128]{1,0:T(8,128)(2,1)S(1)}, bf16[128,128]{1,0:T(8,128)(2,1)S(1)}, u32[]{:S(2)}, u32[]{:S(2)}) %collective-permute-start.16) | collective-permute-done | bytes 32800 | tf_op jit(solution)/shard_map/ppermute | solution.py:465
  63.7 0.0 collective-permute-done.17.beside
  63.7 1.4 %shard_map.70 = bf16[48,128,128]{2,1,0:T(8,128)(2,1)} custom-call(bf16[128,128]{1,0:T(8,128)(2,1)S(1)} %collective-permute-done.16.beyond, bf16[128,128]{1,0:T(8,128)(2,1)S(1)} %collective-permute-done.17.beside, f32[24,128,256]{2,1,0:T(8,128)S(1)} %shard_map.69.part, bf16[24,256,256]{2,1,0:T(8,128)(2,1)S(1)} %get-tuple-element.92.sides), custom_call_target="tpu_custom_call" | custom-call | flops 2000000000 | bytes 100000 | tf_op jit(solution)/shard_map/pallas_call | solution.py:398
  (7 shorter events, 0.0 us)
Async XLA Ops:
  0.0 5.1 %copy-start = (bf16[48,128,128]{2,1,0:T(8,128)(2,1)S(1)}, bf16[48,128,128]{2,1,0:T(8,128)(2,1)}, u32[]{:S(2)}) copy-start(bf16[48,128,128]{2,1,0:T(8,128)(2,1)} %state.1) | copy-start | bytes 4718596
  1.8 10.4 %collective-permute-start = (bf16[272,512]{1,0:T(8,128)(2,1)S(1)}, bf16[272,512]{1,0:T(8,128)(2,1)S(1)}, u32[]{:S(2)}, u32[]{:S(2)}) collective-permute-start(bf16[272,512]{1,0:T(8,128)(2,1)S(1)} %get-tuple-element.69), channel_id=1, source_target_pairs={{0,2},{1,3},{2,4},{3,5},{4,6},{5,7},{6,0},{7,1},{8,10},{9,11},{10,... | collective-permute-start | bytes 835592 | tf_op jit(solution)/shard_map/ppermute | solution.py:41
  3.3 9.6 %collective-permute-start.3 = (bf16[272,512]{1,0:T(8,128)(2,1)S(1)}, bf16[272,512]{1,0:T(8,128)(2,1)S(1)}, u32[]{:S(2)}, u32[]{:S(2)}) collective-permute-start(bf16[272,512]{1,0:T(8,128)(2,1)S(1)} %get-tuple-element.68), channel_id=1, source_target_pairs={{0,6},{1,7},{2,0},{3,1},{4,2},{5,3},{6,4},{7,5},{8,14},{9,15},{10,... | collective-permute-start | bytes 835592 | tf_op jit(solution)/shard_map/ppermute | solution.py:41
  5.1 4.5 %collective-permute-start.1 = (bf16[544,512]{1,0:T(8,128)(2,1)S(1)}, bf16[544,512]{1,0:T(8,128)(2,1)S(1)}, u32[]{:S(2)}, u32[]{:S(2)}) collective-permute-start(bf16[544,512]{1,0:T(8,128)(2,1)S(1)} %get-tuple-element.50.refs_0_), channel_id=1, source_target_pairs={{0,1},{1,0},{2,3},{3,2},{4,5},{5,4},{6,7},{7,6},{8,9},{9,8},{10,11... | collective-permute-start | bytes 1671176 | tf_op jit(solution)/shard_map/ppermute | solution.py:41
  6.3 11.9 %collective-permute-start.7 = (bf16[272,512]{1,0:T(8,128)(2,1)S(1)}, bf16[272,512]{1,0:T(8,128)(2,1)S(1)}, u32[]{:S(2)}, u32[]{:S(2)}) collective-permute-start(bf16[272,512]{1,0:T(8,128)(2,1)S(1)} %get-tuple-element.68), channel_id=1, source_target_pairs={{0,2},{1,3},{2,4},{3,5},{4,6},{5,7},{6,0},{7,1},{8,10},{9,11},{10,... | collective-permute-start | bytes 835592 | tf_op jit(solution)/shard_map/ppermute | solution.py:41
  6.6 12.3 %collective-permute-start.8 = (bf16[272,512]{1,0:T(8,128)(2,1)S(1)}, bf16[272,512]{1,0:T(8,128)(2,1)S(1)}, u32[]{:S(2)}, u32[]{:S(2)}) collective-permute-start(bf16[272,512]{1,0:T(8,128)(2,1)S(1)} %get-tuple-element.69), channel_id=1, source_target_pairs={{0,6},{1,7},{2,0},{3,1},{4,2},{5,3},{6,4},{7,5},{8,14},{9,15},{10,... | collective-permute-start | bytes 835592 | tf_op jit(solution)/shard_map/ppermute | solution.py:41
  12.2 11.5 %collective-permute-start.2 = (bf16[272,512]{1,0:T(8,128)(2,1)S(1)}, bf16[272,512]{1,0:T(8,128)(2,1)S(1)}, u32[]{:S(2)}, u32[]{:S(2)}) collective-permute-start(bf16[272,512]{1,0:T(8,128)(2,1)S(1)} %collective-permute-done.refs_0_), channel_id=1, source_target_pairs={{0,2},{1,3},{2,4},{3,5},{4,6},{5,7},{6,0},{7,1},{8,10},{9,11},{10,... | collective-permute-start | bytes 835592 | tf_op jit(solution)/shard_map/ppermute | solution.py:41
  12.9 10.8 %collective-permute-start.4 = (bf16[272,512]{1,0:T(8,128)(2,1)S(1)}, bf16[272,512]{1,0:T(8,128)(2,1)S(1)}, u32[]{:S(2)}, u32[]{:S(2)}) collective-permute-start(bf16[272,512]{1,0:T(8,128)(2,1)S(1)} %collective-permute-done.3.refs_1_), channel_id=1, source_target_pairs={{0,6},{1,7},{2,0},{3,1},{4,2},{5,3},{6,4},{7,5},{8,14},{9,15},{10,... | collective-permute-start | bytes 835592 | tf_op jit(solution)/shard_map/ppermute | solution.py:41
  16.8 3.6 %collective-permute-start.5 = (bf16[272,512]{1,0:T(8,128)(2,1)S(1)}, bf16[272,512]{1,0:T(8,128)(2,1)S(1)}, u32[]{:S(2)}, u32[]{:S(2)}) collective-permute-start(bf16[272,512]{1,0:T(8,128)(2,1)S(1)} %collective-permute-done.refs_0_), channel_id=1, source_target_pairs={{0,1},{1,0},{2,3},{3,2},{4,5},{5,4},{6,7},{7,6},{8,9},{9,8},{10,11... | collective-permute-start | bytes 835592 | tf_op jit(solution)/shard_map/ppermute | solution.py:41
  18.2 2.7 %collective-permute-start.6 = (bf16[272,512]{1,0:T(8,128)(2,1)S(1)}, bf16[272,512]{1,0:T(8,128)(2,1)S(1)}, u32[]{:S(2)}, u32[]{:S(2)}) collective-permute-start(bf16[272,512]{1,0:T(8,128)(2,1)S(1)} %collective-permute-done.3.refs_1_), channel_id=1, source_target_pairs={{0,1},{1,0},{2,3},{3,2},{4,5},{5,4},{6,7},{7,6},{8,9},{9,8},{10,11... | collective-permute-start | bytes 835592 | tf_op jit(solution)/shard_map/ppermute | solution.py:41
  20.3 2.0 %collective-permute-start.9 = (bf16[272,512]{1,0:T(8,128)(2,1)S(1)}, bf16[272,512]{1,0:T(8,128)(2,1)S(1)}, u32[]{:S(2)}, u32[]{:S(2)}) collective-permute-start(bf16[272,512]{1,0:T(8,128)(2,1)S(1)} %collective-permute-done.7.refs_2_), channel_id=1, source_target_pairs={{0,1},{1,0},{2,3},{3,2},{4,5},{5,4},{6,7},{7,6},{8,9},{9,8},{10,11... | collective-permute-start | bytes 835592 | tf_op jit(solution)/shard_map/ppermute | solution.py:41
  20.4 1.9 %collective-permute-start.10 = (bf16[272,512]{1,0:T(8,128)(2,1)S(1)}, bf16[272,512]{1,0:T(8,128)(2,1)S(1)}, u32[]{:S(2)}, u32[]{:S(2)}) collective-permute-start(bf16[272,512]{1,0:T(8,128)(2,1)S(1)} %collective-permute-done.8.refs_3_), channel_id=1, source_target_pairs={{0,1},{1,0},{2,3},{3,2},{4,5},{5,4},{6,7},{7,6},{8,9},{9,8},{10,11... | collective-permute-start | bytes 835592 | tf_op jit(solution)/shard_map/ppermute | solution.py:41
  23.7 2.0 %collective-permute-start.11 = (bf16[272,512]{1,0:T(8,128)(2,1)S(1)}, bf16[272,512]{1,0:T(8,128)(2,1)S(1)}, u32[]{:S(2)}, u32[]{:S(2)}) collective-permute-start(bf16[272,512]{1,0:T(8,128)(2,1)S(1)} %collective-permute-done.2.refs_0_), channel_id=1, source_target_pairs={{0,1},{1,0},{2,3},{3,2},{4,5},{5,4},{6,7},{7,6},{8,9},{9,8},{10,11... | collective-permute-start | bytes 835592 | tf_op jit(solution)/shard_map/ppermute | solution.py:41
  23.9 1.8 %collective-permute-start.12 = (bf16[272,512]{1,0:T(8,128)(2,1)S(1)}, bf16[272,512]{1,0:T(8,128)(2,1)S(1)}, u32[]{:S(2)}, u32[]{:S(2)}) collective-permute-start(bf16[272,512]{1,0:T(8,128)(2,1)S(1)} %collective-permute-done.4.refs_1_), channel_id=1, source_target_pairs={{0,1},{1,0},{2,3},{3,2},{4,5},{5,4},{6,7},{7,6},{8,9},{9,8},{10,11... | collective-permute-start | bytes 835592 | tf_op jit(solution)/shard_map/ppermute | solution.py:41
  26.8 9.9 %collective-permute-start.13 = (bf16[528,128]{1,0:T(8,128)(2,1)S(1)}, bf16[528,128]{1,0:T(8,128)(2,1)S(1)}, u32[]{:S(2)}, u32[]{:S(2)}) collective-permute-start(bf16[528,128]{1,0:T(8,128)(2,1)S(1)} %shard_map.64), channel_id=1, source_target_pairs={{0,16},{1,17},{2,18},{3,19},{4,20},{5,21},{6,22},{7,23},{8,24},{9,... | collective-permute-start | bytes 405512 | tf_op jit(solution)/shard_map/ppermute | solution.py:41
  31.2 6.6 %collective-permute-start.14 = (bf16[528,128]{1,0:T(8,128)(2,1)S(1)}, bf16[528,128]{1,0:T(8,128)(2,1)S(1)}, u32[]{:S(2)}, u32[]{:S(2)}) collective-permute-start(bf16[528,128]{1,0:T(8,128)(2,1)S(1)} %shard_map.65), channel_id=1, source_target_pairs={{0,8},{1,9},{2,10},{3,11},{4,12},{5,13},{6,14},{7,15},{8,16},{9,17... | collective-permute-start | bytes 405512 | tf_op jit(solution)/shard_map/ppermute | solution.py:41
  33.0 5.2 %collective-permute-start.15 = (bf16[528,128]{1,0:T(8,128)(2,1)S(1)}, bf16[528,128]{1,0:T(8,128)(2,1)S(1)}, u32[]{:S(2)}, u32[]{:S(2)}) collective-permute-start(bf16[528,128]{1,0:T(8,128)(2,1)S(1)} %shard_map.66), channel_id=1, source_target_pairs={{0,24},{1,25},{2,26},{3,27},{4,28},{5,29},{6,30},{7,31},{8,0},{9,1... | collective-permute-start | bytes 405512 | tf_op jit(solution)/shard_map/ppermute | solution.py:41
  57.0 6.7 %collective-permute-start.16 = (bf16[128,128]{1,0:T(8,128)(2,1)S(1)}, bf16[128,128]{1,0:T(8,128)(2,1)S(1)}, u32[]{:S(2)}, u32[]{:S(2)}) collective-permute-start(bf16[128,128]{1,0:T(8,128)(2,1)S(1)} %shard_map.68.own), channel_id=1, source_target_pairs={{0,31},{1,2},{2,1},{3,4},{4,3},{5,6},{6,5},{7,8},{8,7},{9,10},{10,... | collective-permute-start | bytes 98312 | tf_op jit(solution)/shard_map/ppermute | solution.py:465
  59.9 3.9 %collective-permute-start.17 = (bf16[128,128]{1,0:T(8,128)(2,1)S(1)}, bf16[128,128]{1,0:T(8,128)(2,1)S(1)}, u32[]{:S(2)}, u32[]{:S(2)}) collective-permute-start(bf16[128,128]{1,0:T(8,128)(2,1)S(1)} %shard_map.68.own), channel_id=1, source_target_pairs={{0,1},{1,0},{2,3},{3,2},{4,5},{5,4},{6,7},{7,6},{8,9},{9,8},{10,11... | collective-permute-start | bytes 98312 | tf_op jit(solution)/shard_map/ppermute | solution.py:41

commit v15 on v14

--- a/solution.py
+++ b/solution.py
@@ -23,6 +23,7 @@
 
 
 LONG, SHORT = 6e10, 1e6
+AWAY = (1, 2, 3)
 
 
 def cost(flops):
@@ -156,23 +157,28 @@
     return read_picks(ref[at + 2 * K : at + HALF, :].astype(F32)[row : row + 4])
 
 
-def pick_kernel(sources, count, *refs):
-    outs = refs[count:]
-    picks = [tail_picks(refs[which], at, row) for _, (which, at, row), _ in sources]
-    for step in range(2 * Y):
-        y, span = step // 2, slice(step % 2 * 256, step % 2 * 256 + 256)
-        for out, (parts, _, before), values in zip(outs, sources, picks):
-            tables = [(half, refs[which][at : at + HALF, :]) for half, which, at in parts]
-            found = pick(tables, values[y : y + 1, span])
-            out[step] = found if before is None else found + refs[before][step]
-
-
-def pick_rows(sources, flops, *args):
-    return pl.pallas_call(
-        functools.partial(pick_kernel, sources, len(args)),
+def pick_kernel(sources, shifts, count, *refs):
+    outs, scratch = refs[count:-1], refs[-1]
+    place = lax.div(lax.axis_index("grid"), X * CORES)
+    for n, (_, (which, at, row), _) in enumerate(sources):
+        scratch[n] = tail_picks(refs[which], at, row)
+    for shift in shifts:
+        y = lax.rem(place + shift, Y)
+        for i in range(2):
+            span = slice(i * 256, i * 256 + 256)
+            for n, (out, (parts, _, before)) in enumerate(zip(outs, sources)):
+                tables = [(half, refs[which][at : at + HALF, :]) for half, which, at in parts]
+                found = pick(tables, scratch[n, pl.ds(y, 1), :][:, span])
+                out[2 * y + i] = found if before is None else found + refs[before][2 * y + i]
+
+
+def pick_rows(sources, shifts, flops, *args):
+    return pl.pallas_call(
+        functools.partial(pick_kernel, sources, shifts, len(args)),
         out_shape=[jax.ShapeDtypeStruct((2 * Y, 144, 256), BF16)] * len(sources),
         in_specs=in_vmem(len(args)),
         out_specs=in_vmem(len(sources)),
+        scratch_shapes=[pltpu.VMEM((len(sources), Y, LOW), jnp.int32)],
         compiler_params=params(),
         cost_estimate=cost(flops),
     )(*args)
@@ -204,6 +210,24 @@
     return off + off.T + diagonal, packed[65:66]
 
 
+def write_grams(out, i, shards, tail):
+    tail_row = lax.broadcasted_iota(jnp.int32, (16, K), 0)
+    for half in range(2):
+        span = slice(half * K, half * K + K)
+        pairs = [
+            join(shards[n][:, span], shards[n + 1][:, span]) for n in range(0, len(shards), 2)
+        ]
+        for side in range(2):
+            rows = jnp.concatenate([pair[side] for pair in pairs], axis=1)
+            total = lax.dot_general(rows, rows[:K], dims(1, 1), preferred_element_type=F32)
+            patch = i + 2 * half + 4 * side
+            upper, diagonal, pull = pack(total)
+            out[patch * 64 : patch * 64 + 64, :] = upper.astype(out.dtype)
+            tail = jnp.where(tail_row == 2 * patch, diagonal, tail)
+            tail = jnp.where(tail_row == 2 * patch + 1, pull, tail)
+    return tail
+
+
 def last_kernel(shifts, low, high, same, *rest):
     found, outs, picks = rest[:6], rest[6:-1], rest[-1]
     place = lax.div(lax.axis_index("grid"), X * CORES)
@@ -211,27 +235,41 @@
     table = ((0, low[...]), (1, high[...]))
     for out, shift in zip(outs, shifts):
         y = lax.rem(place + shift, Y)
-        tail_row = lax.broadcasted_iota(jnp.int32, (16, K), 0)
         tail = jnp.zeros((16, K), F32)
         for i in range(2):
             span = slice(i * 256, i * 256 + 256)
             last = pick(table, picks[pl.ds(y, 1), :][:, span])
             shards = [ref[2 * y + i] for ref in (*found, same)] + [last]
-            for half in range(2):
-                span = slice(half * K, half * K + K)
-                pairs = [
-                    join(shards[n][:, span], shards[n + 1][:, span])
-                    for n in range(0, len(shards), 2)
-                ]
-                for side in range(2):
-                    rows = jnp.concatenate([pair[side] for pair in pairs], axis=1)
-                    total = lax.dot_general(rows, rows[:K], dims(1, 1), preferred_element_type=F32)
-                    patch = i + 2 * half + 4 * side
-                    upper, diagonal, pull = pack(total)
-                    out[patch * 64 : patch * 64 + 64, :] = upper.astype(out.dtype)
-                    tail = jnp.where(tail_row == 2 * patch, diagonal, tail)
-                    tail = jnp.where(tail_row == 2 * patch + 1, pull, tail)
+            tail = write_grams(out, i, shards, tail)
         out[8 * 64 :, :] = tail.astype(out.dtype)
+
+
+def own_grams_kernel(sources, *refs):
+    found, tables, (out, scratch) = refs[:2], refs[2:-2], refs[-2:]
+    y = lax.div(lax.axis_index("grid"), X * CORES)
+    for n, (_, _, which, row) in enumerate(sources):
+        scratch[n] = tail_picks(tables[which], 0, row)
+    tail = jnp.zeros((16, K), F32)
+    for i in range(2):
+        span = slice(i * 256, i * 256 + 256)
+        shards = [ref[2 * y + i] for ref in found]
+        for n, (low, high, _, _) in enumerate(sources):
+            parts = ((0, tables[low][...]), (1, tables[high][...]))
+            shards.append(pick(parts, scratch[n, pl.ds(y, 1), :][:, span]))
+        tail = write_grams(out, i, shards, tail)
+    out[8 * 64 :, :] = tail
+
+
+def own_grams(sources, *args):
+    return pl.pallas_call(
+        functools.partial(own_grams_kernel, sources),
+        out_shape=jax.ShapeDtypeStruct((8 * 64 + 16, K), F32),
+        in_specs=in_vmem(len(args)),
+        out_specs=in_vmem(1)[0],
+        scratch_shapes=[pltpu.VMEM((len(sources), Y, LOW), jnp.int32)],
+        compiler_params=params(),
+        cost_estimate=cost(1e9),
+    )(*args)
 
 
 def last_grams(shifts, dtype, *args):
@@ -417,7 +455,7 @@
 
     whole = lambda which: ((0, which, 0), (1, which, HALF))
     found = pick_rows(
-        ((whole(0), (0, 0, 8), None), (whole(1), (1, 0, 12), None)), SHORT, near, other
+        ((whole(0), (0, 0, 8), None), (whole(1), (1, 0, 12), None)), (0, 1, 2, 3), SHORT, near, other
     )
     mean, perturb, sides = perturbations(state)
     low_half, high_half, mean, perturb, sides = lax.optimization_barrier(
@@ -438,26 +476,42 @@
         row = 8 + 4 * core
         return (((1, 2, 0),), (0, 0, row), 4), (((0, 3, 0),), (1, 0, row), 5)
 
-    same = pick_rows(firsts(0), SHORT, left, right)
+    same = pick_rows(firsts(0), AWAY, SHORT, left, right)
     left, right, same = lax.optimization_barrier((left, right, same))
     left_other, right_other = hop(left, 0, 0, 1), hop(right, 0, 0, 1)
-    same = pick_rows(seconds(0), LONG, left, right, left_more, right_more, *same)
+    same = pick_rows(seconds(0), AWAY, LONG, left, right, left_more, right_more, *same)
     left_more, right_more, same = lax.optimization_barrier((left_more, right_more, same))
     left_more_other, right_more_other = hop(left_more, 0, 0, 1), hop(right_more, 0, 0, 1)
-    cross = pick_rows(firsts(1), LONG, left_other, right_other)
+    cross = pick_rows(firsts(1), AWAY, LONG, left_other, right_other)
     cross = pick_rows(
-        seconds(1), SHORT, left_other, right_other, left_more_other, right_more_other, *cross
+        seconds(1), AWAY, SHORT, left_other, right_other, left_more_other, right_more_other, *cross
     )
     far_low, far_high, cross = lax.optimization_barrier((far_low, far_high, cross))
     far_low_other, far_high_other = hop(far_low, 0, 0, 1), hop(far_high, 0, 0, 1)
-    far = pick_rows(((((0, 0, 0), (1, 1, 0)), (0, 0, 4), None),), SHORT, far_low, far_high)[0]
+    far = pick_rows(((((0, 0, 0), (1, 1, 0)), (0, 0, 4), None),), AWAY, SHORT, far_low, far_high)[0]
     last = (far_low_other, far_high_other, far, *found, same[0], cross[0], same[1], cross[1])
 
     across = last_grams((2,), BF16, *last)[0]
     from_across = hop(across, 2, 0, 0)
     from_up = hop(last_grams((1,), BF16, *last)[0], 1, 0, 0)
     from_down = hop(last_grams((3,), BF16, *last)[0], -1, 0, 0)
-    own = last_grams((0,), F32, *last)[0]
+    sources = ((0, 2, 0, 8), (1, 3, 1, 12), (6, 4, 4, 8), (7, 5, 5, 12), (8, 9, 8, 4), (10, 11, 11, 4))
+    own = own_grams(
+        sources,
+        *found,
+        left,
+        left_other,
+        left_more,
+        left_more_other,
+        right,
+        right_other,
+        right_more,
+        right_more_other,
+        far_low,
+        far_high,
+        far_low_other,
+        far_high_other,
+    )
     parts = sum_parts(own, from_across, from_up, from_down)
     parts = lax.all_to_all(parts, "obs", 0, 0, tiled=True)
 

time: 66.3 us -> 65.9 us (level)
  waiting for transfers between devices: 7.54 us -> 6.49 us
    pallas_call x6 -> x7, Pallas kernels: 9.32 us -> 10.6 us  [the longest x6 8.04 us: pick_rows(): pl.pallas_call(functools.partial(pick_kernel, sources, shifts, len(args))...]
    pallas_call x4 -> x3, Pallas kernels: 4.27 us -> 3.2 us  [last_grams(): pl.pallas_call(functools.partial(last_kernel, shifts), out_shape=[jax.Sha...]
    ppermute x17, waiting for transfers between devices: 3.77 us -> 3.05 us  [hop(): return lax.ppermute(value, 'grid', pairs)]
  transfers between devices with their start and end apart: 18 -> 18, of which waited for: 8 -> 6; matrix products, arithmetic and copies ran while one was open for 0% -> 0% of each run, Pallas kernels for 22% -> 22%
where the time goes in v15:
time: 65.9 us; the launch traced here: 65 us
  Pallas kernels  21.2 us (32%)
  starting transfers between devices  20.7 us (31%)
  blocking collectives  16.3 us (25%)
  waiting for transfers between devices  6.49 us (10%)
    ppermute x17, starting transfers between devices, hop(): return lax.ppermute(value, 'grid', pairs)  18 us
    all_to_all x1, blocking collectives, on_device(): parts = lax.all_to_all(parts, 'obs', 0, 0, tiled=True)  16.3 us
    pallas_call x6, Pallas kernels, pick_rows(): pl.pallas_call(functools.partial(pick_kernel, sources, shifts, len(args))...  8.04 us
    ppermute x1, waiting for transfers between devices, on_device(): lax.ppermute(own, 'grid', [(j, (j + 2 * (j % 2) - 1) % n_grid) for j in r...  3.44 us
    pallas_call x3, Pallas kernels, last_grams(): pl.pallas_call(functools.partial(last_kernel, shifts), out_shape=[jax.Sha...  3.2 us
    ppermute x17, waiting for transfers between devices, hop(): return lax.ppermute(value, 'grid', pairs)  3.05 us
    ppermute x1, starting transfers between devices, on_device(): lax.ppermute(own, 'grid', [(j, (j + 2 * (j % 2) - 1) % n_grid) for j in r...  2.64 us
    pallas_call x1, Pallas kernels, own_grams(): pl.pallas_call(functools.partial(own_grams_kernel, sources), out_shape=ja...  2.6 us
  transfers between devices with their start and end apart: 18, of which 6 were waited for; matrix products, arithmetic and copies ran while one was open for 0% of the time, Pallas kernels for 22%

profile of v15, /device:TPU:32, one launch (start us, length us, event | category | flops | bytes accessed | tf_op | source)
XLA Modules:
  0.0 65.0 jit_solution(8243841852160911897)
XLA Ops:
  0.0 1.8 %shard_map.55 = (bf16[272,512]{1,0:T(8,128)(2,1)S(1)}, bf16[272,512]{1,0:T(8,128)(2,1)S(1)}, bf16[544,512]{1,0:T(8,128)(2,1)S(1)}) custom-call(bf16[2048,128]{1,0:T(8,128)(2,1)} %departures.1, f32[2048]{0:T(1024)} %innovation.1, f32[2048]{0:T(1024)} %obs_weight.1, s32[64,256]{1,0:T(8,128)} %bitcast.3), custom_call_target="tpu_custom_call" | custom-call | flops 2000000000 | bytes 100000 | tf_op jit(solution)/shard_map/pallas_call | solution.py:122
  1.8 1.6 %collective-permute-start = (bf16[272,512]{1,0:T(8,128)(2,1)S(1)}, bf16[272,512]{1,0:T(8,128)(2,1)S(1)}, u32[]{:S(2)}, u32[]{:S(2)}) collective-permute-start(bf16[272,512]{1,0:T(8,128)(2,1)S(1)} %get-tuple-element.70), channel_id=1, source_target_pairs={{0,2},{1,3},{2,4},{3,5},{4,6},{5,7},{6,0},{7,1},{8,10},{9,11},{10,... | collective-permute-start | bytes 835592 | tf_op jit(solution)/shard_map/ppermute | solution.py:42
  3.3 1.7 %collective-permute-start.2 = (bf16[272,512]{1,0:T(8,128)(2,1)S(1)}, bf16[272,512]{1,0:T(8,128)(2,1)S(1)}, u32[]{:S(2)}, u32[]{:S(2)}) collective-permute-start(bf16[272,512]{1,0:T(8,128)(2,1)S(1)} %get-tuple-element.69), channel_id=1, source_target_pairs={{0,6},{1,7},{2,0},{3,1},{4,2},{5,3},{6,4},{7,5},{8,14},{9,15},{10,... | collective-permute-start | bytes 835592 | tf_op jit(solution)/shard_map/ppermute | solution.py:42
  5.1 0.0 collective-permute-start.1
  5.1 1.2 %shard_map.57 = (f32[24,256]{1,0:T(8,128)S(1)}, bf16[24,128,256]{2,1,0:T(8,128)(2,1)S(1)}, bf16[24,256,256]{2,1,0:T(8,128)(2,1)S(1)}) custom-call(bf16[48,128,128]{2,1,0:T(8,128)(2,1)S(1)} %copy-done), custom_call_target="tpu_custom_call" | custom-call | flops 60000002048 | bytes 100000 | tf_op jit(solution)/shard_map/pallas_call | solution.py:380
  6.3 0.4 collective-permute-start.4
  6.6 3.0 %collective-permute-start.5 = (bf16[272,512]{1,0:T(8,128)(2,1)S(1)}, bf16[272,512]{1,0:T(8,128)(2,1)S(1)}, u32[]{:S(2)}, u32[]{:S(2)}) collective-permute-start(bf16[272,512]{1,0:T(8,128)(2,1)S(1)} %get-tuple-element.70), channel_id=1, source_target_pairs={{0,6},{1,7},{2,0},{3,1},{4,2},{5,3},{6,4},{7,5},{8,14},{9,15},{10,... | collective-permute-start | bytes 835592 | tf_op jit(solution)/shard_map/ppermute | solution.py:42
  9.6 0.0 collective-permute-done.1.refs_1_
  9.6 2.6 %shard_map.56 = (bf16[8,144,256]{2,1,0:T(8,128)(2,1)S(1)}, bf16[8,144,256]{2,1,0:T(8,128)(2,1)S(1)}) custom-call(bf16[544,512]{1,0:T(8,128)(2,1)S(1)} %get-tuple-element.50.refs_0_, bf16[544,512]{1,0:T(8,128)(2,1)S(1)} %collective-permute-done.1.refs_1_), custom_call_target="tpu_custom_call" | custom-call | flops 1000000 | bytes 100000 | tf_op jit(solution)/shard_map/pallas_call | solution.py:176
  12.2 0.0 collective-permute-done.refs_0_.refs_2_
  12.2 0.7 %collective-permute-start.9 = (bf16[272,512]{1,0:T(8,128)(2,1)S(1)}, bf16[272,512]{1,0:T(8,128)(2,1)S(1)}, u32[]{:S(2)}, u32[]{:S(2)}) collective-permute-start(bf16[272,512]{1,0:T(8,128)(2,1)S(1)} %collective-permute-done.refs_0_.refs_2_), channel_id=1, source_target_pairs={{0,2},{1,3},{2,4},{3,5},{4,6},{5,7},{6,0},{7,1},{8,10},{9,11},{10,... | collective-permute-start | bytes 835592 | tf_op jit(solution)/shard_map/ppermute | solution.py:42
  12.9 0.0 collective-permute-done.2.refs_1_.refs_6_
  12.9 2.6 %collective-permute-start.10 = (bf16[272,512]{1,0:T(8,128)(2,1)S(1)}, bf16[272,512]{1,0:T(8,128)(2,1)S(1)}, u32[]{:S(2)}, u32[]{:S(2)}) collective-permute-start(bf16[272,512]{1,0:T(8,128)(2,1)S(1)} %collective-permute-done.2.refs_1_.refs_6_), channel_id=1, source_target_pairs={{0,6},{1,7},{2,0},{3,1},{4,2},{5,3},{6,4},{7,5},{8,14},{9,15},{10,... | collective-permute-start | bytes 835592 | tf_op jit(solution)/shard_map/ppermute | solution.py:42
  15.5 1.1 %shard_map.58 = (bf16[8,144,256]{2,1,0:T(8,128)(2,1)S(1)}, bf16[8,144,256]{2,1,0:T(8,128)(2,1)S(1)}) custom-call(bf16[272,512]{1,0:T(8,128)(2,1)S(1)} %collective-permute-done.refs_0_.refs_2_, bf16[272,512]{1,0:T(8,128)(2,1)S(1)} %collective-permute-done.2.refs_1_.refs_6_), custom_call_target="tpu_custom_call" | custom-call | flops 1000000 | bytes 100000 | tf_op jit(solution)/shard_map/pallas_call | solution.py:176
  16.6 0.1 collective-permute-start.3
  16.7 1.5 %collective-permute-done.4.refs_2_.refs_4_ = bf16[272,512]{1,0:T(8,128)(2,1)S(1)} collective-permute-done((bf16[272,512]{1,0:T(8,128)(2,1)S(1)}, bf16[272,512]{1,0:T(8,128)(2,1)S(1)}, u32[]{:S(2)}, u32[]{:S(2)}) %collective-permute-start.4) | collective-permute-done | bytes 278560 | tf_op jit(solution)/shard_map/ppermute | solution.py:42
  18.2 0.0 collective-permute-start.7
  18.2 0.7 %collective-permute-done.5.refs_3_.refs_8_ = bf16[272,512]{1,0:T(8,128)(2,1)S(1)} collective-permute-done((bf16[272,512]{1,0:T(8,128)(2,1)S(1)}, bf16[272,512]{1,0:T(8,128)(2,1)S(1)}, u32[]{:S(2)}, u32[]{:S(2)}) %collective-permute-start.5) | collective-permute-done | bytes 278560 | tf_op jit(solution)/shard_map/ppermute | solution.py:42
  18.9 1.1 %shard_map.59 = (bf16[8,144,256]{2,1,0:T(8,128)(2,1)S(1)}, bf16[8,144,256]{2,1,0:T(8,128)(2,1)S(1)}) custom-call(bf16[272,512]{1,0:T(8,128)(2,1)S(1)} %collective-permute-done.refs_0_.refs_2_, bf16[272,512]{1,0:T(8,128)(2,1)S(1)} %collective-permute-done.2.refs_1_.refs_6_, bf16[272,512]{1,0:T(8,128)(2,1)S(1)} %collective-permute-done.4.refs_2_.refs_4_, ...), custom_call_target="tpu_custom_call" | custom-call | flops 60000002048 | bytes 100000 | tf_op jit(solution)/shard_map/pallas_call | solution.py:176
  20.0 0.3 collective-permute-start.6
  20.3 0.5 collective-permute-start.8
  20.8 0.0 collective-permute-done.7.refs_1_.refs_7_
  20.8 1.1 %shard_map.60 = (bf16[8,144,256]{2,1,0:T(8,128)(2,1)S(1)}, bf16[8,144,256]{2,1,0:T(8,128)(2,1)S(1)}) custom-call(bf16[272,512]{1,0:T(8,128)(2,1)S(1)} %collective-permute-done.3.refs_0_.refs_3_, bf16[272,512]{1,0:T(8,128)(2,1)S(1)} %collective-permute-done.7.refs_1_.refs_7_), custom_call_target="tpu_custom_call" | custom-call | flops 60000002048 | bytes 100000 | tf_op jit(solution)/shard_map/pallas_call | solution.py:176
  21.9 0.3 collective-permute-done.8.refs_3_.refs_9_
  22.2 1.1 %shard_map.61 = (bf16[8,144,256]{2,1,0:T(8,128)(2,1)S(1)}, bf16[8,144,256]{2,1,0:T(8,128)(2,1)S(1)}) custom-call(bf16[272,512]{1,0:T(8,128)(2,1)S(1)} %collective-permute-done.3.refs_0_.refs_3_, bf16[272,512]{1,0:T(8,128)(2,1)S(1)} %collective-permute-done.7.refs_1_.refs_7_, bf16[272,512]{1,0:T(8,128)(2,1)S(1)} %collective-permute-done.6.refs_2_.refs_5_, ...), custom_call_target="tpu_custom_call" | custom-call | flops 1000000 | bytes 100000 | tf_op jit(solution)/shard_map/pallas_call | solution.py:176
  23.3 0.1 collective-permute-done.10.refs_11_.refs_1_
  23.4 0.2 collective-permute-start.11
  23.5 0.4 collective-permute-start.12
  23.9 1.1 %shard_map.63.same = bf16[8,144,256]{2,1,0:T(8,128)(2,1)S(1)} custom-call(bf16[272,512]{1,0:T(8,128)(2,1)S(1)} %collective-permute-done.9.refs_10_.refs_0_, bf16[272,512]{1,0:T(8,128)(2,1)S(1)} %collective-permute-done.10.refs_11_.refs_1_), custom_call_target="tpu_custom_call" | custom-call | flops 1000000 | bytes 100000 | tf_op jit(solution)/shard_map/pallas_call | solution.py:176
  25.0 0.4 collective-permute-done.12.refs_13_.high
  25.4 1.1 %shard_map.64 = bf16[528,128]{1,0:T(8,128)(2,1)S(1)} custom-call(bf16[272,512]{1,0:T(8,128)(2,1)S(1)} %collective-permute-done.11.refs_12_.low, bf16[272,512]{1,0:T(8,128)(2,1)S(1)} %collective-permute-done.12.refs_13_.high, bf16[8,144,256]{2,1,0:T(8,128)(2,1)S(1)} %shard_map.63.same, bf16[8,144,256]{2,1,0:T(8,128)(2,1)S(1)} %get-tuple-element.62.refs_0_.rest_0_, ...), custom_call_target="tpu_custom_call" | custom-call | flops 1000000000 | bytes 100000 | tf_op jit(solution)/shard_map/pallas_call | solution.py:276
  26.4 3.3 %collective-permute-start.13 = (bf16[528,128]{1,0:T(8,128)(2,1)S(1)}, bf16[528,128]{1,0:T(8,128)(2,1)S(1)}, u32[]{:S(2)}, u32[]{:S(2)}) collective-permute-start(bf16[528,128]{1,0:T(8,128)(2,1)S(1)} %shard_map.64), channel_id=1, source_target_pairs={{0,16},{1,17},{2,18},{3,19},{4,20},{5,21},{6,22},{7,23},{8,24},{9,... | collective-permute-start | bytes 405512 | tf_op jit(solution)/shard_map/ppermute | solution.py:42
  29.7 1.1 %shard_map.65 = bf16[528,128]{1,0:T(8,128)(2,1)S(1)} custom-call(bf16[272,512]{1,0:T(8,128)(2,1)S(1)} %collective-permute-done.11.refs_12_.low, bf16[272,512]{1,0:T(8,128)(2,1)S(1)} %collective-permute-done.12.refs_13_.high, bf16[8,144,256]{2,1,0:T(8,128)(2,1)S(1)} %shard_map.63.same, bf16[8,144,256]{2,1,0:T(8,128)(2,1)S(1)} %get-tuple-element.62.refs_0_.rest_0_, ...), custom_call_target="tpu_custom_call" | custom-call | flops 1000000000 | bytes 100000 | tf_op jit(solution)/shard_map/pallas_call | solution.py:276
  30.8 0.8 %collective-permute-start.14 = (bf16[528,128]{1,0:T(8,128)(2,1)S(1)}, bf16[528,128]{1,0:T(8,128)(2,1)S(1)}, u32[]{:S(2)}, u32[]{:S(2)}) collective-permute-start(bf16[528,128]{1,0:T(8,128)(2,1)S(1)} %shard_map.65), channel_id=1, source_target_pairs={{0,8},{1,9},{2,10},{3,11},{4,12},{5,13},{6,14},{7,15},{8,16},{9,17... | collective-permute-start | bytes 405512 | tf_op jit(solution)/shard_map/ppermute | solution.py:42
  31.6 1.1 %shard_map.66 = bf16[528,128]{1,0:T(8,128)(2,1)S(1)} custom-call(bf16[272,512]{1,0:T(8,128)(2,1)S(1)} %collective-permute-done.11.refs_12_.low, bf16[272,512]{1,0:T(8,128)(2,1)S(1)} %collective-permute-done.12.refs_13_.high, bf16[8,144,256]{2,1,0:T(8,128)(2,1)S(1)} %shard_map.63.same, bf16[8,144,256]{2,1,0:T(8,128)(2,1)S(1)} %get-tuple-element.62.refs_0_.rest_0_, ...), custom_call_target="tpu_custom_call" | custom-call | flops 1000000000 | bytes 100000 | tf_op jit(solution)/shard_map/pallas_call | solution.py:276
  32.6 2.6 %collective-permute-start.15 = (bf16[528,128]{1,0:T(8,128)(2,1)S(1)}, bf16[528,128]{1,0:T(8,128)(2,1)S(1)}, u32[]{:S(2)}, u32[]{:S(2)}) collective-permute-start(bf16[528,128]{1,0:T(8,128)(2,1)S(1)} %shard_map.66), channel_id=1, source_target_pairs={{0,24},{1,25},{2,26},{3,27},{4,28},{5,29},{6,30},{7,31},{8,0},{9,1... | collective-permute-start | bytes 405512 | tf_op jit(solution)/shard_map/ppermute | solution.py:42
  35.3 2.6 %shard_map.62.own = f32[528,128]{1,0:T(8,128)S(1)} custom-call(bf16[8,144,256]{2,1,0:T(8,128)(2,1)S(1)} %get-tuple-element.62.refs_0_.rest_0_, bf16[8,144,256]{2,1,0:T(8,128)(2,1)S(1)} %get-tuple-element.63.refs_1_.rest_1_, bf16[272,512]{1,0:T(8,128)(2,1)S(1)} %collective-permute-done.refs_0_.refs_2_, ...), custom_call_target="tpu_custom_call" | custom-call | flops 1000000000 | bytes 100000 | tf_op jit(solution)/shard_map/pallas_call | solution.py:264
  37.9 0.0 collective-permute-done.13.a
  37.9 0.0 collective-permute-done.14.b
  37.9 0.1 shard_map.67
  38.0 16.3 %all_to_all.5.parts = bf16[8,80,128]{2,1,0:T(8,128)(2,1)S(1)} all-to-all(bf16[8,80,128]{2,1,0:T(8,128)(2,1)S(1)} %shard_map.67), channel_id=1, replica_groups=mesh['obs'=8,'grid'=32] {'obs'}, dimensions={0} | all-to-all | bytes 327680 | tf_op jit(solution)/shard_map/all_to_all | solution.py:516
  54.3 2.3 %shard_map.68.own = bf16[128,128]{1,0:T(8,128)(2,1)S(1)} custom-call(bf16[8,80,128]{2,1,0:T(8,128)(2,1)S(1)} %all_to_all.5.parts), custom_call_target="tpu_custom_call" | custom-call | flops 4000000000 | bytes 100000 | tf_op jit(solution)/shard_map/pallas_call | solution.py:348
  56.7 2.6 %collective-permute-start.16 = (bf16[128,128]{1,0:T(8,128)(2,1)S(1)}, bf16[128,128]{1,0:T(8,128)(2,1)S(1)}, u32[]{:S(2)}, u32[]{:S(2)}) collective-permute-start(bf16[128,128]{1,0:T(8,128)(2,1)S(1)} %shard_map.68.own), channel_id=1, source_target_pairs={{0,31},{1,2},{2,1},{3,4},{4,3},{5,6},{6,5},{7,8},{8,7},{9,10},{10,... | collective-permute-start | bytes 98312 | tf_op jit(solution)/shard_map/ppermute | solution.py:519
  59.3 0.6 shard_map.69.part
  59.9 0.1 collective-permute-start.17
  60.0 3.4 %collective-permute-done.16.beyond = bf16[128,128]{1,0:T(8,128)(2,1)S(1)} collective-permute-done((bf16[128,128]{1,0:T(8,128)(2,1)S(1)}, bf16[128,128]{1,0:T(8,128)(2,1)S(1)}, u32[]{:S(2)}, u32[]{:S(2)}) %collective-permute-start.16) | collective-permute-done | bytes 32800 | tf_op jit(solution)/shard_map/ppermute | solution.py:519
  63.4 0.0 collective-permute-done.17.beside
  63.4 1.5 %shard_map.70 = bf16[48,128,128]{2,1,0:T(8,128)(2,1)} custom-call(bf16[128,128]{1,0:T(8,128)(2,1)S(1)} %collective-permute-done.16.beyond, bf16[128,128]{1,0:T(8,128)(2,1)S(1)} %collective-permute-done.17.beside, f32[24,128,256]{2,1,0:T(8,128)S(1)} %shard_map.69.part, bf16[24,256,256]{2,1,0:T(8,128)(2,1)S(1)} %get-tuple-element.92.sides), custom_call_target="tpu_custom_call" | custom-call | flops 2000000000 | bytes 100000 | tf_op jit(solution)/shard_map/pallas_call | solution.py:436
  (7 shorter events, 0.0 us)
Async XLA Ops:
  0.0 5.1 %copy-start = (bf16[48,128,128]{2,1,0:T(8,128)(2,1)S(1)}, bf16[48,128,128]{2,1,0:T(8,128)(2,1)}, u32[]{:S(2)}) copy-start(bf16[48,128,128]{2,1,0:T(8,128)(2,1)} %state.1) | copy-start | bytes 4718596
  1.8 10.4 %collective-permute-start = (bf16[272,512]{1,0:T(8,128)(2,1)S(1)}, bf16[272,512]{1,0:T(8,128)(2,1)S(1)}, u32[]{:S(2)}, u32[]{:S(2)}) collective-permute-start(bf16[272,512]{1,0:T(8,128)(2,1)S(1)} %get-tuple-element.70), channel_id=1, source_target_pairs={{0,2},{1,3},{2,4},{3,5},{4,6},{5,7},{6,0},{7,1},{8,10},{9,11},{10,... | collective-permute-start | bytes 835592 | tf_op jit(solution)/shard_map/ppermute | solution.py:42
  3.3 9.6 %collective-permute-start.2 = (bf16[272,512]{1,0:T(8,128)(2,1)S(1)}, bf16[272,512]{1,0:T(8,128)(2,1)S(1)}, u32[]{:S(2)}, u32[]{:S(2)}) collective-permute-start(bf16[272,512]{1,0:T(8,128)(2,1)S(1)} %get-tuple-element.69), channel_id=1, source_target_pairs={{0,6},{1,7},{2,0},{3,1},{4,2},{5,3},{6,4},{7,5},{8,14},{9,15},{10,... | collective-permute-start | bytes 835592 | tf_op jit(solution)/shard_map/ppermute | solution.py:42
  5.1 4.5 %collective-permute-start.1 = (bf16[544,512]{1,0:T(8,128)(2,1)S(1)}, bf16[544,512]{1,0:T(8,128)(2,1)S(1)}, u32[]{:S(2)}, u32[]{:S(2)}) collective-permute-start(bf16[544,512]{1,0:T(8,128)(2,1)S(1)} %get-tuple-element.50.refs_0_), channel_id=1, source_target_pairs={{0,1},{1,0},{2,3},{3,2},{4,5},{5,4},{6,7},{7,6},{8,9},{9,8},{10,11... | collective-permute-start | bytes 1671176 | tf_op jit(solution)/shard_map/ppermute | solution.py:42
  6.3 11.9 %collective-permute-start.4 = (bf16[272,512]{1,0:T(8,128)(2,1)S(1)}, bf16[272,512]{1,0:T(8,128)(2,1)S(1)}, u32[]{:S(2)}, u32[]{:S(2)}) collective-permute-start(bf16[272,512]{1,0:T(8,128)(2,1)S(1)} %get-tuple-element.69), channel_id=1, source_target_pairs={{0,2},{1,3},{2,4},{3,5},{4,6},{5,7},{6,0},{7,1},{8,10},{9,11},{10,... | collective-permute-start | bytes 835592 | tf_op jit(solution)/shard_map/ppermute | solution.py:42
  6.6 12.3 %collective-permute-start.5 = (bf16[272,512]{1,0:T(8,128)(2,1)S(1)}, bf16[272,512]{1,0:T(8,128)(2,1)S(1)}, u32[]{:S(2)}, u32[]{:S(2)}) collective-permute-start(bf16[272,512]{1,0:T(8,128)(2,1)S(1)} %get-tuple-element.70), channel_id=1, source_target_pairs={{0,6},{1,7},{2,0},{3,1},{4,2},{5,3},{6,4},{7,5},{8,14},{9,15},{10,... | collective-permute-start | bytes 835592 | tf_op jit(solution)/shard_map/ppermute | solution.py:42
  12.2 11.2 %collective-permute-start.9 = (bf16[272,512]{1,0:T(8,128)(2,1)S(1)}, bf16[272,512]{1,0:T(8,128)(2,1)S(1)}, u32[]{:S(2)}, u32[]{:S(2)}) collective-permute-start(bf16[272,512]{1,0:T(8,128)(2,1)S(1)} %collective-permute-done.refs_0_.refs_2_), channel_id=1, source_target_pairs={{0,2},{1,3},{2,4},{3,5},{4,6},{5,7},{6,0},{7,1},{8,10},{9,11},{10,... | collective-permute-start | bytes 835592 | tf_op jit(solution)/shard_map/ppermute | solution.py:42
  12.9 10.5 %collective-permute-start.10 = (bf16[272,512]{1,0:T(8,128)(2,1)S(1)}, bf16[272,512]{1,0:T(8,128)(2,1)S(1)}, u32[]{:S(2)}, u32[]{:S(2)}) collective-permute-start(bf16[272,512]{1,0:T(8,128)(2,1)S(1)} %collective-permute-done.2.refs_1_.refs_6_), channel_id=1, source_target_pairs={{0,6},{1,7},{2,0},{3,1},{4,2},{5,3},{6,4},{7,5},{8,14},{9,15},{10,... | collective-permute-start | bytes 835592 | tf_op jit(solution)/shard_map/ppermute | solution.py:42
  16.6 3.7 %collective-permute-start.3 = (bf16[272,512]{1,0:T(8,128)(2,1)S(1)}, bf16[272,512]{1,0:T(8,128)(2,1)S(1)}, u32[]{:S(2)}, u32[]{:S(2)}) collective-permute-start(bf16[272,512]{1,0:T(8,128)(2,1)S(1)} %collective-permute-done.refs_0_.refs_2_), channel_id=1, source_target_pairs={{0,1},{1,0},{2,3},{3,2},{4,5},{5,4},{6,7},{7,6},{8,9},{9,8},{10,11... | collective-permute-start | bytes 835592 | tf_op jit(solution)/shard_map/ppermute | solution.py:42
  18.2 2.6 %collective-permute-start.7 = (bf16[272,512]{1,0:T(8,128)(2,1)S(1)}, bf16[272,512]{1,0:T(8,128)(2,1)S(1)}, u32[]{:S(2)}, u32[]{:S(2)}) collective-permute-start(bf16[272,512]{1,0:T(8,128)(2,1)S(1)} %collective-permute-done.2.refs_1_.refs_6_), channel_id=1, source_target_pairs={{0,1},{1,0},{2,3},{3,2},{4,5},{5,4},{6,7},{7,6},{8,9},{9,8},{10,11... | collective-permute-start | bytes 835592 | tf_op jit(solution)/shard_map/ppermute | solution.py:42
  20.0 1.9 %collective-permute-start.6 = (bf16[272,512]{1,0:T(8,128)(2,1)S(1)}, bf16[272,512]{1,0:T(8,128)(2,1)S(1)}, u32[]{:S(2)}, u32[]{:S(2)}) collective-permute-start(bf16[272,512]{1,0:T(8,128)(2,1)S(1)} %collective-permute-done.4.refs_2_.refs_4_), channel_id=1, source_target_pairs={{0,1},{1,0},{2,3},{3,2},{4,5},{5,4},{6,7},{7,6},{8,9},{9,8},{10,11... | collective-permute-start | bytes 835592 | tf_op jit(solution)/shard_map/ppermute | solution.py:42
  20.3 1.9 %collective-permute-start.8 = (bf16[272,512]{1,0:T(8,128)(2,1)S(1)}, bf16[272,512]{1,0:T(8,128)(2,1)S(1)}, u32[]{:S(2)}, u32[]{:S(2)}) collective-permute-start(bf16[272,512]{1,0:T(8,128)(2,1)S(1)} %collective-permute-done.5.refs_3_.refs_8_), channel_id=1, source_target_pairs={{0,1},{1,0},{2,3},{3,2},{4,5},{5,4},{6,7},{7,6},{8,9},{9,8},{10,11... | collective-permute-start | bytes 835592 | tf_op jit(solution)/shard_map/ppermute | solution.py:42
  23.4 1.6 %collective-permute-start.11 = (bf16[272,512]{1,0:T(8,128)(2,1)S(1)}, bf16[272,512]{1,0:T(8,128)(2,1)S(1)}, u32[]{:S(2)}, u32[]{:S(2)}) collective-permute-start(bf16[272,512]{1,0:T(8,128)(2,1)S(1)} %collective-permute-done.9.refs_10_.refs_0_), channel_id=1, source_target_pairs={{0,1},{1,0},{2,3},{3,2},{4,5},{5,4},{6,7},{7,6},{8,9},{9,8},{10,11... | collective-permute-start | bytes 835592 | tf_op jit(solution)/shard_map/ppermute | solution.py:42
  23.5 1.8 %collective-permute-start.12 = (bf16[272,512]{1,0:T(8,128)(2,1)S(1)}, bf16[272,512]{1,0:T(8,128)(2,1)S(1)}, u32[]{:S(2)}, u32[]{:S(2)}) collective-permute-start(bf16[272,512]{1,0:T(8,128)(2,1)S(1)} %collective-permute-done.10.refs_11_.refs_1_), channel_id=1, source_target_pairs={{0,1},{1,0},{2,3},{3,2},{4,5},{5,4},{6,7},{7,6},{8,9},{9,8},{10,11... | collective-permute-start | bytes 835592 | tf_op jit(solution)/shard_map/ppermute | solution.py:42
  26.4 11.4 %collective-permute-start.13 = (bf16[528,128]{1,0:T(8,128)(2,1)S(1)}, bf16[528,128]{1,0:T(8,128)(2,1)S(1)}, u32[]{:S(2)}, u32[]{:S(2)}) collective-permute-start(bf16[528,128]{1,0:T(8,128)(2,1)S(1)} %shard_map.64), channel_id=1, source_target_pairs={{0,16},{1,17},{2,18},{3,19},{4,20},{5,21},{6,22},{7,23},{8,24},{9,... | collective-permute-start | bytes 405512 | tf_op jit(solution)/shard_map/ppermute | solution.py:42
  30.8 7.1 %collective-permute-start.14 = (bf16[528,128]{1,0:T(8,128)(2,1)S(1)}, bf16[528,128]{1,0:T(8,128)(2,1)S(1)}, u32[]{:S(2)}, u32[]{:S(2)}) collective-permute-start(bf16[528,128]{1,0:T(8,128)(2,1)S(1)} %shard_map.65), channel_id=1, source_target_pairs={{0,8},{1,9},{2,10},{3,11},{4,12},{5,13},{6,14},{7,15},{8,16},{9,17... | collective-permute-start | bytes 405512 | tf_op jit(solution)/shard_map/ppermute | solution.py:42
  32.6 5.3 %collective-permute-start.15 = (bf16[528,128]{1,0:T(8,128)(2,1)S(1)}, bf16[528,128]{1,0:T(8,128)(2,1)S(1)}, u32[]{:S(2)}, u32[]{:S(2)}) collective-permute-start(bf16[528,128]{1,0:T(8,128)(2,1)S(1)} %shard_map.66), channel_id=1, source_target_pairs={{0,24},{1,25},{2,26},{3,27},{4,28},{5,29},{6,30},{7,31},{8,0},{9,1... | collective-permute-start | bytes 405512 | tf_op jit(solution)/shard_map/ppermute | solution.py:42
  56.7 6.7 %collective-permute-start.16 = (bf16[128,128]{1,0:T(8,128)(2,1)S(1)}, bf16[128,128]{1,0:T(8,128)(2,1)S(1)}, u32[]{:S(2)}, u32[]{:S(2)}) collective-permute-start(bf16[128,128]{1,0:T(8,128)(2,1)S(1)} %shard_map.68.own), channel_id=1, source_target_pairs={{0,31},{1,2},{2,1},{3,4},{4,3},{5,6},{6,5},{7,8},{8,7},{9,10},{10,... | collective-permute-start | bytes 98312 | tf_op jit(solution)/shard_map/ppermute | solution.py:519
  59.9 3.5 %collective-permute-start.17 = (bf16[128,128]{1,0:T(8,128)(2,1)S(1)}, bf16[128,128]{1,0:T(8,128)(2,1)S(1)}, u32[]{:S(2)}, u32[]{:S(2)}) collective-permute-start(bf16[128,128]{1,0:T(8,128)(2,1)S(1)} %shard_map.68.own), channel_id=1, source_target_pairs={{0,1},{1,0},{2,3},{3,2},{4,5},{5,4},{6,7},{7,6},{8,9},{9,8},{10,11... | collective-permute-start | bytes 98312 | tf_op jit(solution)/shard_map/ppermute | solution.py:42

commit v16 on v15

--- a/solution.py
+++ b/solution.py
@@ -245,7 +245,7 @@
 
 
 def own_grams_kernel(sources, *refs):
-    found, tables, (out, scratch) = refs[:2], refs[2:-2], refs[-2:]
+    found, tables, (same, out, scratch) = refs[:2], refs[2:-3], refs[-3:]
     y = lax.div(lax.axis_index("grid"), X * CORES)
     for n, (_, _, which, row) in enumerate(sources):
         scratch[n] = tail_picks(tables[which], 0, row)
@@ -256,6 +256,7 @@
         for n, (low, high, _, _) in enumerate(sources):
             parts = ((0, tables[low][...]), (1, tables[high][...]))
             shards.append(pick(parts, scratch[n, pl.ds(y, 1), :][:, span]))
+        shards.insert(-1, same[2 * y + i])
         tail = write_grams(out, i, shards, tail)
     out[8 * 64 :, :] = tail
 
@@ -488,14 +489,14 @@
     )
     far_low, far_high, cross = lax.optimization_barrier((far_low, far_high, cross))
     far_low_other, far_high_other = hop(far_low, 0, 0, 1), hop(far_high, 0, 0, 1)
-    far = pick_rows(((((0, 0, 0), (1, 1, 0)), (0, 0, 4), None),), AWAY, SHORT, far_low, far_high)[0]
+    far = pick_rows(((((0, 0, 0), (1, 1, 0)), (0, 0, 4), None),), (0, 1, 2, 3), SHORT, far_low, far_high)[0]
     last = (far_low_other, far_high_other, far, *found, same[0], cross[0], same[1], cross[1])
 
     across = last_grams((2,), BF16, *last)[0]
     from_across = hop(across, 2, 0, 0)
     from_up = hop(last_grams((1,), BF16, *last)[0], 1, 0, 0)
     from_down = hop(last_grams((3,), BF16, *last)[0], -1, 0, 0)
-    sources = ((0, 2, 0, 8), (1, 3, 1, 12), (6, 4, 4, 8), (7, 5, 5, 12), (8, 9, 8, 4), (10, 11, 11, 4))
+    sources = ((0, 2, 0, 8), (1, 3, 1, 12), (6, 4, 4, 8), (7, 5, 5, 12), (10, 11, 11, 4))
     own = own_grams(
         sources,
         *found,
@@ -511,6 +512,7 @@
         far_high,
         far_low_other,
         far_high_other,
+        far,
     )
     parts = sum_parts(own, from_across, from_up, from_down)
     parts = lax.all_to_all(parts, "obs", 0, 0, tiled=True)

time: 65.9 us -> 65.9 us (level)
  transfers between devices with their start and end apart: 18 -> 18, of which waited for: 6 -> 8; matrix products, arithmetic and copies ran while one was open for 0% -> 0% of each run, Pallas kernels for 22% -> 22%
where the time goes in v16:
time: 65.9 us; the launch traced here: 65 us
  Pallas kernels  21 us (32%)
  starting transfers between devices  20.7 us (31%)
  blocking collectives  16.3 us (25%)
  waiting for transfers between devices  6.58 us (10%)
    ppermute x17, starting transfers between devices, hop(): return lax.ppermute(value, 'grid', pairs)  18 us
    all_to_all x1, blocking collectives, on_device(): parts = lax.all_to_all(parts, 'obs', 0, 0, tiled=True)  16.3 us
    pallas_call x6, Pallas kernels, pick_rows(): pl.pallas_call(functools.partial(pick_kernel, sources, shifts, len(args))...  8.22 us
    ppermute x1, waiting for transfers between devices, on_device(): lax.ppermute(own, 'grid', [(j, (j + 2 * (j % 2) - 1) % n_grid) for j in r...  3.38 us
    ppermute x17, waiting for transfers between devices, hop(): return lax.ppermute(value, 'grid', pairs)  3.2 us
    pallas_call x3, Pallas kernels, last_grams(): pl.pallas_call(functools.partial(last_kernel, shifts), out_shape=[jax.Sha...  3.2 us
    ppermute x1, starting transfers between devices, on_device(): lax.ppermute(own, 'grid', [(j, (j + 2 * (j % 2) - 1) % n_grid) for j in r...  2.7 us
    pallas_call x1, Pallas kernels, transposed_weights(): pl.pallas_call(weights_kernel, out_shape=jax.ShapeDtypeStruct((K, K), BF1...  2.34 us
  transfers between devices with their start and end apart: 18, of which 8 were waited for; matrix products, arithmetic and copies ran while one was open for 0% of the time, Pallas kernels for 22%

profile of v16, /device:TPU:32, one launch (start us, length us, event | category | flops | bytes accessed | tf_op | source)
XLA Modules:
  0.0 65.0 jit_solution(3127911064665411131)
XLA Ops:
  0.0 1.8 %shard_map.55 = (bf16[272,512]{1,0:T(8,128)(2,1)S(1)}, bf16[272,512]{1,0:T(8,128)(2,1)S(1)}, bf16[544,512]{1,0:T(8,128)(2,1)S(1)}) custom-call(bf16[2048,128]{1,0:T(8,128)(2,1)} %departures.1, f32[2048]{0:T(1024)} %innovation.1, f32[2048]{0:T(1024)} %obs_weight.1, s32[64,256]{1,0:T(8,128)} %bitcast.3), custom_call_target="tpu_custom_call" | custom-call | flops 2000000000 | bytes 100000 | tf_op jit(solution)/shard_map/pallas_call | solution.py:122
  1.8 1.6 %collective-permute-start = (bf16[272,512]{1,0:T(8,128)(2,1)S(1)}, bf16[272,512]{1,0:T(8,128)(2,1)S(1)}, u32[]{:S(2)}, u32[]{:S(2)}) collective-permute-start(bf16[272,512]{1,0:T(8,128)(2,1)S(1)} %get-tuple-element.70), channel_id=1, source_target_pairs={{0,2},{1,3},{2,4},{3,5},{4,6},{5,7},{6,0},{7,1},{8,10},{9,11},{10,... | collective-permute-start | bytes 835592 | tf_op jit(solution)/shard_map/ppermute | solution.py:42
  3.3 1.7 %collective-permute-start.2 = (bf16[272,512]{1,0:T(8,128)(2,1)S(1)}, bf16[272,512]{1,0:T(8,128)(2,1)S(1)}, u32[]{:S(2)}, u32[]{:S(2)}) collective-permute-start(bf16[272,512]{1,0:T(8,128)(2,1)S(1)} %get-tuple-element.69), channel_id=1, source_target_pairs={{0,6},{1,7},{2,0},{3,1},{4,2},{5,3},{6,4},{7,5},{8,14},{9,15},{10,... | collective-permute-start | bytes 835592 | tf_op jit(solution)/shard_map/ppermute | solution.py:42
  5.1 0.0 collective-permute-start.1
  5.1 1.2 %shard_map.57 = (f32[24,256]{1,0:T(8,128)S(1)}, bf16[24,128,256]{2,1,0:T(8,128)(2,1)S(1)}, bf16[24,256,256]{2,1,0:T(8,128)(2,1)S(1)}) custom-call(bf16[48,128,128]{2,1,0:T(8,128)(2,1)S(1)} %copy-done), custom_call_target="tpu_custom_call" | custom-call | flops 60000002048 | bytes 100000 | tf_op jit(solution)/shard_map/pallas_call | solution.py:381
  6.3 0.4 collective-permute-start.4
  6.6 3.0 %collective-permute-start.5 = (bf16[272,512]{1,0:T(8,128)(2,1)S(1)}, bf16[272,512]{1,0:T(8,128)(2,1)S(1)}, u32[]{:S(2)}, u32[]{:S(2)}) collective-permute-start(bf16[272,512]{1,0:T(8,128)(2,1)S(1)} %get-tuple-element.70), channel_id=1, source_target_pairs={{0,6},{1,7},{2,0},{3,1},{4,2},{5,3},{6,4},{7,5},{8,14},{9,15},{10,... | collective-permute-start | bytes 835592 | tf_op jit(solution)/shard_map/ppermute | solution.py:42
  9.6 0.0 collective-permute-done.1.refs_1_
  9.6 2.5 %shard_map.56 = (bf16[8,144,256]{2,1,0:T(8,128)(2,1)S(1)}, bf16[8,144,256]{2,1,0:T(8,128)(2,1)S(1)}) custom-call(bf16[544,512]{1,0:T(8,128)(2,1)S(1)} %get-tuple-element.50.refs_0_, bf16[544,512]{1,0:T(8,128)(2,1)S(1)} %collective-permute-done.1.refs_1_), custom_call_target="tpu_custom_call" | custom-call | flops 1000000 | bytes 100000 | tf_op jit(solution)/shard_map/pallas_call | solution.py:176
  12.1 0.1 collective-permute-done.refs_0_.refs_2_
  12.2 0.7 %collective-permute-start.9 = (bf16[272,512]{1,0:T(8,128)(2,1)S(1)}, bf16[272,512]{1,0:T(8,128)(2,1)S(1)}, u32[]{:S(2)}, u32[]{:S(2)}) collective-permute-start(bf16[272,512]{1,0:T(8,128)(2,1)S(1)} %collective-permute-done.refs_0_.refs_2_), channel_id=1, source_target_pairs={{0,2},{1,3},{2,4},{3,5},{4,6},{5,7},{6,0},{7,1},{8,10},{9,11},{10,... | collective-permute-start | bytes 835592 | tf_op jit(solution)/shard_map/ppermute | solution.py:42
  12.9 0.0 collective-permute-done.2.refs_1_.refs_6_
  12.9 2.5 %collective-permute-start.10 = (bf16[272,512]{1,0:T(8,128)(2,1)S(1)}, bf16[272,512]{1,0:T(8,128)(2,1)S(1)}, u32[]{:S(2)}, u32[]{:S(2)}) collective-permute-start(bf16[272,512]{1,0:T(8,128)(2,1)S(1)} %collective-permute-done.2.refs_1_.refs_6_), channel_id=1, source_target_pairs={{0,6},{1,7},{2,0},{3,1},{4,2},{5,3},{6,4},{7,5},{8,14},{9,15},{10,... | collective-permute-start | bytes 835592 | tf_op jit(solution)/shard_map/ppermute | solution.py:42
  15.4 1.1 %shard_map.58 = (bf16[8,144,256]{2,1,0:T(8,128)(2,1)S(1)}, bf16[8,144,256]{2,1,0:T(8,128)(2,1)S(1)}) custom-call(bf16[272,512]{1,0:T(8,128)(2,1)S(1)} %collective-permute-done.refs_0_.refs_2_, bf16[272,512]{1,0:T(8,128)(2,1)S(1)} %collective-permute-done.2.refs_1_.refs_6_), custom_call_target="tpu_custom_call" | custom-call | flops 1000000 | bytes 100000 | tf_op jit(solution)/shard_map/pallas_call | solution.py:176
  16.5 0.1 collective-permute-start.3
  16.6 1.5 %collective-permute-done.4.refs_2_.refs_4_ = bf16[272,512]{1,0:T(8,128)(2,1)S(1)} collective-permute-done((bf16[272,512]{1,0:T(8,128)(2,1)S(1)}, bf16[272,512]{1,0:T(8,128)(2,1)S(1)}, u32[]{:S(2)}, u32[]{:S(2)}) %collective-permute-start.4) | collective-permute-done | bytes 278560 | tf_op jit(solution)/shard_map/ppermute | solution.py:42
  18.2 0.0 collective-permute-start.7
  18.2 0.7 %collective-permute-done.5.refs_3_.refs_8_ = bf16[272,512]{1,0:T(8,128)(2,1)S(1)} collective-permute-done((bf16[272,512]{1,0:T(8,128)(2,1)S(1)}, bf16[272,512]{1,0:T(8,128)(2,1)S(1)}, u32[]{:S(2)}, u32[]{:S(2)}) %collective-permute-start.5) | collective-permute-done | bytes 278560 | tf_op jit(solution)/shard_map/ppermute | solution.py:42
  18.9 1.1 %shard_map.59 = (bf16[8,144,256]{2,1,0:T(8,128)(2,1)S(1)}, bf16[8,144,256]{2,1,0:T(8,128)(2,1)S(1)}) custom-call(bf16[272,512]{1,0:T(8,128)(2,1)S(1)} %collective-permute-done.refs_0_.refs_2_, bf16[272,512]{1,0:T(8,128)(2,1)S(1)} %collective-permute-done.2.refs_1_.refs_6_, bf16[272,512]{1,0:T(8,128)(2,1)S(1)} %collective-permute-done.4.refs_2_.refs_4_, ...), custom_call_target="tpu_custom_call" | custom-call | flops 60000002048 | bytes 100000 | tf_op jit(solution)/shard_map/pallas_call | solution.py:176
  20.0 0.3 collective-permute-start.6
  20.3 0.0 collective-permute-done.3.refs_0_.refs_3_
  20.3 0.5 collective-permute-start.8
  20.8 1.1 %shard_map.60 = (bf16[8,144,256]{2,1,0:T(8,128)(2,1)S(1)}, bf16[8,144,256]{2,1,0:T(8,128)(2,1)S(1)}) custom-call(bf16[272,512]{1,0:T(8,128)(2,1)S(1)} %collective-permute-done.3.refs_0_.refs_3_, bf16[272,512]{1,0:T(8,128)(2,1)S(1)} %collective-permute-done.7.refs_1_.refs_7_), custom_call_target="tpu_custom_call" | custom-call | flops 60000002048 | bytes 100000 | tf_op jit(solution)/shard_map/pallas_call | solution.py:176
  21.9 0.3 collective-permute-done.8.refs_3_.refs_9_
  22.2 1.1 %shard_map.61 = (bf16[8,144,256]{2,1,0:T(8,128)(2,1)S(1)}, bf16[8,144,256]{2,1,0:T(8,128)(2,1)S(1)}) custom-call(bf16[272,512]{1,0:T(8,128)(2,1)S(1)} %collective-permute-done.3.refs_0_.refs_3_, bf16[272,512]{1,0:T(8,128)(2,1)S(1)} %collective-permute-done.7.refs_1_.refs_7_, bf16[272,512]{1,0:T(8,128)(2,1)S(1)} %collective-permute-done.6.refs_2_.refs_5_, ...), custom_call_target="tpu_custom_call" | custom-call | flops 1000000 | bytes 100000 | tf_op jit(solution)/shard_map/pallas_call | solution.py:176
  23.3 0.1 collective-permute-done.10.refs_1_.refs_11_
  23.4 0.2 collective-permute-start.11
  23.6 0.4 collective-permute-start.12
  23.9 1.4 %shard_map.62.refs_14_.same = bf16[8,144,256]{2,1,0:T(8,128)(2,1)S(1)} custom-call(bf16[272,512]{1,0:T(8,128)(2,1)S(1)} %collective-permute-done.9.refs_0_.refs_10_, bf16[272,512]{1,0:T(8,128)(2,1)S(1)} %collective-permute-done.10.refs_1_.refs_11_), custom_call_target="tpu_custom_call" | custom-call | flops 1000000 | bytes 100000 | tf_op jit(solution)/shard_map/pallas_call | solution.py:176
  25.3 0.0 collective-permute-done.11.refs_12_.low
  25.3 0.1 collective-permute-done.12.refs_13_.high
  25.4 1.1 %shard_map.64 = bf16[528,128]{1,0:T(8,128)(2,1)S(1)} custom-call(bf16[272,512]{1,0:T(8,128)(2,1)S(1)} %collective-permute-done.11.refs_12_.low, bf16[272,512]{1,0:T(8,128)(2,1)S(1)} %collective-permute-done.12.refs_13_.high, bf16[8,144,256]{2,1,0:T(8,128)(2,1)S(1)} %shard_map.62.refs_14_.same, bf16[8,144,256]{2,1,0:T(8,128)(2,1)S(1)} %get-tuple-element.62.refs_0_.rest_0_, ...), custom_call_target="tpu_custom_call" | custom-call | flops 1000000000 | bytes 100000 | tf_op jit(solution)/shard_map/pallas_call | solution.py:277
  26.4 3.3 %collective-permute-start.13 = (bf16[528,128]{1,0:T(8,128)(2,1)S(1)}, bf16[528,128]{1,0:T(8,128)(2,1)S(1)}, u32[]{:S(2)}, u32[]{:S(2)}) collective-permute-start(bf16[528,128]{1,0:T(8,128)(2,1)S(1)} %shard_map.64), channel_id=1, source_target_pairs={{0,16},{1,17},{2,18},{3,19},{4,20},{5,21},{6,22},{7,23},{8,24},{9,... | collective-permute-start | bytes 405512 | tf_op jit(solution)/shard_map/ppermute | solution.py:42
  29.7 1.1 %shard_map.65 = bf16[528,128]{1,0:T(8,128)(2,1)S(1)} custom-call(bf16[272,512]{1,0:T(8,128)(2,1)S(1)} %collective-permute-done.11.refs_12_.low, bf16[272,512]{1,0:T(8,128)(2,1)S(1)} %collective-permute-done.12.refs_13_.high, bf16[8,144,256]{2,1,0:T(8,128)(2,1)S(1)} %shard_map.62.refs_14_.same, bf16[8,144,256]{2,1,0:T(8,128)(2,1)S(1)} %get-tuple-element.62.refs_0_.rest_0_, ...), custom_call_target="tpu_custom_call" | custom-call | flops 1000000000 | bytes 100000 | tf_op jit(solution)/shard_map/pallas_call | solution.py:277
  30.8 0.8 %collective-permute-start.14 = (bf16[528,128]{1,0:T(8,128)(2,1)S(1)}, bf16[528,128]{1,0:T(8,128)(2,1)S(1)}, u32[]{:S(2)}, u32[]{:S(2)}) collective-permute-start(bf16[528,128]{1,0:T(8,128)(2,1)S(1)} %shard_map.65), channel_id=1, source_target_pairs={{0,8},{1,9},{2,10},{3,11},{4,12},{5,13},{6,14},{7,15},{8,16},{9,17... | collective-permute-start | bytes 405512 | tf_op jit(solution)/shard_map/ppermute | solution.py:42
  31.6 1.1 %shard_map.66 = bf16[528,128]{1,0:T(8,128)(2,1)S(1)} custom-call(bf16[272,512]{1,0:T(8,128)(2,1)S(1)} %collective-permute-done.11.refs_12_.low, bf16[272,512]{1,0:T(8,128)(2,1)S(1)} %collective-permute-done.12.refs_13_.high, bf16[8,144,256]{2,1,0:T(8,128)(2,1)S(1)} %shard_map.62.refs_14_.same, bf16[8,144,256]{2,1,0:T(8,128)(2,1)S(1)} %get-tuple-element.62.refs_0_.rest_0_, ...), custom_call_target="tpu_custom_call" | custom-call | flops 1000000000 | bytes 100000 | tf_op jit(solution)/shard_map/pallas_call | solution.py:277
  32.6 2.6 %collective-permute-start.15 = (bf16[528,128]{1,0:T(8,128)(2,1)S(1)}, bf16[528,128]{1,0:T(8,128)(2,1)S(1)}, u32[]{:S(2)}, u32[]{:S(2)}) collective-permute-start(bf16[528,128]{1,0:T(8,128)(2,1)S(1)} %shard_map.66), channel_id=1, source_target_pairs={{0,24},{1,25},{2,26},{3,27},{4,28},{5,29},{6,30},{7,31},{8,0},{9,1... | collective-permute-start | bytes 405512 | tf_op jit(solution)/shard_map/ppermute | solution.py:42
  35.3 2.3 %shard_map.63.own = f32[528,128]{1,0:T(8,128)S(1)} custom-call(bf16[8,144,256]{2,1,0:T(8,128)(2,1)S(1)} %get-tuple-element.62.refs_0_.rest_0_, bf16[8,144,256]{2,1,0:T(8,128)(2,1)S(1)} %get-tuple-element.63.refs_1_.rest_1_, bf16[272,512]{1,0:T(8,128)(2,1)S(1)} %collective-permute-done.refs_0_.refs_2_, ...), custom_call_target="tpu_custom_call" | custom-call | flops 1000000000 | bytes 100000 | tf_op jit(solution)/shard_map/pallas_call | solution.py:265
  37.6 0.3 collective-permute-done.15.c
  37.9 0.1 shard_map.67
  37.9 16.3 %all_to_all.5.parts = bf16[8,80,128]{2,1,0:T(8,128)(2,1)S(1)} all-to-all(bf16[8,80,128]{2,1,0:T(8,128)(2,1)S(1)} %shard_map.67), channel_id=1, replica_groups=mesh['obs'=8,'grid'=32] {'obs'}, dimensions={0} | all-to-all | bytes 327680 | tf_op jit(solution)/shard_map/all_to_all | solution.py:518
  54.3 2.3 %shard_map.68.own = bf16[128,128]{1,0:T(8,128)(2,1)S(1)} custom-call(bf16[8,80,128]{2,1,0:T(8,128)(2,1)S(1)} %all_to_all.5.parts), custom_call_target="tpu_custom_call" | custom-call | flops 4000000000 | bytes 100000 | tf_op jit(solution)/shard_map/pallas_call | solution.py:349
  56.6 2.7 %collective-permute-start.16 = (bf16[128,128]{1,0:T(8,128)(2,1)S(1)}, bf16[128,128]{1,0:T(8,128)(2,1)S(1)}, u32[]{:S(2)}, u32[]{:S(2)}) collective-permute-start(bf16[128,128]{1,0:T(8,128)(2,1)S(1)} %shard_map.68.own), channel_id=1, source_target_pairs={{0,31},{1,2},{2,1},{3,4},{4,3},{5,6},{6,5},{7,8},{8,7},{9,10},{10,... | collective-permute-start | bytes 98312 | tf_op jit(solution)/shard_map/ppermute | solution.py:521
  59.3 0.6 shard_map.69.part
  59.9 0.1 collective-permute-start.17
  60.0 3.4 %collective-permute-done.16.beyond = bf16[128,128]{1,0:T(8,128)(2,1)S(1)} collective-permute-done((bf16[128,128]{1,0:T(8,128)(2,1)S(1)}, bf16[128,128]{1,0:T(8,128)(2,1)S(1)}, u32[]{:S(2)}, u32[]{:S(2)}) %collective-permute-start.16) | collective-permute-done | bytes 32800 | tf_op jit(solution)/shard_map/ppermute | solution.py:521
  63.4 0.0 collective-permute-done.17.beside
  63.4 1.4 %shard_map.70 = bf16[48,128,128]{2,1,0:T(8,128)(2,1)} custom-call(bf16[128,128]{1,0:T(8,128)(2,1)S(1)} %collective-permute-done.16.beyond, bf16[128,128]{1,0:T(8,128)(2,1)S(1)} %collective-permute-done.17.beside, f32[24,128,256]{2,1,0:T(8,128)S(1)} %shard_map.69.part, bf16[24,256,256]{2,1,0:T(8,128)(2,1)S(1)} %get-tuple-element.92.sides), custom_call_target="tpu_custom_call" | custom-call | flops 2000000000 | bytes 100000 | tf_op jit(solution)/shard_map/pallas_call | solution.py:437
  (7 shorter events, 0.0 us)
Async XLA Ops:
  0.0 5.1 %copy-start = (bf16[48,128,128]{2,1,0:T(8,128)(2,1)S(1)}, bf16[48,128,128]{2,1,0:T(8,128)(2,1)}, u32[]{:S(2)}) copy-start(bf16[48,128,128]{2,1,0:T(8,128)(2,1)} %state.1) | copy-start | bytes 4718596
  1.8 10.4 %collective-permute-start = (bf16[272,512]{1,0:T(8,128)(2,1)S(1)}, bf16[272,512]{1,0:T(8,128)(2,1)S(1)}, u32[]{:S(2)}, u32[]{:S(2)}) collective-permute-start(bf16[272,512]{1,0:T(8,128)(2,1)S(1)} %get-tuple-element.70), channel_id=1, source_target_pairs={{0,2},{1,3},{2,4},{3,5},{4,6},{5,7},{6,0},{7,1},{8,10},{9,11},{10,... | collective-permute-start | bytes 835592 | tf_op jit(solution)/shard_map/ppermute | solution.py:42
  3.3 9.6 %collective-permute-start.2 = (bf16[272,512]{1,0:T(8,128)(2,1)S(1)}, bf16[272,512]{1,0:T(8,128)(2,1)S(1)}, u32[]{:S(2)}, u32[]{:S(2)}) collective-permute-start(bf16[272,512]{1,0:T(8,128)(2,1)S(1)} %get-tuple-element.69), channel_id=1, source_target_pairs={{0,6},{1,7},{2,0},{3,1},{4,2},{5,3},{6,4},{7,5},{8,14},{9,15},{10,... | collective-permute-start | bytes 835592 | tf_op jit(solution)/shard_map/ppermute | solution.py:42
  5.1 4.5 %collective-permute-start.1 = (bf16[544,512]{1,0:T(8,128)(2,1)S(1)}, bf16[544,512]{1,0:T(8,128)(2,1)S(1)}, u32[]{:S(2)}, u32[]{:S(2)}) collective-permute-start(bf16[544,512]{1,0:T(8,128)(2,1)S(1)} %get-tuple-element.50.refs_0_), channel_id=1, source_target_pairs={{0,1},{1,0},{2,3},{3,2},{4,5},{5,4},{6,7},{7,6},{8,9},{9,8},{10,11... | collective-permute-start | bytes 1671176 | tf_op jit(solution)/shard_map/ppermute | solution.py:42
  6.3 11.9 %collective-permute-start.4 = (bf16[272,512]{1,0:T(8,128)(2,1)S(1)}, bf16[272,512]{1,0:T(8,128)(2,1)S(1)}, u32[]{:S(2)}, u32[]{:S(2)}) collective-permute-start(bf16[272,512]{1,0:T(8,128)(2,1)S(1)} %get-tuple-element.69), channel_id=1, source_target_pairs={{0,2},{1,3},{2,4},{3,5},{4,6},{5,7},{6,0},{7,1},{8,10},{9,11},{10,... | collective-permute-start | bytes 835592 | tf_op jit(solution)/shard_map/ppermute | solution.py:42
  6.6 12.3 %collective-permute-start.5 = (bf16[272,512]{1,0:T(8,128)(2,1)S(1)}, bf16[272,512]{1,0:T(8,128)(2,1)S(1)}, u32[]{:S(2)}, u32[]{:S(2)}) collective-permute-start(bf16[272,512]{1,0:T(8,128)(2,1)S(1)} %get-tuple-element.70), channel_id=1, source_target_pairs={{0,6},{1,7},{2,0},{3,1},{4,2},{5,3},{6,4},{7,5},{8,14},{9,15},{10,... | collective-permute-start | bytes 835592 | tf_op jit(solution)/shard_map/ppermute | solution.py:42
  12.2 11.2 %collective-permute-start.9 = (bf16[272,512]{1,0:T(8,128)(2,1)S(1)}, bf16[272,512]{1,0:T(8,128)(2,1)S(1)}, u32[]{:S(2)}, u32[]{:S(2)}) collective-permute-start(bf16[272,512]{1,0:T(8,128)(2,1)S(1)} %collective-permute-done.refs_0_.refs_2_), channel_id=1, source_target_pairs={{0,2},{1,3},{2,4},{3,5},{4,6},{5,7},{6,0},{7,1},{8,10},{9,11},{10,... | collective-permute-start | bytes 835592 | tf_op jit(solution)/shard_map/ppermute | solution.py:42
  12.9 10.5 %collective-permute-start.10 = (bf16[272,512]{1,0:T(8,128)(2,1)S(1)}, bf16[272,512]{1,0:T(8,128)(2,1)S(1)}, u32[]{:S(2)}, u32[]{:S(2)}) collective-permute-start(bf16[272,512]{1,0:T(8,128)(2,1)S(1)} %collective-permute-done.2.refs_1_.refs_6_), channel_id=1, source_target_pairs={{0,6},{1,7},{2,0},{3,1},{4,2},{5,3},{6,4},{7,5},{8,14},{9,15},{10,... | collective-permute-start | bytes 835592 | tf_op jit(solution)/shard_map/ppermute | solution.py:42
  16.5 3.8 %collective-permute-start.3 = (bf16[272,512]{1,0:T(8,128)(2,1)S(1)}, bf16[272,512]{1,0:T(8,128)(2,1)S(1)}, u32[]{:S(2)}, u32[]{:S(2)}) collective-permute-start(bf16[272,512]{1,0:T(8,128)(2,1)S(1)} %collective-permute-done.refs_0_.refs_2_), channel_id=1, source_target_pairs={{0,1},{1,0},{2,3},{3,2},{4,5},{5,4},{6,7},{7,6},{8,9},{9,8},{10,11... | collective-permute-start | bytes 835592 | tf_op jit(solution)/shard_map/ppermute | solution.py:42
  18.2 2.6 %collective-permute-start.7 = (bf16[272,512]{1,0:T(8,128)(2,1)S(1)}, bf16[272,512]{1,0:T(8,128)(2,1)S(1)}, u32[]{:S(2)}, u32[]{:S(2)}) collective-permute-start(bf16[272,512]{1,0:T(8,128)(2,1)S(1)} %collective-permute-done.2.refs_1_.refs_6_), channel_id=1, source_target_pairs={{0,1},{1,0},{2,3},{3,2},{4,5},{5,4},{6,7},{7,6},{8,9},{9,8},{10,11... | collective-permute-start | bytes 835592 | tf_op jit(solution)/shard_map/ppermute | solution.py:42
  20.0 1.9 %collective-permute-start.6 = (bf16[272,512]{1,0:T(8,128)(2,1)S(1)}, bf16[272,512]{1,0:T(8,128)(2,1)S(1)}, u32[]{:S(2)}, u32[]{:S(2)}) collective-permute-start(bf16[272,512]{1,0:T(8,128)(2,1)S(1)} %collective-permute-done.4.refs_2_.refs_4_), channel_id=1, source_target_pairs={{0,1},{1,0},{2,3},{3,2},{4,5},{5,4},{6,7},{7,6},{8,9},{9,8},{10,11... | collective-permute-start | bytes 835592 | tf_op jit(solution)/shard_map/ppermute | solution.py:42
  20.3 1.9 %collective-permute-start.8 = (bf16[272,512]{1,0:T(8,128)(2,1)S(1)}, bf16[272,512]{1,0:T(8,128)(2,1)S(1)}, u32[]{:S(2)}, u32[]{:S(2)}) collective-permute-start(bf16[272,512]{1,0:T(8,128)(2,1)S(1)} %collective-permute-done.5.refs_3_.refs_8_), channel_id=1, source_target_pairs={{0,1},{1,0},{2,3},{3,2},{4,5},{5,4},{6,7},{7,6},{8,9},{9,8},{10,11... | collective-permute-start | bytes 835592 | tf_op jit(solution)/shard_map/ppermute | solution.py:42
  23.4 1.9 %collective-permute-start.11 = (bf16[272,512]{1,0:T(8,128)(2,1)S(1)}, bf16[272,512]{1,0:T(8,128)(2,1)S(1)}, u32[]{:S(2)}, u32[]{:S(2)}) collective-permute-start(bf16[272,512]{1,0:T(8,128)(2,1)S(1)} %collective-permute-done.9.refs_0_.refs_10_), channel_id=1, source_target_pairs={{0,1},{1,0},{2,3},{3,2},{4,5},{5,4},{6,7},{7,6},{8,9},{9,8},{10,11... | collective-permute-start | bytes 835592 | tf_op jit(solution)/shard_map/ppermute | solution.py:42
  23.6 1.8 %collective-permute-start.12 = (bf16[272,512]{1,0:T(8,128)(2,1)S(1)}, bf16[272,512]{1,0:T(8,128)(2,1)S(1)}, u32[]{:S(2)}, u32[]{:S(2)}) collective-permute-start(bf16[272,512]{1,0:T(8,128)(2,1)S(1)} %collective-permute-done.10.refs_1_.refs_11_), channel_id=1, source_target_pairs={{0,1},{1,0},{2,3},{3,2},{4,5},{5,4},{6,7},{7,6},{8,9},{9,8},{10,11... | collective-permute-start | bytes 835592 | tf_op jit(solution)/shard_map/ppermute | solution.py:42
  26.4 11.1 %collective-permute-start.13 = (bf16[528,128]{1,0:T(8,128)(2,1)S(1)}, bf16[528,128]{1,0:T(8,128)(2,1)S(1)}, u32[]{:S(2)}, u32[]{:S(2)}) collective-permute-start(bf16[528,128]{1,0:T(8,128)(2,1)S(1)} %shard_map.64), channel_id=1, source_target_pairs={{0,16},{1,17},{2,18},{3,19},{4,20},{5,21},{6,22},{7,23},{8,24},{9,... | collective-permute-start | bytes 405512 | tf_op jit(solution)/shard_map/ppermute | solution.py:42
  30.8 6.8 %collective-permute-start.14 = (bf16[528,128]{1,0:T(8,128)(2,1)S(1)}, bf16[528,128]{1,0:T(8,128)(2,1)S(1)}, u32[]{:S(2)}, u32[]{:S(2)}) collective-permute-start(bf16[528,128]{1,0:T(8,128)(2,1)S(1)} %shard_map.65), channel_id=1, source_target_pairs={{0,8},{1,9},{2,10},{3,11},{4,12},{5,13},{6,14},{7,15},{8,16},{9,17... | collective-permute-start | bytes 405512 | tf_op jit(solution)/shard_map/ppermute | solution.py:42
  32.6 5.2 %collective-permute-start.15 = (bf16[528,128]{1,0:T(8,128)(2,1)S(1)}, bf16[528,128]{1,0:T(8,128)(2,1)S(1)}, u32[]{:S(2)}, u32[]{:S(2)}) collective-permute-start(bf16[528,128]{1,0:T(8,128)(2,1)S(1)} %shard_map.66), channel_id=1, source_target_pairs={{0,24},{1,25},{2,26},{3,27},{4,28},{5,29},{6,30},{7,31},{8,0},{9,1... | collective-permute-start | bytes 405512 | tf_op jit(solution)/shard_map/ppermute | solution.py:42
  56.6 6.7 %collective-permute-start.16 = (bf16[128,128]{1,0:T(8,128)(2,1)S(1)}, bf16[128,128]{1,0:T(8,128)(2,1)S(1)}, u32[]{:S(2)}, u32[]{:S(2)}) collective-permute-start(bf16[128,128]{1,0:T(8,128)(2,1)S(1)} %shard_map.68.own), channel_id=1, source_target_pairs={{0,31},{1,2},{2,1},{3,4},{4,3},{5,6},{6,5},{7,8},{8,7},{9,10},{10,... | collective-permute-start | bytes 98312 | tf_op jit(solution)/shard_map/ppermute | solution.py:521
  59.9 3.5 %collective-permute-start.17 = (bf16[128,128]{1,0:T(8,128)(2,1)S(1)}, bf16[128,128]{1,0:T(8,128)(2,1)S(1)}, u32[]{:S(2)}, u32[]{:S(2)}) collective-permute-start(bf16[128,128]{1,0:T(8,128)(2,1)S(1)} %shard_map.68.own), channel_id=1, source_target_pairs={{0,1},{1,0},{2,3},{3,2},{4,5},{5,4},{6,7},{7,6},{8,9},{9,8},{10,11... | collective-permute-start | bytes 98312 | tf_op jit(solution)/shard_map/ppermute | solution.py:42

commit v17 on v15

--- a/solution.py
+++ b/solution.py
@@ -371,8 +371,7 @@
             rounded = (values - average).astype(BF16)
             perturb[pair, :, span] = rounded
             for side, coef in enumerate(column_coefs()):
-                scaled = coef[:, span] * rounded.astype(F32)
-                sides[pair, side * K : (side + 1) * K, span] = scaled.astype(BF16)
+                sides[pair, side * K : (side + 1) * K, span] = coef[:, span].astype(BF16) * rounded
 
 
 def perturbations(state):

time: 65.9 us -> 65.9 us (level)
  transfers between devices with their start and end apart: 18 -> 18, of which waited for: 6 -> 7; matrix products, arithmetic and copies ran while one was open for 0% -> 0% of each run, Pallas kernels for 22% -> 22%
where the time goes in v17:
time: 65.9 us; the launch traced here: 65 us
  Pallas kernels  21 us (32%)
  starting transfers between devices  20.6 us (31%)
  blocking collectives  16.3 us (25%)
  waiting for transfers between devices  6.72 us (10%)
    ppermute x17, starting transfers between devices, hop(): return lax.ppermute(value, 'grid', pairs)  18 us
    all_to_all x1, blocking collectives, on_device(): parts = lax.all_to_all(parts, 'obs', 0, 0, tiled=True)  16.3 us
    pallas_call x6, Pallas kernels, pick_rows(): pl.pallas_call(functools.partial(pick_kernel, sources, shifts, len(args))...  8.05 us
    ppermute x1, waiting for transfers between devices, on_device(): lax.ppermute(own, 'grid', [(j, (j + 2 * (j % 2) - 1) % n_grid) for j in r...  3.44 us
    ppermute x17, waiting for transfers between devices, hop(): return lax.ppermute(value, 'grid', pairs)  3.29 us
    pallas_call x3, Pallas kernels, last_grams(): pl.pallas_call(functools.partial(last_kernel, shifts), out_shape=[jax.Sha...  3.2 us
    ppermute x1, starting transfers between devices, on_device(): lax.ppermute(own, 'grid', [(j, (j + 2 * (j % 2) - 1) % n_grid) for j in r...  2.64 us
    pallas_call x1, Pallas kernels, own_grams(): pl.pallas_call(functools.partial(own_grams_kernel, sources), out_shape=ja...  2.6 us
  transfers between devices with their start and end apart: 18, of which 7 were waited for; matrix products, arithmetic and copies ran while one was open for 0% of the time, Pallas kernels for 22%

profile of v17, /device:TPU:32, one launch (start us, length us, event | category | flops | bytes accessed | tf_op | source)
XLA Modules:
  0.0 65.0 jit_solution(6725793847907896508)
XLA Ops:
  0.0 1.8 %shard_map.55 = (bf16[272,512]{1,0:T(8,128)(2,1)S(1)}, bf16[272,512]{1,0:T(8,128)(2,1)S(1)}, bf16[544,512]{1,0:T(8,128)(2,1)S(1)}) custom-call(bf16[2048,128]{1,0:T(8,128)(2,1)} %departures.1, f32[2048]{0:T(1024)} %innovation.1, f32[2048]{0:T(1024)} %obs_weight.1, s32[64,256]{1,0:T(8,128)} %bitcast.3), custom_call_target="tpu_custom_call" | custom-call | flops 2000000000 | bytes 100000 | tf_op jit(solution)/shard_map/pallas_call | solution.py:122
  1.8 1.6 %collective-permute-start = (bf16[272,512]{1,0:T(8,128)(2,1)S(1)}, bf16[272,512]{1,0:T(8,128)(2,1)S(1)}, u32[]{:S(2)}, u32[]{:S(2)}) collective-permute-start(bf16[272,512]{1,0:T(8,128)(2,1)S(1)} %get-tuple-element.70), channel_id=1, source_target_pairs={{0,2},{1,3},{2,4},{3,5},{4,6},{5,7},{6,0},{7,1},{8,10},{9,11},{10,... | collective-permute-start | bytes 835592 | tf_op jit(solution)/shard_map/ppermute | solution.py:42
  3.3 1.7 %collective-permute-start.2 = (bf16[272,512]{1,0:T(8,128)(2,1)S(1)}, bf16[272,512]{1,0:T(8,128)(2,1)S(1)}, u32[]{:S(2)}, u32[]{:S(2)}) collective-permute-start(bf16[272,512]{1,0:T(8,128)(2,1)S(1)} %get-tuple-element.69), channel_id=1, source_target_pairs={{0,6},{1,7},{2,0},{3,1},{4,2},{5,3},{6,4},{7,5},{8,14},{9,15},{10,... | collective-permute-start | bytes 835592 | tf_op jit(solution)/shard_map/ppermute | solution.py:42
  5.1 0.0 collective-permute-start.1
  5.1 1.0 %shard_map.57 = (f32[24,256]{1,0:T(8,128)S(1)}, bf16[24,128,256]{2,1,0:T(8,128)(2,1)S(1)}, bf16[24,256,256]{2,1,0:T(8,128)(2,1)S(1)}) custom-call(bf16[48,128,128]{2,1,0:T(8,128)(2,1)S(1)} %copy-done), custom_call_target="tpu_custom_call" | custom-call | flops 60000002048 | bytes 100000 | tf_op jit(solution)/shard_map/pallas_call | solution.py:379
  6.1 0.4 collective-permute-start.4
  6.4 3.0 %collective-permute-start.5 = (bf16[272,512]{1,0:T(8,128)(2,1)S(1)}, bf16[272,512]{1,0:T(8,128)(2,1)S(1)}, u32[]{:S(2)}, u32[]{:S(2)}) collective-permute-start(bf16[272,512]{1,0:T(8,128)(2,1)S(1)} %get-tuple-element.70), channel_id=1, source_target_pairs={{0,6},{1,7},{2,0},{3,1},{4,2},{5,3},{6,4},{7,5},{8,14},{9,15},{10,... | collective-permute-start | bytes 835592 | tf_op jit(solution)/shard_map/ppermute | solution.py:42
  9.4 0.0 collective-permute-done.1.refs_1_
  9.4 2.6 %shard_map.56 = (bf16[8,144,256]{2,1,0:T(8,128)(2,1)S(1)}, bf16[8,144,256]{2,1,0:T(8,128)(2,1)S(1)}) custom-call(bf16[544,512]{1,0:T(8,128)(2,1)S(1)} %get-tuple-element.50.refs_0_, bf16[544,512]{1,0:T(8,128)(2,1)S(1)} %collective-permute-done.1.refs_1_), custom_call_target="tpu_custom_call" | custom-call | flops 1000000 | bytes 100000 | tf_op jit(solution)/shard_map/pallas_call | solution.py:176
  12.0 0.4 collective-permute-done.refs_0_.refs_2_
  12.4 0.5 collective-permute-start.9
  12.9 0.0 collective-permute-done.2.refs_1_.refs_6_
  12.9 2.7 %collective-permute-start.10 = (bf16[272,512]{1,0:T(8,128)(2,1)S(1)}, bf16[272,512]{1,0:T(8,128)(2,1)S(1)}, u32[]{:S(2)}, u32[]{:S(2)}) collective-permute-start(bf16[272,512]{1,0:T(8,128)(2,1)S(1)} %collective-permute-done.2.refs_1_.refs_6_), channel_id=1, source_target_pairs={{0,6},{1,7},{2,0},{3,1},{4,2},{5,3},{6,4},{7,5},{8,14},{9,15},{10,... | collective-permute-start | bytes 835592 | tf_op jit(solution)/shard_map/ppermute | solution.py:42
  15.6 1.1 %shard_map.58 = (bf16[8,144,256]{2,1,0:T(8,128)(2,1)S(1)}, bf16[8,144,256]{2,1,0:T(8,128)(2,1)S(1)}) custom-call(bf16[272,512]{1,0:T(8,128)(2,1)S(1)} %collective-permute-done.refs_0_.refs_2_, bf16[272,512]{1,0:T(8,128)(2,1)S(1)} %collective-permute-done.2.refs_1_.refs_6_), custom_call_target="tpu_custom_call" | custom-call | flops 1000000 | bytes 100000 | tf_op jit(solution)/shard_map/pallas_call | solution.py:176
  16.7 0.1 collective-permute-start.3
  16.8 1.5 %collective-permute-done.4.refs_2_.refs_4_ = bf16[272,512]{1,0:T(8,128)(2,1)S(1)} collective-permute-done((bf16[272,512]{1,0:T(8,128)(2,1)S(1)}, bf16[272,512]{1,0:T(8,128)(2,1)S(1)}, u32[]{:S(2)}, u32[]{:S(2)}) %collective-permute-start.4) | collective-permute-done | bytes 278560 | tf_op jit(solution)/shard_map/ppermute | solution.py:42
  18.3 0.0 collective-permute-start.7
  18.3 0.5 collective-permute-done.5.refs_3_.refs_8_
  18.9 1.1 %shard_map.59 = (bf16[8,144,256]{2,1,0:T(8,128)(2,1)S(1)}, bf16[8,144,256]{2,1,0:T(8,128)(2,1)S(1)}) custom-call(bf16[272,512]{1,0:T(8,128)(2,1)S(1)} %collective-permute-done.refs_0_.refs_2_, bf16[272,512]{1,0:T(8,128)(2,1)S(1)} %collective-permute-done.2.refs_1_.refs_6_, bf16[272,512]{1,0:T(8,128)(2,1)S(1)} %collective-permute-done.4.refs_2_.refs_4_, ...), custom_call_target="tpu_custom_call" | custom-call | flops 60000002048 | bytes 100000 | tf_op jit(solution)/shard_map/pallas_call | solution.py:176
  20.0 0.3 collective-permute-start.6
  20.3 0.5 collective-permute-start.8
  20.8 0.0 collective-permute-done.7.refs_1_.refs_7_
  20.8 1.1 %shard_map.60 = (bf16[8,144,256]{2,1,0:T(8,128)(2,1)S(1)}, bf16[8,144,256]{2,1,0:T(8,128)(2,1)S(1)}) custom-call(bf16[272,512]{1,0:T(8,128)(2,1)S(1)} %collective-permute-done.3.refs_0_.refs_3_, bf16[272,512]{1,0:T(8,128)(2,1)S(1)} %collective-permute-done.7.refs_1_.refs_7_), custom_call_target="tpu_custom_call" | custom-call | flops 60000002048 | bytes 100000 | tf_op jit(solution)/shard_map/pallas_call | solution.py:176
  21.9 0.3 collective-permute-done.8.refs_3_.refs_9_
  22.2 1.1 %shard_map.61 = (bf16[8,144,256]{2,1,0:T(8,128)(2,1)S(1)}, bf16[8,144,256]{2,1,0:T(8,128)(2,1)S(1)}) custom-call(bf16[272,512]{1,0:T(8,128)(2,1)S(1)} %collective-permute-done.3.refs_0_.refs_3_, bf16[272,512]{1,0:T(8,128)(2,1)S(1)} %collective-permute-done.7.refs_1_.refs_7_, bf16[272,512]{1,0:T(8,128)(2,1)S(1)} %collective-permute-done.6.refs_2_.refs_5_, ...), custom_call_target="tpu_custom_call" | custom-call | flops 1000000 | bytes 100000 | tf_op jit(solution)/shard_map/pallas_call | solution.py:176
  23.3 0.1 collective-permute-done.10.refs_11_.refs_1_
  23.4 0.2 collective-permute-start.11
  23.5 0.4 collective-permute-start.12
  23.9 1.1 %shard_map.63.same = bf16[8,144,256]{2,1,0:T(8,128)(2,1)S(1)} custom-call(bf16[272,512]{1,0:T(8,128)(2,1)S(1)} %collective-permute-done.9.refs_10_.refs_0_, bf16[272,512]{1,0:T(8,128)(2,1)S(1)} %collective-permute-done.10.refs_11_.refs_1_), custom_call_target="tpu_custom_call" | custom-call | flops 1000000 | bytes 100000 | tf_op jit(solution)/shard_map/pallas_call | solution.py:176
  25.0 0.4 collective-permute-done.12.refs_13_.high
  25.4 1.1 %shard_map.64 = bf16[528,128]{1,0:T(8,128)(2,1)S(1)} custom-call(bf16[272,512]{1,0:T(8,128)(2,1)S(1)} %collective-permute-done.11.refs_12_.low, bf16[272,512]{1,0:T(8,128)(2,1)S(1)} %collective-permute-done.12.refs_13_.high, bf16[8,144,256]{2,1,0:T(8,128)(2,1)S(1)} %shard_map.63.same, bf16[8,144,256]{2,1,0:T(8,128)(2,1)S(1)} %get-tuple-element.62.refs_0_.rest_0_, ...), custom_call_target="tpu_custom_call" | custom-call | flops 1000000000 | bytes 100000 | tf_op jit(solution)/shard_map/pallas_call | solution.py:276
  26.4 3.3 %collective-permute-start.13 = (bf16[528,128]{1,0:T(8,128)(2,1)S(1)}, bf16[528,128]{1,0:T(8,128)(2,1)S(1)}, u32[]{:S(2)}, u32[]{:S(2)}) collective-permute-start(bf16[528,128]{1,0:T(8,128)(2,1)S(1)} %shard_map.64), channel_id=1, source_target_pairs={{0,16},{1,17},{2,18},{3,19},{4,20},{5,21},{6,22},{7,23},{8,24},{9,... | collective-permute-start | bytes 405512 | tf_op jit(solution)/shard_map/ppermute | solution.py:42
  29.7 1.1 %shard_map.65 = bf16[528,128]{1,0:T(8,128)(2,1)S(1)} custom-call(bf16[272,512]{1,0:T(8,128)(2,1)S(1)} %collective-permute-done.11.refs_12_.low, bf16[272,512]{1,0:T(8,128)(2,1)S(1)} %collective-permute-done.12.refs_13_.high, bf16[8,144,256]{2,1,0:T(8,128)(2,1)S(1)} %shard_map.63.same, bf16[8,144,256]{2,1,0:T(8,128)(2,1)S(1)} %get-tuple-element.62.refs_0_.rest_0_, ...), custom_call_target="tpu_custom_call" | custom-call | flops 1000000000 | bytes 100000 | tf_op jit(solution)/shard_map/pallas_call | solution.py:276
  30.8 0.8 %collective-permute-start.14 = (bf16[528,128]{1,0:T(8,128)(2,1)S(1)}, bf16[528,128]{1,0:T(8,128)(2,1)S(1)}, u32[]{:S(2)}, u32[]{:S(2)}) collective-permute-start(bf16[528,128]{1,0:T(8,128)(2,1)S(1)} %shard_map.65), channel_id=1, source_target_pairs={{0,8},{1,9},{2,10},{3,11},{4,12},{5,13},{6,14},{7,15},{8,16},{9,17... | collective-permute-start | bytes 405512 | tf_op jit(solution)/shard_map/ppermute | solution.py:42
  31.6 1.1 %shard_map.66 = bf16[528,128]{1,0:T(8,128)(2,1)S(1)} custom-call(bf16[272,512]{1,0:T(8,128)(2,1)S(1)} %collective-permute-done.11.refs_12_.low, bf16[272,512]{1,0:T(8,128)(2,1)S(1)} %collective-permute-done.12.refs_13_.high, bf16[8,144,256]{2,1,0:T(8,128)(2,1)S(1)} %shard_map.63.same, bf16[8,144,256]{2,1,0:T(8,128)(2,1)S(1)} %get-tuple-element.62.refs_0_.rest_0_, ...), custom_call_target="tpu_custom_call" | custom-call | flops 1000000000 | bytes 100000 | tf_op jit(solution)/shard_map/pallas_call | solution.py:276
  32.6 2.6 %collective-permute-start.15 = (bf16[528,128]{1,0:T(8,128)(2,1)S(1)}, bf16[528,128]{1,0:T(8,128)(2,1)S(1)}, u32[]{:S(2)}, u32[]{:S(2)}) collective-permute-start(bf16[528,128]{1,0:T(8,128)(2,1)S(1)} %shard_map.66), channel_id=1, source_target_pairs={{0,24},{1,25},{2,26},{3,27},{4,28},{5,29},{6,30},{7,31},{8,0},{9,1... | collective-permute-start | bytes 405512 | tf_op jit(solution)/shard_map/ppermute | solution.py:42
  35.3 2.6 %shard_map.62.own = f32[528,128]{1,0:T(8,128)S(1)} custom-call(bf16[8,144,256]{2,1,0:T(8,128)(2,1)S(1)} %get-tuple-element.62.refs_0_.rest_0_, bf16[8,144,256]{2,1,0:T(8,128)(2,1)S(1)} %get-tuple-element.63.refs_1_.rest_1_, bf16[272,512]{1,0:T(8,128)(2,1)S(1)} %collective-permute-done.refs_0_.refs_2_, ...), custom_call_target="tpu_custom_call" | custom-call | flops 1000000000 | bytes 100000 | tf_op jit(solution)/shard_map/pallas_call | solution.py:264
  37.9 0.0 collective-permute-done.13.a
  37.9 0.0 collective-permute-done.14.b
  37.9 0.1 shard_map.67
  38.0 16.3 %all_to_all.5.parts = bf16[8,80,128]{2,1,0:T(8,128)(2,1)S(1)} all-to-all(bf16[8,80,128]{2,1,0:T(8,128)(2,1)S(1)} %shard_map.67), channel_id=1, replica_groups=mesh['obs'=8,'grid'=32] {'obs'}, dimensions={0} | all-to-all | bytes 327680 | tf_op jit(solution)/shard_map/all_to_all | solution.py:515
  54.3 2.3 %shard_map.68.own = bf16[128,128]{1,0:T(8,128)(2,1)S(1)} custom-call(bf16[8,80,128]{2,1,0:T(8,128)(2,1)S(1)} %all_to_all.5.parts), custom_call_target="tpu_custom_call" | custom-call | flops 4000000000 | bytes 100000 | tf_op jit(solution)/shard_map/pallas_call | solution.py:348
  56.7 2.6 %collective-permute-start.16 = (bf16[128,128]{1,0:T(8,128)(2,1)S(1)}, bf16[128,128]{1,0:T(8,128)(2,1)S(1)}, u32[]{:S(2)}, u32[]{:S(2)}) collective-permute-start(bf16[128,128]{1,0:T(8,128)(2,1)S(1)} %shard_map.68.own), channel_id=1, source_target_pairs={{0,31},{1,2},{2,1},{3,4},{4,3},{5,6},{6,5},{7,8},{8,7},{9,10},{10,... | collective-permute-start | bytes 98312 | tf_op jit(solution)/shard_map/ppermute | solution.py:518
  59.3 0.6 shard_map.69.part
  59.9 0.1 collective-permute-start.17
  60.0 3.4 %collective-permute-done.16.beyond = bf16[128,128]{1,0:T(8,128)(2,1)S(1)} collective-permute-done((bf16[128,128]{1,0:T(8,128)(2,1)S(1)}, bf16[128,128]{1,0:T(8,128)(2,1)S(1)}, u32[]{:S(2)}, u32[]{:S(2)}) %collective-permute-start.16) | collective-permute-done | bytes 32800 | tf_op jit(solution)/shard_map/ppermute | solution.py:518
  63.4 0.0 collective-permute-done.17.beside
  63.4 1.5 %shard_map.70 = bf16[48,128,128]{2,1,0:T(8,128)(2,1)} custom-call(bf16[128,128]{1,0:T(8,128)(2,1)S(1)} %collective-permute-done.16.beyond, bf16[128,128]{1,0:T(8,128)(2,1)S(1)} %collective-permute-done.17.beside, f32[24,128,256]{2,1,0:T(8,128)S(1)} %shard_map.69.part, bf16[24,256,256]{2,1,0:T(8,128)(2,1)S(1)} %get-tuple-element.92.sides), custom_call_target="tpu_custom_call" | custom-call | flops 2000000000 | bytes 100000 | tf_op jit(solution)/shard_map/pallas_call | solution.py:435
  (7 shorter events, 0.0 us)
Async XLA Ops:
  0.0 5.1 %copy-start = (bf16[48,128,128]{2,1,0:T(8,128)(2,1)S(1)}, bf16[48,128,128]{2,1,0:T(8,128)(2,1)}, u32[]{:S(2)}) copy-start(bf16[48,128,128]{2,1,0:T(8,128)(2,1)} %state.1) | copy-start | bytes 4718596
  1.8 10.6 %collective-permute-start = (bf16[272,512]{1,0:T(8,128)(2,1)S(1)}, bf16[272,512]{1,0:T(8,128)(2,1)S(1)}, u32[]{:S(2)}, u32[]{:S(2)}) collective-permute-start(bf16[272,512]{1,0:T(8,128)(2,1)S(1)} %get-tuple-element.70), channel_id=1, source_target_pairs={{0,2},{1,3},{2,4},{3,5},{4,6},{5,7},{6,0},{7,1},{8,10},{9,11},{10,... | collective-permute-start | bytes 835592 | tf_op jit(solution)/shard_map/ppermute | solution.py:42
  3.3 9.6 %collective-permute-start.2 = (bf16[272,512]{1,0:T(8,128)(2,1)S(1)}, bf16[272,512]{1,0:T(8,128)(2,1)S(1)}, u32[]{:S(2)}, u32[]{:S(2)}) collective-permute-start(bf16[272,512]{1,0:T(8,128)(2,1)S(1)} %get-tuple-element.69), channel_id=1, source_target_pairs={{0,6},{1,7},{2,0},{3,1},{4,2},{5,3},{6,4},{7,5},{8,14},{9,15},{10,... | collective-permute-start | bytes 835592 | tf_op jit(solution)/shard_map/ppermute | solution.py:42
  5.1 4.3 %collective-permute-start.1 = (bf16[544,512]{1,0:T(8,128)(2,1)S(1)}, bf16[544,512]{1,0:T(8,128)(2,1)S(1)}, u32[]{:S(2)}, u32[]{:S(2)}) collective-permute-start(bf16[544,512]{1,0:T(8,128)(2,1)S(1)} %get-tuple-element.50.refs_0_), channel_id=1, source_target_pairs={{0,1},{1,0},{2,3},{3,2},{4,5},{5,4},{6,7},{7,6},{8,9},{9,8},{10,11... | collective-permute-start | bytes 1671176 | tf_op jit(solution)/shard_map/ppermute | solution.py:42
  6.1 12.3 %collective-permute-start.4 = (bf16[272,512]{1,0:T(8,128)(2,1)S(1)}, bf16[272,512]{1,0:T(8,128)(2,1)S(1)}, u32[]{:S(2)}, u32[]{:S(2)}) collective-permute-start(bf16[272,512]{1,0:T(8,128)(2,1)S(1)} %get-tuple-element.69), channel_id=1, source_target_pairs={{0,2},{1,3},{2,4},{3,5},{4,6},{5,7},{6,0},{7,1},{8,10},{9,11},{10,... | collective-permute-start | bytes 835592 | tf_op jit(solution)/shard_map/ppermute | solution.py:42
  6.4 12.5 %collective-permute-start.5 = (bf16[272,512]{1,0:T(8,128)(2,1)S(1)}, bf16[272,512]{1,0:T(8,128)(2,1)S(1)}, u32[]{:S(2)}, u32[]{:S(2)}) collective-permute-start(bf16[272,512]{1,0:T(8,128)(2,1)S(1)} %get-tuple-element.70), channel_id=1, source_target_pairs={{0,6},{1,7},{2,0},{3,1},{4,2},{5,3},{6,4},{7,5},{8,14},{9,15},{10,... | collective-permute-start | bytes 835592 | tf_op jit(solution)/shard_map/ppermute | solution.py:42
  12.4 11.0 %collective-permute-start.9 = (bf16[272,512]{1,0:T(8,128)(2,1)S(1)}, bf16[272,512]{1,0:T(8,128)(2,1)S(1)}, u32[]{:S(2)}, u32[]{:S(2)}) collective-permute-start(bf16[272,512]{1,0:T(8,128)(2,1)S(1)} %collective-permute-done.refs_0_.refs_2_), channel_id=1, source_target_pairs={{0,2},{1,3},{2,4},{3,5},{4,6},{5,7},{6,0},{7,1},{8,10},{9,11},{10,... | collective-permute-start | bytes 835592 | tf_op jit(solution)/shard_map/ppermute | solution.py:42
  12.9 10.5 %collective-permute-start.10 = (bf16[272,512]{1,0:T(8,128)(2,1)S(1)}, bf16[272,512]{1,0:T(8,128)(2,1)S(1)}, u32[]{:S(2)}, u32[]{:S(2)}) collective-permute-start(bf16[272,512]{1,0:T(8,128)(2,1)S(1)} %collective-permute-done.2.refs_1_.refs_6_), channel_id=1, source_target_pairs={{0,6},{1,7},{2,0},{3,1},{4,2},{5,3},{6,4},{7,5},{8,14},{9,15},{10,... | collective-permute-start | bytes 835592 | tf_op jit(solution)/shard_map/ppermute | solution.py:42
  16.7 3.5 %collective-permute-start.3 = (bf16[272,512]{1,0:T(8,128)(2,1)S(1)}, bf16[272,512]{1,0:T(8,128)(2,1)S(1)}, u32[]{:S(2)}, u32[]{:S(2)}) collective-permute-start(bf16[272,512]{1,0:T(8,128)(2,1)S(1)} %collective-permute-done.refs_0_.refs_2_), channel_id=1, source_target_pairs={{0,1},{1,0},{2,3},{3,2},{4,5},{5,4},{6,7},{7,6},{8,9},{9,8},{10,11... | collective-permute-start | bytes 835592 | tf_op jit(solution)/shard_map/ppermute | solution.py:42
  18.3 2.4 %collective-permute-start.7 = (bf16[272,512]{1,0:T(8,128)(2,1)S(1)}, bf16[272,512]{1,0:T(8,128)(2,1)S(1)}, u32[]{:S(2)}, u32[]{:S(2)}) collective-permute-start(bf16[272,512]{1,0:T(8,128)(2,1)S(1)} %collective-permute-done.2.refs_1_.refs_6_), channel_id=1, source_target_pairs={{0,1},{1,0},{2,3},{3,2},{4,5},{5,4},{6,7},{7,6},{8,9},{9,8},{10,11... | collective-permute-start | bytes 835592 | tf_op jit(solution)/shard_map/ppermute | solution.py:42
  20.0 1.9 %collective-permute-start.6 = (bf16[272,512]{1,0:T(8,128)(2,1)S(1)}, bf16[272,512]{1,0:T(8,128)(2,1)S(1)}, u32[]{:S(2)}, u32[]{:S(2)}) collective-permute-start(bf16[272,512]{1,0:T(8,128)(2,1)S(1)} %collective-permute-done.4.refs_2_.refs_4_), channel_id=1, source_target_pairs={{0,1},{1,0},{2,3},{3,2},{4,5},{5,4},{6,7},{7,6},{8,9},{9,8},{10,11... | collective-permute-start | bytes 835592 | tf_op jit(solution)/shard_map/ppermute | solution.py:42
  20.3 1.9 %collective-permute-start.8 = (bf16[272,512]{1,0:T(8,128)(2,1)S(1)}, bf16[272,512]{1,0:T(8,128)(2,1)S(1)}, u32[]{:S(2)}, u32[]{:S(2)}) collective-permute-start(bf16[272,512]{1,0:T(8,128)(2,1)S(1)} %collective-permute-done.5.refs_3_.refs_8_), channel_id=1, source_target_pairs={{0,1},{1,0},{2,3},{3,2},{4,5},{5,4},{6,7},{7,6},{8,9},{9,8},{10,11... | collective-permute-start | bytes 835592 | tf_op jit(solution)/shard_map/ppermute | solution.py:42
  23.4 1.6 %collective-permute-start.11 = (bf16[272,512]{1,0:T(8,128)(2,1)S(1)}, bf16[272,512]{1,0:T(8,128)(2,1)S(1)}, u32[]{:S(2)}, u32[]{:S(2)}) collective-permute-start(bf16[272,512]{1,0:T(8,128)(2,1)S(1)} %collective-permute-done.9.refs_10_.refs_0_), channel_id=1, source_target_pairs={{0,1},{1,0},{2,3},{3,2},{4,5},{5,4},{6,7},{7,6},{8,9},{9,8},{10,11... | collective-permute-start | bytes 835592 | tf_op jit(solution)/shard_map/ppermute | solution.py:42
  23.5 1.8 %collective-permute-start.12 = (bf16[272,512]{1,0:T(8,128)(2,1)S(1)}, bf16[272,512]{1,0:T(8,128)(2,1)S(1)}, u32[]{:S(2)}, u32[]{:S(2)}) collective-permute-start(bf16[272,512]{1,0:T(8,128)(2,1)S(1)} %collective-permute-done.10.refs_11_.refs_1_), channel_id=1, source_target_pairs={{0,1},{1,0},{2,3},{3,2},{4,5},{5,4},{6,7},{7,6},{8,9},{9,8},{10,11... | collective-permute-start | bytes 835592 | tf_op jit(solution)/shard_map/ppermute | solution.py:42
  26.4 11.4 %collective-permute-start.13 = (bf16[528,128]{1,0:T(8,128)(2,1)S(1)}, bf16[528,128]{1,0:T(8,128)(2,1)S(1)}, u32[]{:S(2)}, u32[]{:S(2)}) collective-permute-start(bf16[528,128]{1,0:T(8,128)(2,1)S(1)} %shard_map.64), channel_id=1, source_target_pairs={{0,16},{1,17},{2,18},{3,19},{4,20},{5,21},{6,22},{7,23},{8,24},{9,... | collective-permute-start | bytes 405512 | tf_op jit(solution)/shard_map/ppermute | solution.py:42
  30.8 7.1 %collective-permute-start.14 = (bf16[528,128]{1,0:T(8,128)(2,1)S(1)}, bf16[528,128]{1,0:T(8,128)(2,1)S(1)}, u32[]{:S(2)}, u32[]{:S(2)}) collective-permute-start(bf16[528,128]{1,0:T(8,128)(2,1)S(1)} %shard_map.65), channel_id=1, source_target_pairs={{0,8},{1,9},{2,10},{3,11},{4,12},{5,13},{6,14},{7,15},{8,16},{9,17... | collective-permute-start | bytes 405512 | tf_op jit(solution)/shard_map/ppermute | solution.py:42
  32.6 5.3 %collective-permute-start.15 = (bf16[528,128]{1,0:T(8,128)(2,1)S(1)}, bf16[528,128]{1,0:T(8,128)(2,1)S(1)}, u32[]{:S(2)}, u32[]{:S(2)}) collective-permute-start(bf16[528,128]{1,0:T(8,128)(2,1)S(1)} %shard_map.66), channel_id=1, source_target_pairs={{0,24},{1,25},{2,26},{3,27},{4,28},{5,29},{6,30},{7,31},{8,0},{9,1... | collective-permute-start | bytes 405512 | tf_op jit(solution)/shard_map/ppermute | solution.py:42
  56.7 6.7 %collective-permute-start.16 = (bf16[128,128]{1,0:T(8,128)(2,1)S(1)}, bf16[128,128]{1,0:T(8,128)(2,1)S(1)}, u32[]{:S(2)}, u32[]{:S(2)}) collective-permute-start(bf16[128,128]{1,0:T(8,128)(2,1)S(1)} %shard_map.68.own), channel_id=1, source_target_pairs={{0,31},{1,2},{2,1},{3,4},{4,3},{5,6},{6,5},{7,8},{8,7},{9,10},{10,... | collective-permute-start | bytes 98312 | tf_op jit(solution)/shard_map/ppermute | solution.py:518
  59.9 3.5 %collective-permute-start.17 = (bf16[128,128]{1,0:T(8,128)(2,1)S(1)}, bf16[128,128]{1,0:T(8,128)(2,1)S(1)}, u32[]{:S(2)}, u32[]{:S(2)}) collective-permute-start(bf16[128,128]{1,0:T(8,128)(2,1)S(1)} %shard_map.68.own), channel_id=1, source_target_pairs={{0,1},{1,0},{2,3},{3,2},{4,5},{5,4},{6,7},{7,6},{8,9},{9,8},{10,11... | collective-permute-start | bytes 98312 | tf_op jit(solution)/shard_map/ppermute | solution.py:42
